TPU v7x, 32 devices: a whole 2x2x4 slice. The times are simulated.
32 devices in a mesh: expert: 16 (over z, y, x), replica: 2 (over core).
Axes of the slice: x: 2, y: 2, z: 4, core: 2. Of those that a mesh axis runs over, the one named last changes fastest.
Arguments:
- cotangent: bfloat16 [4096, 2048], P(('expert', 'replica')), may hold values from -2 to 2
- hidden: bfloat16 [4096, 6, 704], P(('expert', 'replica')), may hold values from -24 to 24
- routes: int32 [4096, 6], P(('expert', 'replica')), may hold values from 0 to 15, all different within a row; in each aligned block of 128 rows (0 to 127, 128 to 255, ...) at most 72 rows name the same one
- numerators: int32 [4096, 6], P(('expert', 'replica')), may hold values from 1 to 1024
- w_down: bfloat16 [16, 704, 2048], P('expert'), may hold values from -0.21875 to 0.21875
Outputs:
- gate_grad: float32 [4096, 6], P(('expert', 'replica'))
- grad_scales: float32 [16, 704, 16], P('expert', 'replica')
- grad_mantissa: float32 [16, 704, 2048], P('expert', 'replica')
Inputs may be any that keep to these rules, and one draw needn't show every extreme that they name: `routes`: no expert is named by more than 72 rows of one device's tokens, a bound that some blocks reach.
All inputs are finite; a program needn't handle non-finite values. Where the computation divides by a largest or mean magnitude, that divisor is 1e-20 or more.
Results may differ from a plain program's by a relative error of at most 0.023.
Values may be sent and summed in bfloat16 or wider, within the bound.
No kernel may reach another device: no remote copies, remote signals or barrier semaphores. Data moves between devices by JAX's collectives and lax.ppermute only.
A program may use at most 64 MiB of HBM per device.

v0:
```python
import jax
import jax.numpy as jnp
from jax import lax
from jax.sharding import PartitionSpec as P

BLOCK = 128


def per_device(cotangent, hidden, routes, numerators, w_down):
    tok_count = cotangent.shape[0]
    model_width = cotangent.shape[1]
    top_k = hidden.shape[1]
    hidden_width = hidden.shape[2]
    experts = lax.axis_size("expert")
    replicas = lax.axis_size("replica")
    slot_count = 3 * tok_count * top_k // (2 * experts)
    routed = tok_count * top_k
    total_slots = experts * slot_count
    flat_routes = routes.reshape(routed)
    one_hot = (flat_routes[:, None] == jnp.arange(experts, dtype=jnp.int32)[None, :]).astype(
        jnp.int32
    )
    before = jnp.cumsum(one_hot, axis=0) - one_hot
    rank_in = jnp.sum(before * one_hot, axis=1)
    slot_of = flat_routes * slot_count + rank_in
    source_row = (
        jnp.full((total_slots,), routed, jnp.int32)
        .at[slot_of]
        .set(jnp.arange(routed, dtype=jnp.int32))
    )
    in_use = source_row < routed
    token_row = jnp.where(in_use, source_row // top_k, tok_count)
    padded_cot = jnp.concatenate([cotangent, jnp.zeros((1, model_width), cotangent.dtype)], axis=0)
    send_cot = padded_cot[token_row].reshape(experts, slot_count, model_width)
    padded_hid = jnp.concatenate(
        [hidden.reshape(routed, hidden_width), jnp.zeros((1, hidden_width), hidden.dtype)], axis=0
    )
    send_hid = padded_hid[source_row].reshape(experts, slot_count, hidden_width)
    weights_flat = numerators.reshape(routed).astype(jnp.float32) / 1024.0
    padded_w = jnp.concatenate([weights_flat, jnp.zeros((1,), jnp.float32)], axis=0)
    send_w = padded_w[source_row].reshape(experts, slot_count)
    matrix = w_down[0]
    contract_width = (((1,), (1,)), ((), ()))
    got_cot, got_w, got_hid = (
        lax.all_to_all(send_cot, "expert", split_axis=0, concat_axis=0, tiled=True),
        lax.all_to_all(
            send_w.astype(jnp.bfloat16), "expert", split_axis=0, concat_axis=0, tiled=True
        ).astype(send_w.dtype),
        lax.all_to_all(send_hid, "expert", split_axis=0, concat_axis=0, tiled=True),
    )
    cot_flat = got_cot.reshape(total_slots, model_width)
    back_proj = lax.dot_general(
        cot_flat, matrix, contract_width, preferred_element_type=jnp.float32
    )
    hid_flat = got_hid.reshape(total_slots, hidden_width)
    gate_local = jnp.sum(back_proj * hid_flat.astype(jnp.float32), axis=1)
    returned = lax.all_to_all(
        gate_local.reshape(experts, slot_count), "expert", split_axis=0, concat_axis=0, tiled=True
    )
    gate_grad = returned.reshape(total_slots)[slot_of].reshape(tok_count, top_k)
    scaled = (got_w.reshape(total_slots)[:, None] * cot_flat.astype(jnp.float32)).astype(
        jnp.bfloat16
    )
    partial_value = lax.dot_general(
        hid_flat, scaled, (((0,), (0,)), ((), ())), preferred_element_type=jnp.float32
    )
    blocks = partial_value.reshape(hidden_width, model_width // BLOCK, BLOCK)
    local_max = jnp.max(jnp.abs(blocks), axis=2)
    scales = lax.pmax(local_max.astype(jnp.bfloat16), "replica").astype(local_max.dtype) + 1e-06
    mantissa = (blocks / scales[:, :, None]).astype(jnp.bfloat16)
    mantissa = (
        lax.optimization_barrier(mantissa).astype(jnp.float32).reshape(hidden_width, model_width)
    )
    share_rows = hidden_width // replicas
    share_start = lax.axis_index("replica") * share_rows
    whole_sum = lax.psum(mantissa.astype(jnp.bfloat16), "replica").astype(jnp.float32)
    summed = lax.dynamic_slice_in_dim(whole_sum, share_start, share_rows, 0)
    scale_share = lax.dynamic_slice_in_dim(scales, share_start, share_rows, 0)
    return (gate_grad, scale_share[None], summed[None])


def solution(mesh):
    return jax.shard_map(
        per_device,
        mesh=mesh,
        in_specs=(
            P(("expert", "replica"), None),
            P(("expert", "replica"), None, None),
            P(("expert", "replica"), None),
            P(("expert", "replica"), None),
            P("expert", None, None),
        ),
        out_specs=(
            P(("expert", "replica"), None),
            P("expert", "replica", None),
            P("expert", "replica", None),
        ),
        check_vma=False,
    )
```

profile of v0, /device:TPU:0, one launch (start us, length us, event | category | flops | bytes accessed | tf_op | source)
XLA Modules:
  0.0 256.5 jit_solution(9666137839444129145)
XLA Ops:
  7.2 0.8 broadcast_multiply_fusion
  8.0 0.8 copy.23
  9.4 1.7 reduce-window.6
  11.5 3.4 %scatter_custom_fusion = s32[1152]{0:T(1024)S(1)} fusion(s32[768]{0:T(1024)S(1)} %fusion.12, s32[768]{0:T(1024)S(1)} %iota.11, s32[]{:T(128)} %constant.20.clone.1), kind=kCustom, calls=%fused_computation.38 | custom fusion | bytes 4612 | tf_op jit(solution)/shard_map/scatter | solution.py:29
  14.9 0.7 convert_multiply_fusion
  16.0 7.3 %gather_fusion.3 = bf16[1152]{0:T(1024)(128)(2,1)S(1)} fusion(bf16[769]{0:T(1024)(128)(2,1)S(1)} %pad_maximum_fusion, s32[2048]{0:T(1024)S(1)} %get-tuple-element.13), kind=kCustom, calls=%fused_computation.3 | custom fusion | bytes 9216 | tf_op jit(solution)/shard_map/gather | solution.py:41
  23.2 0.7 convert_element_type.76
  23.9 8.3 %all-to-all-start.3 = ((bf16[16,1,72]{2,1,0:T(2,128)(2,1)}), bf16[16,1,72]{2,1,0:T(2,128)(2,1)S(1)}, u32[]{:S(2)}, u32[]{:S(2)}) async-start(bf16[16,1,72]{2,1,0:T(2,128)(2,1)} %convert_element_type.76), calls=%async_computation.3 | async-start | bytes 16384 | tf_op jit(solution)/shard_map/all_to_all | solution.py:46
  32.3 1.1 concatenate.9
  33.3 5.9 %gather_fusion = bf16[1152,2048]{1,0:T(8,128)(2,1)} fusion(bf16[129,2048]{1,0:T(8,128)(2,1)S(1)} %concatenate.9, s32[2048]{0:T(1024)S(1)} %get-tuple-element.14), kind=kCustom, calls=%fused_computation | custom fusion | bytes 9441792 | tf_op jit(solution)/shard_map/gather | solution.py:34
  39.5 6.8 %all-to-all-start = ((bf16[16,72,2048]{2,1,0:T(8,128)(2,1)}), bf16[16,72,2048]{2,1,0:T(8,128)(2,1)}, u32[]{:S(2)}, u32[]{:S(2)}) async-start(bf16[16,72,2048]{2,1,0:T(8,128)(2,1)} %bitcast.46), calls=%async_computation | async-start | bytes 9437184 | tf_op jit(solution)/shard_map/all_to_all | solution.py:45
  46.3 2.8 %copy.26 = bf16[128,6,704]{2,1,0:T(8,128)(2,1)} copy(bf16[128,6,704]{0,2,1:T(8,128)(2,1)} %param.6) | data formatting | bytes 2162688 | tf_op args[1]
  49.1 3.3 %reshape.111 = bf16[768,704]{1,0:T(8,128)(2,1)} reshape(bf16[128,6,704]{2,1,0:T(8,128)(2,1)} %copy.26) | data formatting | bytes 2162688 | tf_op jit(solution)/shard_map/reshape | solution.py:36
  52.4 2.4 concatenate.10
  54.8 7.2 %gather_fusion.1 = bf16[1152,704]{1,0:T(8,128)(2,1)} fusion(bf16[769,704]{1,0:T(8,128)(2,1)} %concatenate.10, s32[2048]{0:T(1024)S(1)} %get-tuple-element.13), kind=kCustom, calls=%fused_computation.1 | custom fusion | bytes 3248640 | tf_op jit(solution)/shard_map/gather | solution.py:38
  62.0 72.2 %all-to-all-done = bf16[16,72,2048]{2,1,0:T(8,128)(2,1)} async-done(((bf16[16,72,2048]{2,1,0:T(8,128)(2,1)}), bf16[16,72,2048]{2,1,0:T(8,128)(2,1)}, u32[]{:S(2)}, u32[]{:S(2)}) %all-to-all-start) | async-done | bytes 4718624 | tf_op jit(solution)/shard_map/all_to_all | solution.py:45
  134.2 21.9 %all-to-all-start.1 = ((bf16[16,72,704]{2,1,0:T(8,128)(2,1)}), bf16[16,72,704]{2,1,0:T(8,128)(2,1)}, u32[]{:S(2)}, u32[]{:S(2)}) async-start(bf16[16,72,704]{2,1,0:T(8,128)(2,1)} %bitcast.47), calls=%async_computation.1 | async-start | bytes 3538944 | tf_op jit(solution)/shard_map/all_to_all | solution.py:49
  156.3 6.8 %copy.30 = bf16[1152,2048]{0,1:T(8,128)(2,1)} copy(bf16[1152,2048]{1,0:T(8,128)(2,1)} %bitcast.2) | data formatting | bytes 9437184 | tf_op jit(solution)/shard_map/reshape | solution.py:51
  163.1 5.4 %multiply_convert_fusion = bf16[1152,2048]{0,1:T(8,128)(2,1)} fusion(bf16[1152,2048]{0,1:T(8,128)(2,1)} %copy.30, f32[1152]{0:T(1024)S(1)} %reshape.116), kind=kLoop, calls=%fused_computation.5 | loop fusion | flops 7077888 | bytes 9441792 | tf_op jit(solution)/shard_map/convert_element_type | solution.py:61
  168.5 24.6 %all-to-all-done.1 = bf16[16,72,704]{2,1,0:T(8,128)(2,1)} async-done(((bf16[16,72,704]{2,1,0:T(8,128)(2,1)}), bf16[16,72,704]{2,1,0:T(8,128)(2,1)}, u32[]{:S(2)}, u32[]{:S(2)}) %all-to-all-start.1) | async-done | bytes 1622048 | tf_op jit(solution)/shard_map/all_to_all | solution.py:49
  193.1 9.1 %abs_reduce_fusion = (bf16[704,16]{0,1:T(8,128)(2,1)S(1)}, f32[704,16,128]{2,0,1:T(8,128)}) fusion(bf16[1152,704,1]{1,0,2:T(8,128)(2,1)} %bitcast.6, bf16[16,128,1152]{2,1,0:T(8,128)(2,1)} %bitcast.48), kind=kOutput, calls=%fused_computation.7 | convolution fusion | flops 3326202880 | bytes 12130304 | tf_op jit(solution)/shard_map/dot_general | solution.py:64
  202.2 3.6 %pmax.7 = bf16[704,16]{0,1:T(8,128)(2,1)S(1)} all-reduce(bf16[704,16]{0,1:T(8,128)(2,1)S(1)} %get-tuple-element.11), channel_id=1, replica_groups=mesh['expert'=16,'replica'=2] {'replica'}, use_global_device_ids=true, to_apply=%region_6.7 | all-reduce | flops 11264 | bytes 45056 | tf_op jit(solution)/shard_map/pmax | solution.py:69
  205.8 4.3 %divide_convert_fusion = bf16[704,16,128]{2,0,1:T(8,128)(2,1)S(1)} fusion(f32[704,16,128]{2,0,1:T(8,128)} %get-tuple-element.12, f32[704,16]{0,1:T(8,128)S(1)} %convert_add_fusion), kind=kLoop, calls=%fused_computation.6 | loop fusion | flops 2883584 | bytes 8695808 | tf_op jit(solution)/shard_map/convert_element_type | solution.py:70
  210.1 2.0 copy_bitcast_fusion
  212.1 3.8 %copy.27 = bf16[1152,704]{0,1:T(8,128)(2,1)} copy(bf16[1152,704]{1,0:T(8,128)(2,1)} %bitcast.5) | data formatting | bytes 3244032 | tf_op jit(solution)/shard_map/reshape | solution.py:55
  216.0 6.8 %fusion.1 = f32[1152]{0:T(1024)S(1)} fusion(bf16[1152,704]{0,1:T(8,128)(2,1)} %copy.27, bf16[1152,2048]{1,0:T(8,128)(2,1)} %bitcast.2, bf16[1,704,2048]{2,1,0:T(8,128)(2,1)S(1)} %copy-done), kind=kOutput, calls=%fused_computation.12 | convolution fusion | flops 3324320768 | bytes 9228800 | tf_op jit(solution)/shard_map/dot_general | solution.py:52
  222.7 0.7 all_to_all.18
  223.4 9.1 %all-to-all-start.2 = ((f32[16,1,72]{2,1,0:T(1,128)}), f32[16,1,72]{2,1,0:T(1,128)S(1)}, u32[]{:S(2)}, u32[]{:S(2)}) async-start(f32[16,1,72]{2,1,0:T(1,128)} %all_to_all.18), calls=%async_computation.2 | async-start | bytes 16384 | tf_op jit(solution)/shard_map/all_to_all | solution.py:57
  232.6 0.7 dynamic-slice_bitcast_fusion
  233.2 6.6 %all-to-all-done.2 = f32[16,1,72]{2,1,0:T(1,128)S(1)} async-done(((f32[16,1,72]{2,1,0:T(1,128)}), f32[16,1,72]{2,1,0:T(1,128)S(1)}, u32[]{:S(2)}, u32[]{:S(2)}) %all-to-all-start.2) | async-done | bytes 4640 | tf_op jit(solution)/shard_map/all_to_all | solution.py:57
  241.1 4.5 %gather_fusion.2 = f32[768]{0:T(1024)S(1)} fusion(f32[1152]{0:T(1024)S(1)} %reshape.114, s32[1024]{0:T(1024)S(1)} %pad_clamp_fusion.2), kind=kCustom, calls=%fused_computation.2 | custom fusion | bytes 9216 | tf_op jit(solution)/shard_map/gather | solution.py:60
  246.4 3.3 %convert_bitcast_fusion = f32[1,352,2048]{2,1,0:T(8,128)} fusion(bf16[704,2048]{1,0:T(8,128)(2,1)} %all-reduce.4.cloned.1.call-done, s32[]{:T(128)S(6)} %select_n.36), kind=kLoop, calls=%fused_computation.11 | loop fusion | flops 720896 | bytes 4325380 | tf_op jit(solution)/shard_map/broadcast_in_dim | solution.py:79
  (30 shorter events, 3.6 us)
Async XLA Ops:
  7.2 208.8 %copy-start = (bf16[1,704,2048]{2,1,0:T(8,128)(2,1)S(1)}, bf16[1,704,2048]{2,1,0:T(8,128)(2,1)}, u32[]{:S(2)}) copy-start(bf16[1,704,2048]{2,1,0:T(8,128)(2,1)} %param.9) | copy-start | bytes 8650756
  23.9 15.5 %all-to-all-start.3 = ((bf16[16,1,72]{2,1,0:T(2,128)(2,1)}), bf16[16,1,72]{2,1,0:T(2,128)(2,1)S(1)}, u32[]{:S(2)}, u32[]{:S(2)}) async-start(bf16[16,1,72]{2,1,0:T(2,128)(2,1)} %convert_element_type.76), calls=%async_computation.3 | async-start | bytes 16384 | tf_op jit(solution)/shard_map/all_to_all | solution.py:46
  39.5 94.8 %all-to-all-start = ((bf16[16,72,2048]{2,1,0:T(8,128)(2,1)}), bf16[16,72,2048]{2,1,0:T(8,128)(2,1)}, u32[]{:S(2)}, u32[]{:S(2)}) async-start(bf16[16,72,2048]{2,1,0:T(8,128)(2,1)} %bitcast.46), calls=%async_computation | async-start | bytes 9437184 | tf_op jit(solution)/shard_map/all_to_all | solution.py:45
  134.2 58.9 %all-to-all-start.1 = ((bf16[16,72,704]{2,1,0:T(8,128)(2,1)}), bf16[16,72,704]{2,1,0:T(8,128)(2,1)}, u32[]{:S(2)}, u32[]{:S(2)}) async-start(bf16[16,72,704]{2,1,0:T(8,128)(2,1)} %bitcast.47), calls=%async_computation.1 | async-start | bytes 3538944 | tf_op jit(solution)/shard_map/all_to_all | solution.py:49
  156.1 90.3 %all-reduce.4.cloned.1.call-start = ((), (), s32[]{:S(2)}) async-start(), calls=%async_computation.4 | async-start | bytes 5767168 | tf_op jit(solution)/shard_map/psum | solution.py:76
  223.4 16.4 %all-to-all-start.2 = ((f32[16,1,72]{2,1,0:T(1,128)}), f32[16,1,72]{2,1,0:T(1,128)S(1)}, u32[]{:S(2)}, u32[]{:S(2)}) async-start(f32[16,1,72]{2,1,0:T(1,128)} %all_to_all.18), calls=%async_computation.2 | async-start | bytes 16384 | tf_op jit(solution)/shard_map/all_to_all | solution.py:57
Sparse Core Ops, SparseCore 0:
  212.2 25.2 all-reduce.3
where the time goes:
time: 257 us
  waiting for transfers between devices  104 us (40%)
  local copies, waits for them, and re-layouts  55.9 us (22%)
  starting transfers between devices  46.1 us (18%)
  other arithmetic  17.1 us (7%)
  matrix products  15.9 us (6%)
  between operations  14.3 us (6%)
  blocking collectives  3.59 us (1%)
    all_to_all x1, waiting for transfers between devices, per_device(): lax.all_to_all(send_cot, 'expert', split_axis=0, concat_axis=0, tiled=True)  72.2 us
    all_to_all x1, waiting for transfers between devices, per_device(): lax.all_to_all(send_hid, 'expert', split_axis=0, concat_axis=0, tiled=True)  24.6 us
    all_to_all x1, starting transfers between devices, per_device(): lax.all_to_all(send_hid, 'expert', split_axis=0, concat_axis=0, tiled=True)  21.9 us
    all_to_all x1, starting transfers between devices, per_device(): lax.all_to_all(gate_local.reshape(experts, slot_count), 'expert', split_a...  9.13 us
    dot_general x1, matrix products, per_device(): lax.dot_general(hid_flat, scaled, (((0,), (0,)), ((), ())), preferred_ele...  9.11 us
    all_to_all x1, starting transfers between devices, per_device(): lax.all_to_all(send_w.astype(jnp.bfloat16), 'expert', split_axis=0, conca...  8.31 us
    gather x1, local copies, waits for them, and re-layouts, per_device(): send_w = padded_w[source_row].reshape(experts, slot_count)  7.27 us
    gather x1, local copies, waits for them, and re-layouts, per_device(): send_hid = padded_hid[source_row].reshape(experts, slot_count, hidden_width)  7.15 us
  transfers between devices with their start and end apart: 5, of which 4 were waited for; matrix products, arithmetic and copies ran while one was open for 21% of the time, Pallas kernels for 0%

commit v1 on v0

v1 whole, which is shorter than its diff:
```python
import functools

import jax
import jax.numpy as jnp
from jax import lax
from jax.experimental import pallas as pl
from jax.experimental.pallas import tpu as pltpu
from jax.sharding import PartitionSpec as P

BLOCK = 128
PLANE = 4
BF = jnp.bfloat16
F32 = jnp.float32
NT = (((1,), (1,)), ((), ()))
VMEM_BYTES = 48 * 1024 * 1024


def up(value, unit):
    return -(-value // unit) * unit


def call(kernel, out_shape, flops, nbytes, **kw):
    return pl.pallas_call(
        kernel,
        out_shape=out_shape,
        cost_estimate=pl.CostEstimate(flops=flops, bytes_accessed=nbytes, transcendentals=0),
        compiler_params=pltpu.CompilerParams(vmem_limit_bytes=VMEM_BYTES),
        **kw,
    )


def meta_kernel(outer, stride, routes_ref, slot_ref, rel_ref, code_ref):
    me = lax.axis_index("expert")
    experts, tokens = slot_ref.shape
    top_k = routes_ref.shape[0]
    routes = routes_ref[...]
    steps = (routes >> 2) - (me >> 2)
    steps = jnp.where(steps < 0, steps + outer, steps)
    rel = steps * PLANE + ((routes & 3) ^ (me & 3))
    rel_ref[...] = rel
    ids = lax.broadcasted_iota(jnp.int32, (experts, tokens), 0)
    mask = jnp.zeros((experts, tokens), F32)
    for k in range(top_k):
        mask += jnp.where(rel[k : k + 1, :] == ids, 1.0, 0.0)
    earlier = lax.broadcasted_iota(jnp.int32, (tokens, tokens), 0) < lax.broadcasted_iota(
        jnp.int32, (tokens, tokens), 1
    )
    rank = jnp.dot(
        mask.astype(BF), jnp.where(earlier, 1.0, 0.0).astype(BF), preferred_element_type=F32
    )
    slot = jnp.where(mask > 0.5, rank, -1.0)
    slot_ref[...] = slot
    for k in range(top_k):
        own = jnp.sum(
            jnp.where(rel[k : k + 1, :] == ids, slot, 0.0), axis=0, keepdims=True
        ).astype(jnp.int32)
        code_ref[k : k + 1, :] = rel[k : k + 1, :] * stride + own


def pack_kernel(outer, slots, stride, code_ref, num_ref, hid_ref, *rest):
    outs, table = rest[:PLANE], rest[PLANE]
    top_k, width, tokens = hid_ref.shape
    padded = table.shape[0]
    for k in range(top_k):
        lanes = slice(k * tokens, (k + 1) * tokens)
        table[0:width, lanes] = hid_ref[k]
        weight = num_ref[k : k + 1, :].astype(F32) * (1.0 / 1024.0)
        high = weight.astype(BF).astype(F32)
        rows = lax.broadcasted_iota(jnp.int32, (padded - width, tokens), 0)
        tail = jnp.where(rows == 0, high, jnp.where(rows == 1, weight - high, 0.0))
        table[width:padded, lanes] = tail.astype(BF)
    code = jnp.concatenate([code_ref[k : k + 1, :] for k in range(top_k)], axis=1)
    group = PLANE * stride
    for s in range(outer):
        rows = lax.broadcasted_iota(jnp.int32, (group, top_k * tokens), 0) + s * group
        pick = jnp.where(rows == code, 1.0, 0.0).astype(BF)
        got = lax.dot_general(pick, table[...], NT, preferred_element_type=F32)
        for k in range(PLANE):
            outs[k][s] = got[k * stride : k * stride + slots, :].astype(BF)


def relay_kernel(stage, slots, stride, slot_ref, cot_ref, *outs):
    tokens = cot_ref.shape[0]
    rows = lax.broadcasted_iota(jnp.int32, (stride, tokens), 0).astype(F32)
    pick = jnp.concatenate(
        [
            jnp.where(slot_ref[stage * PLANE + k : stage * PLANE + k + 1, :] == rows, 1.0, 0.0)
            for k in range(PLANE)
        ],
        axis=0,
    ).astype(BF)
    width = cot_ref.shape[1]
    step = min(512, width)
    for c in range(0, width, step):
        got = jnp.dot(pick, cot_ref[:, c : c + step], preferred_element_type=F32)
        for k in range(PLANE):
            outs[k][:, c : c + step] = got[k * stride : k * stride + slots, :].astype(BF)


def fill(table, pieces, slots, stride):
    for k, piece in enumerate(pieces):
        wide = piece.astype(F32)
        if stride > slots:
            wide = jnp.concatenate([wide, jnp.zeros((stride - slots, wide.shape[1]), F32)], axis=0)
        table[k * stride : (k + 1) * stride, :] = wide.astype(BF)


def back_kernel(slots, stride, c0, c1, c2, c3, hid_ref, w_ref, gate_ref, hidw_ref, rows, hids, acc):
    step = pl.program_id(0)
    width = w_ref.shape[0]
    fill(rows, [c0[...], c1[...], c2[...], c3[...]], slots, stride)
    part = lax.dot_general(w_ref[...], rows[...], NT, preferred_element_type=F32)

    @pl.when(step == 0)
    def _():
        acc[...] = part

    @pl.when(step > 0)
    def _():
        acc[...] += part

    @pl.when(step == pl.num_programs(0) - 1)
    def _():
        fill(hids, [hid_ref[k] for k in range(PLANE)], slots, stride)
        flipped = hids[...].astype(F32).T
        hid = flipped[0:width, :]
        gate = jnp.sum(acc[...] * hid, axis=0, keepdims=True)
        weight = flipped[width : width + 1, :] + flipped[width + 1 : width + 2, :]
        hidw_ref[...] = (hid * weight).astype(BF)
        gate_ref[...] = jnp.zeros_like(gate_ref)
        for k in range(PLANE):
            gate_ref[k : k + 1, 0:stride] = gate[:, k * stride : (k + 1) * stride]


def partial_kernel(slots, stride, count, has_acc, last, *refs):
    cots = refs[: PLANE * count]
    hidw = refs[PLANE * count : PLANE * count + count]
    refs = refs[PLANE * count + count :]
    total = None
    acc_ref = refs[0] if has_acc else None
    refs = refs[1:] if has_acc else refs
    rows, sums = refs[-2:]
    for s in range(count):
        fill(rows, [cots[s * PLANE + k][...] for k in range(PLANE)], slots, stride)
        part = jnp.dot(hidw[s][...], rows[...], preferred_element_type=F32)
        total = part if total is None else total + part
    if has_acc:
        total = total + acc_ref[...]
    if not last:
        refs[0][...] = total
        return
    mine_ref, send_ref = refs[0], refs[1]
    share = mine_ref.shape[0]
    me = lax.axis_index("replica")
    sums[...] = total
    mine_ref[...] = sums[pl.ds(pl.multiple_of(me * share, 8), share), :]
    if send_ref.shape[0] == share:
        send_ref[...] = sums[pl.ds(pl.multiple_of((1 - me) * share, 8), share), :].astype(BF)
    else:
        send_ref[...] = total.astype(BF)


def final_kernel(own_in_parts, mine_ref, parts_ref, out_ref, scale_ref, table):
    step = pl.program_id(0)
    count = parts_ref.shape[0]
    share, width = mine_ref.shape
    me = lax.axis_index("replica")
    lanes = lax.broadcasted_iota(jnp.int32, (share, BLOCK), 1)

    @pl.when(step == 0)
    def _():
        table[...] = jnp.zeros_like(table)

    kept = table[0:share, :]
    for b in range(width // BLOCK):
        span = slice(b * BLOCK, (b + 1) * BLOCK)
        own = mine_ref[:, span]
        top = jnp.abs(own)
        total = own
        for n in range(count):
            other = parts_ref[n, :, span].astype(F32)
            if own_in_parts:
                other = jnp.where(me == n, 0.0, other)
            top = jnp.maximum(top, jnp.abs(other))
            total = total + other
        scale = jnp.max(top, axis=1, keepdims=True) + 1e-6
        out_ref[:, span] = total / scale
        kept = jnp.where(lanes == step * (width // BLOCK) + b, scale, kept)
    table[0:share, :] = kept

    @pl.when(step == pl.num_programs(0) - 1)
    def _():
        scale_ref[...] = table[...].T[0 : scale_ref.shape[0], 0:share]


def gate_kernel(slot_ref, rel_ref, *refs):
    rows, out_ref = refs[:-1], refs[-1]
    experts, tokens = slot_ref.shape
    table = jnp.concatenate(
        [row[m % PLANE : m % PLANE + 1, :] for m, row in enumerate(rows)], axis=0
    )
    slot = jnp.maximum(slot_ref[...], 0.0).astype(jnp.int32)
    value = jnp.take_along_axis(table, slot, axis=1)
    ids = lax.broadcasted_iota(jnp.int32, (experts, tokens), 0)
    for k in range(out_ref.shape[0]):
        out_ref[k : k + 1, :] = jnp.sum(
            jnp.where(rel_ref[k : k + 1, :] == ids, value, 0.0), axis=0, keepdims=True
        )


def per_device(cotangent, hidden, routes, numerators, w_down):
    tokens, model = cotangent.shape
    top_k, width = hidden.shape[1], hidden.shape[2]
    experts, replicas = lax.axis_size("expert"), lax.axis_size("replica")
    outer = experts // PLANE
    slots = up(3 * tokens * top_k // (2 * experts), 8)
    stride = up(slots, 16)
    padded = up(width + 2, 128)
    share = width // replicas
    group = PLANE * stride
    sds = jax.ShapeDtypeStruct

    def ring(array, s):
        pairs = [(e, (e + s * PLANE) % experts) for e in range(experts)]
        return lax.ppermute(array, "expert", pairs)

    def swap(array, k):
        return lax.ppermute(array, "expert", [(e, e ^ k) for e in range(experts)])

    def home(array, s, k):
        pairs = [(e, ((e - s * PLANE) % experts) ^ k) for e in range(experts)]
        return lax.ppermute(array, "expert", pairs)

    cots = [cotangent]
    for s in range(1, outer):
        cots.append(ring(cots[-1], 1))

    slot, rel, code = call(
        functools.partial(meta_kernel, outer, stride),
        (
            sds((experts, tokens), F32),
            sds((top_k, tokens), jnp.int32),
            sds((top_k, tokens), jnp.int32),
        ),
        4 * experts * tokens * tokens,
        1 << 16,
    )(routes.T)
    metas = [slot] + [ring(slot, s) for s in range(1, outer)]

    def relay(s):
        return call(
            functools.partial(relay_kernel, s, slots, stride),
            [sds((slots, model), BF)] * PLANE,
            2 * group * tokens * model,
            2 * tokens * model + 2 * group * model,
        )(metas[s], cots[s])

    packed = call(
        functools.partial(pack_kernel, outer, slots, stride),
        [sds((outer, slots, padded), BF)] * PLANE,
        2 * experts * stride * top_k * tokens * padded,
        2 * top_k * tokens * padded + 2 * experts * slots * padded,
        scratch_shapes=[pltpu.VMEM((padded, top_k * tokens), BF)],
    )(code, numerators.T, jnp.transpose(hidden, (1, 2, 0)))
    in_plane = [packed[0]] + [swap(packed[k], k) for k in range(1, PLANE)]
    hids = []
    for s in range(outer):
        regrouped = jnp.stack([part[s] for part in in_plane])
        hids.append(ring(regrouped, s) if s else regrouped)

    got = []
    for s in range(outer):
        sent = relay(s)
        got.append([sent[0]] + [swap(sent[k], k) for k in range(1, PLANE)])

    matrix = w_down[0]
    step = 512
    steps = model // step

    def back(s):
        cot_spec = pl.BlockSpec((slots, step), lambda j: (0, j))
        return call(
            functools.partial(back_kernel, slots, stride),
            [sds((PLANE, BLOCK), F32), sds((width, group), BF)],
            2 * group * model * width,
            2 * model * (width + group),
            grid=(steps,),
            in_specs=[cot_spec] * PLANE
            + [
                pl.BlockSpec((PLANE, slots, padded), lambda j: (0, 0, 0)),
                pl.BlockSpec((width, step), lambda j: (0, j)),
            ],
            out_specs=[
                pl.BlockSpec((PLANE, BLOCK), lambda j: (0, 0)),
                pl.BlockSpec((width, group), lambda j: (0, 0)),
            ],
            scratch_shapes=[
                pltpu.VMEM((group, step), BF),
                pltpu.VMEM((group, padded), BF),
                pltpu.VMEM((width, group), F32),
            ],
        )(*got[s], hids[s], matrix)

    def partial(stages, hidws, acc, last):
        count = len(stages)
        cot_spec = pl.BlockSpec((slots, step), lambda j: (0, j))
        in_specs = [cot_spec] * (PLANE * count)
        in_specs += [pl.BlockSpec((width, group), lambda j: (0, 0))] * count
        args = [c for s in stages for c in got[s]] + hidws
        whole = pl.BlockSpec((width, step), lambda j: (0, j))
        if acc is not None:
            in_specs.append(whole)
            args.append(acc)
        if last:
            sent = share if replicas == 2 else width
            outs = [sds((share, model), F32), sds((sent, model), BF)]
            out_specs = [
                pl.BlockSpec((share, step), lambda j: (0, j)),
                pl.BlockSpec((sent, step), lambda j: (0, j)),
            ]
        else:
            outs, out_specs = [sds((width, model), F32)], [whole]
        return call(
            functools.partial(partial_kernel, slots, stride, count, acc is not None, last),
            outs,
            2 * group * count * model * width,
            4 * model * width * 2,
            grid=(steps,),
            in_specs=in_specs,
            out_specs=out_specs,
            scratch_shapes=[pltpu.VMEM((group, step), BF), pltpu.VMEM((width, step), F32)],
        )(*args)

    rows, hidws = [], []
    acc = None
    for s in range(outer):
        gate, hidw = back(s)
        rows += [home(gate, s, k) if s or k else gate for k in range(PLANE)]
        hidws.append(hidw)
        if s < outer - 1:
            acc = partial([s], [hidw], acc, False)[0]
    mine, send = partial([outer - 1], hidws[-1:], acc, True)

    if replicas == 2:
        parts = lax.ppermute(send, "replica", [(0, 1), (1, 0)])[None]
    else:
        parts = lax.all_to_all(
            send.reshape(replicas, share, model), "replica", 0, 0, tiled=True
        )
    out, scales = call(
        functools.partial(final_kernel, replicas != 2),
        [sds((share, model), F32), sds((model // BLOCK, share), F32)],
        8 * share * model,
        10 * share * model,
        grid=(steps,),
        in_specs=[
            pl.BlockSpec((share, step), lambda j: (0, j)),
            pl.BlockSpec((parts.shape[0], share, step), lambda j: (0, 0, j)),
        ],
        out_specs=[
            pl.BlockSpec((share, step), lambda j: (0, j)),
            pl.BlockSpec((model // BLOCK, share), lambda j: (0, 0)),
        ],
        scratch_shapes=[pltpu.VMEM((up(share, 128), BLOCK), F32)],
    )(mine, parts)
    gate_grad = call(
        gate_kernel,
        sds((top_k, tokens), F32),
        1 << 16,
        1 << 16,
    )(slot, rel, *rows)
    return gate_grad.T, scales.T[None], out[None]


def solution(mesh):
    return jax.shard_map(
        per_device,
        mesh=mesh,
        in_specs=(
            P(("expert", "replica"), None),
            P(("expert", "replica"), None, None),
            P(("expert", "replica"), None),
            P(("expert", "replica"), None),
            P("expert", None, None),
        ),
        out_specs=(
            P(("expert", "replica"), None),
            P("expert", "replica", None),
            P("expert", "replica", None),
        ),
        check_vma=False,
    )
```

time: 257 us -> 164 us (0.64)
  waiting for transfers between devices: 104 us -> 46.3 us
  local copies, waits for them, and re-layouts: 55.9 us -> 2.73 us
  Pallas kernels: 0 us -> 43.6 us
  starting transfers between devices: 46.1 us -> 69.3 us
  other arithmetic: 17.1 us -> 0.23 us
  matrix products: 15.9 us -> 0 us
  between operations: 14.3 us -> 0.86 us
  blocking collectives: 3.59 us -> 0 us
    all_to_all x4 -> x0, waiting for transfers between devices: 104 us -> none  [the longest x1 72.2 us: per_device(): lax.all_to_all(send_cot, 'expert', split_axis=0, concat_axis=0, tiled=True)]
    ppermute x0 -> x40, starting transfers between devices: none -> 69.3 us  [the longest x15 33.8 us: home(): return lax.ppermute(array, 'expert', pairs)]
    ppermute x0 -> x40, waiting for transfers between devices: none -> 46.3 us  [the longest x15 30.3 us: swap(): return lax.ppermute(array, 'expert', [(e, e ^ k) for e in range(experts)])]
    all_to_all x4 -> x0, starting transfers between devices: 46.1 us -> none  [the longest x1 21.9 us: per_device(): lax.all_to_all(send_hid, 'expert', split_axis=0, concat_axis=0, tiled=True)]
    pallas_call x0 -> x16, Pallas kernels: none -> 43.6 us  [the longest x4 22.6 us: partial(): call(functools.partial(partial_kernel, slots, stride, count, acc is not N...]
    gather x4 -> x0, local copies, waits for them, and re-layouts: 24.8 us -> none  [the longest x1 7.27 us: per_device(): send_w = padded_w[source_row].reshape(experts, slot_count)]
    dot_general x2 -> x0, matrix products: 15.9 us -> none  [the longest x1 9.11 us: per_device(): lax.dot_general(hid_flat, scaled, (((0,), (0,)), ((), ())), preferred_ele...]
    reshape x5 -> x0, local copies, waits for them, and re-layouts: 14.1 us -> none  [the longest x1 6.79 us: per_device(): cot_flat = got_cot.reshape(total_slots, model_width)]
  transfers between devices with their start and end apart: 5 -> 40, of which waited for: 4 -> 10; matrix products, arithmetic and copies ran while one was open for 21% -> 0% of each run, Pallas kernels for 0% -> 18%
where the time goes in v1:
time: 164 us; the launch traced here: 163 us
  starting transfers between devices  69.3 us (42%)
  waiting for transfers between devices  46.3 us (28%)
  Pallas kernels  43.6 us (27%)
  local copies, waits for them, and re-layouts  2.73 us (2%)
    ppermute x15, starting transfers between devices, home(): return lax.ppermute(array, 'expert', pairs)  33.8 us
    ppermute x15, waiting for transfers between devices, swap(): return lax.ppermute(array, 'expert', [(e, e ^ k) for e in range(experts)])  30.3 us
    pallas_call x4, Pallas kernels, partial(): call(functools.partial(partial_kernel, slots, stride, count, acc is not N...  22.6 us
    ppermute x15, starting transfers between devices, swap(): return lax.ppermute(array, 'expert', [(e, e ^ k) for e in range(experts)])  22.2 us
    pallas_call x4, Pallas kernels, back(): call(functools.partial(back_kernel, slots, stride), [sds((PLANE, BLOCK),...  13.6 us
    ppermute x9, starting transfers between devices, ring(): return lax.ppermute(array, 'expert', pairs)  13.3 us
    ppermute x9, waiting for transfers between devices, ring(): return lax.ppermute(array, 'expert', pairs)  9.23 us
    ppermute x15, waiting for transfers between devices, home(): return lax.ppermute(array, 'expert', pairs)  6.74 us
  transfers between devices with their start and end apart: 40, of which 10 were waited for; matrix products, arithmetic and copies ran while one was open for 0% of the time, Pallas kernels for 18%

profile of v1, /device:TPU:0, one launch (start us, length us, event | category | flops | bytes accessed | tf_op | source)
XLA Modules:
  0.0 163.1 jit_solution(14216244517229900919)
XLA Ops:
  5.2 3.0 %collective-permute-start.3 = (bf16[4,72,768]{2,1,0:T(8,128)(2,1)S(1)}, bf16[4,72,768]{2,1,0:T(8,128)(2,1)S(1)}, u32[]{:S(2)}, u32[]{:S(2)}) collective-permute-start(bf16[4,72,768]{2,1,0:T(8,128)(2,1)S(1)} %get-tuple-element.46), channel_id=1, source_target_pairs={{0,2},{2,0},{4,6},{6,4},{8,10},{10,8},{12,14},{14,12},{16,18},{18,... | collective-permute-start | bytes 1327112 | tf_op jit(solution)/shard_map/ppermute | solution.py:228
  14.6 3.7 %collective-permute-done.3 = bf16[4,72,768]{2,1,0:T(8,128)(2,1)S(1)} collective-permute-done((bf16[4,72,768]{2,1,0:T(8,128)(2,1)S(1)}, bf16[4,72,768]{2,1,0:T(8,128)(2,1)S(1)}, u32[]{:S(2)}, u32[]{:S(2)}) %collective-permute-start.3) | collective-permute-done | bytes 442400 | tf_op jit(solution)/shard_map/ppermute | solution.py:228
  18.3 2.7 %collective-permute-start.5 = (bf16[4,72,768]{2,1,0:T(8,128)(2,1)S(1)}, bf16[4,72,768]{2,1,0:T(8,128)(2,1)S(1)}, u32[]{:S(2)}, u32[]{:S(2)}) collective-permute-start(bf16[4,72,768]{2,1,0:T(8,128)(2,1)S(1)} %get-tuple-element.48), channel_id=1, source_target_pairs={{0,6},{2,4},{4,2},{6,0},{8,14},{10,12},{12,10},{14,8},{16,22},{18,... | collective-permute-start | bytes 1327112 | tf_op jit(solution)/shard_map/ppermute | solution.py:228
  21.1 13.3 %collective-permute-done.4 = bf16[4,72,768]{2,1,0:T(8,128)(2,1)S(1)} collective-permute-done((bf16[4,72,768]{2,1,0:T(8,128)(2,1)S(1)}, bf16[4,72,768]{2,1,0:T(8,128)(2,1)S(1)}, u32[]{:S(2)}, u32[]{:S(2)}) %collective-permute-start.4) | collective-permute-done | bytes 442400 | tf_op jit(solution)/shard_map/ppermute | solution.py:228
  34.4 5.3 %collective-permute-start.20 = (bf16[128,2048]{1,0:T(8,128)(2,1)S(1)}, bf16[128,2048]{1,0:T(8,128)(2,1)S(1)}, u32[]{:S(2)}, u32[]{:S(2)}) collective-permute-start(bf16[128,2048]{1,0:T(8,128)(2,1)S(1)} %collective-permute-done.10.cot_ref), channel_id=1, source_target_pairs={{0,8},{2,10},{4,12},{6,14},{8,16},{10,18},{12,20},{14,22},{16,24},... | collective-permute-start | bytes 1572872 | tf_op jit(solution)/shard_map/ppermute | solution.py:225
  41.4 2.0 %collective-permute-start.2 = (bf16[72,2048]{1,0:T(8,128)(2,1)S(1)}, bf16[72,2048]{1,0:T(8,128)(2,1)S(1)}, u32[]{:S(2)}, u32[]{:S(2)}) collective-permute-start(bf16[72,2048]{1,0:T(8,128)(2,1)S(1)} %get-tuple-element.43), channel_id=1, source_target_pairs={{0,6},{2,4},{4,2},{6,0},{8,14},{10,12},{12,10},{14,8},{16,22},{18,... | collective-permute-start | bytes 884744 | tf_op jit(solution)/shard_map/ppermute | solution.py:228
  43.9 8.3 %collective-permute-done.29.slot_ref = f32[16,128]{1,0:T(8,128)S(1)} collective-permute-done((f32[16,128]{1,0:T(8,128)S(1)}, f32[16,128]{1,0:T(8,128)S(1)}, u32[]{:S(2)}, u32[]{:S(2)}) %collective-permute-start.29) | collective-permute-done | bytes 8224 | tf_op jit(solution)/shard_map/ppermute | solution.py:225
  52.3 2.0 %collective-permute-start.11 = (bf16[72,2048]{1,0:T(8,128)(2,1)S(1)}, bf16[72,2048]{1,0:T(8,128)(2,1)S(1)}, u32[]{:S(2)}, u32[]{:S(2)}) collective-permute-start(bf16[72,2048]{1,0:T(8,128)(2,1)S(1)} %get-tuple-element.51), channel_id=1, source_target_pairs={{0,2},{2,0},{4,6},{6,4},{8,10},{10,8},{12,14},{14,12},{16,18},{18,... | collective-permute-start | bytes 884744 | tf_op jit(solution)/shard_map/ppermute | solution.py:228
  58.2 2.3 %collective-permute-done.11.c1.refs_1_ = bf16[72,2048]{1,0:T(8,128)(2,1)S(1)} collective-permute-done((bf16[72,2048]{1,0:T(8,128)(2,1)S(1)}, bf16[72,2048]{1,0:T(8,128)(2,1)S(1)}, u32[]{:S(2)}, u32[]{:S(2)}) %collective-permute-start.11) | collective-permute-done | bytes 294944 | tf_op jit(solution)/shard_map/ppermute | solution.py:228
  61.7 9.7 %collective-permute-done.12.c2.refs_2_ = bf16[72,2048]{1,0:T(8,128)(2,1)S(1)} collective-permute-done((bf16[72,2048]{1,0:T(8,128)(2,1)S(1)}, bf16[72,2048]{1,0:T(8,128)(2,1)S(1)}, u32[]{:S(2)}, u32[]{:S(2)}) %collective-permute-start.12) | collective-permute-done | bytes 294944 | tf_op jit(solution)/shard_map/ppermute | solution.py:228
  72.5 2.0 %collective-permute-start.22 = (bf16[72,2048]{1,0:T(8,128)(2,1)S(1)}, bf16[72,2048]{1,0:T(8,128)(2,1)S(1)}, u32[]{:S(2)}, u32[]{:S(2)}) collective-permute-start(bf16[72,2048]{1,0:T(8,128)(2,1)S(1)} %get-tuple-element.57), channel_id=1, source_target_pairs={{0,4},{2,6},{4,0},{6,2},{8,12},{10,14},{12,8},{14,10},{16,20},{18,... | collective-permute-start | bytes 884744 | tf_op jit(solution)/shard_map/ppermute | solution.py:228
  75.0 3.4 %shard_map.79 = (f32[4,128]{1,0:T(4,128)S(1)}, bf16[704,320]{1,0:T(8,128)(2,1)S(1)}) custom-call(bf16[72,2048]{1,0:T(8,128)(2,1)S(1)} %get-tuple-element.40.c0.refs_0_, bf16[72,2048]{1,0:T(8,128)(2,1)S(1)} %collective-permute-done.c1.refs_1_, bf16[72,2048]{1,0:T(8,128)(2,1)S(1)} %collective-permute-done.1.c2.refs_2_, ...), custom_call_target="tpu_custom_call" | custom-call | flops 922746880 | bytes 4194304 | tf_op jit(solution)/shard_map/pallas_call | solution.py:282
  78.4 2.7 %collective-permute-start.34 = (bf16[4,72,768]{2,1,0:T(8,128)(2,1)S(1)}, bf16[4,72,768]{2,1,0:T(8,128)(2,1)S(1)}, u32[]{:S(2)}, u32[]{:S(2)}) collective-permute-start(bf16[4,72,768]{2,1,0:T(8,128)(2,1)S(1)} %pad_maximum_fusion.3), channel_id=1, source_target_pairs={{0,24},{2,26},{4,28},{6,30},{8,0},{10,2},{12,4},{14,6},{16,8},{18,... | collective-permute-start | bytes 1327112 | tf_op jit(solution)/shard_map/ppermute | solution.py:225
  81.1 4.1 %shard_map.87.refs_5_ = f32[704,2048]{1,0:T(8,128)} custom-call(bf16[72,2048]{1,0:T(8,128)(2,1)S(1)} %get-tuple-element.40.c0.refs_0_, bf16[72,2048]{1,0:T(8,128)(2,1)S(1)} %collective-permute-done.c1.refs_1_, bf16[72,2048]{1,0:T(8,128)(2,1)S(1)} %collective-permute-done.1.c2.refs_2_, bf16[72,2048]{1,0:T(8,128)(2,1)S(1)} %collective-permute-done.2.c3.refs_3_, ...), custom_call_target="tpu_custom_call" | custom-call | flops 922746880 | bytes 11534336 | tf_op jit(solution)/shard_map/pallas_call | solution.py:323
  86.5 2.0 %collective-permute-start.31 = (bf16[72,2048]{1,0:T(8,128)(2,1)S(1)}, bf16[72,2048]{1,0:T(8,128)(2,1)S(1)}, u32[]{:S(2)}, u32[]{:S(2)}) collective-permute-start(bf16[72,2048]{1,0:T(8,128)(2,1)S(1)} %get-tuple-element.61), channel_id=1, source_target_pairs={{0,2},{2,0},{4,6},{6,4},{8,10},{10,8},{12,14},{14,12},{16,18},{18,... | collective-permute-start | bytes 884744 | tf_op jit(solution)/shard_map/ppermute | solution.py:228
  90.0 3.4 %shard_map.81 = (f32[4,128]{1,0:T(4,128)S(1)}, bf16[704,320]{1,0:T(8,128)(2,1)S(1)}) custom-call(bf16[72,2048]{1,0:T(8,128)(2,1)S(1)} %get-tuple-element.50.c0.refs_0_, bf16[72,2048]{1,0:T(8,128)(2,1)S(1)} %collective-permute-done.11.c1.refs_1_, bf16[72,2048]{1,0:T(8,128)(2,1)S(1)} %collective-permute-done.12.c2.refs_2_, ...), custom_call_target="tpu_custom_call" | custom-call | flops 922746880 | bytes 4194304 | tf_op jit(solution)/shard_map/pallas_call | solution.py:282
  93.4 6.6 %shard_map.88.refs_5_ = f32[704,2048]{1,0:T(8,128)} custom-call(bf16[72,2048]{1,0:T(8,128)(2,1)S(1)} %get-tuple-element.50.c0.refs_0_, bf16[72,2048]{1,0:T(8,128)(2,1)S(1)} %collective-permute-done.11.c1.refs_1_, bf16[72,2048]{1,0:T(8,128)(2,1)S(1)} %collective-permute-done.12.c2.refs_2_, bf16[72,2048]{1,0:T(8,128)(2,1)S(1)} %collective-permute-done.13.c3.refs_3_, ...), custom_call_target="tpu_custom_call" | custom-call | flops 922746880 | bytes 11534336 | tf_op jit(solution)/shard_map/pallas_call | solution.py:323
  100.1 3.4 %shard_map.83 = (f32[4,128]{1,0:T(4,128)S(1)}, bf16[704,320]{1,0:T(8,128)(2,1)S(1)}) custom-call(bf16[72,2048]{1,0:T(8,128)(2,1)S(1)} %get-tuple-element.55.c0.refs_0_, bf16[72,2048]{1,0:T(8,128)(2,1)S(1)} %collective-permute-done.21.c1.refs_1_, bf16[72,2048]{1,0:T(8,128)(2,1)S(1)} %collective-permute-done.22.c2.refs_2_, ...), custom_call_target="tpu_custom_call" | custom-call | flops 922746880 | bytes 4194304 | tf_op jit(solution)/shard_map/pallas_call | solution.py:282
  103.5 6.6 %shard_map.89.refs_5_ = f32[704,2048]{1,0:T(8,128)} custom-call(bf16[72,2048]{1,0:T(8,128)(2,1)S(1)} %get-tuple-element.55.c0.refs_0_, bf16[72,2048]{1,0:T(8,128)(2,1)S(1)} %collective-permute-done.21.c1.refs_1_, bf16[72,2048]{1,0:T(8,128)(2,1)S(1)} %collective-permute-done.22.c2.refs_2_, bf16[72,2048]{1,0:T(8,128)(2,1)S(1)} %collective-permute-done.23.c3.refs_3_, ...), custom_call_target="tpu_custom_call" | custom-call | flops 922746880 | bytes 11534336 | tf_op jit(solution)/shard_map/pallas_call | solution.py:323
  110.1 3.4 %shard_map.85 = (f32[4,128]{1,0:T(4,128)S(1)}, bf16[704,320]{1,0:T(8,128)(2,1)S(1)}) custom-call(bf16[72,2048]{1,0:T(8,128)(2,1)S(1)} %get-tuple-element.60.c0.refs_0_, bf16[72,2048]{1,0:T(8,128)(2,1)S(1)} %collective-permute-done.31.c1.refs_1_, bf16[72,2048]{1,0:T(8,128)(2,1)S(1)} %collective-permute-done.32.c2.refs_2_, ...), custom_call_target="tpu_custom_call" | custom-call | flops 922746880 | bytes 4194304 | tf_op jit(solution)/shard_map/pallas_call | solution.py:282
  113.5 5.3 %shard_map.90 = (f32[352,2048]{1,0:T(8,128)S(1)}, bf16[352,2048]{1,0:T(8,128)(2,1)S(1)}) custom-call(bf16[72,2048]{1,0:T(8,128)(2,1)S(1)} %get-tuple-element.60.c0.refs_0_, bf16[72,2048]{1,0:T(8,128)(2,1)S(1)} %collective-permute-done.31.c1.refs_1_, bf16[72,2048]{1,0:T(8,128)(2,1)S(1)} %collective-permute-done.32.c2.refs_2_, ...), custom_call_target="tpu_custom_call" | custom-call | flops 922746880 | bytes 11534336 | tf_op jit(solution)/shard_map/pallas_call | solution.py:323
  118.9 2.1 %collective-permute-start.6 = (f32[4,128]{1,0:T(4,128)S(1)}, f32[4,128]{1,0:T(4,128)S(1)}, u32[]{:S(2)}, u32[]{:S(2)}) collective-permute-start(f32[4,128]{1,0:T(4,128)S(1)} %get-tuple-element.49.refs_0_), channel_id=1, source_target_pairs={{0,2},{2,0},{4,6},{6,4},{8,10},{10,8},{12,14},{14,12},{16,18},{18,... | collective-permute-start | bytes 6152 | tf_op jit(solution)/shard_map/ppermute | solution.py:232
  122.5 11.9 %collective-permute-start.15 = (f32[4,128]{1,0:T(4,128)S(1)}, f32[4,128]{1,0:T(4,128)S(1)}, u32[]{:S(2)}, u32[]{:S(2)}) collective-permute-start(f32[4,128]{1,0:T(4,128)S(1)} %get-tuple-element.54), channel_id=1, source_target_pairs={{0,24},{2,26},{4,28},{6,30},{8,0},{10,2},{12,4},{14,6},{16,8},{18,... | collective-permute-start | bytes 6152 | tf_op jit(solution)/shard_map/ppermute | solution.py:232
  135.4 2.0 %collective-permute-start.17 = (f32[4,128]{1,0:T(4,128)S(1)}, f32[4,128]{1,0:T(4,128)S(1)}, u32[]{:S(2)}, u32[]{:S(2)}) collective-permute-start(f32[4,128]{1,0:T(4,128)S(1)} %get-tuple-element.54), channel_id=1, source_target_pairs={{0,28},{2,30},{4,24},{6,26},{8,4},{10,6},{12,0},{14,2},{16,12},{18... | collective-permute-start | bytes 6152 | tf_op jit(solution)/shard_map/ppermute | solution.py:232
  138.3 2.0 %collective-permute-start.25 = (f32[4,128]{1,0:T(4,128)S(1)}, f32[4,128]{1,0:T(4,128)S(1)}, u32[]{:S(2)}, u32[]{:S(2)}) collective-permute-start(f32[4,128]{1,0:T(4,128)S(1)} %get-tuple-element.59), channel_id=1, source_target_pairs={{0,16},{2,18},{4,20},{6,22},{8,24},{10,26},{12,28},{14,30},{16,0},... | collective-permute-start | bytes 6152 | tf_op jit(solution)/shard_map/ppermute | solution.py:232
  140.3 1.9 %collective-permute-start.26 = (f32[4,128]{1,0:T(4,128)S(1)}, f32[4,128]{1,0:T(4,128)S(1)}, u32[]{:S(2)}, u32[]{:S(2)}) collective-permute-start(f32[4,128]{1,0:T(4,128)S(1)} %get-tuple-element.59), channel_id=1, source_target_pairs={{0,18},{2,16},{4,22},{6,20},{8,26},{10,24},{12,30},{14,28},{16,2},... | collective-permute-start | bytes 6152 | tf_op jit(solution)/shard_map/ppermute | solution.py:232
  142.2 2.9 %collective-permute-start.27 = (f32[4,128]{1,0:T(4,128)S(1)}, f32[4,128]{1,0:T(4,128)S(1)}, u32[]{:S(2)}, u32[]{:S(2)}) collective-permute-start(f32[4,128]{1,0:T(4,128)S(1)} %get-tuple-element.59), channel_id=1, source_target_pairs={{0,20},{2,22},{4,16},{6,18},{8,28},{10,30},{12,24},{14,26},{16,4},... | collective-permute-start | bytes 6152 | tf_op jit(solution)/shard_map/ppermute | solution.py:232
  147.0 2.4 %collective-permute-start.36 = (f32[4,128]{1,0:T(4,128)S(1)}, f32[4,128]{1,0:T(4,128)S(1)}, u32[]{:S(2)}, u32[]{:S(2)}) collective-permute-start(f32[4,128]{1,0:T(4,128)S(1)} %get-tuple-element.64), channel_id=1, source_target_pairs={{0,10},{2,8},{4,14},{6,12},{8,18},{10,16},{12,22},{14,20},{16,26},... | collective-permute-start | bytes 6152 | tf_op jit(solution)/shard_map/ppermute | solution.py:232
  149.4 2.9 %collective-permute-start.37 = (f32[4,128]{1,0:T(4,128)S(1)}, f32[4,128]{1,0:T(4,128)S(1)}, u32[]{:S(2)}, u32[]{:S(2)}) collective-permute-start(f32[4,128]{1,0:T(4,128)S(1)} %get-tuple-element.64), channel_id=1, source_target_pairs={{0,12},{2,14},{4,8},{6,10},{8,20},{10,22},{12,16},{14,18},{16,28},... | collective-permute-start | bytes 6152 | tf_op jit(solution)/shard_map/ppermute | solution.py:232
  153.3 2.4 %collective-permute-done.37.refs_14_ = f32[4,128]{1,0:T(4,128)S(1)} collective-permute-done((f32[4,128]{1,0:T(4,128)S(1)}, f32[4,128]{1,0:T(4,128)S(1)}, u32[]{:S(2)}, u32[]{:S(2)}) %collective-permute-start.37) | collective-permute-done | bytes 2080 | tf_op jit(solution)/shard_map/ppermute | solution.py:232
  155.7 3.8 %collective-permute-done.38.refs_15_ = f32[4,128]{1,0:T(4,128)S(1)} collective-permute-done((f32[4,128]{1,0:T(4,128)S(1)}, f32[4,128]{1,0:T(4,128)S(1)}, u32[]{:S(2)}, u32[]{:S(2)}) %collective-permute-start.38) | collective-permute-done | bytes 2080 | tf_op jit(solution)/shard_map/ppermute | solution.py:232
  160.1 2.9 %shard_map.91 = (f32[352,2048]{1,0:T(8,128)}, f32[16,352]{1,0:T(8,128)}) custom-call(f32[352,2048]{1,0:T(8,128)S(1)} %get-tuple-element.69.mine_ref, bf16[1,352,2048]{2,1,0:T(8,128)(2,1)S(1)} %bitcast.14), custom_call_target="tpu_custom_call" | custom-call | flops 5767168 | bytes 7208960 | tf_op jit(solution)/shard_map/pallas_call | solution.py:350
  (82 shorter events, 30.0 us)
Async XLA Ops:
  5.2 13.2 %collective-permute-start.3 = (bf16[4,72,768]{2,1,0:T(8,128)(2,1)S(1)}, bf16[4,72,768]{2,1,0:T(8,128)(2,1)S(1)}, u32[]{:S(2)}, u32[]{:S(2)}) collective-permute-start(bf16[4,72,768]{2,1,0:T(8,128)(2,1)S(1)} %get-tuple-element.46), channel_id=1, source_target_pairs={{0,2},{2,0},{4,6},{6,4},{8,10},{10,8},{12,14},{14,12},{16,18},{18,... | collective-permute-start | bytes 1327112 | tf_op jit(solution)/shard_map/ppermute | solution.py:228
  8.2 26.2 %collective-permute-start.10 = (bf16[128,2048]{1,0:T(8,128)(2,1)S(1)}, bf16[128,2048]{1,0:T(8,128)(2,1)S(1)}, u32[]{:S(2)}, u32[]{:S(2)}) collective-permute-start(bf16[128,2048]{1,0:T(8,128)(2,1)S(1)} %copy-done.3), channel_id=1, source_target_pairs={{0,8},{2,10},{4,12},{6,14},{8,16},{10,18},{12,20},{14,22},{16,24},... | collective-permute-start | bytes 1572872 | tf_op jit(solution)/shard_map/ppermute | solution.py:225
  9.8 30.0 %collective-permute-start.9 = (f32[16,128]{1,0:T(8,128)S(1)}, f32[16,128]{1,0:T(8,128)S(1)}, u32[]{:S(2)}, u32[]{:S(2)}) collective-permute-start(f32[16,128]{1,0:T(8,128)S(1)} %get-tuple-element.38.slot_ref), channel_id=1, source_target_pairs={{0,8},{2,10},{4,12},{6,14},{8,16},{10,18},{12,20},{14,22},{16,24},... | collective-permute-start | bytes 24584 | tf_op jit(solution)/shard_map/ppermute | solution.py:225
  11.3 32.0 %collective-permute-start.19 = (f32[16,128]{1,0:T(8,128)S(1)}, f32[16,128]{1,0:T(8,128)S(1)}, u32[]{:S(2)}, u32[]{:S(2)}) collective-permute-start(f32[16,128]{1,0:T(8,128)S(1)} %get-tuple-element.38.slot_ref), channel_id=1, source_target_pairs={{0,16},{2,18},{4,20},{6,22},{8,24},{10,26},{12,28},{14,30},{16,0},... | collective-permute-start | bytes 24584 | tf_op jit(solution)/shard_map/ppermute | solution.py:225
  12.6 21.8 %collective-permute-start.4 = (bf16[4,72,768]{2,1,0:T(8,128)(2,1)S(1)}, bf16[4,72,768]{2,1,0:T(8,128)(2,1)S(1)}, u32[]{:S(2)}, u32[]{:S(2)}) collective-permute-start(bf16[4,72,768]{2,1,0:T(8,128)(2,1)S(1)} %get-tuple-element.47), channel_id=1, source_target_pairs={{0,4},{2,6},{4,0},{6,2},{8,12},{10,14},{12,8},{14,10},{16,20},{18,... | collective-permute-start | bytes 1327112 | tf_op jit(solution)/shard_map/ppermute | solution.py:228
  18.3 23.0 %collective-permute-start.5 = (bf16[4,72,768]{2,1,0:T(8,128)(2,1)S(1)}, bf16[4,72,768]{2,1,0:T(8,128)(2,1)S(1)}, u32[]{:S(2)}, u32[]{:S(2)}) collective-permute-start(bf16[4,72,768]{2,1,0:T(8,128)(2,1)S(1)} %get-tuple-element.48), channel_id=1, source_target_pairs={{0,6},{2,4},{4,2},{6,0},{8,14},{10,12},{12,10},{14,8},{16,22},{18,... | collective-permute-start | bytes 1327112 | tf_op jit(solution)/shard_map/ppermute | solution.py:228
  34.4 20.0 %collective-permute-start = (bf16[72,2048]{1,0:T(8,128)(2,1)S(1)}, bf16[72,2048]{1,0:T(8,128)(2,1)S(1)}, u32[]{:S(2)}, u32[]{:S(2)}) collective-permute-start(bf16[72,2048]{1,0:T(8,128)(2,1)S(1)} %get-tuple-element.41), channel_id=1, source_target_pairs={{0,2},{2,0},{4,6},{6,4},{8,10},{10,8},{12,14},{14,12},{16,18},{18,... | collective-permute-start | bytes 884744 | tf_op jit(solution)/shard_map/ppermute | solution.py:228
  34.4 20.1 %collective-permute-start.20 = (bf16[128,2048]{1,0:T(8,128)(2,1)S(1)}, bf16[128,2048]{1,0:T(8,128)(2,1)S(1)}, u32[]{:S(2)}, u32[]{:S(2)}) collective-permute-start(bf16[128,2048]{1,0:T(8,128)(2,1)S(1)} %collective-permute-done.10.cot_ref), channel_id=1, source_target_pairs={{0,8},{2,10},{4,12},{6,14},{8,16},{10,18},{12,20},{14,22},{16,24},... | collective-permute-start | bytes 1572872 | tf_op jit(solution)/shard_map/ppermute | solution.py:225
  39.8 16.0 %collective-permute-start.1 = (bf16[72,2048]{1,0:T(8,128)(2,1)S(1)}, bf16[72,2048]{1,0:T(8,128)(2,1)S(1)}, u32[]{:S(2)}, u32[]{:S(2)}) collective-permute-start(bf16[72,2048]{1,0:T(8,128)(2,1)S(1)} %get-tuple-element.42), channel_id=1, source_target_pairs={{0,4},{2,6},{4,0},{6,2},{8,12},{10,14},{12,8},{14,10},{16,20},{18,... | collective-permute-start | bytes 884744 | tf_op jit(solution)/shard_map/ppermute | solution.py:228
  41.4 15.8 %collective-permute-start.2 = (bf16[72,2048]{1,0:T(8,128)(2,1)S(1)}, bf16[72,2048]{1,0:T(8,128)(2,1)S(1)}, u32[]{:S(2)}, u32[]{:S(2)}) collective-permute-start(bf16[72,2048]{1,0:T(8,128)(2,1)S(1)} %get-tuple-element.43), channel_id=1, source_target_pairs={{0,6},{2,4},{4,2},{6,0},{8,14},{10,12},{12,10},{14,8},{16,22},{18,... | collective-permute-start | bytes 884744 | tf_op jit(solution)/shard_map/ppermute | solution.py:228
  43.4 8.9 %collective-permute-start.29 = (f32[16,128]{1,0:T(8,128)S(1)}, f32[16,128]{1,0:T(8,128)S(1)}, u32[]{:S(2)}, u32[]{:S(2)}) collective-permute-start(f32[16,128]{1,0:T(8,128)S(1)} %get-tuple-element.38.slot_ref), channel_id=1, source_target_pairs={{0,24},{2,26},{4,28},{6,30},{8,0},{10,2},{12,4},{14,6},{16,8},{18,... | collective-permute-start | bytes 24584 | tf_op jit(solution)/shard_map/ppermute | solution.py:225
  52.3 8.2 %collective-permute-start.11 = (bf16[72,2048]{1,0:T(8,128)(2,1)S(1)}, bf16[72,2048]{1,0:T(8,128)(2,1)S(1)}, u32[]{:S(2)}, u32[]{:S(2)}) collective-permute-start(bf16[72,2048]{1,0:T(8,128)(2,1)S(1)} %get-tuple-element.51), channel_id=1, source_target_pairs={{0,2},{2,0},{4,6},{6,4},{8,10},{10,8},{12,14},{14,12},{16,18},{18,... | collective-permute-start | bytes 884744 | tf_op jit(solution)/shard_map/ppermute | solution.py:228
  54.4 20.2 %collective-permute-start.14 = (bf16[4,72,768]{2,1,0:T(8,128)(2,1)S(1)}, bf16[4,72,768]{2,1,0:T(8,128)(2,1)S(1)}, u32[]{:S(2)}, u32[]{:S(2)}) collective-permute-start(bf16[4,72,768]{2,1,0:T(8,128)(2,1)S(1)} %pad_maximum_fusion.1), channel_id=1, source_target_pairs={{0,8},{2,10},{4,12},{6,14},{8,16},{10,18},{12,20},{14,22},{16,24},... | collective-permute-start | bytes 1327112 | tf_op jit(solution)/shard_map/ppermute | solution.py:225
  54.4 24.0 %collective-permute-start.30 = (bf16[128,2048]{1,0:T(8,128)(2,1)S(1)}, bf16[128,2048]{1,0:T(8,128)(2,1)S(1)}, u32[]{:S(2)}, u32[]{:S(2)}) collective-permute-start(bf16[128,2048]{1,0:T(8,128)(2,1)S(1)} %collective-permute-done.20.cot_ref), channel_id=1, source_target_pairs={{0,8},{2,10},{4,12},{6,14},{8,16},{10,18},{12,20},{14,22},{16,24},... | collective-permute-start | bytes 1572872 | tf_op jit(solution)/shard_map/ppermute | solution.py:225
  55.8 15.6 %collective-permute-start.12 = (bf16[72,2048]{1,0:T(8,128)(2,1)S(1)}, bf16[72,2048]{1,0:T(8,128)(2,1)S(1)}, u32[]{:S(2)}, u32[]{:S(2)}) collective-permute-start(bf16[72,2048]{1,0:T(8,128)(2,1)S(1)} %get-tuple-element.52), channel_id=1, source_target_pairs={{0,4},{2,6},{4,0},{6,2},{8,12},{10,14},{12,8},{14,10},{16,20},{18,... | collective-permute-start | bytes 884744 | tf_op jit(solution)/shard_map/ppermute | solution.py:228
  57.2 15.4 %collective-permute-start.13 = (bf16[72,2048]{1,0:T(8,128)(2,1)S(1)}, bf16[72,2048]{1,0:T(8,128)(2,1)S(1)}, u32[]{:S(2)}, u32[]{:S(2)}) collective-permute-start(bf16[72,2048]{1,0:T(8,128)(2,1)S(1)} %get-tuple-element.53), channel_id=1, source_target_pairs={{0,6},{2,4},{4,2},{6,0},{8,14},{10,12},{12,10},{14,8},{16,22},{18,... | collective-permute-start | bytes 884744 | tf_op jit(solution)/shard_map/ppermute | solution.py:228
  60.5 26.0 %collective-permute-start.24 = (bf16[4,72,768]{2,1,0:T(8,128)(2,1)S(1)}, bf16[4,72,768]{2,1,0:T(8,128)(2,1)S(1)}, u32[]{:S(2)}, u32[]{:S(2)}) collective-permute-start(bf16[4,72,768]{2,1,0:T(8,128)(2,1)S(1)} %pad_maximum_fusion.2), channel_id=1, source_target_pairs={{0,16},{2,18},{4,20},{6,22},{8,24},{10,26},{12,28},{14,30},{16,0},... | collective-permute-start | bytes 1327112 | tf_op jit(solution)/shard_map/ppermute | solution.py:225
  71.4 17.2 %collective-permute-start.21 = (bf16[72,2048]{1,0:T(8,128)(2,1)S(1)}, bf16[72,2048]{1,0:T(8,128)(2,1)S(1)}, u32[]{:S(2)}, u32[]{:S(2)}) collective-permute-start(bf16[72,2048]{1,0:T(8,128)(2,1)S(1)} %get-tuple-element.56), channel_id=1, source_target_pairs={{0,2},{2,0},{4,6},{6,4},{8,10},{10,8},{12,14},{14,12},{16,18},{18,... | collective-permute-start | bytes 884744 | tf_op jit(solution)/shard_map/ppermute | solution.py:228
  72.5 16.0 %collective-permute-start.22 = (bf16[72,2048]{1,0:T(8,128)(2,1)S(1)}, bf16[72,2048]{1,0:T(8,128)(2,1)S(1)}, u32[]{:S(2)}, u32[]{:S(2)}) collective-permute-start(bf16[72,2048]{1,0:T(8,128)(2,1)S(1)} %get-tuple-element.57), channel_id=1, source_target_pairs={{0,4},{2,6},{4,0},{6,2},{8,12},{10,14},{12,8},{14,10},{16,20},{18,... | collective-permute-start | bytes 884744 | tf_op jit(solution)/shard_map/ppermute | solution.py:228
  74.6 25.5 %collective-permute-start.23 = (bf16[72,2048]{1,0:T(8,128)(2,1)S(1)}, bf16[72,2048]{1,0:T(8,128)(2,1)S(1)}, u32[]{:S(2)}, u32[]{:S(2)}) collective-permute-start(bf16[72,2048]{1,0:T(8,128)(2,1)S(1)} %get-tuple-element.58), channel_id=1, source_target_pairs={{0,6},{2,4},{4,2},{6,0},{8,14},{10,12},{12,10},{14,8},{16,22},{18,... | collective-permute-start | bytes 884744 | tf_op jit(solution)/shard_map/ppermute | solution.py:228
  78.4 31.7 %collective-permute-start.34 = (bf16[4,72,768]{2,1,0:T(8,128)(2,1)S(1)}, bf16[4,72,768]{2,1,0:T(8,128)(2,1)S(1)}, u32[]{:S(2)}, u32[]{:S(2)}) collective-permute-start(bf16[4,72,768]{2,1,0:T(8,128)(2,1)S(1)} %pad_maximum_fusion.3), channel_id=1, source_target_pairs={{0,24},{2,26},{4,28},{6,30},{8,0},{10,2},{12,4},{14,6},{16,8},{18,... | collective-permute-start | bytes 1327112 | tf_op jit(solution)/shard_map/ppermute | solution.py:225
  86.5 23.6 %collective-permute-start.31 = (bf16[72,2048]{1,0:T(8,128)(2,1)S(1)}, bf16[72,2048]{1,0:T(8,128)(2,1)S(1)}, u32[]{:S(2)}, u32[]{:S(2)}) collective-permute-start(bf16[72,2048]{1,0:T(8,128)(2,1)S(1)} %get-tuple-element.61), channel_id=1, source_target_pairs={{0,2},{2,0},{4,6},{6,4},{8,10},{10,8},{12,14},{14,12},{16,18},{18,... | collective-permute-start | bytes 884744 | tf_op jit(solution)/shard_map/ppermute | solution.py:228
  88.6 21.5 %collective-permute-start.32 = (bf16[72,2048]{1,0:T(8,128)(2,1)S(1)}, bf16[72,2048]{1,0:T(8,128)(2,1)S(1)}, u32[]{:S(2)}, u32[]{:S(2)}) collective-permute-start(bf16[72,2048]{1,0:T(8,128)(2,1)S(1)} %get-tuple-element.62), channel_id=1, source_target_pairs={{0,4},{2,6},{4,0},{6,2},{8,12},{10,14},{12,8},{14,10},{16,20},{18,... | collective-permute-start | bytes 884744 | tf_op jit(solution)/shard_map/ppermute | solution.py:228
  88.6 21.5 %collective-permute-start.33 = (bf16[72,2048]{1,0:T(8,128)(2,1)S(1)}, bf16[72,2048]{1,0:T(8,128)(2,1)S(1)}, u32[]{:S(2)}, u32[]{:S(2)}) collective-permute-start(bf16[72,2048]{1,0:T(8,128)(2,1)S(1)} %get-tuple-element.63), channel_id=1, source_target_pairs={{0,6},{2,4},{4,2},{6,0},{8,14},{10,12},{12,10},{14,8},{16,22},{18,... | collective-permute-start | bytes 884744 | tf_op jit(solution)/shard_map/ppermute | solution.py:228
  118.8 41.3 %collective-permute-start.39 = (bf16[352,2048]{1,0:T(8,128)(2,1)S(1)}, bf16[352,2048]{1,0:T(8,128)(2,1)S(1)}, u32[]{:S(2)}, u32[]{:S(2)}) collective-permute-start(bf16[352,2048]{1,0:T(8,128)(2,1)S(1)} %get-tuple-element.70), channel_id=1, source_target_pairs={{0,1},{1,0},{2,3},{3,2},{4,5},{5,4},{6,7},{7,6},{8,9},{9,8},{10,11... | collective-permute-start | bytes 4325384 | tf_op jit(solution)/shard_map/ppermute | solution.py:345
  118.9 15.5 %collective-permute-start.6 = (f32[4,128]{1,0:T(4,128)S(1)}, f32[4,128]{1,0:T(4,128)S(1)}, u32[]{:S(2)}, u32[]{:S(2)}) collective-permute-start(f32[4,128]{1,0:T(4,128)S(1)} %get-tuple-element.49.refs_0_), channel_id=1, source_target_pairs={{0,2},{2,0},{4,6},{6,4},{8,10},{10,8},{12,14},{14,12},{16,18},{18,... | collective-permute-start | bytes 6152 | tf_op jit(solution)/shard_map/ppermute | solution.py:232
  121.0 14.4 %collective-permute-start.7 = (f32[4,128]{1,0:T(4,128)S(1)}, f32[4,128]{1,0:T(4,128)S(1)}, u32[]{:S(2)}, u32[]{:S(2)}) collective-permute-start(f32[4,128]{1,0:T(4,128)S(1)} %get-tuple-element.49.refs_0_), channel_id=1, source_target_pairs={{0,4},{2,6},{4,0},{6,2},{8,12},{10,14},{12,8},{14,10},{16,20},{18,... | collective-permute-start | bytes 6152 | tf_op jit(solution)/shard_map/ppermute | solution.py:232
  121.0 16.3 %collective-permute-start.8 = (f32[4,128]{1,0:T(4,128)S(1)}, f32[4,128]{1,0:T(4,128)S(1)}, u32[]{:S(2)}, u32[]{:S(2)}) collective-permute-start(f32[4,128]{1,0:T(4,128)S(1)} %get-tuple-element.49.refs_0_), channel_id=1, source_target_pairs={{0,6},{2,4},{4,2},{6,0},{8,14},{10,12},{12,10},{14,8},{16,22},{18,... | collective-permute-start | bytes 6152 | tf_op jit(solution)/shard_map/ppermute | solution.py:232
  122.5 15.8 %collective-permute-start.15 = (f32[4,128]{1,0:T(4,128)S(1)}, f32[4,128]{1,0:T(4,128)S(1)}, u32[]{:S(2)}, u32[]{:S(2)}) collective-permute-start(f32[4,128]{1,0:T(4,128)S(1)} %get-tuple-element.54), channel_id=1, source_target_pairs={{0,24},{2,26},{4,28},{6,30},{8,0},{10,2},{12,4},{14,6},{16,8},{18,... | collective-permute-start | bytes 6152 | tf_op jit(solution)/shard_map/ppermute | solution.py:232
  137.4 7.7 %collective-permute-start.18 = (f32[4,128]{1,0:T(4,128)S(1)}, f32[4,128]{1,0:T(4,128)S(1)}, u32[]{:S(2)}, u32[]{:S(2)}) collective-permute-start(f32[4,128]{1,0:T(4,128)S(1)} %get-tuple-element.54), channel_id=1, source_target_pairs={{0,30},{2,28},{4,26},{6,24},{8,6},{10,4},{12,2},{14,0},{16,14},{18... | collective-permute-start | bytes 6152 | tf_op jit(solution)/shard_map/ppermute | solution.py:232
  138.3 7.7 %collective-permute-start.25 = (f32[4,128]{1,0:T(4,128)S(1)}, f32[4,128]{1,0:T(4,128)S(1)}, u32[]{:S(2)}, u32[]{:S(2)}) collective-permute-start(f32[4,128]{1,0:T(4,128)S(1)} %get-tuple-element.59), channel_id=1, source_target_pairs={{0,16},{2,18},{4,20},{6,22},{8,24},{10,26},{12,28},{14,30},{16,0},... | collective-permute-start | bytes 6152 | tf_op jit(solution)/shard_map/ppermute | solution.py:232
  145.0 7.2 %collective-permute-start.28 = (f32[4,128]{1,0:T(4,128)S(1)}, f32[4,128]{1,0:T(4,128)S(1)}, u32[]{:S(2)}, u32[]{:S(2)}) collective-permute-start(f32[4,128]{1,0:T(4,128)S(1)} %get-tuple-element.59), channel_id=1, source_target_pairs={{0,22},{2,20},{4,18},{6,16},{8,30},{10,28},{12,26},{14,24},{16,6},... | collective-permute-start | bytes 6152 | tf_op jit(solution)/shard_map/ppermute | solution.py:232
  (13 other events, 95.8 us)

commit v2 on v0

v2 whole, which is shorter than its diff:
```python
import functools

import jax
import jax.numpy as jnp
from jax import lax
from jax.experimental import pallas as pl
from jax.experimental.pallas import tpu as pltpu
from jax.sharding import PartitionSpec as P

BLOCK = 128
PLANE = 4
BF = jnp.bfloat16
F32 = jnp.float32
NT = (((1,), (1,)), ((), ()))
VMEM_BYTES = 48 * 1024 * 1024


def up(value, unit):
    return -(-value // unit) * unit


def call(kernel, out_shape, flops, nbytes, **kw):
    return pl.pallas_call(
        kernel,
        out_shape=out_shape,
        cost_estimate=pl.CostEstimate(flops=flops, bytes_accessed=nbytes, transcendentals=0),
        compiler_params=pltpu.CompilerParams(vmem_limit_bytes=VMEM_BYTES),
        **kw,
    )


def table_kernel(stride, routes_ref, cot_ref, ext_ref, slot_ref, code_ref):
    experts, tokens = slot_ref.shape
    top_k = routes_ref.shape[0]
    model = cot_ref.shape[1]
    routes = routes_ref[...]
    ids = lax.broadcasted_iota(jnp.int32, (experts, tokens), 0)
    mask = jnp.zeros((experts, tokens), F32)
    for k in range(top_k):
        mask += jnp.where(routes[k : k + 1, :] == ids, 1.0, 0.0)
    earlier = lax.broadcasted_iota(jnp.int32, (tokens, tokens), 0) < lax.broadcasted_iota(
        jnp.int32, (tokens, tokens), 1
    )
    rank = jnp.dot(
        mask.astype(BF), jnp.where(earlier, 1.0, 0.0).astype(BF), preferred_element_type=F32
    )
    slot = jnp.where(mask > 0.5, rank, -1.0)
    slot_ref[...] = slot
    for k in range(top_k):
        own = jnp.sum(
            jnp.where(routes[k : k + 1, :] == ids, slot, 0.0), axis=0, keepdims=True
        ).astype(jnp.int32)
        code_ref[k : k + 1, :] = routes[k : k + 1, :] * stride + own
    wide = jnp.concatenate([slot, jnp.zeros((BLOCK - experts, tokens), F32)], axis=0)
    ext_ref[:, 0:model] = cot_ref[...]
    ext_ref[:, model : model + BLOCK] = wide.T.astype(BF)


def pack_kernel(slots, stride, flip, code_ref, num_ref, hid_ref, first_ref, second_ref, table):
    top_k, width, tokens = hid_ref.shape
    half = width // 2
    padded = table.shape[0]
    experts = first_ref.shape[0]
    code = jnp.concatenate([code_ref[k : k + 1, :] for k in range(top_k)], axis=1)
    group = PLANE * stride
    begin = lax.axis_index("replica") if flip else 1
    for out_ref, part in ((first_ref, 1 - begin), (second_ref, begin)):
        at = pl.multiple_of(part * half, 16) if flip else part * half
        for k in range(top_k):
            lanes = slice(k * tokens, (k + 1) * tokens)
            table[0:half, lanes] = hid_ref[k, pl.ds(at, half), :]
            weight = num_ref[k : k + 1, :].astype(F32) * (1.0 / 1024.0)
            high = weight.astype(BF).astype(F32)
            rows = lax.broadcasted_iota(jnp.int32, (padded - half, tokens), 0)
            tail = jnp.where(rows == 0, high, jnp.where(rows == 1, weight - high, 0.0))
            table[half:padded, lanes] = tail.astype(BF)
        for s in range(experts // PLANE):
            rows = lax.broadcasted_iota(jnp.int32, (group, top_k * tokens), 0) + s * group
            pick = jnp.where(rows == code, 1.0, 0.0).astype(BF)
            got = lax.dot_general(pick, table[...], NT, preferred_element_type=F32)
            for k in range(PLANE):
                out_ref[s * PLANE + k] = got[k * stride : k * stride + slots, :].astype(BF)


def relay_kernel(slots, stride, ext_ref, *refs):
    outs, table = refs[:-1], refs[-1]
    tokens = ext_ref.shape[0]
    model = outs[0].shape[1]
    me = lax.axis_index("expert")
    table[...] = ext_ref[:, model : model + BLOCK].astype(F32).T
    rows = lax.broadcasted_iota(jnp.int32, (stride, tokens), 0).astype(F32)
    pick = jnp.concatenate(
        [jnp.where(table[pl.ds(me ^ k, 1), :] == rows, 1.0, 0.0) for k in range(PLANE)], axis=0
    ).astype(BF)
    step = min(512, model)
    for c in range(0, model, step):
        got = jnp.dot(pick, ext_ref[:, c : c + step], preferred_element_type=F32)
        for k in range(PLANE):
            outs[k][:, c : c + step] = got[k * stride : k * stride + slots, :].astype(BF)


def fill(table, at, piece, stride):
    wide = piece.astype(F32)
    short = stride - wide.shape[0]
    if short:
        wide = jnp.concatenate([wide, jnp.zeros((short, wide.shape[1]), F32)], axis=0)
    table[at : at + stride, :] = wide.astype(table.dtype)


def back_kernel(stride, c0, c1, c2, c3, w_ref, rows_ref, back_ref):
    step = pl.program_id(0)
    for k, piece in enumerate((c0, c1, c2, c3)):
        fill(rows_ref, k * stride, piece[...], stride)
    part = lax.dot_general(w_ref[...], rows_ref[...], NT, preferred_element_type=F32)

    @pl.when(step == 0)
    def _():
        back_ref[...] = part

    @pl.when(step > 0)
    def _():
        back_ref[...] += part


def source(outer, s, k):
    me = lax.axis_index("expert")
    ring = (me >> 2) - s
    ring = jnp.where(ring < 0, ring + outer, ring)
    return ring * PLANE + ((me & 3) ^ k)


def gate_kernel(outer, stride, second, flip, *refs):
    backs, refs = refs[:outer], refs[outer:]
    hid_ref, before_ref, gate_ref, hidw_ref, table = refs
    half = hidw_ref.shape[0]
    mine = lax.axis_index("replica") if flip else 1
    part = mine if second else 1 - mine
    at = pl.multiple_of(part * half, 8) if flip else part * half
    gate_ref[...] = before_ref[...]
    group = PLANE * stride
    for s in range(outer):
        for k in range(PLANE):
            fill(table, k * stride, hid_ref[source(outer, s, k)], stride)
        flipped = table[...].T
        hid = flipped[0:half, :]
        gate = jnp.sum(backs[s][pl.ds(at, half), :] * hid, axis=0, keepdims=True)
        weight = flipped[half : half + 1, :] + flipped[half + 1 : half + 2, :]
        hidw_ref[:, s * group : (s + 1) * group] = (hid * weight).astype(BF)
        for k in range(PLANE):
            gate_ref[pl.ds(source(outer, s, k), 1), 0:stride] += gate[:, k * stride : (k + 1) * stride]


def product(hidw_ref, cots, rows):
    group = cots[0].shape[0]
    for s, piece in enumerate(cots):
        rows[s * group : (s + 1) * group, :] = piece[...]
    return jnp.dot(hidw_ref[...], rows[...], preferred_element_type=F32)


def partial_kernel(outer, *refs):
    hidw_ref, out_ref, rows = refs[outer:]
    out_ref[...] = product(hidw_ref, refs[:outer], rows).astype(BF)


def scale_sum(own, others, step, out_ref, scale_ref, table):
    share, width = out_ref.shape
    lanes = lax.broadcasted_iota(jnp.int32, (share, BLOCK), 1)

    @pl.when(step == 0)
    def _():
        table[...] = jnp.zeros_like(table)

    kept = table[0:share, :]
    for b in range(width // BLOCK):
        span = slice(b * BLOCK, (b + 1) * BLOCK)
        terms = ([] if own is None else [own[:, span]]) + [o[:, span].astype(F32) for o in others]
        top = functools.reduce(jnp.maximum, [jnp.abs(term) for term in terms])
        scale = jnp.max(top, axis=1, keepdims=True) + 1e-6
        out_ref[:, span] = sum(terms) / scale
        kept = jnp.where(lanes == step * (width // BLOCK) + b, scale, kept)
    table[0:share, :] = kept

    @pl.when(step == pl.num_programs(0) - 1)
    def _():
        scale_ref[...] = table[...].T[0 : scale_ref.shape[0], 0:share]


def finish_kernel(outer, *refs):
    cots = refs[:outer]
    hidw_ref, other_ref, out_ref, scale_ref, rows, table = refs[outer:]
    own = product(hidw_ref, cots, rows)
    scale_sum(own, [other_ref], pl.program_id(0), out_ref, scale_ref, table)


def gather_sum_kernel(parts_ref, out_ref, scale_ref, table):
    others = [parts_ref.at[n] for n in range(parts_ref.shape[0])]
    scale_sum(None, others, pl.program_id(0), out_ref, scale_ref, table)


def pick_kernel(slot_ref, routes_ref, rows_ref, out_ref):
    experts, tokens = slot_ref.shape
    slot = jnp.maximum(slot_ref[...], 0.0).astype(jnp.int32)
    value = jnp.take_along_axis(rows_ref[...], slot, axis=1)
    ids = lax.broadcasted_iota(jnp.int32, (experts, tokens), 0)
    for k in range(out_ref.shape[0]):
        out_ref[k : k + 1, :] = jnp.sum(
            jnp.where(routes_ref[k : k + 1, :] == ids, value, 0.0), axis=0, keepdims=True
        )


def per_device(cotangent, hidden, routes, numerators, w_down):
    tokens, model = cotangent.shape
    top_k, width = hidden.shape[1], hidden.shape[2]
    experts, replicas = lax.axis_size("expert"), lax.axis_size("replica")
    outer = experts // PLANE
    slots = up(3 * tokens * top_k // (2 * experts), 8)
    stride = up(slots, 16)
    half = width // 2
    padded = up(half + 2, 128)
    share = width // replicas
    group = PLANE * stride
    flip = replicas == 2
    sds = jax.ShapeDtypeStruct
    step = 512
    steps = model // step

    def ring(array):
        pairs = [(e, (e + PLANE) % experts) for e in range(experts)]
        return lax.ppermute(array, "expert", pairs)

    def swap(array, k):
        return lax.ppermute(array, "expert", [(e, e ^ k) for e in range(experts)])

    def exchange(array):
        return lax.all_to_all(array, "expert", split_axis=0, concat_axis=0, tiled=True)

    ext, slot, code = call(
        functools.partial(table_kernel, stride),
        (
            sds((tokens, model + BLOCK), BF),
            sds((experts, tokens), F32),
            sds((top_k, tokens), jnp.int32),
        ),
        4 * experts * tokens * tokens,
        4 * tokens * model,
    )(routes.T, cotangent)

    first, second = call(
        functools.partial(pack_kernel, slots, stride, flip),
        [sds((experts, slots, padded), BF)] * 2,
        4 * experts * stride * top_k * tokens * padded,
        4 * top_k * tokens * padded + 4 * experts * slots * padded,
        scratch_shapes=[pltpu.VMEM((padded, top_k * tokens), BF)],
    )(code, numerators.T, jnp.transpose(hidden, (1, 2, 0)))

    matrix = w_down[0]
    rows, backs = [], []
    block = ext
    for s in range(outer):
        if s:
            block = ring(block)
        sent = call(
            functools.partial(relay_kernel, slots, stride),
            [sds((slots, model), BF)] * PLANE,
            2 * group * tokens * model,
            2 * tokens * model + 2 * group * model,
            scratch_shapes=[pltpu.VMEM((BLOCK, tokens), F32)],
        )(block)
        got = [sent[0]] + [swap(sent[k], k) for k in range(1, PLANE)]
        row, back = call(
            functools.partial(back_kernel, stride),
            [sds((group, model), BF), sds((width, group), F32)],
            2 * group * model * width,
            2 * model * (width + 2 * group),
            grid=(steps,),
            in_specs=[pl.BlockSpec((slots, step), lambda j: (0, j))] * PLANE
            + [pl.BlockSpec((width, step), lambda j: (0, j))],
            out_specs=[
                pl.BlockSpec((group, step), lambda j: (0, j)),
                pl.BlockSpec((width, group), lambda j: (0, 0)),
            ],
        )(*got, matrix)
        rows.append(row)
        backs.append(back)

    def gate(hid, before, is_second):
        return call(
            functools.partial(gate_kernel, outer, stride, is_second, flip),
            [sds((experts, BLOCK), F32), sds((half, outer * group), BF)],
            8 * outer * group * half,
            4 * outer * group * width + 4 * outer * group * half,
            scratch_shapes=[pltpu.VMEM((group, padded), F32)],
        )(*backs, hid, before)

    row_specs = [pl.BlockSpec((group, step), lambda j: (0, j))] * outer
    row_specs.append(pl.BlockSpec((half, outer * group), lambda j: (0, 0)))
    flat = pl.BlockSpec((half, step), lambda j: (0, j))
    row_scratch = pltpu.VMEM((outer * group, step), BF)

    def partial(hidw):
        return call(
            functools.partial(partial_kernel, outer),
            sds((half, model), BF),
            2 * outer * group * model * half,
            2 * model * (outer * group + half),
            grid=(steps,),
            in_specs=row_specs,
            out_specs=flat,
            scratch_shapes=[row_scratch],
        )(*rows, hidw)

    got_first = exchange(first)
    got_second = exchange(second)
    gate_first, hidw_first = gate(got_first, jnp.zeros((experts, BLOCK), F32), False)
    part_first = partial(hidw_first)
    gates, hidw_second = gate(got_second, gate_first, True)
    returned = exchange(gates)
    outs = [sds((share, model), F32), sds((model // BLOCK, share), F32)]
    out_specs = [
        pl.BlockSpec((share, step), lambda j: (0, j)),
        pl.BlockSpec((model // BLOCK, share), lambda j: (0, 0)),
    ]
    table = pltpu.VMEM((up(share, 128), BLOCK), F32)
    if flip:
        other = lax.ppermute(part_first, "replica", [(0, 1), (1, 0)])
        out, scales = call(
            functools.partial(finish_kernel, outer),
            outs,
            2 * outer * group * model * half,
            2 * model * (outer * group + 3 * half),
            grid=(steps,),
            in_specs=row_specs + [flat],
            out_specs=out_specs,
            scratch_shapes=[row_scratch, table],
        )(*rows, hidw_second, other)
    else:
        whole = jnp.concatenate([part_first, partial(hidw_second)], axis=0)
        parts = lax.all_to_all(
            whole.reshape(replicas, share, model), "replica", 0, 0, tiled=True
        )
        out, scales = call(
            gather_sum_kernel,
            outs,
            8 * share * model,
            10 * share * model,
            grid=(steps,),
            in_specs=[pl.BlockSpec((replicas, share, step), lambda j: (0, 0, j))],
            out_specs=out_specs,
            scratch_shapes=[table],
        )(parts)
    gate_grad = call(pick_kernel, sds((top_k, tokens), F32), 1 << 16, 1 << 16)(
        slot, routes.T, returned
    )
    return gate_grad.T, scales.T[None], out[None]


def solution(mesh):
    return jax.shard_map(
        per_device,
        mesh=mesh,
        in_specs=(
            P(("expert", "replica"), None),
            P(("expert", "replica"), None, None),
            P(("expert", "replica"), None),
            P(("expert", "replica"), None),
            P("expert", None, None),
        ),
        out_specs=(
            P(("expert", "replica"), None),
            P("expert", "replica", None),
            P("expert", "replica", None),
        ),
        check_vma=False,
    )
```

time: 257 us -> 157 us (0.61)
  waiting for transfers between devices: 104 us -> 53.1 us
  local copies, waits for them, and re-layouts: 55.9 us -> 15.6 us
  Pallas kernels: 0 us -> 37.8 us
  other arithmetic: 17.1 us -> 0 us
  matrix products: 15.9 us -> 0 us
  between operations: 14.3 us -> 0.89 us
  starting transfers between devices: 46.1 us -> 35.7 us
  blocking collectives: 3.59 us -> 12.6 us
    all_to_all x4 -> x2, waiting for transfers between devices: 104 us -> 6.24 us  [exchange(): lax.all_to_all(array, 'expert', split_axis=0, concat_axis=0, tiled=True)]
    ppermute x0 -> x16, waiting for transfers between devices: none -> 46.8 us  [the longest x3 29.3 us: ring(): return lax.ppermute(array, 'expert', pairs)]
    pallas_call x0 -> x15, Pallas kernels: none -> 37.8 us  [the longest x4 18.6 us: per_device(): call(functools.partial(back_kernel, stride), [sds((group, model), BF), sd...]
    all_to_all x4 -> x2, starting transfers between devices: 46.1 us -> 11.6 us  [exchange(): lax.all_to_all(array, 'expert', split_axis=0, concat_axis=0, tiled=True)]
    gather x4 -> x0, local copies, waits for them, and re-layouts: 24.8 us -> none  [the longest x1 7.27 us: per_device(): send_w = padded_w[source_row].reshape(experts, slot_count)]
    ppermute x0 -> x16, starting transfers between devices: none -> 24.1 us  [the longest x12 17 us: swap(): return lax.ppermute(array, 'expert', [(e, e ^ k) for e in range(experts)])]
    dot_general x2 -> x0, matrix products: 15.9 us -> none  [the longest x1 9.11 us: per_device(): lax.dot_general(hid_flat, scaled, (((0,), (0,)), ((), ())), preferred_ele...]
    reshape x5 -> x0, local copies, waits for them, and re-layouts: 14.1 us -> none  [the longest x1 6.79 us: per_device(): cot_flat = got_cot.reshape(total_slots, model_width)]
  transfers between devices with their start and end apart: 5 -> 18, of which waited for: 4 -> 10; matrix products, arithmetic and copies ran while one was open for 21% -> 0% of each run, Pallas kernels for 0% -> 20%
where the time goes in v2:
time: 157 us; the launch traced here: 156 us
  waiting for transfers between devices  53.1 us (34%)
  Pallas kernels  37.8 us (24%)
  starting transfers between devices  35.7 us (23%)
  local copies, waits for them, and re-layouts  15.6 us (10%)
  blocking collectives  12.6 us (8%)
    ppermute x3, waiting for transfers between devices, ring(): return lax.ppermute(array, 'expert', pairs)  29.3 us
    pallas_call x4, Pallas kernels, per_device(): call(functools.partial(back_kernel, stride), [sds((group, model), BF), sd...  18.6 us
    ppermute x12, waiting for transfers between devices, swap(): return lax.ppermute(array, 'expert', [(e, e ^ k) for e in range(experts)])  17.5 us
    ppermute x12, starting transfers between devices, swap(): return lax.ppermute(array, 'expert', [(e, e ^ k) for e in range(experts)])  17 us
    unnamed x48, local copies, waits for them, and re-layouts  15.5 us
    all_to_all x1, blocking collectives, exchange(): lax.all_to_all(array, 'expert', split_axis=0, concat_axis=0, tiled=True)  12.6 us
    all_to_all x2, starting transfers between devices, exchange(): lax.all_to_all(array, 'expert', split_axis=0, concat_axis=0, tiled=True)  11.6 us
    ppermute x3, starting transfers between devices, ring(): return lax.ppermute(array, 'expert', pairs)  7.14 us
  transfers between devices with their start and end apart: 18, of which 10 were waited for; matrix products, arithmetic and copies ran while one was open for 0% of the time, Pallas kernels for 20%

profile of v2, /device:TPU:0, one launch (start us, length us, event | category | flops | bytes accessed | tf_op | source)
XLA Modules:
  0.0 155.5 jit_solution(9519663190266773826)
XLA Ops:
  2.6 3.1 %collective-permute-start.3 = (bf16[128,2176]{1,0:T(8,128)(2,1)S(1)}, bf16[128,2176]{1,0:T(8,128)(2,1)S(1)}, u32[]{:S(2)}, u32[]{:S(2)}) collective-permute-start(bf16[128,2176]{1,0:T(8,128)(2,1)S(1)} %get-tuple-element.39.ext_ref), channel_id=1, source_target_pairs={{0,8},{2,10},{4,12},{6,14},{8,16},{10,18},{12,20},{14,22},{16,24},... | collective-permute-start | bytes 1671176 | tf_op jit(solution)/shard_map/ppermute | solution.py:229
  5.7 1.2 copy-done.22
  7.6 2.3 %shard_map.85 = (bf16[16,72,384]{2,1,0:T(8,128)(2,1)}, bf16[16,72,384]{2,1,0:T(8,128)(2,1)S(1)}) custom-call(s32[6,128]{1,0:T(8,128)S(1)} %get-tuple-element.60.code_ref, s32[6,128]{1,0:T(8,128)S(1)} %bitcast.18, bf16[6,704,128]{2,1,0:T(8,128)(2,1)S(1)} %bitcast.17), custom_call_target="tpu_custom_call" | custom-call | flops 1509949440 | bytes 2949120 | tf_op jit(solution)/shard_map/pallas_call | solution.py:248
  10.8 5.9 %all-to-all-start.1 = ((bf16[16,72,384]{2,1,0:T(8,128)(2,1)}), bf16[16,72,384]{2,1,0:T(8,128)(2,1)S(1)}, u32[]{:S(2)}, u32[]{:S(2)}) async-start(bf16[16,72,384]{2,1,0:T(8,128)(2,1)} %get-tuple-element.62), calls=%async_computation.1 | async-start | bytes 1769472 | tf_op jit(solution)/shard_map/all_to_all | solution.py:235
  16.6 3.9 %collective-permute-done.3.ext_ref = bf16[128,2176]{1,0:T(8,128)(2,1)S(1)} collective-permute-done((bf16[128,2176]{1,0:T(8,128)(2,1)S(1)}, bf16[128,2176]{1,0:T(8,128)(2,1)S(1)}, u32[]{:S(2)}, u32[]{:S(2)}) %collective-permute-start.3) | collective-permute-done | bytes 557088 | tf_op jit(solution)/shard_map/ppermute | solution.py:229
  21.1 25.5 %collective-permute-done.7.ext_ref = bf16[128,2176]{1,0:T(8,128)(2,1)S(1)} collective-permute-done((bf16[128,2176]{1,0:T(8,128)(2,1)S(1)}, bf16[128,2176]{1,0:T(8,128)(2,1)S(1)}, u32[]{:S(2)}, u32[]{:S(2)}) %collective-permute-start.7) | collective-permute-done | bytes 557088 | tf_op jit(solution)/shard_map/ppermute | solution.py:229
  46.6 3.5 %collective-permute-start.11 = (bf16[128,2176]{1,0:T(8,128)(2,1)S(1)}, bf16[128,2176]{1,0:T(8,128)(2,1)S(1)}, u32[]{:S(2)}, u32[]{:S(2)}) collective-permute-start(bf16[128,2176]{1,0:T(8,128)(2,1)S(1)} %collective-permute-done.7.ext_ref), channel_id=1, source_target_pairs={{0,8},{2,10},{4,12},{6,14},{8,16},{10,18},{12,20},{14,22},{16,24},... | collective-permute-start | bytes 1671176 | tf_op jit(solution)/shard_map/ppermute | solution.py:229
  50.6 1.6 collective-permute-start
  52.2 1.5 collective-permute-start.1
  54.7 1.6 collective-permute-start.4
  56.9 3.8 %collective-permute-done.c1 = bf16[72,2048]{1,0:T(8,128)(2,1)S(1)} collective-permute-done((bf16[72,2048]{1,0:T(8,128)(2,1)S(1)}, bf16[72,2048]{1,0:T(8,128)(2,1)S(1)}, u32[]{:S(2)}, u32[]{:S(2)}) %collective-permute-start) | collective-permute-done | bytes 294944 | tf_op jit(solution)/shard_map/ppermute | solution.py:232
  60.6 1.5 collective-permute-start.5
  62.1 4.9 %collective-permute-done.1.c2 = bf16[72,2048]{1,0:T(8,128)(2,1)S(1)} collective-permute-done((bf16[72,2048]{1,0:T(8,128)(2,1)S(1)}, bf16[72,2048]{1,0:T(8,128)(2,1)S(1)}, u32[]{:S(2)}, u32[]{:S(2)}) %collective-permute-start.1) | collective-permute-done | bytes 294944 | tf_op jit(solution)/shard_map/ppermute | solution.py:232
  67.9 2.9 %collective-permute-start.8 = (bf16[72,2048]{1,0:T(8,128)(2,1)S(1)}, bf16[72,2048]{1,0:T(8,128)(2,1)S(1)}, u32[]{:S(2)}, u32[]{:S(2)}) collective-permute-start(bf16[72,2048]{1,0:T(8,128)(2,1)S(1)} %get-tuple-element.51), channel_id=1, source_target_pairs={{0,2},{2,0},{4,6},{6,4},{8,10},{10,8},{12,14},{14,12},{16,18},{18,... | collective-permute-start | bytes 884744 | tf_op jit(solution)/shard_map/ppermute | solution.py:232
  70.8 2.5 %collective-permute-done.4.c1 = bf16[72,2048]{1,0:T(8,128)(2,1)S(1)} collective-permute-done((bf16[72,2048]{1,0:T(8,128)(2,1)S(1)}, bf16[72,2048]{1,0:T(8,128)(2,1)S(1)}, u32[]{:S(2)}, u32[]{:S(2)}) %collective-permute-start.4) | collective-permute-done | bytes 294944 | tf_op jit(solution)/shard_map/ppermute | solution.py:232
  73.3 1.5 collective-permute-start.9
  74.8 1.4 collective-permute-start.10
  76.3 1.5 shard_map.83
  80.6 1.4 collective-permute-start.13
  82.0 4.0 %collective-permute-done.8.c1 = bf16[72,2048]{1,0:T(8,128)(2,1)S(1)} collective-permute-done((bf16[72,2048]{1,0:T(8,128)(2,1)S(1)}, bf16[72,2048]{1,0:T(8,128)(2,1)S(1)}, u32[]{:S(2)}, u32[]{:S(2)}) %collective-permute-start.8) | collective-permute-done | bytes 294944 | tf_op jit(solution)/shard_map/ppermute | solution.py:232
  86.0 2.4 %collective-permute-start.14 = (bf16[72,2048]{1,0:T(8,128)(2,1)}, bf16[72,2048]{1,0:T(8,128)(2,1)}, u32[]{:S(2)}, u32[]{:S(2)}) collective-permute-start(bf16[72,2048]{1,0:T(8,128)(2,1)} %get-tuple-element.58), channel_id=1, source_target_pairs={{0,6},{2,4},{4,2},{6,0},{8,14},{10,12},{12,10},{14,8},{16,22},{18,... | collective-permute-start | bytes 884744 | tf_op jit(solution)/shard_map/ppermute | solution.py:232
  88.4 4.5 %shard_map.78 = (bf16[320,2048]{1,0:T(8,128)(2,1)S(1)}, f32[704,320]{1,0:T(8,128)S(1)}) custom-call(bf16[72,2048]{1,0:T(8,128)(2,1)S(1)} %get-tuple-element.40.c0, bf16[72,2048]{1,0:T(8,128)(2,1)S(1)} %collective-permute-done.c1, bf16[72,2048]{1,0:T(8,128)(2,1)S(1)} %collective-permute-done.1.c2, bf16[72,2048]{1,0:T(8,128)(2,1)S(1)} %collective-permute-done.2.c3, ...), custom_call_target="tpu_custom_call" | custom-call | flops 922746880 | bytes 5505024 | tf_op jit(solution)/shard_map/pallas_call | solution.py:270
  92.9 4.8 %shard_map.80 = (bf16[320,2048]{1,0:T(8,128)(2,1)S(1)}, f32[704,320]{1,0:T(8,128)S(1)}) custom-call(bf16[72,2048]{1,0:T(8,128)(2,1)S(1)} %get-tuple-element.45.c0, bf16[72,2048]{1,0:T(8,128)(2,1)S(1)} %collective-permute-done.4.c1, bf16[72,2048]{1,0:T(8,128)(2,1)S(1)} %collective-permute-done.5.c2, bf16[72,2048]{1,0:T(8,128)(2,1)S(1)} %collective-permute-done.6.c3, ...), custom_call_target="tpu_custom_call" | custom-call | flops 922746880 | bytes 5505024 | tf_op jit(solution)/shard_map/pallas_call | solution.py:270
  98.8 4.5 %shard_map.82 = (bf16[320,2048]{1,0:T(8,128)(2,1)S(1)}, f32[704,320]{1,0:T(8,128)S(1)}) custom-call(bf16[72,2048]{1,0:T(8,128)(2,1)S(1)} %get-tuple-element.50.c0, bf16[72,2048]{1,0:T(8,128)(2,1)S(1)} %collective-permute-done.8.c1, bf16[72,2048]{1,0:T(8,128)(2,1)S(1)} %collective-permute-done.9.c2, bf16[72,2048]{1,0:T(8,128)(2,1)S(1)} %collective-permute-done.10.c3, ...), custom_call_target="tpu_custom_call" | custom-call | flops 922746880 | bytes 5505024 | tf_op jit(solution)/shard_map/pallas_call | solution.py:270
  105.3 5.8 %all-to-all-start = ((bf16[16,72,384]{2,1,0:T(8,128)(2,1)}), bf16[16,72,384]{2,1,0:T(8,128)(2,1)}, u32[]{:S(2)}, u32[]{:S(2)}) async-start(bf16[16,72,384]{2,1,0:T(8,128)(2,1)} %copy-done.16), calls=%async_computation | async-start | bytes 1769472 | tf_op jit(solution)/shard_map/all_to_all | solution.py:235
  112.1 4.8 %shard_map.84 = (bf16[320,2048]{1,0:T(8,128)(2,1)S(1)}, f32[704,320]{1,0:T(8,128)S(1)}) custom-call(bf16[72,2048]{1,0:T(8,128)(2,1)S(1)} %copy-done.19, bf16[72,2048]{1,0:T(8,128)(2,1)} %collective-permute-done.12.c1, bf16[72,2048]{1,0:T(8,128)(2,1)} %collective-permute-done.13.c2, bf16[72,2048]{1,0:T(8,128)(2,1)} %collective-permute-done.14.c3, ...), custom_call_target="tpu_custom_call" | custom-call | flops 922746880 | bytes 5505024 | tf_op jit(solution)/shard_map/pallas_call | solution.py:270
  119.1 3.7 %shard_map.89 = bf16[352,2048]{1,0:T(8,128)(2,1)} custom-call(bf16[320,2048]{1,0:T(8,128)(2,1)S(1)} %get-tuple-element.65.refs_0_, bf16[320,2048]{1,0:T(8,128)(2,1)S(1)} %get-tuple-element.66.refs_1_, bf16[320,2048]{1,0:T(8,128)(2,1)S(1)} %copy-done.1, bf16[320,2048]{1,0:T(8,128)(2,1)S(1)} %get-tuple-element.68.refs_3_, ...), custom_call_target="tpu_custom_call" | custom-call | flops 1845493760 | bytes 6684672 | tf_op jit(solution)/shard_map/pallas_call | solution.py:301
  122.8 6.2 %all-to-all-done.refs_4_ = bf16[16,72,384]{2,1,0:T(8,128)(2,1)} async-done(((bf16[16,72,384]{2,1,0:T(8,128)(2,1)}), bf16[16,72,384]{2,1,0:T(8,128)(2,1)}, u32[]{:S(2)}, u32[]{:S(2)}) %all-to-all-start) | async-done | bytes 884768 | tf_op jit(solution)/shard_map/all_to_all | solution.py:235
  129.1 1.2 copy-done.7
  134.0 2.1 %shard_map.87 = (f32[16,128]{1,0:T(8,128)S(1)}, bf16[352,1280]{1,0:T(8,128)(2,1)S(1)}) custom-call(f32[704,320]{1,0:T(8,128)S(1)} %copy-done.7, f32[704,320]{1,0:T(8,128)S(1)} %copy-done.10, f32[704,320]{1,0:T(8,128)S(1)} %copy-done.13, f32[704,320]{1,0:T(8,128)S(1)} %copy-done.15, bf16[16,72,384]{2,1,0:T(8,128)(2,1)} %all-to-all-done.refs_4_, ...), custom_call_target="tpu_custom_call" | custom-call | flops 3604480 | bytes 5406720 | tf_op jit(solution)/shard_map/pallas_call | solution.py:287
  136.1 12.6 %all_to_all.21 = f32[16,1,128]{2,1,0:T(1,128)S(1)} all-to-all(f32[16,1,128]{2,1,0:T(1,128)S(1)} %bitcast.16), channel_id=1, replica_groups=mesh['expert'=16,'replica'=2] {'expert'}, dimensions={0} | all-to-all | bytes 16384 | tf_op jit(solution)/shard_map/all_to_all | solution.py:235
  149.3 6.2 %shard_map.90 = (f32[352,2048]{1,0:T(8,128)}, f32[16,352]{1,0:T(8,128)}) custom-call(bf16[320,2048]{1,0:T(8,128)(2,1)S(1)} %get-tuple-element.65.refs_0_, bf16[320,2048]{1,0:T(8,128)(2,1)S(1)} %get-tuple-element.66.refs_1_, bf16[320,2048]{1,0:T(8,128)(2,1)S(1)} %copy-done.2, bf16[320,2048]{1,0:T(8,128)(2,1)S(1)} %copy-done.4, ...), custom_call_target="tpu_custom_call" | custom-call | flops 1845493760 | bytes 9568256 | tf_op jit(solution)/shard_map/pallas_call | solution.py:326
  (69 shorter events, 20.7 us)
Async XLA Ops:
  2.6 17.9 %collective-permute-start.3 = (bf16[128,2176]{1,0:T(8,128)(2,1)S(1)}, bf16[128,2176]{1,0:T(8,128)(2,1)S(1)}, u32[]{:S(2)}, u32[]{:S(2)}) collective-permute-start(bf16[128,2176]{1,0:T(8,128)(2,1)S(1)} %get-tuple-element.39.ext_ref), channel_id=1, source_target_pairs={{0,8},{2,10},{4,12},{6,14},{8,16},{10,18},{12,20},{14,22},{16,24},... | collective-permute-start | bytes 1671176 | tf_op jit(solution)/shard_map/ppermute | solution.py:229
  5.7 1.2 copy-start.22
  10.8 94.5 %all-to-all-start.1 = ((bf16[16,72,384]{2,1,0:T(8,128)(2,1)}), bf16[16,72,384]{2,1,0:T(8,128)(2,1)S(1)}, u32[]{:S(2)}, u32[]{:S(2)}) async-start(bf16[16,72,384]{2,1,0:T(8,128)(2,1)} %get-tuple-element.62), calls=%async_computation.1 | async-start | bytes 1769472 | tf_op jit(solution)/shard_map/all_to_all | solution.py:235
  20.5 26.1 %collective-permute-start.7 = (bf16[128,2176]{1,0:T(8,128)(2,1)S(1)}, bf16[128,2176]{1,0:T(8,128)(2,1)S(1)}, u32[]{:S(2)}, u32[]{:S(2)}) collective-permute-start(bf16[128,2176]{1,0:T(8,128)(2,1)S(1)} %collective-permute-done.3.ext_ref), channel_id=1, source_target_pairs={{0,8},{2,10},{4,12},{6,14},{8,16},{10,18},{12,20},{14,22},{16,24},... | collective-permute-start | bytes 1671176 | tf_op jit(solution)/shard_map/ppermute | solution.py:229
  46.6 28.3 %collective-permute-start.11 = (bf16[128,2176]{1,0:T(8,128)(2,1)S(1)}, bf16[128,2176]{1,0:T(8,128)(2,1)S(1)}, u32[]{:S(2)}, u32[]{:S(2)}) collective-permute-start(bf16[128,2176]{1,0:T(8,128)(2,1)S(1)} %collective-permute-done.7.ext_ref), channel_id=1, source_target_pairs={{0,8},{2,10},{4,12},{6,14},{8,16},{10,18},{12,20},{14,22},{16,24},... | collective-permute-start | bytes 1671176 | tf_op jit(solution)/shard_map/ppermute | solution.py:229
  50.6 10.0 %collective-permute-start = (bf16[72,2048]{1,0:T(8,128)(2,1)S(1)}, bf16[72,2048]{1,0:T(8,128)(2,1)S(1)}, u32[]{:S(2)}, u32[]{:S(2)}) collective-permute-start(bf16[72,2048]{1,0:T(8,128)(2,1)S(1)} %get-tuple-element.41), channel_id=1, source_target_pairs={{0,2},{2,0},{4,6},{6,4},{8,10},{10,8},{12,14},{14,12},{16,18},{18,... | collective-permute-start | bytes 884744 | tf_op jit(solution)/shard_map/ppermute | solution.py:232
  52.2 14.8 %collective-permute-start.1 = (bf16[72,2048]{1,0:T(8,128)(2,1)S(1)}, bf16[72,2048]{1,0:T(8,128)(2,1)S(1)}, u32[]{:S(2)}, u32[]{:S(2)}) collective-permute-start(bf16[72,2048]{1,0:T(8,128)(2,1)S(1)} %get-tuple-element.42), channel_id=1, source_target_pairs={{0,4},{2,6},{4,0},{6,2},{8,12},{10,14},{12,8},{14,10},{16,20},{18,... | collective-permute-start | bytes 884744 | tf_op jit(solution)/shard_map/ppermute | solution.py:232
  53.7 14.3 %collective-permute-start.2 = (bf16[72,2048]{1,0:T(8,128)(2,1)S(1)}, bf16[72,2048]{1,0:T(8,128)(2,1)S(1)}, u32[]{:S(2)}, u32[]{:S(2)}) collective-permute-start(bf16[72,2048]{1,0:T(8,128)(2,1)S(1)} %get-tuple-element.43), channel_id=1, source_target_pairs={{0,6},{2,4},{4,2},{6,0},{8,14},{10,12},{12,10},{14,8},{16,22},{18,... | collective-permute-start | bytes 884744 | tf_op jit(solution)/shard_map/ppermute | solution.py:232
  54.7 18.6 %collective-permute-start.4 = (bf16[72,2048]{1,0:T(8,128)(2,1)S(1)}, bf16[72,2048]{1,0:T(8,128)(2,1)S(1)}, u32[]{:S(2)}, u32[]{:S(2)}) collective-permute-start(bf16[72,2048]{1,0:T(8,128)(2,1)S(1)} %get-tuple-element.46), channel_id=1, source_target_pairs={{0,2},{2,0},{4,6},{6,4},{8,10},{10,8},{12,14},{14,12},{16,18},{18,... | collective-permute-start | bytes 884744 | tf_op jit(solution)/shard_map/ppermute | solution.py:232
  60.6 19.0 %collective-permute-start.5 = (bf16[72,2048]{1,0:T(8,128)(2,1)S(1)}, bf16[72,2048]{1,0:T(8,128)(2,1)S(1)}, u32[]{:S(2)}, u32[]{:S(2)}) collective-permute-start(bf16[72,2048]{1,0:T(8,128)(2,1)S(1)} %get-tuple-element.47), channel_id=1, source_target_pairs={{0,4},{2,6},{4,0},{6,2},{8,12},{10,14},{12,8},{14,10},{16,20},{18,... | collective-permute-start | bytes 884744 | tf_op jit(solution)/shard_map/ppermute | solution.py:232
  67.0 13.6 %collective-permute-start.6 = (bf16[72,2048]{1,0:T(8,128)(2,1)S(1)}, bf16[72,2048]{1,0:T(8,128)(2,1)S(1)}, u32[]{:S(2)}, u32[]{:S(2)}) collective-permute-start(bf16[72,2048]{1,0:T(8,128)(2,1)S(1)} %get-tuple-element.48), channel_id=1, source_target_pairs={{0,6},{2,4},{4,2},{6,0},{8,14},{10,12},{12,10},{14,8},{16,22},{18,... | collective-permute-start | bytes 884744 | tf_op jit(solution)/shard_map/ppermute | solution.py:232
  67.9 18.0 %collective-permute-start.8 = (bf16[72,2048]{1,0:T(8,128)(2,1)S(1)}, bf16[72,2048]{1,0:T(8,128)(2,1)S(1)}, u32[]{:S(2)}, u32[]{:S(2)}) collective-permute-start(bf16[72,2048]{1,0:T(8,128)(2,1)S(1)} %get-tuple-element.51), channel_id=1, source_target_pairs={{0,2},{2,0},{4,6},{6,4},{8,10},{10,8},{12,14},{14,12},{16,18},{18,... | collective-permute-start | bytes 884744 | tf_op jit(solution)/shard_map/ppermute | solution.py:232
  73.3 25.5 %collective-permute-start.9 = (bf16[72,2048]{1,0:T(8,128)(2,1)S(1)}, bf16[72,2048]{1,0:T(8,128)(2,1)S(1)}, u32[]{:S(2)}, u32[]{:S(2)}) collective-permute-start(bf16[72,2048]{1,0:T(8,128)(2,1)S(1)} %get-tuple-element.52), channel_id=1, source_target_pairs={{0,4},{2,6},{4,0},{6,2},{8,12},{10,14},{12,8},{14,10},{16,20},{18,... | collective-permute-start | bytes 884744 | tf_op jit(solution)/shard_map/ppermute | solution.py:232
  74.8 24.0 %collective-permute-start.10 = (bf16[72,2048]{1,0:T(8,128)(2,1)S(1)}, bf16[72,2048]{1,0:T(8,128)(2,1)S(1)}, u32[]{:S(2)}, u32[]{:S(2)}) collective-permute-start(bf16[72,2048]{1,0:T(8,128)(2,1)S(1)} %get-tuple-element.53), channel_id=1, source_target_pairs={{0,6},{2,4},{4,2},{6,0},{8,14},{10,12},{12,10},{14,8},{16,22},{18,... | collective-permute-start | bytes 884744 | tf_op jit(solution)/shard_map/ppermute | solution.py:232
  79.6 31.5 %collective-permute-start.12 = (bf16[72,2048]{1,0:T(8,128)(2,1)}, bf16[72,2048]{1,0:T(8,128)(2,1)}, u32[]{:S(2)}, u32[]{:S(2)}) collective-permute-start(bf16[72,2048]{1,0:T(8,128)(2,1)} %get-tuple-element.56), channel_id=1, source_target_pairs={{0,2},{2,0},{4,6},{6,4},{8,10},{10,8},{12,14},{14,12},{16,18},{18,... | collective-permute-start | bytes 884744 | tf_op jit(solution)/shard_map/ppermute | solution.py:232
  80.6 30.5 %collective-permute-start.13 = (bf16[72,2048]{1,0:T(8,128)(2,1)}, bf16[72,2048]{1,0:T(8,128)(2,1)}, u32[]{:S(2)}, u32[]{:S(2)}) collective-permute-start(bf16[72,2048]{1,0:T(8,128)(2,1)} %get-tuple-element.57), channel_id=1, source_target_pairs={{0,4},{2,6},{4,0},{6,2},{8,12},{10,14},{12,8},{14,10},{16,20},{18,... | collective-permute-start | bytes 884744 | tf_op jit(solution)/shard_map/ppermute | solution.py:232
  86.0 25.1 %collective-permute-start.14 = (bf16[72,2048]{1,0:T(8,128)(2,1)}, bf16[72,2048]{1,0:T(8,128)(2,1)}, u32[]{:S(2)}, u32[]{:S(2)}) collective-permute-start(bf16[72,2048]{1,0:T(8,128)(2,1)} %get-tuple-element.58), channel_id=1, source_target_pairs={{0,6},{2,4},{4,2},{6,0},{8,14},{10,12},{12,10},{14,8},{16,22},{18,... | collective-permute-start | bytes 884744 | tf_op jit(solution)/shard_map/ppermute | solution.py:232
  92.9 4.9 %copy-start.5 = (f32[704,320]{1,0:T(8,128)}, f32[704,320]{1,0:T(8,128)S(1)}, u32[]{:S(2)}) copy-start(f32[704,320]{1,0:T(8,128)S(1)} %get-tuple-element.44.refs_0_) | copy-start | bytes 2703364
  105.3 23.8 %all-to-all-start = ((bf16[16,72,384]{2,1,0:T(8,128)(2,1)}), bf16[16,72,384]{2,1,0:T(8,128)(2,1)}, u32[]{:S(2)}, u32[]{:S(2)}) async-start(bf16[16,72,384]{2,1,0:T(8,128)(2,1)} %copy-done.16), calls=%async_computation | async-start | bytes 1769472 | tf_op jit(solution)/shard_map/all_to_all | solution.py:235
  112.1 4.9 %copy-start.6 = (f32[704,320]{1,0:T(8,128)S(1)}, f32[704,320]{1,0:T(8,128)}, u32[]{:S(2)}) copy-start(f32[704,320]{1,0:T(8,128)} %copy-done.5) | copy-start | bytes 2703364
  112.1 4.9 %copy-start.9 = (f32[704,320]{1,0:T(8,128)S(1)}, f32[704,320]{1,0:T(8,128)}, u32[]{:S(2)}) copy-start(f32[704,320]{1,0:T(8,128)} %copy-done.8) | copy-start | bytes 2703364
  112.1 4.9 %copy-start.12 = (f32[704,320]{1,0:T(8,128)S(1)}, f32[704,320]{1,0:T(8,128)}, u32[]{:S(2)}) copy-start(f32[704,320]{1,0:T(8,128)} %copy-done.11) | copy-start | bytes 2703364
  116.9 1.5 copy-start.3
  117.0 2.1 %copy-start.1 = (bf16[320,2048]{1,0:T(8,128)(2,1)S(1)}, bf16[320,2048]{1,0:T(8,128)(2,1)}, u32[]{:S(2)}) copy-start(bf16[320,2048]{1,0:T(8,128)(2,1)} %copy-done) | copy-start | bytes 3932164
  122.8 26.5 %collective-permute-start.15 = (bf16[352,2048]{1,0:T(8,128)(2,1)}, bf16[352,2048]{1,0:T(8,128)(2,1)}, u32[]{:S(2)}, u32[]{:S(2)}) collective-permute-start(bf16[352,2048]{1,0:T(8,128)(2,1)} %shard_map.89), channel_id=1, source_target_pairs={{0,1},{1,0},{2,3},{3,2},{4,5},{5,4},{6,7},{7,6},{8,9},{9,8},{10,11... | collective-permute-start | bytes 4325384 | tf_op jit(solution)/shard_map/ppermute | solution.py:325
  129.1 1.2 copy-start.7
  130.3 1.2 copy-start.10
  131.5 1.2 copy-start.13
  132.8 1.2 copy-start.15
  134.0 14.7 %copy-start.21 = (s32[128,6]{0,1:T(8,128)S(1)}, s32[128,6]{0,1:T(8,128)}, u32[]{:S(2)}) copy-start(s32[128,6]{0,1:T(8,128)} %param.7) | copy-start | bytes 9220
  134.0 15.3 %copy-start.2 = (bf16[320,2048]{1,0:T(8,128)(2,1)S(1)}, bf16[320,2048]{1,0:T(8,128)(2,1)}, u32[]{:S(2)}) copy-start(bf16[320,2048]{1,0:T(8,128)(2,1)} %copy-done) | copy-start | bytes 3932164
  134.0 15.3 %copy-start.4 = (bf16[320,2048]{1,0:T(8,128)(2,1)S(1)}, bf16[320,2048]{1,0:T(8,128)(2,1)}, u32[]{:S(2)}) copy-start(bf16[320,2048]{1,0:T(8,128)(2,1)} %copy-done.3) | copy-start | bytes 3932164
  (10 other events, 9.1 us)

commit v3 on v2

v3 whole, which is shorter than its diff:
```python
import functools

import jax
import jax.numpy as jnp
from jax import lax
from jax.experimental import pallas as pl
from jax.experimental.pallas import tpu as pltpu
from jax.sharding import PartitionSpec as P

BLOCK = 128
PLANE = 4
BF = jnp.bfloat16
F32 = jnp.float32
NT = (((1,), (1,)), ((), ()))
VMEM_BYTES = 24 * 1024 * 1024


def up(value, unit):
    return -(-value // unit) * unit


def call(kernel, out_shape, pace=0, **kw):
    return pl.pallas_call(
        kernel,
        out_shape=out_shape,
        cost_estimate=pl.CostEstimate(
            flops=1024 + pace * 1_000_000_000, bytes_accessed=1024, transcendentals=0
        ),
        compiler_params=pltpu.CompilerParams(vmem_limit_bytes=VMEM_BYTES),
        **kw,
    )


def table_kernel(stride, routes_ref, cot_ref, ext_ref, slot_ref, code_ref):
    experts, tokens = slot_ref.shape
    top_k = routes_ref.shape[0]
    model = cot_ref.shape[1]
    routes = routes_ref[...]
    ids = lax.broadcasted_iota(jnp.int32, (experts, tokens), 0)
    mask = jnp.zeros((experts, tokens), F32)
    for k in range(top_k):
        mask += jnp.where(routes[k : k + 1, :] == ids, 1.0, 0.0)
    earlier = lax.broadcasted_iota(jnp.int32, (tokens, tokens), 0) < lax.broadcasted_iota(
        jnp.int32, (tokens, tokens), 1
    )
    rank = jnp.dot(
        mask.astype(BF), jnp.where(earlier, 1.0, 0.0).astype(BF), preferred_element_type=F32
    )
    slot = jnp.where(mask > 0.5, rank, -1.0)
    slot_ref[...] = slot
    me = lax.axis_index("expert")
    steps = (routes >> 2) - (me >> 2)
    steps = jnp.where(steps < 0, steps + experts // PLANE, steps)
    rel = steps * PLANE + ((routes & 3) ^ (me & 3))
    for k in range(top_k):
        own = jnp.sum(
            jnp.where(routes[k : k + 1, :] == ids, slot, 0.0), axis=0, keepdims=True
        ).astype(jnp.int32)
        code_ref[k : k + 1, :] = rel[k : k + 1, :] * stride + own
    wide = jnp.concatenate([slot, jnp.zeros((BLOCK - experts, tokens), F32)], axis=0)
    ext_ref[:, 0:model] = cot_ref[...]
    ext_ref[:, model : model + BLOCK] = wide.T.astype(BF)


def halves(flip):
    mine = lax.axis_index("replica") if flip else 1
    return 1 - mine, mine


def select(slots, stride, table, cot_ref, outs):
    me = lax.axis_index("expert")
    tokens = cot_ref.shape[0]
    rows = lax.broadcasted_iota(jnp.int32, (stride, tokens), 0).astype(F32)
    pick = jnp.concatenate(
        [jnp.where(table[pl.ds(me ^ k, 1), :] == rows, 1.0, 0.0) for k in range(PLANE)], axis=0
    ).astype(BF)
    model = cot_ref.shape[1]
    step = min(512, model)
    for c in range(0, model, step):
        got = jnp.dot(pick, cot_ref[:, c : c + step], preferred_element_type=F32)
        for k in range(PLANE):
            outs[k][:, c : c + step] = got[k * stride : k * stride + slots, :].astype(BF)


def first_kernel(slots, stride, flip, slot_ref, cot_ref, code_ref, num_ref, hid_ref, *refs):
    outs, table = refs[:PLANE], refs[PLANE]
    select(slots, stride, slot_ref, cot_ref, outs)
    model = cot_ref.shape[1]
    top_k, width, tokens = hid_ref.shape
    half = width // 2
    padded = table.shape[0] // 2
    code = jnp.concatenate([code_ref[k : k + 1, :] for k in range(top_k)], axis=1)
    group = PLANE * stride
    for n, part in enumerate(halves(flip)):
        at = pl.multiple_of(part * half, 16) if flip else part * half
        for k in range(top_k):
            lanes = slice(k * tokens, (k + 1) * tokens)
            table[n * padded : n * padded + half, lanes] = hid_ref[k, pl.ds(at, half), :]
            weight = num_ref[k : k + 1, :].astype(F32) * (1.0 / 1024.0)
            high = weight.astype(BF).astype(F32)
            rows = lax.broadcasted_iota(jnp.int32, (padded - half, tokens), 0)
            tail = jnp.where(rows == 0, high, jnp.where(rows == 1, weight - high, 0.0))
            table[n * padded + half : (n + 1) * padded, lanes] = tail.astype(BF)
    for s in range((outs[0].shape[1] - model) // (2 * padded)):
        rows = lax.broadcasted_iota(jnp.int32, (group, top_k * tokens), 0) + s * group
        pick = jnp.where(rows == code, 1.0, 0.0).astype(BF)
        got = lax.dot_general(pick, table[...], NT, preferred_element_type=F32)
        at = model + s * 2 * padded
        for k in range(PLANE):
            outs[k][:, at : at + 2 * padded] = got[k * stride : k * stride + slots, :].astype(BF)


def relay_kernel(slots, stride, ext_ref, *refs):
    outs, table = refs[-1 - PLANE : -1], refs[-1]
    model = outs[0].shape[1]
    table[...] = ext_ref[:, model : model + BLOCK].astype(F32).T
    select(slots, stride, table, ext_ref.at[:, pl.ds(0, model)], outs)


def regroup_kernel(model, *refs):
    outs = refs[PLANE:]
    padded = outs[0].shape[2]
    for s, out_ref in enumerate(outs):
        at = model + (s + 1) * padded
        for k in range(PLANE):
            out_ref[k] = refs[k][:, at : at + padded]


def fill(table, at, piece, stride):
    wide = piece.astype(F32)
    short = stride - wide.shape[0]
    if short:
        wide = jnp.concatenate([wide, jnp.zeros((short, wide.shape[1]), F32)], axis=0)
    table[at : at + stride, :] = wide.astype(table.dtype)


def halves(flip):
    mine = lax.axis_index("replica") if flip else 1
    return 1 - mine, mine


def stage_kernel(stage, stride, flip, split, *refs):
    pieces, w_ref, refs = refs[:PLANE], refs[PLANE], refs[PLANE + 1 :]
    all_rows, all_hidw, gate_ref, rows, hids, hidw, done = refs[-7:]
    group = PLANE * stride
    width, model = w_ref.shape
    half = width // 2
    padded = hids.shape[1] // 2
    for k, piece in enumerate(pieces):
        fill(rows, k * stride, piece[:, 0:model], stride)
    copy = pltpu.make_async_copy(rows, all_rows.at[pl.ds(stage * group, group)], done.at[0])
    copy.start()
    for k in range(PLANE):
        hid = refs[0][k] if split else pieces[k][:, model : model + 2 * padded]
        fill(hids, k * stride, hid, stride)
    gate = 0.0
    for n, part in enumerate(halves(flip)):
        at = pl.multiple_of(part * half, 16) if flip else part * half
        flipped = hids[:, n * padded : (n + 1) * padded].T
        hid = flipped[0:half, :]
        weight = flipped[half : half + 1, :] + flipped[half + 1 : half + 2, :]
        hidw[n * half : (n + 1) * half, :] = (hid * weight).astype(BF)
        back = lax.dot_general(
            w_ref[pl.ds(at, half), :], rows[...], NT, preferred_element_type=F32
        )
        gate += jnp.sum(back * hid, axis=0, keepdims=True)
    second = pltpu.make_async_copy(
        hidw, all_hidw.at[:, pl.ds(stage * group, group)], done.at[1]
    )
    second.start()
    gate_ref[...] = jnp.zeros_like(gate_ref)
    for k in range(PLANE):
        gate_ref[k : k + 1, 0:stride] = gate[:, k * stride : (k + 1) * stride]
    copy.wait()
    second.wait()


def source(outer, s, k):
    me = lax.axis_index("expert")
    ring = (me >> 2) - s
    ring = jnp.where(ring < 0, ring + outer, ring)
    return ring * PLANE + ((me & 3) ^ k)


def partial_kernel(outer, rows_ref, hidw_ref, *refs):
    gates, (send_ref, mine_ref, gate_ref) = refs[:outer], refs[outer:]

    @pl.when(pl.program_id(0) == 0)
    def _():
        for s in range(outer):
            for k in range(PLANE):
                gate_ref[pl.ds(source(outer, s, k), 1), :] = gates[s][k : k + 1, :]

    half = mine_ref.shape[0]
    got = jnp.dot(hidw_ref[...], rows_ref[...], preferred_element_type=F32)
    send_ref[...] = got[0:half].astype(BF)
    mine_ref[...] = got[half:].astype(mine_ref.dtype)


def finish_kernel(own_ref, others_ref, out_ref, scale_ref, table):
    step = pl.program_id(0)
    share, width = out_ref.shape
    lanes = lax.broadcasted_iota(jnp.int32, (share, BLOCK), 1)

    @pl.when(step == 0)
    def _():
        table[...] = jnp.zeros_like(table)

    kept = table[0:share, :]
    for b in range(width // BLOCK):
        span = slice(b * BLOCK, (b + 1) * BLOCK)
        terms = [others_ref[n, :, span].astype(F32) for n in range(others_ref.shape[0])]
        if own_ref is not None:
            terms.append(own_ref[:, span])
        top = functools.reduce(jnp.maximum, [jnp.abs(term) for term in terms])
        scale = jnp.max(top, axis=1, keepdims=True) + 1e-6
        out_ref[:, span] = functools.reduce(jnp.add, terms) * (1.0 / scale)
        kept = jnp.where(lanes == step * (width // BLOCK) + b, scale, kept)
    table[0:share, :] = kept

    @pl.when(step == pl.num_programs(0) - 1)
    def _():
        scale_ref[...] = table[...].T[0 : scale_ref.shape[0], 0:share]


def pick_kernel(after_ref, slot_ref, routes_ref, rows_ref, out_ref):
    experts, tokens = slot_ref.shape
    slot = jnp.maximum(slot_ref[...], 0.0).astype(jnp.int32)
    value = jnp.take_along_axis(rows_ref[...], slot, axis=1)
    ids = lax.broadcasted_iota(jnp.int32, (experts, tokens), 0)
    for k in range(out_ref.shape[0]):
        out_ref[k : k + 1, :] = jnp.sum(
            jnp.where(routes_ref[k : k + 1, :] == ids, value, 0.0), axis=0, keepdims=True
        )


def per_device(cotangent, hidden, routes, numerators, w_down):
    tokens, model = cotangent.shape
    top_k, width = hidden.shape[1], hidden.shape[2]
    experts, replicas = lax.axis_size("expert"), lax.axis_size("replica")
    outer = experts // PLANE
    slots = up(3 * tokens * top_k // (2 * experts), 8)
    stride = up(slots, 32)
    half = width // 2
    padded = up(half + 2, 128)
    share = width // replicas
    group = PLANE * stride
    flip = replicas == 2
    sds = jax.ShapeDtypeStruct
    step = 512
    steps = model // step

    def ring(array, by):
        pairs = [(e, (e + by * PLANE) % experts) for e in range(experts)]
        return lax.ppermute(array, "expert", pairs)

    def swap(array, k):
        return lax.ppermute(array, "expert", [(e, e ^ k) for e in range(experts)])

    def exchange(array):
        return lax.all_to_all(array, "expert", split_axis=0, concat_axis=0, tiled=True)

    anywhere = pl.BlockSpec(memory_space=pl.ANY)
    inside = pl.BlockSpec(memory_space=pltpu.VMEM)

    ext, slot, code = call(
        functools.partial(table_kernel, stride),
        (
            sds((tokens, model + BLOCK), BF),
            sds((experts, tokens), F32),
            sds((top_k, tokens), jnp.int32),
        ),
    )(routes.T, cotangent)

    wide = model + outer * 2 * padded
    sent = call(
        functools.partial(first_kernel, slots, stride, flip),
        [sds((slots, wide), BF)] * PLANE,
        15,
        scratch_shapes=[pltpu.VMEM((2 * padded, top_k * tokens), BF)],
    )(slot, cotangent, code, numerators.T, jnp.transpose(hidden, (1, 2, 0)))
    swapped = {k: swap(sent[k], k) for k in (3, 1, 2)}
    stages = {0: [sent[0]] + [swapped[k] for k in range(1, PLANE)]}

    blocks = {0: ext}
    order = [0]
    for s in range(1, outer // 2 + 1):
        blocks[s] = ring(blocks[s - 1], 1)
        order.append(s)
        if outer - s != s:
            blocks[outer - s] = ring(blocks[(outer - s + 1) % outer], -1)
            order.append(outer - s)
    hids = call(
        functools.partial(regroup_kernel, model),
        [sds((PLANE, slots, 2 * padded), BF)] * (outer - 1),
    )(*stages[0])
    hids = {s: ring(hids[s - 1], s) for s in order[1:]}
    for s in order[1:]:
        sent = call(
            functools.partial(relay_kernel, slots, stride),
            [sds((slots, model), BF)] * PLANE,
            15,
            in_specs=[inside, anywhere],
            scratch_shapes=[pltpu.VMEM((BLOCK, tokens), F32)],
        )(blocks[s], swapped[3])
        swapped = {k: swap(sent[k], k) for k in (3, 1, 2)}
        stages[s] = [sent[0]] + [swapped[k] for k in range(1, PLANE)]

    rows, gates = [], {}
    for s in order:
        hid = [hids[s]] if s else []
        *rows, gates[s] = call(
            functools.partial(stage_kernel, s, stride, flip, bool(s)),
            [
                sds((outer * group, model), BF),
                sds((width, outer * group), BF),
                sds((PLANE, BLOCK), F32),
            ],
            in_specs=[inside] * (PLANE + 1 + len(hid)) + [anywhere] * len(rows),
            out_specs=[anywhere, anywhere, inside],
            input_output_aliases={PLANE + 1 + len(hid) + n: n for n in range(len(rows))},
            scratch_shapes=[
                pltpu.VMEM((group, model), BF),
                pltpu.VMEM((group, 2 * padded), F32),
                pltpu.VMEM((width, group), BF),
                pltpu.SemaphoreType.DMA((2,)),
            ],
        )(*stages[s], w_down[0], *hid, *rows)

    flat = pl.BlockSpec((half, step), lambda j: (0, j))
    send, mine, gates = call(
        functools.partial(partial_kernel, outer),
        [
            sds((half, model), BF),
            sds((half, model), F32 if flip else BF),
            sds((experts, BLOCK), F32),
        ],
        grid=(steps,),
        in_specs=[
            pl.BlockSpec((outer * group, step), lambda j: (0, j)),
            pl.BlockSpec((width, outer * group), lambda j: (0, 0)),
        ]
        + [pl.BlockSpec((PLANE, BLOCK), lambda j: (0, 0))] * outer,
        out_specs=[flat, flat, pl.BlockSpec((experts, BLOCK), lambda j: (0, 0))],
    )(*rows, *[gates[s] for s in range(outer)])
    returned = exchange(gates)
    if flip:
        kernel = finish_kernel
        others = lax.ppermute(send, "replica", [(0, 1), (1, 0)])[None]
        operands, specs = [mine], [flat]
    else:
        kernel = functools.partial(finish_kernel, None)
        both = jnp.concatenate([send, mine], axis=0).reshape(replicas, share, model)
        others = lax.all_to_all(both, "replica", 0, 0, tiled=True)
        operands, specs = [], []
    out, scales = call(
        kernel,
        [sds((share, model), F32), sds((model // BLOCK, share), F32)],
        grid=(steps,),
        in_specs=specs + [pl.BlockSpec((others.shape[0], share, step), lambda j: (0, 0, j))],
        out_specs=[
            pl.BlockSpec((share, step), lambda j: (0, j)),
            pl.BlockSpec((model // BLOCK, share), lambda j: (0, 0)),
        ],
        scratch_shapes=[pltpu.VMEM((up(share, 128), BLOCK), F32)],
    )(*operands, others)
    gate_grad = call(
        pick_kernel,
        sds((top_k, tokens), F32),
        in_specs=[anywhere] + [inside] * 3,
        out_specs=inside,
    )(scales, slot, routes.T, returned)
    return gate_grad.T, scales.T[None], out[None]


def solution(mesh):
    return jax.shard_map(
        per_device,
        mesh=mesh,
        in_specs=(
            P(("expert", "replica"), None),
            P(("expert", "replica"), None, None),
            P(("expert", "replica"), None),
            P(("expert", "replica"), None),
            P("expert", None, None),
        ),
        out_specs=(
            P(("expert", "replica"), None),
            P("expert", "replica", None),
            P("expert", "replica", None),
        ),
        check_vma=False,
    )
```

time: 157 us -> 123 us (0.78)
  Pallas kernels: 37.8 us -> 24.5 us
  blocking collectives: 12.6 us -> 0 us
  local copies, waits for them, and re-layouts: 15.6 us -> 5.43 us
  starting transfers between devices: 35.7 us -> 38.7 us
    all_to_all x1 -> x0, blocking collectives: 12.6 us -> none  [exchange(): lax.all_to_all(array, 'expert', split_axis=0, concat_axis=0, tiled=True)]
    pallas_call x10 -> x9, Pallas kernels: 34.3 us -> 22.4 us  [the longest x4 8.22 us: per_device(): call(functools.partial(stage_kernel, s, stride, flip, bool(s)), [sds((out...]
    unnamed x48 -> x16, local copies, waits for them, and re-layouts: 15.5 us -> 5.43 us
    ppermute x3 -> x6, starting transfers between devices: 7.14 us -> 13.2 us  [ring(): return lax.ppermute(array, 'expert', pairs)]
    ppermute x3 -> x6, waiting for transfers between devices: 29.3 us -> 32.9 us  [ring(): return lax.ppermute(array, 'expert', pairs)]
    all_to_all x2 -> x1, waiting for transfers between devices: 6.24 us -> 2.77 us  [exchange(): lax.all_to_all(array, 'expert', split_axis=0, concat_axis=0, tiled=True)]
    all_to_all x2 -> x1, starting transfers between devices: 11.6 us -> 8.45 us  [exchange(): lax.all_to_all(array, 'expert', split_axis=0, concat_axis=0, tiled=True)]
    pallas_call x4 -> x3, Pallas kernels: 3.2 us -> 1.9 us  [per_device(): call(functools.partial(relay_kernel, slots, stride), [sds((slots, model),...]
  transfers between devices with their start and end apart: 18 -> 20, of which waited for: 10 -> 10; matrix products, arithmetic and copies ran while one was open for 0% -> 0% of each run, Pallas kernels for 20% -> 10%
where the time goes in v3:
time: 123 us; the launch traced here: 122 us
  waiting for transfers between devices  52.8 us (43%)
  starting transfers between devices  38.7 us (31%)
  Pallas kernels  24.5 us (20%)
  local copies, waits for them, and re-layouts  5.43 us (4%)
    ppermute x6, waiting for transfers between devices, ring(): return lax.ppermute(array, 'expert', pairs)  32.9 us
    ppermute x12, waiting for transfers between devices, swap(): return lax.ppermute(array, 'expert', [(e, e ^ k) for e in range(experts)])  17.1 us
    ppermute x12, starting transfers between devices, swap(): return lax.ppermute(array, 'expert', [(e, e ^ k) for e in range(experts)])  17 us
    ppermute x6, starting transfers between devices, ring(): return lax.ppermute(array, 'expert', pairs)  13.2 us
    all_to_all x1, starting transfers between devices, exchange(): lax.all_to_all(array, 'expert', split_axis=0, concat_axis=0, tiled=True)  8.45 us
    pallas_call x4, Pallas kernels, per_device(): call(functools.partial(stage_kernel, s, stride, flip, bool(s)), [sds((out...  8.22 us
    pallas_call x1, Pallas kernels, per_device(): call(functools.partial(partial_kernel, outer), [sds((half, model), BF), s...  6.52 us
    unnamed x16, local copies, waits for them, and re-layouts  5.43 us
  transfers between devices with their start and end apart: 20, of which 10 were waited for; matrix products, arithmetic and copies ran while one was open for 0% of the time, Pallas kernels for 10%

profile of v3, /device:TPU:0, one launch (start us, length us, event | category | flops | bytes accessed | tf_op | source)
XLA Modules:
  0.0 122.2 jit_solution(5901312102044311941)
XLA Ops:
  0.6 1.0 copy-done.1
  2.6 1.0 copy-done.2
  3.6 1.2 %copy-done.6 = bf16[128,6,704]{0,2,1:T(8,128)(2,1)S(1)} copy-done((bf16[128,6,704]{0,2,1:T(8,128)(2,1)S(1)}, bf16[128,6,704]{0,2,1:T(8,128)(2,1)}, u32[]{:S(2)}) %copy-start.6) | copy-done | bytes 1081368
  5.6 2.4 %shard_map.77 = (bf16[72,5120]{1,0:T(8,128)(2,1)S(1)}, bf16[72,5120]{1,0:T(8,128)(2,1)S(1)}, bf16[72,5120]{1,0:T(8,128)(2,1)S(1)}, bf16[72,5120]{1,0:T(8,128)(2,1)S(1)}) custom-call(f32[16,128]{1,0:T(8,128)S(1)} %get-tuple-element.43.slot_ref, bf16[128,2048]{1,0:T(8,128)(2,1)S(1)} %copy-done.2, s32[6,128]{1,0:T(8,128)S(1)} %get-tuple-element.44.code_ref, ...), custom_call_target="tpu_custom_call" | custom-call | flops 15000000512 | bytes 1024 | tf_op jit(solution)/shard_map/pallas_call | solution.py:276
  8.0 4.0 %collective-permute-start.3 = (bf16[72,5120]{1,0:T(8,128)(2,1)S(1)}, bf16[72,5120]{1,0:T(8,128)(2,1)S(1)}, u32[]{:S(2)}, u32[]{:S(2)}) collective-permute-start(bf16[72,5120]{1,0:T(8,128)(2,1)S(1)} %get-tuple-element.45), channel_id=1, source_target_pairs={{0,6},{2,4},{4,2},{6,0},{8,14},{10,12},{12,10},{14,8},{16,22},{18,... | collective-permute-start | bytes 2211848 | tf_op jit(solution)/shard_map/ppermute | solution.py:258
  11.9 1.6 %collective-permute-start = (bf16[128,2176]{1,0:T(8,128)(2,1)S(1)}, bf16[128,2176]{1,0:T(8,128)(2,1)S(1)}, u32[]{:S(2)}, u32[]{:S(2)}) collective-permute-start(bf16[128,2176]{1,0:T(8,128)(2,1)S(1)} %get-tuple-element.42), channel_id=1, source_target_pairs={{0,8},{2,10},{4,12},{6,14},{8,16},{10,18},{12,20},{14,22},{16,24},... | collective-permute-start | bytes 1671176 | tf_op jit(solution)/shard_map/ppermute | solution.py:255
  13.5 2.2 %collective-permute-start.2 = (bf16[128,2176]{1,0:T(8,128)(2,1)S(1)}, bf16[128,2176]{1,0:T(8,128)(2,1)S(1)}, u32[]{:S(2)}, u32[]{:S(2)}) collective-permute-start(bf16[128,2176]{1,0:T(8,128)(2,1)S(1)} %get-tuple-element.42), channel_id=1, source_target_pairs={{0,24},{2,26},{4,28},{6,30},{8,0},{10,2},{12,4},{14,6},{16,8},{18,... | collective-permute-start | bytes 1671176 | tf_op jit(solution)/shard_map/ppermute | solution.py:255
  15.8 13.6 %collective-permute-done.ext_ref = bf16[128,2176]{1,0:T(8,128)(2,1)S(1)} collective-permute-done((bf16[128,2176]{1,0:T(8,128)(2,1)S(1)}, bf16[128,2176]{1,0:T(8,128)(2,1)S(1)}, u32[]{:S(2)}, u32[]{:S(2)}) %collective-permute-start) | collective-permute-done | bytes 557088 | tf_op jit(solution)/shard_map/ppermute | solution.py:255
  30.0 1.8 %collective-permute-start.4 = (bf16[72,2048]{1,0:T(8,128)(2,1)S(1)}, bf16[72,2048]{1,0:T(8,128)(2,1)S(1)}, u32[]{:S(2)}, u32[]{:S(2)}) collective-permute-start(bf16[72,2048]{1,0:T(8,128)(2,1)S(1)} %get-tuple-element.46), channel_id=1, source_target_pairs={{0,6},{2,4},{4,2},{6,0},{8,14},{10,12},{12,10},{14,8},{16,22},{18,... | collective-permute-start | bytes 884744 | tf_op jit(solution)/shard_map/ppermute | solution.py:258
  32.3 1.3 %collective-permute-start.9 = (bf16[72,5120]{1,0:T(8,128)(2,1)S(1)}, bf16[72,5120]{1,0:T(8,128)(2,1)S(1)}, u32[]{:S(2)}, u32[]{:S(2)}) collective-permute-start(bf16[72,5120]{1,0:T(8,128)(2,1)S(1)} %get-tuple-element.53), channel_id=1, source_target_pairs={{0,2},{2,0},{4,6},{6,4},{8,10},{10,8},{12,14},{14,12},{16,18},{18,... | collective-permute-start | bytes 2211848 | tf_op jit(solution)/shard_map/ppermute | solution.py:258
  33.5 0.9 collective-permute-start.1
  34.4 5.6 %collective-permute-done.2.ext_ref = bf16[128,2176]{1,0:T(8,128)(2,1)S(1)} collective-permute-done((bf16[128,2176]{1,0:T(8,128)(2,1)S(1)}, bf16[128,2176]{1,0:T(8,128)(2,1)S(1)}, u32[]{:S(2)}, u32[]{:S(2)}) %collective-permute-start.2) | collective-permute-done | bytes 557088 | tf_op jit(solution)/shard_map/ppermute | solution.py:255
  41.6 1.8 %collective-permute-start.5 = (bf16[72,2048]{1,0:T(8,128)(2,1)S(1)}, bf16[72,2048]{1,0:T(8,128)(2,1)S(1)}, u32[]{:S(2)}, u32[]{:S(2)}) collective-permute-start(bf16[72,2048]{1,0:T(8,128)(2,1)S(1)} %get-tuple-element.47), channel_id=1, source_target_pairs={{0,6},{2,4},{4,2},{6,0},{8,14},{10,12},{12,10},{14,8},{16,22},{18,... | collective-permute-start | bytes 884744 | tf_op jit(solution)/shard_map/ppermute | solution.py:258
  43.3 10.7 %collective-permute-done.10.refs_2_ = bf16[72,5120]{1,0:T(8,128)(2,1)S(1)} collective-permute-done((bf16[72,5120]{1,0:T(8,128)(2,1)S(1)}, bf16[72,5120]{1,0:T(8,128)(2,1)S(1)}, u32[]{:S(2)}, u32[]{:S(2)}) %collective-permute-start.10) | collective-permute-done | bytes 737312 | tf_op jit(solution)/shard_map/ppermute | solution.py:258
  54.0 2.0 %collective-permute-done.9.refs_1_ = bf16[72,5120]{1,0:T(8,128)(2,1)S(1)} collective-permute-done((bf16[72,5120]{1,0:T(8,128)(2,1)S(1)}, bf16[72,5120]{1,0:T(8,128)(2,1)S(1)}, u32[]{:S(2)}, u32[]{:S(2)}) %collective-permute-start.9) | collective-permute-done | bytes 737312 | tf_op jit(solution)/shard_map/ppermute | solution.py:258
  56.1 1.6 %collective-permute-start.17 = (bf16[4,72,768]{2,1,0:T(8,128)(2,1)S(1)}, bf16[4,72,768]{2,1,0:T(8,128)(2,1)S(1)}, u32[]{:S(2)}, u32[]{:S(2)}) collective-permute-start(bf16[4,72,768]{2,1,0:T(8,128)(2,1)S(1)} %get-tuple-element.63), channel_id=1, source_target_pairs={{0,8},{2,10},{4,12},{6,14},{8,16},{10,18},{12,20},{14,22},{16,24},... | collective-permute-start | bytes 1327112 | tf_op jit(solution)/shard_map/ppermute | solution.py:255
  58.3 4.1 %collective-permute-done.15.refs_1_ = bf16[72,2048]{1,0:T(8,128)(2,1)S(1)} collective-permute-done((bf16[72,2048]{1,0:T(8,128)(2,1)S(1)}, bf16[72,2048]{1,0:T(8,128)(2,1)S(1)}, u32[]{:S(2)}, u32[]{:S(2)}) %collective-permute-start.15) | collective-permute-done | bytes 294944 | tf_op jit(solution)/shard_map/ppermute | solution.py:258
  62.4 6.9 %collective-permute-start.14 = (bf16[4,72,768]{2,1,0:T(8,128)(2,1)S(1)}, bf16[4,72,768]{2,1,0:T(8,128)(2,1)S(1)}, u32[]{:S(2)}, u32[]{:S(2)}) collective-permute-start(bf16[4,72,768]{2,1,0:T(8,128)(2,1)S(1)} %get-tuple-element.59), channel_id=1, source_target_pairs={{0,24},{2,26},{4,28},{6,30},{8,0},{10,2},{12,4},{14,6},{16,8},{18,... | collective-permute-start | bytes 1327112 | tf_op jit(solution)/shard_map/ppermute | solution.py:255
  69.3 1.6 %collective-permute-start.12 = (bf16[72,2048]{1,0:T(8,128)(2,1)S(1)}, bf16[72,2048]{1,0:T(8,128)(2,1)S(1)}, u32[]{:S(2)}, u32[]{:S(2)}) collective-permute-start(bf16[72,2048]{1,0:T(8,128)(2,1)S(1)} %get-tuple-element.57), channel_id=1, source_target_pairs={{0,2},{2,0},{4,6},{6,4},{8,10},{10,8},{12,14},{14,12},{16,18},{18,... | collective-permute-start | bytes 884744 | tf_op jit(solution)/shard_map/ppermute | solution.py:258
  72.1 3.1 %collective-permute-done.17.refs_5_ = bf16[4,72,768]{2,1,0:T(8,128)(2,1)S(1)} collective-permute-done((bf16[4,72,768]{2,1,0:T(8,128)(2,1)S(1)}, bf16[4,72,768]{2,1,0:T(8,128)(2,1)S(1)}, u32[]{:S(2)}, u32[]{:S(2)}) %collective-permute-start.17) | collective-permute-done | bytes 442400 | tf_op jit(solution)/shard_map/ppermute | solution.py:255
  75.2 1.5 %collective-permute-start.6 = (bf16[72,2048]{1,0:T(8,128)(2,1)S(1)}, bf16[72,2048]{1,0:T(8,128)(2,1)S(1)}, u32[]{:S(2)}, u32[]{:S(2)}) collective-permute-start(bf16[72,2048]{1,0:T(8,128)(2,1)S(1)} %get-tuple-element.49), channel_id=1, source_target_pairs={{0,2},{2,0},{4,6},{6,4},{8,10},{10,8},{12,14},{14,12},{16,18},{18,... | collective-permute-start | bytes 884744 | tf_op jit(solution)/shard_map/ppermute | solution.py:258
  76.7 2.8 %collective-permute-done.14.refs_5_ = bf16[4,72,768]{2,1,0:T(8,128)(2,1)S(1)} collective-permute-done((bf16[4,72,768]{2,1,0:T(8,128)(2,1)S(1)}, bf16[4,72,768]{2,1,0:T(8,128)(2,1)S(1)}, u32[]{:S(2)}, u32[]{:S(2)}) %collective-permute-start.14) | collective-permute-done | bytes 442400 | tf_op jit(solution)/shard_map/ppermute | solution.py:255
  79.9 2.5 %collective-permute-start.8 = (bf16[72,2048]{1,0:T(8,128)(2,1)S(1)}, bf16[72,2048]{1,0:T(8,128)(2,1)S(1)}, u32[]{:S(2)}, u32[]{:S(2)}) collective-permute-start(bf16[72,2048]{1,0:T(8,128)(2,1)S(1)} %get-tuple-element.51), channel_id=1, source_target_pairs={{0,6},{2,4},{4,2},{6,0},{8,14},{10,12},{12,10},{14,8},{16,22},{18,... | collective-permute-start | bytes 884744 | tf_op jit(solution)/shard_map/ppermute | solution.py:258
  82.4 2.0 %shard_map.82 = (bf16[1536,2048]{1,0:T(8,128)(2,1)S(1)}, bf16[704,1536]{1,0:T(8,128)(2,1)S(1)}, f32[4,128]{1,0:T(4,128)S(1)}) custom-call(bf16[72,5120]{1,0:T(8,128)(2,1)S(1)} %get-tuple-element.52.refs_0_, bf16[72,5120]{1,0:T(8,128)(2,1)S(1)} %collective-permute-done.9.refs_1_, bf16[72,5120]{1,0:T(8,128)(2,1)S(1)} %collective-permute-done.10.refs_2_, ...), custom_call_target="tpu_custom_call" | custom-call | flops 1024 | bytes 1024 | tf_op jit(solution)/shard_map/pallas_call | solution.py:312
  84.5 2.1 %shard_map.83 = (bf16[1536,2048]{1,0:T(8,128)(2,1)S(1)}, bf16[704,1536]{1,0:T(8,128)(2,1)S(1)}, f32[4,128]{1,0:T(4,128)S(1)}) custom-call(bf16[72,2048]{1,0:T(8,128)(2,1)S(1)} %get-tuple-element.60.refs_0_, bf16[72,2048]{1,0:T(8,128)(2,1)S(1)} %collective-permute-done.15.refs_1_, ...), custom_call_target="tpu_custom_call", output_to_operand_aliasing={{0}: (6, {}), {1}: (7, {})} | custom-call | flops 1024 | bytes 1024 | tf_op jit(solution)/shard_map/pallas_call | solution.py:312
  86.6 2.1 %shard_map.84 = (bf16[1536,2048]{1,0:T(8,128)(2,1)S(1)}, bf16[704,1536]{1,0:T(8,128)(2,1)S(1)}, f32[4,128]{1,0:T(4,128)S(1)}) custom-call(bf16[72,2048]{1,0:T(8,128)(2,1)S(1)} %get-tuple-element.56.refs_0_, bf16[72,2048]{1,0:T(8,128)(2,1)S(1)} %collective-permute-done.12.refs_1_, ...), custom_call_target="tpu_custom_call", output_to_operand_aliasing={{0}: (6, {}), {1}: (7, {})} | custom-call | flops 1024 | bytes 1024 | tf_op jit(solution)/shard_map/pallas_call | solution.py:312
  88.6 7.8 %collective-permute-done.11.refs_5_ = bf16[4,72,768]{2,1,0:T(8,128)(2,1)S(1)} collective-permute-done((bf16[4,72,768]{2,1,0:T(8,128)(2,1)S(1)}, bf16[4,72,768]{2,1,0:T(8,128)(2,1)S(1)}, u32[]{:S(2)}, u32[]{:S(2)}) %collective-permute-start.11) | collective-permute-done | bytes 442400 | tf_op jit(solution)/shard_map/ppermute | solution.py:255
  96.5 2.1 %shard_map.85 = (bf16[1536,2048]{1,0:T(8,128)(2,1)S(1)}, bf16[704,1536]{1,0:T(8,128)(2,1)S(1)}, f32[4,128]{1,0:T(4,128)S(1)}) custom-call(bf16[72,2048]{1,0:T(8,128)(2,1)S(1)} %get-tuple-element.48.refs_0_, bf16[72,2048]{1,0:T(8,128)(2,1)S(1)} %collective-permute-done.6.refs_1_, ...), custom_call_target="tpu_custom_call", output_to_operand_aliasing={{0}: (6, {}), {1}: (7, {})} | custom-call | flops 1024 | bytes 1024 | tf_op jit(solution)/shard_map/pallas_call | solution.py:312
  98.6 6.5 %shard_map.86 = (bf16[352,2048]{1,0:T(8,128)(2,1)}, f32[352,2048]{1,0:T(8,128)S(1)}, f32[16,128]{1,0:T(8,128)}) custom-call(bf16[1536,2048]{1,0:T(8,128)(2,1)S(1)} %get-tuple-element.70.rows_ref, bf16[704,1536]{1,0:T(8,128)(2,1)S(1)} %get-tuple-element.71.hidw_ref, f32[4,128]{1,0:T(4,128)S(1)} %get-tuple-element.72.refs_0_, ...), custom_call_target="tpu_custom_call" | custom-call | flops 1024 | bytes 1024 | tf_op jit(solution)/shard_map/pallas_call | solution.py:331
  105.1 8.5 %all-to-all-start = ((f32[16,1,128]{2,1,0:T(1,128)}), f32[16,1,128]{2,1,0:T(1,128)S(1)}, u32[]{:S(2)}, u32[]{:S(2)}) async-start(f32[16,1,128]{2,1,0:T(1,128)} %bitcast.6), calls=%async_computation | async-start | bytes 16384 | tf_op jit(solution)/shard_map/all_to_all | solution.py:261
  113.6 4.5 %shard_map.87 = (f32[352,2048]{1,0:T(8,128)}, f32[16,352]{1,0:T(8,128)}) custom-call(f32[352,2048]{1,0:T(8,128)S(1)} %get-tuple-element.76.own_ref, bf16[1,352,2048]{2,1,0:T(8,128)(2,1)} %bitcast.4.others_ref), custom_call_target="tpu_custom_call" | custom-call | flops 1024 | bytes 1024 | tf_op jit(solution)/shard_map/pallas_call | solution.py:356
  118.0 2.8 %all-to-all-done = f32[16,1,128]{2,1,0:T(1,128)S(1)} async-done(((f32[16,1,128]{2,1,0:T(1,128)}), f32[16,1,128]{2,1,0:T(1,128)S(1)}, u32[]{:S(2)}, u32[]{:S(2)}) %all-to-all-start) | async-done | bytes 8224 | tf_op jit(solution)/shard_map/all_to_all | solution.py:261
  (37 shorter events, 8.0 us)
Async XLA Ops:
  0.6 1.0 copy-start.1
  1.7 0.7 copy-start.4
  2.6 1.0 copy-start.2
  3.6 1.2 %copy-start.6 = (bf16[128,6,704]{0,2,1:T(8,128)(2,1)S(1)}, bf16[128,6,704]{0,2,1:T(8,128)(2,1)}, u32[]{:S(2)}) copy-start(bf16[128,6,704]{0,2,1:T(8,128)(2,1)} %param.6) | copy-start | bytes 3244036
  4.9 0.7 copy-start.7
  8.0 21.4 %collective-permute-start.3 = (bf16[72,5120]{1,0:T(8,128)(2,1)S(1)}, bf16[72,5120]{1,0:T(8,128)(2,1)S(1)}, u32[]{:S(2)}, u32[]{:S(2)}) collective-permute-start(bf16[72,5120]{1,0:T(8,128)(2,1)S(1)} %get-tuple-element.45), channel_id=1, source_target_pairs={{0,6},{2,4},{4,2},{6,0},{8,14},{10,12},{12,10},{14,8},{16,22},{18,... | collective-permute-start | bytes 2211848 | tf_op jit(solution)/shard_map/ppermute | solution.py:258
  11.9 17.4 %collective-permute-start = (bf16[128,2176]{1,0:T(8,128)(2,1)S(1)}, bf16[128,2176]{1,0:T(8,128)(2,1)S(1)}, u32[]{:S(2)}, u32[]{:S(2)}) collective-permute-start(bf16[128,2176]{1,0:T(8,128)(2,1)S(1)} %get-tuple-element.42), channel_id=1, source_target_pairs={{0,8},{2,10},{4,12},{6,14},{8,16},{10,18},{12,20},{14,22},{16,24},... | collective-permute-start | bytes 1671176 | tf_op jit(solution)/shard_map/ppermute | solution.py:255
  13.5 26.5 %collective-permute-start.2 = (bf16[128,2176]{1,0:T(8,128)(2,1)S(1)}, bf16[128,2176]{1,0:T(8,128)(2,1)S(1)}, u32[]{:S(2)}, u32[]{:S(2)}) collective-permute-start(bf16[128,2176]{1,0:T(8,128)(2,1)S(1)} %get-tuple-element.42), channel_id=1, source_target_pairs={{0,24},{2,26},{4,28},{6,30},{8,0},{10,2},{12,4},{14,6},{16,8},{18,... | collective-permute-start | bytes 1671176 | tf_op jit(solution)/shard_map/ppermute | solution.py:255
  30.0 11.0 %collective-permute-start.4 = (bf16[72,2048]{1,0:T(8,128)(2,1)S(1)}, bf16[72,2048]{1,0:T(8,128)(2,1)S(1)}, u32[]{:S(2)}, u32[]{:S(2)}) collective-permute-start(bf16[72,2048]{1,0:T(8,128)(2,1)S(1)} %get-tuple-element.46), channel_id=1, source_target_pairs={{0,6},{2,4},{4,2},{6,0},{8,14},{10,12},{12,10},{14,8},{16,22},{18,... | collective-permute-start | bytes 884744 | tf_op jit(solution)/shard_map/ppermute | solution.py:258
  31.8 22.2 %collective-permute-start.10 = (bf16[72,5120]{1,0:T(8,128)(2,1)S(1)}, bf16[72,5120]{1,0:T(8,128)(2,1)S(1)}, u32[]{:S(2)}, u32[]{:S(2)}) collective-permute-start(bf16[72,5120]{1,0:T(8,128)(2,1)S(1)} %get-tuple-element.54), channel_id=1, source_target_pairs={{0,4},{2,6},{4,0},{6,2},{8,12},{10,14},{12,8},{14,10},{16,20},{18,... | collective-permute-start | bytes 2211848 | tf_op jit(solution)/shard_map/ppermute | solution.py:258
  32.3 23.8 %collective-permute-start.9 = (bf16[72,5120]{1,0:T(8,128)(2,1)S(1)}, bf16[72,5120]{1,0:T(8,128)(2,1)S(1)}, u32[]{:S(2)}, u32[]{:S(2)}) collective-permute-start(bf16[72,5120]{1,0:T(8,128)(2,1)S(1)} %get-tuple-element.53), channel_id=1, source_target_pairs={{0,2},{2,0},{4,6},{6,4},{8,10},{10,8},{12,14},{14,12},{16,18},{18,... | collective-permute-start | bytes 2211848 | tf_op jit(solution)/shard_map/ppermute | solution.py:258
  33.5 35.7 %collective-permute-start.1 = (bf16[128,2176]{1,0:T(8,128)(2,1)S(1)}, bf16[128,2176]{1,0:T(8,128)(2,1)S(1)}, u32[]{:S(2)}, u32[]{:S(2)}) collective-permute-start(bf16[128,2176]{1,0:T(8,128)(2,1)S(1)} %collective-permute-done.ext_ref), channel_id=1, source_target_pairs={{0,8},{2,10},{4,12},{6,14},{8,16},{10,18},{12,20},{14,22},{16,24},... | collective-permute-start | bytes 1671176 | tf_op jit(solution)/shard_map/ppermute | solution.py:255
  40.0 22.3 %collective-permute-start.15 = (bf16[72,2048]{1,0:T(8,128)(2,1)S(1)}, bf16[72,2048]{1,0:T(8,128)(2,1)S(1)}, u32[]{:S(2)}, u32[]{:S(2)}) collective-permute-start(bf16[72,2048]{1,0:T(8,128)(2,1)S(1)} %get-tuple-element.61), channel_id=1, source_target_pairs={{0,2},{2,0},{4,6},{6,4},{8,10},{10,8},{12,14},{14,12},{16,18},{18,... | collective-permute-start | bytes 884744 | tf_op jit(solution)/shard_map/ppermute | solution.py:258
  41.6 27.7 %collective-permute-start.5 = (bf16[72,2048]{1,0:T(8,128)(2,1)S(1)}, bf16[72,2048]{1,0:T(8,128)(2,1)S(1)}, u32[]{:S(2)}, u32[]{:S(2)}) collective-permute-start(bf16[72,2048]{1,0:T(8,128)(2,1)S(1)} %get-tuple-element.47), channel_id=1, source_target_pairs={{0,6},{2,4},{4,2},{6,0},{8,14},{10,12},{12,10},{14,8},{16,22},{18,... | collective-permute-start | bytes 884744 | tf_op jit(solution)/shard_map/ppermute | solution.py:258
  56.1 19.1 %collective-permute-start.17 = (bf16[4,72,768]{2,1,0:T(8,128)(2,1)S(1)}, bf16[4,72,768]{2,1,0:T(8,128)(2,1)S(1)}, u32[]{:S(2)}, u32[]{:S(2)}) collective-permute-start(bf16[4,72,768]{2,1,0:T(8,128)(2,1)S(1)} %get-tuple-element.63), channel_id=1, source_target_pairs={{0,8},{2,10},{4,12},{6,14},{8,16},{10,18},{12,20},{14,22},{16,24},... | collective-permute-start | bytes 1327112 | tf_op jit(solution)/shard_map/ppermute | solution.py:255
  57.8 13.7 %collective-permute-start.16 = (bf16[72,2048]{1,0:T(8,128)(2,1)S(1)}, bf16[72,2048]{1,0:T(8,128)(2,1)S(1)}, u32[]{:S(2)}, u32[]{:S(2)}) collective-permute-start(bf16[72,2048]{1,0:T(8,128)(2,1)S(1)} %get-tuple-element.62), channel_id=1, source_target_pairs={{0,4},{2,6},{4,0},{6,2},{8,12},{10,14},{12,8},{14,10},{16,20},{18,... | collective-permute-start | bytes 884744 | tf_op jit(solution)/shard_map/ppermute | solution.py:258
  62.4 17.1 %collective-permute-start.14 = (bf16[4,72,768]{2,1,0:T(8,128)(2,1)S(1)}, bf16[4,72,768]{2,1,0:T(8,128)(2,1)S(1)}, u32[]{:S(2)}, u32[]{:S(2)}) collective-permute-start(bf16[4,72,768]{2,1,0:T(8,128)(2,1)S(1)} %get-tuple-element.59), channel_id=1, source_target_pairs={{0,24},{2,26},{4,28},{6,30},{8,0},{10,2},{12,4},{14,6},{16,8},{18,... | collective-permute-start | bytes 1327112 | tf_op jit(solution)/shard_map/ppermute | solution.py:255
  69.3 27.2 %collective-permute-start.11 = (bf16[4,72,768]{2,1,0:T(8,128)(2,1)S(1)}, bf16[4,72,768]{2,1,0:T(8,128)(2,1)S(1)}, u32[]{:S(2)}, u32[]{:S(2)}) collective-permute-start(bf16[4,72,768]{2,1,0:T(8,128)(2,1)S(1)} %get-tuple-element.55), channel_id=1, source_target_pairs={{0,16},{2,18},{4,20},{6,22},{8,24},{10,26},{12,28},{14,30},{16,0},... | collective-permute-start | bytes 1327112 | tf_op jit(solution)/shard_map/ppermute | solution.py:255
  69.3 13.2 %copy-start = (bf16[1,704,2048]{2,1,0:T(8,128)(2,1)S(1)}, bf16[1,704,2048]{2,1,0:T(8,128)(2,1)}, u32[]{:S(2)}) copy-start(bf16[1,704,2048]{2,1,0:T(8,128)(2,1)} %param.9) | copy-start | bytes 8650756
  69.3 10.6 %collective-permute-start.12 = (bf16[72,2048]{1,0:T(8,128)(2,1)S(1)}, bf16[72,2048]{1,0:T(8,128)(2,1)S(1)}, u32[]{:S(2)}, u32[]{:S(2)}) collective-permute-start(bf16[72,2048]{1,0:T(8,128)(2,1)S(1)} %get-tuple-element.57), channel_id=1, source_target_pairs={{0,2},{2,0},{4,6},{6,4},{8,10},{10,8},{12,14},{14,12},{16,18},{18,... | collective-permute-start | bytes 884744 | tf_op jit(solution)/shard_map/ppermute | solution.py:258
  71.5 15.1 %collective-permute-start.13 = (bf16[72,2048]{1,0:T(8,128)(2,1)S(1)}, bf16[72,2048]{1,0:T(8,128)(2,1)S(1)}, u32[]{:S(2)}, u32[]{:S(2)}) collective-permute-start(bf16[72,2048]{1,0:T(8,128)(2,1)S(1)} %get-tuple-element.58), channel_id=1, source_target_pairs={{0,4},{2,6},{4,0},{6,2},{8,12},{10,14},{12,8},{14,10},{16,20},{18,... | collective-permute-start | bytes 884744 | tf_op jit(solution)/shard_map/ppermute | solution.py:258
  75.2 21.3 %collective-permute-start.6 = (bf16[72,2048]{1,0:T(8,128)(2,1)S(1)}, bf16[72,2048]{1,0:T(8,128)(2,1)S(1)}, u32[]{:S(2)}, u32[]{:S(2)}) collective-permute-start(bf16[72,2048]{1,0:T(8,128)(2,1)S(1)} %get-tuple-element.49), channel_id=1, source_target_pairs={{0,2},{2,0},{4,6},{6,4},{8,10},{10,8},{12,14},{14,12},{16,18},{18,... | collective-permute-start | bytes 884744 | tf_op jit(solution)/shard_map/ppermute | solution.py:258
  79.5 17.0 %collective-permute-start.7 = (bf16[72,2048]{1,0:T(8,128)(2,1)S(1)}, bf16[72,2048]{1,0:T(8,128)(2,1)S(1)}, u32[]{:S(2)}, u32[]{:S(2)}) collective-permute-start(bf16[72,2048]{1,0:T(8,128)(2,1)S(1)} %get-tuple-element.50), channel_id=1, source_target_pairs={{0,4},{2,6},{4,0},{6,2},{8,12},{10,14},{12,8},{14,10},{16,20},{18,... | collective-permute-start | bytes 884744 | tf_op jit(solution)/shard_map/ppermute | solution.py:258
  79.9 16.6 %collective-permute-start.8 = (bf16[72,2048]{1,0:T(8,128)(2,1)S(1)}, bf16[72,2048]{1,0:T(8,128)(2,1)S(1)}, u32[]{:S(2)}, u32[]{:S(2)}) collective-permute-start(bf16[72,2048]{1,0:T(8,128)(2,1)S(1)} %get-tuple-element.51), channel_id=1, source_target_pairs={{0,6},{2,4},{4,2},{6,0},{8,14},{10,12},{12,10},{14,8},{16,22},{18,... | collective-permute-start | bytes 884744 | tf_op jit(solution)/shard_map/ppermute | solution.py:258
  105.1 15.7 %copy-start.5 = (s32[128,6]{0,1:T(8,128)S(1)}, s32[128,6]{0,1:T(8,128)}, u32[]{:S(2)}) copy-start(s32[128,6]{0,1:T(8,128)} %param.7) | copy-start | bytes 9220
  105.1 8.5 %collective-permute-start.18 = (bf16[352,2048]{1,0:T(8,128)(2,1)}, bf16[352,2048]{1,0:T(8,128)(2,1)}, u32[]{:S(2)}, u32[]{:S(2)}) collective-permute-start(bf16[352,2048]{1,0:T(8,128)(2,1)} %get-tuple-element.77), channel_id=1, source_target_pairs={{0,1},{1,0},{2,3},{3,2},{4,5},{5,4},{6,7},{7,6},{8,9},{9,8},{10,11... | collective-permute-start | bytes 4325384 | tf_op jit(solution)/shard_map/ppermute | solution.py:349
  105.1 15.7 %all-to-all-start = ((f32[16,1,128]{2,1,0:T(1,128)}), f32[16,1,128]{2,1,0:T(1,128)S(1)}, u32[]{:S(2)}, u32[]{:S(2)}) async-start(f32[16,1,128]{2,1,0:T(1,128)} %bitcast.6), calls=%async_computation | async-start | bytes 16384 | tf_op jit(solution)/shard_map/all_to_all | solution.py:261
  120.8 0.7 copy-start.3

commit v4 on v3

--- a/solution.py
+++ b/solution.py
@@ -13,28 +13,34 @@
 F32 = jnp.float32
 NT = (((1,), (1,)), ((), ()))
 VMEM_BYTES = 24 * 1024 * 1024
+ALL_VMEM = 56 * 1024 * 1024
 
 
 def up(value, unit):
     return -(-value // unit) * unit
 
 
-def call(kernel, out_shape, pace=0, **kw):
+def call(kernel, out_shape, room=VMEM_BYTES, **kw):
     return pl.pallas_call(
         kernel,
         out_shape=out_shape,
         cost_estimate=pl.CostEstimate(
-            flops=1024 + pace * 1_000_000_000, bytes_accessed=1024, transcendentals=0
+            flops=1024, bytes_accessed=1024, transcendentals=0
         ),
-        compiler_params=pltpu.CompilerParams(vmem_limit_bytes=VMEM_BYTES),
+        compiler_params=pltpu.CompilerParams(vmem_limit_bytes=room),
         **kw,
     )
 
 
-def table_kernel(stride, routes_ref, cot_ref, ext_ref, slot_ref, code_ref):
+def table_kernel(stride, routes_hbm, cot_hbm, ext_ref, slot_ref, code_ref, routes_ref, done):
     experts, tokens = slot_ref.shape
     top_k = routes_ref.shape[0]
-    model = cot_ref.shape[1]
+    model = cot_hbm.shape[1]
+    cot_copy = pltpu.make_async_copy(cot_hbm, ext_ref.at[:, pl.ds(0, model)], done.at[0])
+    routes_copy = pltpu.make_async_copy(routes_hbm, routes_ref, done.at[1])
+    cot_copy.start()
+    routes_copy.start()
+    routes_copy.wait()
     routes = routes_ref[...]
     ids = lax.broadcasted_iota(jnp.int32, (experts, tokens), 0)
     mask = jnp.zeros((experts, tokens), F32)
@@ -58,8 +64,8 @@
         ).astype(jnp.int32)
         code_ref[k : k + 1, :] = rel[k : k + 1, :] * stride + own
     wide = jnp.concatenate([slot, jnp.zeros((BLOCK - experts, tokens), F32)], axis=0)
-    ext_ref[:, 0:model] = cot_ref[...]
     ext_ref[:, model : model + BLOCK] = wide.T.astype(BF)
+    cot_copy.wait()
 
 
 def halves(flip):
@@ -67,7 +73,7 @@
     return 1 - mine, mine
 
 
-def select(slots, stride, table, cot_ref, outs):
+def select(slots, stride, table, cot_ref, outs, at=0):
     me = lax.axis_index("expert")
     tokens = cot_ref.shape[0]
     rows = lax.broadcasted_iota(jnp.int32, (stride, tokens), 0).astype(F32)
@@ -79,13 +85,17 @@
     for c in range(0, model, step):
         got = jnp.dot(pick, cot_ref[:, c : c + step], preferred_element_type=F32)
         for k in range(PLANE):
-            outs[k][:, c : c + step] = got[k * stride : k * stride + slots, :].astype(BF)
-
-
-def first_kernel(slots, stride, flip, slot_ref, cot_ref, code_ref, num_ref, hid_ref, *refs):
-    outs, table = refs[:PLANE], refs[PLANE]
-    select(slots, stride, slot_ref, cot_ref, outs)
-    model = cot_ref.shape[1]
+            outs[k][:, at + c : at + c + step] = got[k * stride : k * stride + slots, :].astype(BF)
+
+
+def pack_kernel(slots, stride, flip, code_ref, num_hbm, hid_hbm, *refs):
+    outs, (table, num_ref, hid_ref, done) = refs[:PLANE], refs[PLANE:]
+    num_copy = pltpu.make_async_copy(num_hbm, num_ref, done.at[0])
+    hid_copy = pltpu.make_async_copy(hid_hbm, hid_ref, done.at[1])
+    num_copy.start()
+    hid_copy.start()
+    num_copy.wait()
+    hid_copy.wait()
     top_k, width, tokens = hid_ref.shape
     half = width // 2
     padded = table.shape[0] // 2
@@ -101,27 +111,28 @@
             rows = lax.broadcasted_iota(jnp.int32, (padded - half, tokens), 0)
             tail = jnp.where(rows == 0, high, jnp.where(rows == 1, weight - high, 0.0))
             table[n * padded + half : (n + 1) * padded, lanes] = tail.astype(BF)
-    for s in range((outs[0].shape[1] - model) // (2 * padded)):
+    for s in range(outs[0].shape[1] // (2 * padded)):
         rows = lax.broadcasted_iota(jnp.int32, (group, top_k * tokens), 0) + s * group
         pick = jnp.where(rows == code, 1.0, 0.0).astype(BF)
         got = lax.dot_general(pick, table[...], NT, preferred_element_type=F32)
-        at = model + s * 2 * padded
+        at = s * 2 * padded
         for k in range(PLANE):
             outs[k][:, at : at + 2 * padded] = got[k * stride : k * stride + slots, :].astype(BF)
 
 
-def relay_kernel(slots, stride, ext_ref, *refs):
-    outs, table = refs[-1 - PLANE : -1], refs[-1]
-    model = outs[0].shape[1]
-    table[...] = ext_ref[:, model : model + BLOCK].astype(F32).T
-    select(slots, stride, table, ext_ref.at[:, pl.ds(0, model)], outs)
-
-
-def regroup_kernel(model, *refs):
+def relay_kernel(slots, stride, count, *refs):
+    blocks, outs, table = refs[:count], refs[-1 - PLANE : -1], refs[-1]
+    model = outs[0].shape[1] // count
+    for n, ext_ref in enumerate(blocks):
+        table[...] = ext_ref[:, model : model + BLOCK].astype(F32).T
+        select(slots, stride, table, ext_ref.at[:, pl.ds(0, model)], outs, n * model)
+
+
+def regroup_kernel(*refs):
     outs = refs[PLANE:]
     padded = outs[0].shape[2]
     for s, out_ref in enumerate(outs):
-        at = model + (s + 1) * padded
+        at = s * padded
         for k in range(PLANE):
             out_ref[k] = refs[k][:, at : at + padded]
 
@@ -139,20 +150,20 @@
     return 1 - mine, mine
 
 
-def stage_kernel(stage, stride, flip, split, *refs):
+def stage_kernel(place, at, stride, flip, *refs):
     pieces, w_ref, refs = refs[:PLANE], refs[PLANE], refs[PLANE + 1 :]
+    hid_ref = refs[0]
     all_rows, all_hidw, gate_ref, rows, hids, hidw, done = refs[-7:]
     group = PLANE * stride
     width, model = w_ref.shape
     half = width // 2
     padded = hids.shape[1] // 2
     for k, piece in enumerate(pieces):
-        fill(rows, k * stride, piece[:, 0:model], stride)
-    copy = pltpu.make_async_copy(rows, all_rows.at[pl.ds(stage * group, group)], done.at[0])
+        fill(rows, k * stride, piece[:, at : at + model], stride)
+    copy = pltpu.make_async_copy(rows, all_rows.at[pl.ds(place * group, group)], done.at[0])
     copy.start()
     for k in range(PLANE):
-        hid = refs[0][k] if split else pieces[k][:, model : model + 2 * padded]
-        fill(hids, k * stride, hid, stride)
+        fill(hids, k * stride, hid_ref[k], stride)
     gate = 0.0
     for n, part in enumerate(halves(flip)):
         at = pl.multiple_of(part * half, 16) if flip else part * half
@@ -165,7 +176,7 @@
         )
         gate += jnp.sum(back * hid, axis=0, keepdims=True)
     second = pltpu.make_async_copy(
-        hidw, all_hidw.at[:, pl.ds(stage * group, group)], done.at[1]
+        hidw, all_hidw.at[:, pl.ds(place * group, group)], done.at[1]
     )
     second.start()
     gate_ref[...] = jnp.zeros_like(gate_ref)
@@ -182,17 +193,23 @@
     return ring * PLANE + ((me & 3) ^ k)
 
 
-def partial_kernel(outer, rows_ref, hidw_ref, *refs):
+def early_kernel(rows_ref, hidw_ref, out_ref, mark_ref):
+    mark_ref[...] = jnp.zeros_like(mark_ref)
+    out_ref[...] = jnp.dot(hidw_ref[...], rows_ref[...], preferred_element_type=F32)
+
+
+def partial_kernel(order, rows_ref, hidw_ref, early_ref, *refs):
+    outer = len(order)
     gates, (send_ref, mine_ref, gate_ref) = refs[:outer], refs[outer:]
 
     @pl.when(pl.program_id(0) == 0)
     def _():
-        for s in range(outer):
+        for n, s in enumerate(order):
             for k in range(PLANE):
-                gate_ref[pl.ds(source(outer, s, k), 1), :] = gates[s][k : k + 1, :]
+                gate_ref[pl.ds(source(outer, s, k), 1), :] = gates[n][k : k + 1, :]
 
     half = mine_ref.shape[0]
-    got = jnp.dot(hidw_ref[...], rows_ref[...], preferred_element_type=F32)
+    got = early_ref[...] + jnp.dot(hidw_ref[...], rows_ref[...], preferred_element_type=F32)
     send_ref[...] = got[0:half].astype(BF)
     mine_ref[...] = got[half:].astype(mine_ref.dtype)
 
@@ -270,17 +287,24 @@
             sds((experts, tokens), F32),
             sds((top_k, tokens), jnp.int32),
         ),
+        ALL_VMEM,
+        in_specs=[anywhere] * 2,
+        scratch_shapes=[pltpu.VMEM((top_k, tokens), jnp.int32), pltpu.SemaphoreType.DMA((2,))],
     )(routes.T, cotangent)
 
-    wide = model + outer * 2 * padded
-    sent = call(
-        functools.partial(first_kernel, slots, stride, flip),
-        [sds((slots, wide), BF)] * PLANE,
-        15,
-        scratch_shapes=[pltpu.VMEM((2 * padded, top_k * tokens), BF)],
-    )(slot, cotangent, code, numerators.T, jnp.transpose(hidden, (1, 2, 0)))
-    swapped = {k: swap(sent[k], k) for k in (3, 1, 2)}
-    stages = {0: [sent[0]] + [swapped[k] for k in range(1, PLANE)]}
+    packed = call(
+        functools.partial(pack_kernel, slots, stride, flip),
+        [sds((slots, outer * 2 * padded), BF)] * PLANE,
+        ALL_VMEM,
+        in_specs=[inside] + [anywhere] * 2,
+        scratch_shapes=[
+            pltpu.VMEM((2 * padded, top_k * tokens), BF),
+            pltpu.VMEM((top_k, tokens), jnp.int32),
+            pltpu.VMEM((top_k, width, tokens), BF),
+            pltpu.SemaphoreType.DMA((2,)),
+        ],
+    )(code, numerators.T, jnp.transpose(hidden, (1, 2, 0)))
+    opening = [packed[0]] + [swap(packed[k], k) for k in range(1, PLANE)]
 
     blocks = {0: ext}
     order = [0]
@@ -291,58 +315,74 @@
             blocks[outer - s] = ring(blocks[(outer - s + 1) % outer], -1)
             order.append(outer - s)
     hids = call(
-        functools.partial(regroup_kernel, model),
-        [sds((PLANE, slots, 2 * padded), BF)] * (outer - 1),
-    )(*stages[0])
-    hids = {s: ring(hids[s - 1], s) for s in order[1:]}
-    for s in order[1:]:
+        regroup_kernel,
+        [sds((PLANE, slots, 2 * padded), BF)] * outer,
+    )(*opening)
+    hids = {s: ring(hids[s], s) if s else hids[s] for s in order}
+
+    def relay(batch):
         sent = call(
-            functools.partial(relay_kernel, slots, stride),
-            [sds((slots, model), BF)] * PLANE,
-            15,
-            in_specs=[inside, anywhere],
+            functools.partial(relay_kernel, slots, stride, len(batch)),
+            [sds((slots, len(batch) * model), BF)] * PLANE,
             scratch_shapes=[pltpu.VMEM((BLOCK, tokens), F32)],
-        )(blocks[s], swapped[3])
-        swapped = {k: swap(sent[k], k) for k in (3, 1, 2)}
-        stages[s] = [sent[0]] + [swapped[k] for k in range(1, PLANE)]
-
-    rows, gates = [], {}
-    for s in order:
-        hid = [hids[s]] if s else []
-        *rows, gates[s] = call(
-            functools.partial(stage_kernel, s, stride, flip, bool(s)),
+        )(*[blocks[s] for s in batch])
+        return [sent[0]] + [swap(sent[k], k) for k in range(1, PLANE)]
+
+    middle, final = relay(order[:-1]), relay(order[-1:])
+
+    def stage(got, n, count, after, rows):
+        hid = hids[order[n] if count > 1 else order[-1]]
+        return call(
+            functools.partial(stage_kernel, n, n * model, stride, flip),
             [
-                sds((outer * group, model), BF),
-                sds((width, outer * group), BF),
+                sds((count * group, model), BF),
+                sds((width, count * group), BF),
                 sds((PLANE, BLOCK), F32),
             ],
-            in_specs=[inside] * (PLANE + 1 + len(hid)) + [anywhere] * len(rows),
+            in_specs=[inside] * (PLANE + 2) + [anywhere] * len(rows) + [inside] * len(after),
             out_specs=[anywhere, anywhere, inside],
-            input_output_aliases={PLANE + 1 + len(hid) + n: n for n in range(len(rows))},
+            input_output_aliases={PLANE + 2 + i: i for i in range(len(rows))},
             scratch_shapes=[
                 pltpu.VMEM((group, model), BF),
                 pltpu.VMEM((group, 2 * padded), F32),
                 pltpu.VMEM((width, group), BF),
                 pltpu.SemaphoreType.DMA((2,)),
             ],
-        )(*stages[s], w_down[0], *hid, *rows)
+        )(*got, w_down[0], hid, *rows, *after)
+
+    def products(count):
+        return [
+            pl.BlockSpec((count * group, step), lambda j: (0, j)),
+            pl.BlockSpec((width, count * group), lambda j: (0, 0)),
+        ]
+
+    rows, gates = [], []
+    for n in range(outer - 1):
+        *rows, gate = stage(middle, n, outer - 1, [], rows)
+        gates.append(gate)
+    full = pl.BlockSpec((width, step), lambda j: (0, j))
+    early, mark = call(
+        early_kernel,
+        [sds((width, model), F32), sds((8, BLOCK), F32)],
+        grid=(steps,),
+        in_specs=products(outer - 1),
+        out_specs=[full, pl.BlockSpec((8, BLOCK), lambda j: (0, 0))],
+    )(*rows)
+    *rows, gate = stage(final, 0, 1, [mark], [])
+    gates.append(gate)
 
     flat = pl.BlockSpec((half, step), lambda j: (0, j))
     send, mine, gates = call(
-        functools.partial(partial_kernel, outer),
+        functools.partial(partial_kernel, order),
         [
             sds((half, model), BF),
             sds((half, model), F32 if flip else BF),
             sds((experts, BLOCK), F32),
         ],
         grid=(steps,),
-        in_specs=[
-            pl.BlockSpec((outer * group, step), lambda j: (0, j)),
-            pl.BlockSpec((width, outer * group), lambda j: (0, 0)),
-        ]
-        + [pl.BlockSpec((PLANE, BLOCK), lambda j: (0, 0))] * outer,
+        in_specs=products(1) + [full] + [pl.BlockSpec((PLANE, BLOCK), lambda j: (0, 0))] * outer,
         out_specs=[flat, flat, pl.BlockSpec((experts, BLOCK), lambda j: (0, 0))],
-    )(*rows, *[gates[s] for s in range(outer)])
+    )(*rows, early, *gates)
     returned = exchange(gates)
     if flip:
         kernel = finish_kernel

time: 123 us -> 111 us (0.902)
  starting transfers between devices: 38.7 us -> 25 us
  Pallas kernels: 24.5 us -> 31.6 us
  local copies, waits for them, and re-layouts: 5.43 us -> 2.82 us
  waiting for transfers between devices: 52.8 us -> 50.9 us
    ppermute x12 -> x9, waiting for transfers between devices: 17.1 us -> 9.65 us  [swap(): return lax.ppermute(array, 'expert', [(e, e ^ k) for e in range(experts)])]
    ppermute x6, waiting for transfers between devices: 32.9 us -> 38.5 us  [ring(): return lax.ppermute(array, 'expert', pairs)]
    ppermute x12 -> x9, starting transfers between devices: 17 us -> 11.5 us  [swap(): return lax.ppermute(array, 'expert', [(e, e ^ k) for e in range(experts)])]
    pallas_call x10, Pallas kernels: 19.1 us -> 24.3 us  [the longest x4 8.2 us: stage(): call(functools.partial(stage_kernel, n, n * model, stride, flip), [sds((c...]
    ppermute x6, starting transfers between devices: 13.2 us -> 8.06 us  [ring(): return lax.ppermute(array, 'expert', pairs)]
    all_to_all x1, starting transfers between devices: 8.45 us -> 5.41 us  [exchange(): lax.all_to_all(array, 'expert', split_axis=0, concat_axis=0, tiled=True)]
    unnamed x16 -> x12, local copies, waits for them, and re-layouts: 5.43 us -> 2.82 us
    pallas_call x1, Pallas kernels: 0.23 us -> 2.06 us  [per_device(): call(functools.partial(table_kernel, stride), (sds((tokens, model + BLOCK...]
  transfers between devices with their start and end apart: 20 -> 17, of which waited for: 10 -> 6; matrix products, arithmetic and copies ran while one was open for 0% -> 0% of each run, Pallas kernels for 10% -> 21%
where the time goes in v4:
time: 111 us
  waiting for transfers between devices  50.9 us (46%)
  Pallas kernels  31.6 us (28%)
  starting transfers between devices  25 us (23%)
  local copies, waits for them, and re-layouts  2.82 us (3%)
    ppermute x6, waiting for transfers between devices, ring(): return lax.ppermute(array, 'expert', pairs)  38.5 us
    ppermute x9, starting transfers between devices, swap(): return lax.ppermute(array, 'expert', [(e, e ^ k) for e in range(experts)])  11.5 us
    ppermute x9, waiting for transfers between devices, swap(): return lax.ppermute(array, 'expert', [(e, e ^ k) for e in range(experts)])  9.65 us
    pallas_call x4, Pallas kernels, stage(): call(functools.partial(stage_kernel, n, n * model, stride, flip), [sds((c...  8.2 us
    ppermute x6, starting transfers between devices, ring(): return lax.ppermute(array, 'expert', pairs)  8.06 us
    all_to_all x1, starting transfers between devices, exchange(): lax.all_to_all(array, 'expert', split_axis=0, concat_axis=0, tiled=True)  5.41 us
    pallas_call x1, Pallas kernels, per_device(): call(functools.partial(pack_kernel, slots, stride, flip), [sds((slots, ou...  5.2 us
    pallas_call x1, Pallas kernels, per_device(): call(early_kernel, [sds((width, model), F32), sds((8, BLOCK), F32)], grid...  5.13 us
  transfers between devices with their start and end apart: 17, of which 6 were waited for; matrix products, arithmetic and copies ran while one was open for 0% of the time, Pallas kernels for 21%

profile of v4, /device:TPU:0, one launch (start us, length us, event | category | flops | bytes accessed | tf_op | source)
XLA Modules:
  0.0 111.0 jit_solution(8169694197984900763)
XLA Ops:
  0.6 2.1 %shard_map.76 = (bf16[128,2176]{1,0:T(8,128)(2,1)}, f32[16,128]{1,0:T(8,128)}, s32[6,128]{1,0:T(8,128)}) custom-call(s32[6,128]{1,0:T(8,128)} %bitcast.20, bf16[128,2048]{1,0:T(8,128)(2,1)} %cot_hbm.1), custom_call_target="tpu_custom_call" | custom-call | flops 1024 | bytes 1024 | tf_op jit(solution)/shard_map/pallas_call | solution.py:283
  2.7 3.1 %collective-permute-start = (bf16[128,2176]{1,0:T(8,128)(2,1)}, bf16[128,2176]{1,0:T(8,128)(2,1)S(1)}, u32[]{:S(2)}, u32[]{:S(2)}) collective-permute-start(bf16[128,2176]{1,0:T(8,128)(2,1)} %get-tuple-element.41.refs_0_), channel_id=1, source_target_pairs={{0,8},{2,10},{4,12},{6,14},{8,16},{10,18},{12,20},{14,22},{16,24},... | collective-permute-start | bytes 1671176 | tf_op jit(solution)/shard_map/ppermute | solution.py:272
  5.8 2.1 %collective-permute-start.9 = (bf16[128,2176]{1,0:T(8,128)(2,1)}, bf16[128,2176]{1,0:T(8,128)(2,1)S(1)}, u32[]{:S(2)}, u32[]{:S(2)}) collective-permute-start(bf16[128,2176]{1,0:T(8,128)(2,1)} %get-tuple-element.41.refs_0_), channel_id=1, source_target_pairs={{0,24},{2,26},{4,28},{6,30},{8,0},{10,2},{12,4},{14,6},{16,8},{18,... | collective-permute-start | bytes 1671176 | tf_op jit(solution)/shard_map/ppermute | solution.py:272
  7.9 5.2 %shard_map.78 = (bf16[72,3072]{1,0:T(8,128)(2,1)}, bf16[72,3072]{1,0:T(8,128)(2,1)}, bf16[72,3072]{1,0:T(8,128)(2,1)}, bf16[72,3072]{1,0:T(8,128)(2,1)}) custom-call(s32[6,128]{1,0:T(8,128)} %get-tuple-element.46.code_ref, s32[6,128]{1,0:T(8,128)} %bitcast.23, bf16[6,704,128]{2,1,0:T(8,128)(2,1)} %bitcast.22), custom_call_target="tpu_custom_call" | custom-call | flops 1024 | bytes 1024 | tf_op jit(solution)/shard_map/pallas_call | solution.py:295
  13.1 1.7 %collective-permute-start.5 = (bf16[72,3072]{1,0:T(8,128)(2,1)}, bf16[72,3072]{1,0:T(8,128)(2,1)S(1)}, u32[]{:S(2)}, u32[]{:S(2)}) collective-permute-start(bf16[72,3072]{1,0:T(8,128)(2,1)} %get-tuple-element.48), channel_id=1, source_target_pairs={{0,2},{2,0},{4,6},{6,4},{8,10},{10,8},{12,14},{14,12},{16,18},{18,... | collective-permute-start | bytes 1327112 | tf_op jit(solution)/shard_map/ppermute | solution.py:275
  14.8 1.5 %collective-permute-start.6 = (bf16[72,3072]{1,0:T(8,128)(2,1)}, bf16[72,3072]{1,0:T(8,128)(2,1)S(1)}, u32[]{:S(2)}, u32[]{:S(2)}) collective-permute-start(bf16[72,3072]{1,0:T(8,128)(2,1)} %get-tuple-element.49), channel_id=1, source_target_pairs={{0,4},{2,6},{4,0},{6,2},{8,12},{10,14},{12,8},{14,10},{16,20},{18,... | collective-permute-start | bytes 1327112 | tf_op jit(solution)/shard_map/ppermute | solution.py:275
  16.6 4.9 %collective-permute-done.refs_1_ = bf16[128,2176]{1,0:T(8,128)(2,1)S(1)} collective-permute-done((bf16[128,2176]{1,0:T(8,128)(2,1)}, bf16[128,2176]{1,0:T(8,128)(2,1)S(1)}, u32[]{:S(2)}, u32[]{:S(2)}) %collective-permute-start) | collective-permute-done | bytes 557088 | tf_op jit(solution)/shard_map/ppermute | solution.py:272
  21.5 10.5 %collective-permute-done.9.refs_2_ = bf16[128,2176]{1,0:T(8,128)(2,1)S(1)} collective-permute-done((bf16[128,2176]{1,0:T(8,128)(2,1)}, bf16[128,2176]{1,0:T(8,128)(2,1)S(1)}, u32[]{:S(2)}, u32[]{:S(2)}) %collective-permute-start.9) | collective-permute-done | bytes 557088 | tf_op jit(solution)/shard_map/ppermute | solution.py:272
  32.0 1.1 copy-done.1
  33.1 1.4 %shard_map.80 = (bf16[72,6144]{1,0:T(8,128)(2,1)S(1)}, bf16[72,6144]{1,0:T(8,128)(2,1)S(1)}, bf16[72,6144]{1,0:T(8,128)(2,1)S(1)}, bf16[72,6144]{1,0:T(8,128)(2,1)S(1)}) custom-call(bf16[128,2176]{1,0:T(8,128)(2,1)S(1)} %copy-done.1, bf16[128,2176]{1,0:T(8,128)(2,1)S(1)} %collective-permute-done.refs_1_, bf16[128,2176]{1,0:T(8,128)(2,1)S(1)} %collective-permute-done.9.refs_2_), custom_call_target="tpu_custom_call" | custom-call | flops 1024 | bytes 1024 | tf_op jit(solution)/shard_map/pallas_call | solution.py:324
  34.5 1.6 %collective-permute-start.10 = (bf16[72,6144]{1,0:T(8,128)(2,1)S(1)}, bf16[72,6144]{1,0:T(8,128)(2,1)S(1)}, u32[]{:S(2)}, u32[]{:S(2)}) collective-permute-start(bf16[72,6144]{1,0:T(8,128)(2,1)S(1)} %get-tuple-element.53), channel_id=1, source_target_pairs={{0,2},{2,0},{4,6},{6,4},{8,10},{10,8},{12,14},{14,12},{16,18},{18,... | collective-permute-start | bytes 2654216 | tf_op jit(solution)/shard_map/ppermute | solution.py:275
  36.1 1.5 %collective-permute-start.11 = (bf16[72,6144]{1,0:T(8,128)(2,1)S(1)}, bf16[72,6144]{1,0:T(8,128)(2,1)S(1)}, u32[]{:S(2)}, u32[]{:S(2)}) collective-permute-start(bf16[72,6144]{1,0:T(8,128)(2,1)S(1)} %get-tuple-element.54), channel_id=1, source_target_pairs={{0,4},{2,6},{4,0},{6,2},{8,12},{10,14},{12,8},{14,10},{16,20},{18,... | collective-permute-start | bytes 2654216 | tf_op jit(solution)/shard_map/ppermute | solution.py:275
  38.1 1.1 %collective-permute-start.1 = (bf16[128,2176]{1,0:T(8,128)(2,1)S(1)}, bf16[128,2176]{1,0:T(8,128)(2,1)S(1)}, u32[]{:S(2)}, u32[]{:S(2)}) collective-permute-start(bf16[128,2176]{1,0:T(8,128)(2,1)S(1)} %collective-permute-done.refs_1_), channel_id=1, source_target_pairs={{0,8},{2,10},{4,12},{6,14},{8,16},{10,18},{12,20},{14,22},{16,24},... | collective-permute-start | bytes 1671176 | tf_op jit(solution)/shard_map/ppermute | solution.py:272
  39.2 1.0 copy-done.2
  40.4 0.8 collective-permute-start.14
  41.1 21.8 %collective-permute-done.14.refs_5_ = bf16[4,72,768]{2,1,0:T(8,128)(2,1)S(1)} collective-permute-done((bf16[4,72,768]{2,1,0:T(8,128)(2,1)S(1)}, bf16[4,72,768]{2,1,0:T(8,128)(2,1)S(1)}, u32[]{:S(2)}, u32[]{:S(2)}) %collective-permute-start.14) | collective-permute-done | bytes 442400 | tf_op jit(solution)/shard_map/ppermute | solution.py:272
  62.9 1.0 collective-permute-start.8
  64.5 1.6 %collective-permute-start.2 = (bf16[72,2048]{1,0:T(8,128)(2,1)S(1)}, bf16[72,2048]{1,0:T(8,128)(2,1)S(1)}, u32[]{:S(2)}, u32[]{:S(2)}) collective-permute-start(bf16[72,2048]{1,0:T(8,128)(2,1)S(1)} %get-tuple-element.43), channel_id=1, source_target_pairs={{0,2},{2,0},{4,6},{6,4},{8,10},{10,8},{12,14},{14,12},{16,18},{18,... | collective-permute-start | bytes 884744 | tf_op jit(solution)/shard_map/ppermute | solution.py:275
  66.1 9.6 %collective-permute-done.11.refs_2_ = bf16[72,6144]{1,0:T(8,128)(2,1)S(1)} collective-permute-done((bf16[72,6144]{1,0:T(8,128)(2,1)S(1)}, bf16[72,6144]{1,0:T(8,128)(2,1)S(1)}, u32[]{:S(2)}, u32[]{:S(2)}) %collective-permute-start.11) | collective-permute-done | bytes 884768 | tf_op jit(solution)/shard_map/ppermute | solution.py:275
  75.7 2.6 %collective-permute-start.3 = (bf16[72,2048]{1,0:T(8,128)(2,1)S(1)}, bf16[72,2048]{1,0:T(8,128)(2,1)S(1)}, u32[]{:S(2)}, u32[]{:S(2)}) collective-permute-start(bf16[72,2048]{1,0:T(8,128)(2,1)S(1)} %get-tuple-element.44), channel_id=1, source_target_pairs={{0,4},{2,6},{4,0},{6,2},{8,12},{10,14},{12,8},{14,10},{16,20},{18,... | collective-permute-start | bytes 884744 | tf_op jit(solution)/shard_map/ppermute | solution.py:275
  78.6 2.0 %shard_map.81 = (bf16[1152,2048]{1,0:T(8,128)(2,1)S(1)}, bf16[704,1152]{1,0:T(8,128)(2,1)S(1)}, f32[4,128]{1,0:T(4,128)S(1)}) custom-call(bf16[72,6144]{1,0:T(8,128)(2,1)S(1)} %get-tuple-element.52.refs_0_, bf16[72,6144]{1,0:T(8,128)(2,1)S(1)} %collective-permute-done.10.refs_1_, bf16[72,6144]{1,0:T(8,128)(2,1)S(1)} %collective-permute-done.11.refs_2_, ...), custom_call_target="tpu_custom_call" | custom-call | flops 1024 | bytes 1024 | tf_op jit(solution)/shard_map/pallas_call | solution.py:335
  80.6 2.0 %shard_map.82 = (bf16[1152,2048]{1,0:T(8,128)(2,1)S(1)}, bf16[704,1152]{1,0:T(8,128)(2,1)S(1)}, f32[4,128]{1,0:T(4,128)S(1)}) custom-call(bf16[72,6144]{1,0:T(8,128)(2,1)S(1)} %get-tuple-element.52.refs_0_, bf16[72,6144]{1,0:T(8,128)(2,1)S(1)} %collective-permute-done.10.refs_1_, ...), custom_call_target="tpu_custom_call", output_to_operand_aliasing={{0}: (6, {}), {1}: (7, {})} | custom-call | flops 1024 | bytes 1024 | tf_op jit(solution)/shard_map/pallas_call | solution.py:335
  82.7 2.1 %shard_map.83 = (bf16[1152,2048]{1,0:T(8,128)(2,1)S(1)}, bf16[704,1152]{1,0:T(8,128)(2,1)S(1)}, f32[4,128]{1,0:T(4,128)S(1)}) custom-call(bf16[72,6144]{1,0:T(8,128)(2,1)S(1)} %get-tuple-element.52.refs_0_, bf16[72,6144]{1,0:T(8,128)(2,1)S(1)} %collective-permute-done.10.refs_1_, ...), custom_call_target="tpu_custom_call", output_to_operand_aliasing={{0}: (6, {}), {1}: (7, {})} | custom-call | flops 1024 | bytes 1024 | tf_op jit(solution)/shard_map/pallas_call | solution.py:335
  84.7 5.1 %shard_map.84 = (f32[704,2048]{1,0:T(8,128)S(1)}, f32[8,128]{1,0:T(8,128)S(1)}) custom-call(bf16[1152,2048]{1,0:T(8,128)(2,1)S(1)} %get-tuple-element.63.rows_ref, bf16[704,1152]{1,0:T(8,128)(2,1)S(1)} %get-tuple-element.64.hidw_ref), custom_call_target="tpu_custom_call" | custom-call | flops 1024 | bytes 1024 | tf_op jit(solution)/shard_map/pallas_call | solution.py:364
  89.9 1.3 %collective-permute-done.8.refs_5_ = bf16[4,72,768]{2,1,0:T(8,128)(2,1)S(1)} collective-permute-done((bf16[4,72,768]{2,1,0:T(8,128)(2,1)S(1)}, bf16[4,72,768]{2,1,0:T(8,128)(2,1)S(1)}, u32[]{:S(2)}, u32[]{:S(2)}) %collective-permute-start.8) | collective-permute-done | bytes 442400 | tf_op jit(solution)/shard_map/ppermute | solution.py:272
  91.2 2.1 %shard_map.85 = (bf16[384,2048]{1,0:T(8,128)(2,1)S(1)}, bf16[704,384]{1,0:T(8,128)(2,1)S(1)}, f32[4,128]{1,0:T(4,128)S(1)}) custom-call(bf16[72,2048]{1,0:T(8,128)(2,1)S(1)} %get-tuple-element.42.refs_0_, bf16[72,2048]{1,0:T(8,128)(2,1)S(1)} %collective-permute-done.2.refs_1_, bf16[72,2048]{1,0:T(8,128)(2,1)S(1)} %collective-permute-done.3.refs_2_, ...), custom_call_target="tpu_custom_call" | custom-call | flops 1024 | bytes 1024 | tf_op jit(solution)/shard_map/pallas_call | solution.py:335
  93.3 3.6 %shard_map.86 = (bf16[352,2048]{1,0:T(8,128)(2,1)}, f32[352,2048]{1,0:T(8,128)S(1)}, f32[16,128]{1,0:T(8,128)}) custom-call(bf16[384,2048]{1,0:T(8,128)(2,1)S(1)} %get-tuple-element.66.rows_ref, bf16[704,384]{1,0:T(8,128)(2,1)S(1)} %get-tuple-element.67.hidw_ref, f32[704,2048]{1,0:T(8,128)S(1)} %get-tuple-element.68.early_ref, ...), custom_call_target="tpu_custom_call" | custom-call | flops 1024 | bytes 1024 | tf_op jit(solution)/shard_map/pallas_call | solution.py:375
  96.9 5.4 %all-to-all-start = ((f32[16,1,128]{2,1,0:T(1,128)}), f32[16,1,128]{2,1,0:T(1,128)S(1)}, u32[]{:S(2)}, u32[]{:S(2)}) async-start(f32[16,1,128]{2,1,0:T(1,128)} %bitcast.6), calls=%async_computation | async-start | bytes 16384 | tf_op jit(solution)/shard_map/all_to_all | solution.py:278
  102.3 4.5 %shard_map.87 = (f32[352,2048]{1,0:T(8,128)}, f32[16,352]{1,0:T(8,128)}) custom-call(f32[352,2048]{1,0:T(8,128)S(1)} %get-tuple-element.73.own_ref, bf16[1,352,2048]{2,1,0:T(8,128)(2,1)} %bitcast.4.others_ref), custom_call_target="tpu_custom_call" | custom-call | flops 1024 | bytes 1024 | tf_op jit(solution)/shard_map/pallas_call | solution.py:396
  106.8 2.8 %all-to-all-done = f32[16,1,128]{2,1,0:T(1,128)S(1)} async-done(((f32[16,1,128]{2,1,0:T(1,128)}), f32[16,1,128]{2,1,0:T(1,128)S(1)}, u32[]{:S(2)}, u32[]{:S(2)}) %all-to-all-start) | async-done | bytes 8224 | tf_op jit(solution)/shard_map/all_to_all | solution.py:278
  109.6 0.7 copy-done.3
  110.3 0.7 shard_map.88
  (27 shorter events, 1.8 us)
Async XLA Ops:
  0.6 77.9 %copy-start = (bf16[1,704,2048]{2,1,0:T(8,128)(2,1)S(1)}, bf16[1,704,2048]{2,1,0:T(8,128)(2,1)}, u32[]{:S(2)}) copy-start(bf16[1,704,2048]{2,1,0:T(8,128)(2,1)} %param.9) | copy-start | bytes 8650756
  2.7 18.8 %collective-permute-start = (bf16[128,2176]{1,0:T(8,128)(2,1)}, bf16[128,2176]{1,0:T(8,128)(2,1)S(1)}, u32[]{:S(2)}, u32[]{:S(2)}) collective-permute-start(bf16[128,2176]{1,0:T(8,128)(2,1)} %get-tuple-element.41.refs_0_), channel_id=1, source_target_pairs={{0,8},{2,10},{4,12},{6,14},{8,16},{10,18},{12,20},{14,22},{16,24},... | collective-permute-start | bytes 1671176 | tf_op jit(solution)/shard_map/ppermute | solution.py:272
  5.8 26.2 %collective-permute-start.9 = (bf16[128,2176]{1,0:T(8,128)(2,1)}, bf16[128,2176]{1,0:T(8,128)(2,1)S(1)}, u32[]{:S(2)}, u32[]{:S(2)}) collective-permute-start(bf16[128,2176]{1,0:T(8,128)(2,1)} %get-tuple-element.41.refs_0_), channel_id=1, source_target_pairs={{0,24},{2,26},{4,28},{6,30},{8,0},{10,2},{12,4},{14,6},{16,8},{18,... | collective-permute-start | bytes 1671176 | tf_op jit(solution)/shard_map/ppermute | solution.py:272
  13.1 24.5 %collective-permute-start.5 = (bf16[72,3072]{1,0:T(8,128)(2,1)}, bf16[72,3072]{1,0:T(8,128)(2,1)S(1)}, u32[]{:S(2)}, u32[]{:S(2)}) collective-permute-start(bf16[72,3072]{1,0:T(8,128)(2,1)} %get-tuple-element.48), channel_id=1, source_target_pairs={{0,2},{2,0},{4,6},{6,4},{8,10},{10,8},{12,14},{14,12},{16,18},{18,... | collective-permute-start | bytes 1327112 | tf_op jit(solution)/shard_map/ppermute | solution.py:275
  14.8 23.3 %collective-permute-start.6 = (bf16[72,3072]{1,0:T(8,128)(2,1)}, bf16[72,3072]{1,0:T(8,128)(2,1)S(1)}, u32[]{:S(2)}, u32[]{:S(2)}) collective-permute-start(bf16[72,3072]{1,0:T(8,128)(2,1)} %get-tuple-element.49), channel_id=1, source_target_pairs={{0,4},{2,6},{4,0},{6,2},{8,12},{10,14},{12,8},{14,10},{16,20},{18,... | collective-permute-start | bytes 1327112 | tf_op jit(solution)/shard_map/ppermute | solution.py:275
  16.3 22.9 %collective-permute-start.7 = (bf16[72,3072]{1,0:T(8,128)(2,1)}, bf16[72,3072]{1,0:T(8,128)(2,1)S(1)}, u32[]{:S(2)}, u32[]{:S(2)}) collective-permute-start(bf16[72,3072]{1,0:T(8,128)(2,1)} %get-tuple-element.50), channel_id=1, source_target_pairs={{0,6},{2,4},{4,2},{6,0},{8,14},{10,12},{12,10},{14,8},{16,22},{18,... | collective-permute-start | bytes 1327112 | tf_op jit(solution)/shard_map/ppermute | solution.py:275
  32.0 1.1 copy-start.1
  34.5 30.0 %collective-permute-start.10 = (bf16[72,6144]{1,0:T(8,128)(2,1)S(1)}, bf16[72,6144]{1,0:T(8,128)(2,1)S(1)}, u32[]{:S(2)}, u32[]{:S(2)}) collective-permute-start(bf16[72,6144]{1,0:T(8,128)(2,1)S(1)} %get-tuple-element.53), channel_id=1, source_target_pairs={{0,2},{2,0},{4,6},{6,4},{8,10},{10,8},{12,14},{14,12},{16,18},{18,... | collective-permute-start | bytes 2654216 | tf_op jit(solution)/shard_map/ppermute | solution.py:275
  36.1 39.6 %collective-permute-start.11 = (bf16[72,6144]{1,0:T(8,128)(2,1)S(1)}, bf16[72,6144]{1,0:T(8,128)(2,1)S(1)}, u32[]{:S(2)}, u32[]{:S(2)}) collective-permute-start(bf16[72,6144]{1,0:T(8,128)(2,1)S(1)} %get-tuple-element.54), channel_id=1, source_target_pairs={{0,4},{2,6},{4,0},{6,2},{8,12},{10,14},{12,8},{14,10},{16,20},{18,... | collective-permute-start | bytes 2654216 | tf_op jit(solution)/shard_map/ppermute | solution.py:275
  37.6 40.7 %collective-permute-start.12 = (bf16[72,6144]{1,0:T(8,128)(2,1)S(1)}, bf16[72,6144]{1,0:T(8,128)(2,1)S(1)}, u32[]{:S(2)}, u32[]{:S(2)}) collective-permute-start(bf16[72,6144]{1,0:T(8,128)(2,1)S(1)} %get-tuple-element.55), channel_id=1, source_target_pairs={{0,6},{2,4},{4,2},{6,0},{8,14},{10,12},{12,10},{14,8},{16,22},{18,... | collective-permute-start | bytes 2654216 | tf_op jit(solution)/shard_map/ppermute | solution.py:275
  38.1 24.8 %collective-permute-start.1 = (bf16[128,2176]{1,0:T(8,128)(2,1)S(1)}, bf16[128,2176]{1,0:T(8,128)(2,1)S(1)}, u32[]{:S(2)}, u32[]{:S(2)}) collective-permute-start(bf16[128,2176]{1,0:T(8,128)(2,1)S(1)} %collective-permute-done.refs_1_), channel_id=1, source_target_pairs={{0,8},{2,10},{4,12},{6,14},{8,16},{10,18},{12,20},{14,22},{16,24},... | collective-permute-start | bytes 1671176 | tf_op jit(solution)/shard_map/ppermute | solution.py:272
  39.2 1.0 copy-start.2
  40.4 22.5 %collective-permute-start.14 = (bf16[4,72,768]{2,1,0:T(8,128)(2,1)S(1)}, bf16[4,72,768]{2,1,0:T(8,128)(2,1)S(1)}, u32[]{:S(2)}, u32[]{:S(2)}) collective-permute-start(bf16[4,72,768]{2,1,0:T(8,128)(2,1)S(1)} %get-tuple-element.57), channel_id=1, source_target_pairs={{0,8},{2,10},{4,12},{6,14},{8,16},{10,18},{12,20},{14,22},{16,24},... | collective-permute-start | bytes 1327112 | tf_op jit(solution)/shard_map/ppermute | solution.py:272
  62.9 19.8 %collective-permute-start.13 = (bf16[4,72,768]{2,1,0:T(8,128)(2,1)S(1)}, bf16[4,72,768]{2,1,0:T(8,128)(2,1)S(1)}, u32[]{:S(2)}, u32[]{:S(2)}) collective-permute-start(bf16[4,72,768]{2,1,0:T(8,128)(2,1)S(1)} %get-tuple-element.56), channel_id=1, source_target_pairs={{0,24},{2,26},{4,28},{6,30},{8,0},{10,2},{12,4},{14,6},{16,8},{18,... | collective-permute-start | bytes 1327112 | tf_op jit(solution)/shard_map/ppermute | solution.py:272
  62.9 28.3 %collective-permute-start.8 = (bf16[4,72,768]{2,1,0:T(8,128)(2,1)S(1)}, bf16[4,72,768]{2,1,0:T(8,128)(2,1)S(1)}, u32[]{:S(2)}, u32[]{:S(2)}) collective-permute-start(bf16[4,72,768]{2,1,0:T(8,128)(2,1)S(1)} %get-tuple-element.51), channel_id=1, source_target_pairs={{0,16},{2,18},{4,20},{6,22},{8,24},{10,26},{12,28},{14,30},{16,0},... | collective-permute-start | bytes 1327112 | tf_op jit(solution)/shard_map/ppermute | solution.py:272
  64.5 26.7 %collective-permute-start.2 = (bf16[72,2048]{1,0:T(8,128)(2,1)S(1)}, bf16[72,2048]{1,0:T(8,128)(2,1)S(1)}, u32[]{:S(2)}, u32[]{:S(2)}) collective-permute-start(bf16[72,2048]{1,0:T(8,128)(2,1)S(1)} %get-tuple-element.43), channel_id=1, source_target_pairs={{0,2},{2,0},{4,6},{6,4},{8,10},{10,8},{12,14},{14,12},{16,18},{18,... | collective-permute-start | bytes 884744 | tf_op jit(solution)/shard_map/ppermute | solution.py:275
  75.7 15.5 %collective-permute-start.3 = (bf16[72,2048]{1,0:T(8,128)(2,1)S(1)}, bf16[72,2048]{1,0:T(8,128)(2,1)S(1)}, u32[]{:S(2)}, u32[]{:S(2)}) collective-permute-start(bf16[72,2048]{1,0:T(8,128)(2,1)S(1)} %get-tuple-element.44), channel_id=1, source_target_pairs={{0,4},{2,6},{4,0},{6,2},{8,12},{10,14},{12,8},{14,10},{16,20},{18,... | collective-permute-start | bytes 884744 | tf_op jit(solution)/shard_map/ppermute | solution.py:275
  78.3 12.9 %collective-permute-start.4 = (bf16[72,2048]{1,0:T(8,128)(2,1)S(1)}, bf16[72,2048]{1,0:T(8,128)(2,1)S(1)}, u32[]{:S(2)}, u32[]{:S(2)}) collective-permute-start(bf16[72,2048]{1,0:T(8,128)(2,1)S(1)} %get-tuple-element.45), channel_id=1, source_target_pairs={{0,6},{2,4},{4,2},{6,0},{8,14},{10,12},{12,10},{14,8},{16,22},{18,... | collective-permute-start | bytes 884744 | tf_op jit(solution)/shard_map/ppermute | solution.py:275
  96.9 12.7 %copy-start.4 = (s32[128,6]{0,1:T(8,128)S(1)}, s32[128,6]{0,1:T(8,128)}, u32[]{:S(2)}) copy-start(s32[128,6]{0,1:T(8,128)} %param.7) | copy-start | bytes 9220
  96.9 12.7 %copy-start.5 = (f32[16,128]{1,0:T(8,128)S(1)}, f32[16,128]{1,0:T(8,128)}, u32[]{:S(2)}) copy-start(f32[16,128]{1,0:T(8,128)} %get-tuple-element.76.slot_ref) | copy-start | bytes 24580
  96.9 5.4 %collective-permute-start.15 = (bf16[352,2048]{1,0:T(8,128)(2,1)}, bf16[352,2048]{1,0:T(8,128)(2,1)}, u32[]{:S(2)}, u32[]{:S(2)}) collective-permute-start(bf16[352,2048]{1,0:T(8,128)(2,1)} %get-tuple-element.74), channel_id=1, source_target_pairs={{0,1},{1,0},{2,3},{3,2},{4,5},{5,4},{6,7},{7,6},{8,9},{9,8},{10,11... | collective-permute-start | bytes 4325384 | tf_op jit(solution)/shard_map/ppermute | solution.py:389
  96.9 12.7 %all-to-all-start = ((f32[16,1,128]{2,1,0:T(1,128)}), f32[16,1,128]{2,1,0:T(1,128)S(1)}, u32[]{:S(2)}, u32[]{:S(2)}) async-start(f32[16,1,128]{2,1,0:T(1,128)} %bitcast.6), calls=%async_computation | async-start | bytes 16384 | tf_op jit(solution)/shard_map/all_to_all | solution.py:278
  109.6 0.7 copy-start.3

commit v5 on v4

v5 whole, which is shorter than its diff:
```python
import functools

import jax
import jax.numpy as jnp
from jax import lax
from jax.experimental import pallas as pl
from jax.experimental.pallas import tpu as pltpu
from jax.sharding import PartitionSpec as P

BLOCK = 128
PLANE = 4
BF = jnp.bfloat16
F32 = jnp.float32
NT = (((1,), (1,)), ((), ()))
VMEM_BYTES = 24 * 1024 * 1024
ALL_VMEM = 56 * 1024 * 1024


def up(value, unit):
    return -(-value // unit) * unit


def call(kernel, out_shape, room=VMEM_BYTES, flops=1024, **kw):
    return pl.pallas_call(
        kernel,
        out_shape=out_shape,
        cost_estimate=pl.CostEstimate(
            flops=flops, bytes_accessed=1024, transcendentals=0
        ),
        compiler_params=pltpu.CompilerParams(vmem_limit_bytes=room),
        **kw,
    )


def select(slots, table, cot_ref, outs, at=0):
    me = lax.axis_index("expert")
    tokens = cot_ref.shape[0]
    rows = lax.broadcasted_iota(jnp.int32, (slots, tokens), 0).astype(F32)
    pick = jnp.concatenate(
        [jnp.where(table[pl.ds(me ^ k, 1), :] == rows, 1.0, 0.0) for k in range(PLANE)], axis=0
    ).astype(BF)
    model = cot_ref.shape[1]
    step = min(512, model)
    for c in range(0, model, step):
        got = jnp.dot(pick, cot_ref[:, c : c + step], preferred_element_type=F32)
        for k in range(PLANE):
            outs[k][:, at + c : at + c + step] = got[k * slots : (k + 1) * slots, :].astype(BF)


def open_kernel(slots, flip, *refs):
    routes_hbm, num_hbm, hid_hbm, cot_hbm, ext_hbm, *refs = refs
    sent_hbm, (slot_ref, *refs) = refs[:PLANE], refs[PLANE:]
    ext, sent, table, routes_ref, num_ref, hid_ref, done = refs
    experts, tokens = slot_ref.shape
    top_k, width = hid_ref.shape[:2]
    model = cot_hbm.shape[1]
    half = width // 2
    padded = table.shape[0] // 2
    pairs = (
        (routes_hbm, routes_ref),
        (cot_hbm, ext.at[:, pl.ds(0, model)]),
        (num_hbm, num_ref),
        (hid_hbm, hid_ref),
        (ext, ext_hbm),
    )
    copies = [pltpu.make_async_copy(*pair, done.at[n]) for n, pair in enumerate(pairs)]
    for copy in copies[:4]:
        copy.start()
    copies[0].wait()
    routes = routes_ref[...]
    ids = lax.broadcasted_iota(jnp.int32, (experts, tokens), 0)
    mask = jnp.zeros((experts, tokens), F32)
    for k in range(top_k):
        mask += jnp.where(routes[k : k + 1, :] == ids, 1.0, 0.0)
    earlier = lax.broadcasted_iota(jnp.int32, (tokens, tokens), 0) < lax.broadcasted_iota(
        jnp.int32, (tokens, tokens), 1
    )
    rank = jnp.dot(
        mask.astype(BF), jnp.where(earlier, 1.0, 0.0).astype(BF), preferred_element_type=F32
    )
    slot = jnp.where(mask > 0.5, rank, -1.0)
    slot_ref[...] = slot
    wide = jnp.concatenate([slot, jnp.zeros((BLOCK - experts, tokens), F32)], axis=0)
    ext[:, model : model + BLOCK] = wide.T.astype(BF)
    copies[1].wait()
    copies[4].start()
    parts = experts // PLANE * 2 * padded
    lead = sent.shape[2] - parts
    select(slots, slot_ref, ext.at[:, pl.ds(0, lead)], [sent.at[k] for k in range(PLANE)], parts)
    me = lax.axis_index("expert")
    steps = (routes >> 2) - (me >> 2)
    steps = jnp.where(steps < 0, steps + experts // PLANE, steps)
    rel = steps * PLANE + ((routes & 3) ^ (me & 3))
    codes = []
    for k in range(top_k):
        own = jnp.sum(
            jnp.where(routes[k : k + 1, :] == ids, slot, 0.0), axis=0, keepdims=True
        ).astype(jnp.int32)
        codes.append(rel[k : k + 1, :] * slots + own)
    code = jnp.concatenate(codes, axis=1)
    rows = lax.broadcasted_iota(jnp.int32, (experts * slots, top_k * tokens), 0)
    pick = jnp.where(rows == code, 1.0, 0.0).astype(BF)
    copies[2].wait()
    copies[3].wait()
    for n, part in enumerate(halves(flip)):
        at = pl.multiple_of(part * half, 16) if flip else part * half
        for k in range(top_k):
            lanes = slice(k * tokens, (k + 1) * tokens)
            table[n * padded : n * padded + half, lanes] = hid_ref[k, pl.ds(at, half), :]
            weight = num_ref[k : k + 1, :].astype(F32) * (1.0 / 1024.0)
            high = weight.astype(BF).astype(F32)
            rows = lax.broadcasted_iota(jnp.int32, (padded - half, tokens), 0)
            tail = jnp.where(rows == 0, high, jnp.where(rows == 1, weight - high, 0.0))
            table[n * padded + half : (n + 1) * padded, lanes] = tail.astype(BF)
    got = lax.dot_general(pick, table[...], NT, preferred_element_type=F32)
    for s in range(experts // PLANE):
        lanes = slice(s * 2 * padded, (s + 1) * 2 * padded)
        for k in range(PLANE):
            at = (s * PLANE + k) * slots
            sent[k, :, lanes] = got[at : at + slots, :].astype(BF)
    copies = copies[4:]
    for k in range(PLANE):
        copies.append(pltpu.make_async_copy(sent.at[k], sent_hbm[k], done.at[5 + k]))
        copies[-1].start()
    for copy in copies:
        copy.wait()


def relay_kernel(slots, count, begin, *refs):
    blocks, outs, table = refs[:count], refs[-1 - PLANE : -1], refs[-1]
    part = outs[0].shape[1] // count
    model = begin + part
    for n, ext_ref in enumerate(blocks):
        table[...] = ext_ref[:, model : model + BLOCK].astype(F32).T
        select(slots, table, ext_ref.at[:, pl.ds(begin, part)], outs, n * part)


def forward_kernel(*refs):
    del refs


def regroup_kernel(s, *refs):
    out_ref = refs[-1]
    padded = out_ref.shape[2]
    for k in range(PLANE):
        out_ref[k] = refs[k][:, s * padded : (s + 1) * padded]


def fill(table, at, piece, stride):
    wide = piece.astype(F32)
    short = stride - wide.shape[0]
    if short:
        wide = jnp.concatenate([wide, jnp.zeros((short, wide.shape[1]), F32)], axis=0)
    table[at : at + stride, :] = wide.astype(table.dtype)


def halves(flip):
    mine = lax.axis_index("replica") if flip else 1
    return 1 - mine, mine


def stage_kernel(place, spans, stride, flip, *refs):
    arrays, refs = refs[: PLANE * len(spans)], refs[PLANE * len(spans) :]
    w_ref, refs = refs[0], refs[1:]
    hid_ref = refs[0]
    all_rows, all_hidw, gate_ref, rows, hids, hidw, done = refs[-7:]
    group = PLANE * stride
    width, model = w_ref.shape
    half = width // 2
    padded = hids.shape[1] // 2
    to = 0
    for n, (at, count) in enumerate(spans):
        for k in range(PLANE):
            piece = arrays[n * PLANE + k][:, at : at + count]
            fill(rows.at[:, pl.ds(to, count)], k * stride, piece, stride)
        to += count
    copy = pltpu.make_async_copy(rows, all_rows.at[pl.ds(place * group, group)], done.at[0])
    copy.start()
    for k in range(PLANE):
        fill(hids, k * stride, hid_ref[k], stride)
    gate = 0.0
    for n, part in enumerate(halves(flip)):
        at = pl.multiple_of(part * half, 16) if flip else part * half
        flipped = hids[:, n * padded : (n + 1) * padded].T
        hid = flipped[0:half, :]
        weight = flipped[half : half + 1, :] + flipped[half + 1 : half + 2, :]
        hidw[n * half : (n + 1) * half, :] = (hid * weight).astype(BF)
        back = lax.dot_general(
            w_ref[pl.ds(at, half), :], rows[...], NT, preferred_element_type=F32
        )
        gate += jnp.sum(back * hid, axis=0, keepdims=True)
    second = pltpu.make_async_copy(
        hidw, all_hidw.at[:, pl.ds(place * group, group)], done.at[1]
    )
    second.start()
    gate_ref[...] = jnp.zeros_like(gate_ref)
    for k in range(PLANE):
        gate_ref[k : k + 1, 0:stride] = gate[:, k * stride : (k + 1) * stride]
    copy.wait()
    second.wait()


def source(outer, s, k):
    me = lax.axis_index("expert")
    return lax.rem((me >> 2) - s + outer, outer) * PLANE + ((me & 3) ^ k)


def early_kernel(rows_ref, hidw_ref, out_ref, mark_ref):
    mark_ref[...] = jnp.zeros_like(mark_ref)
    got = jnp.dot(hidw_ref[...], rows_ref[...], preferred_element_type=F32)
    out_ref[...] = got.astype(BF)


def partial_kernel(rows_ref, hidw_ref, early_ref, *refs):
    send_ref, mine_ref = refs[-2:]
    half = mine_ref.shape[0]
    got = early_ref[...].astype(F32) + jnp.dot(
        hidw_ref[...], rows_ref[...], preferred_element_type=F32
    )
    send_ref[...] = got[0:half].astype(BF)
    mine_ref[...] = got[half:].astype(BF)


def combine_kernel(outer, *refs):
    gates, outs = refs[:outer], refs[-PLANE:]
    for k, out_ref in enumerate(outs):
        for s, gate_ref in enumerate(gates):
            out_ref[s : s + 1, :] = gate_ref[k : k + 1, :]


def pick_gates(slot_ref, routes_ref, homes, gate_ref, rows):
    experts, tokens = slot_ref.shape
    for k in range(PLANE):
        for s in range(experts // PLANE):
            rows[pl.ds(source(experts // PLANE, -s, k), 1), :] = homes[k][s : s + 1, :]
    slot = jnp.maximum(slot_ref[...], 0.0).astype(jnp.int32)
    value = jnp.take_along_axis(rows[...], slot, axis=1)
    ids = lax.broadcasted_iota(jnp.int32, (experts, tokens), 0)
    for k in range(gate_ref.shape[0]):
        gate_ref[k : k + 1, :] = jnp.sum(
            jnp.where(routes_ref[k : k + 1, :] == ids, value, 0.0), axis=0, keepdims=True
        )


def finish_kernel(count, *refs):
    own, others_ref, refs = refs[:count], refs[count], refs[count + 1 :]
    if len(refs) > 3:
        slot_ref, routes_ref, *homes = refs[: 2 + PLANE]
        out_ref, scale_ref, gate_ref, table, rows = refs[-5:]

        @pl.when(pl.program_id(0) == 0)
        def _():
            pick_gates(slot_ref, routes_ref, homes, gate_ref, rows)

    else:
        out_ref, scale_ref, table = refs
    step = pl.program_id(0)
    share, width = out_ref.shape
    lanes = lax.broadcasted_iota(jnp.int32, (share, BLOCK), 1)

    @pl.when(step == 0)
    def _():
        table[...] = jnp.zeros_like(table)

    kept = table[0:share, :]
    for b in range(width // BLOCK):
        span = slice(b * BLOCK, (b + 1) * BLOCK)
        terms = [others_ref[n, :, span].astype(F32) for n in range(others_ref.shape[0])]
        terms += [ref[:, span].astype(F32) for ref in own]
        top = functools.reduce(jnp.maximum, [jnp.abs(term) for term in terms])
        scale = jnp.max(top, axis=1, keepdims=True) + 1e-6
        out_ref[:, span] = functools.reduce(jnp.add, terms) * (1.0 / scale)
        kept = jnp.where(lanes == step * (width // BLOCK) + b, scale, kept)
    table[0:share, :] = kept

    @pl.when(step == pl.num_programs(0) - 1)
    def _():
        scale_ref[...] = table[...].T[0 : scale_ref.shape[0], 0:share]


def joined(count, spare, *refs):
    if spare:
        refs = refs[: count + 3 + PLANE] + refs[count + 3 + PLANE + spare :]
    finish_kernel(count, *refs)


def per_device(cotangent, hidden, routes, numerators, w_down):
    tokens, model = cotangent.shape
    top_k, width = hidden.shape[1], hidden.shape[2]
    experts, replicas = lax.axis_size("expert"), lax.axis_size("replica")
    outer = experts // PLANE
    slots = up(3 * tokens * top_k // (2 * experts), 8)
    stride = up(slots, 32)
    half = width // 2
    padded = up(half + 2, 128)
    share = width // replicas
    group = PLANE * stride
    flip = replicas == 2
    sds = jax.ShapeDtypeStruct
    step = 512
    steps = model // step

    def ring(array, by):
        pairs = [(e, (e + by * PLANE) % experts) for e in range(experts)]
        return lax.ppermute(array, "expert", pairs)

    def swap(array, k):
        return lax.ppermute(array, "expert", [(e, e ^ k) for e in range(experts)])

    anywhere = pl.BlockSpec(memory_space=pl.ANY)
    inside = pl.BlockSpec(memory_space=pltpu.VMEM)

    lead = model // 2
    wide = outer * 2 * padded + lead
    ext, *packed, slot = call(
        functools.partial(open_kernel, slots, flip),
        [sds((tokens, model + BLOCK), BF)]
        + [sds((slots, wide), BF)] * PLANE
        + [sds((experts, tokens), F32)],
        ALL_VMEM,
        in_specs=[anywhere] * 4,
        out_specs=[anywhere] * (1 + PLANE) + [inside],
        scratch_shapes=[
            pltpu.VMEM((tokens, model + BLOCK), BF),
            pltpu.VMEM((PLANE, slots, wide), BF),
            pltpu.VMEM((2 * padded, top_k * tokens), BF),
            pltpu.VMEM((top_k, tokens), jnp.int32),
            pltpu.VMEM((top_k, tokens), jnp.int32),
            pltpu.VMEM((top_k, width, tokens), BF),
            pltpu.SemaphoreType.DMA((5 + PLANE,)),
        ],
    )(routes.T, numerators.T, jnp.transpose(hidden, (1, 2, 0)), cotangent)
    opening = [packed[0]] + [swap(packed[k], k) for k in range(1, PLANE)]

    blocks = {0: ext}
    order = [0]
    for s in range(1, outer // 2 + 1):
        blocks[s] = ring(blocks[s - 1], 1)
        order.append(s)
        if outer - s != s:
            blocks[outer - s] = ring(blocks[(outer - s + 1) % outer], -1)
            order.append(outer - s)
    def regroup(s, after):
        return call(
            functools.partial(regroup_kernel, s),
            sds((PLANE, slots, 2 * padded), BF),
            in_specs=[inside] * PLANE + [anywhere] * len(after),
        )(*opening, *after)

    hids = {0: regroup(0, [])}
    for n, s in enumerate(order[1:]):
        hids[s] = ring(regroup(s, [blocks[order[-1]]] if n else []), s)

    def gated(arrays, after):
        return call(
            forward_kernel,
            [sds(array.shape, array.dtype) for array in arrays],
            in_specs=[anywhere] * (len(arrays) + len(after)),
            out_specs=[anywhere] * len(arrays),
            input_output_aliases={n: n for n in range(len(arrays))},
        )(*arrays, *after)

    def relay(batch, after, begin=0):
        sent = call(
            functools.partial(relay_kernel, slots, len(batch), begin),
            [sds((slots, len(batch) * (model - begin)), BF)] * PLANE,
            scratch_shapes=[pltpu.VMEM((BLOCK, tokens), F32)],
        )(*[blocks[s] for s in batch])
        moved = gated(sent[1:], after)
        return [sent[0]] + [swap(moved[k - 1], k) for k in range(1, PLANE)]

    middle = relay(order[1:-1], opening[1:])
    late = relay(order[-1:], [hids[order[1]]])
    final = relay([0], [*middle[1:], hids[order[-2]]], lead)

    def stage(parts, hid, place, count, after, rows):
        arrays = [array for got, _ in parts for array in got]
        fixed = len(arrays) + 2
        return call(
            functools.partial(stage_kernel, place, [span for _, span in parts], stride, flip),
            [
                sds((count * group, model), BF),
                sds((width, count * group), BF),
                sds((PLANE, BLOCK), F32),
            ],
            flops=2_000_000_000,
            in_specs=[inside] * fixed + [anywhere] * len(rows) + [inside] * len(after),
            out_specs=[anywhere, anywhere, inside],
            input_output_aliases={fixed + i: i for i in range(len(rows))},
            scratch_shapes=[
                pltpu.VMEM((group, model), BF),
                pltpu.VMEM((group, 2 * padded), F32),
                pltpu.VMEM((width, group), BF),
                pltpu.SemaphoreType.DMA((2,)),
            ],
        )(*arrays, w_down[0], hid, *rows, *after)

    def products(count):
        return [
            pl.BlockSpec((count * group, step), lambda j: (0, j)),
            pl.BlockSpec((width, count * group), lambda j: (0, 0)),
        ]

    sources = {s: [(middle, (n * model, model))] for n, s in enumerate(order[1:-1])}
    sources[order[-1]] = [(late, (0, model))]
    sources[0] = [(opening, (wide - lead, lead)), (final, (0, model - lead))]
    rows, gates = [], {}
    for n, s in enumerate(order[1:-1]):
        *rows, gates[s] = stage(sources[s], hids[s], n, outer - 2, [], rows)
    full = pl.BlockSpec((width, step), lambda j: (0, j))
    early, mark = call(
        early_kernel,
        [sds((width, model), BF), sds((8, BLOCK), F32)],
        flops=3_500_000_000,
        grid=(steps,),
        in_specs=products(outer - 2),
        out_specs=[full, pl.BlockSpec((8, BLOCK), lambda j: (0, 0))],
    )(*rows)
    *rows, gates[order[-1]] = stage(
        sources[order[-1]], hids[order[-1]], 0, 2, [mark], []
    )
    for s, gate in zip(
        order[1:-1], gated([gates[s] for s in order[1:-1]], [gates[order[-1]]])
    ):
        gates[s] = gate
    *rows, gates[0] = stage(sources[0], hids[0], 1, 2, [], rows)
    gates = [ring(gates[s], -s) if s else gates[s] for s in range(outer)]

    token_spec = pl.BlockSpec((top_k, tokens), lambda j: (0, 0))
    home = pl.BlockSpec((outer, BLOCK), lambda j: (0, 0))
    middle_step = steps // 2

    def column(first, height):
        return pl.BlockSpec((height, step), lambda j: (0, j + first))

    def partial(first, after):
        return call(
            partial_kernel,
            [sds((half, model // 2), BF)] * 2,
            grid=(middle_step,),
            in_specs=[
                column(first, 2 * group),
                pl.BlockSpec((width, 2 * group), lambda j: (0, 0)),
                column(first, width),
            ]
            + [anywhere] * len(after),
            out_specs=[column(0, half)] * 2,
        )(*rows, early, *after)

    def finish(first, send, mine, out, extra):
        if flip:
            others = lax.ppermute(send, "replica", [(0, 1), (1, 0)])[None]
            own = [mine]
        else:
            both = jnp.concatenate([send, mine], axis=0).reshape(replicas, share, model // 2)
            others = lax.all_to_all(both, "replica", 0, 0, tiled=True)
            own = []
        specs = [column(0, half)] * len(own)
        specs.append(pl.BlockSpec((others.shape[0], share, step), lambda j: (0, 0, j)))
        outs = [sds((share, model), F32), sds((model // BLOCK, share), F32)]
        out_specs = [
            column(first, share),
            pl.BlockSpec((model // 2 // BLOCK, share), lambda j: (first // middle_step, 0)),
        ]
        scratch = [pltpu.VMEM((up(share, 128), BLOCK), F32)]
        if extra:
            specs += [pl.BlockSpec((experts, tokens), lambda j: (0, 0)), token_spec]
            specs += [home] * PLANE
            outs.append(sds((top_k, tokens), F32))
            out_specs.append(token_spec)
            scratch.append(pltpu.VMEM((experts, BLOCK), F32))
        fixed = len(own) + 1 + len(extra)
        return call(
            functools.partial(joined, len(own), len(out)),
            outs,
            grid=(middle_step,),
            in_specs=specs + [anywhere] * len(out),
            out_specs=out_specs,
            input_output_aliases={fixed + n: n for n in range(len(out))},
            scratch_shapes=scratch,
        )(*own, others, *extra, *out)

    left = partial(0, [])
    right = partial(middle_step, gates[1:])
    homes = call(
        functools.partial(combine_kernel, outer),
        [sds((outer, BLOCK), F32)] * PLANE,
        in_specs=[inside] * outer + [anywhere],
    )(*gates, right[0])
    homes = [homes[0]] + [swap(homes[k], k) for k in range(1, PLANE)]
    out = finish(0, *left, [], [])
    out, scales, gate_grad = finish(middle_step, *right, out, [slot, routes.T, *homes])
    return gate_grad.T, scales.T[None], out[None]


def solution(mesh):
    return jax.shard_map(
        per_device,
        mesh=mesh,
        in_specs=(
            P(("expert", "replica"), None),
            P(("expert", "replica"), None, None),
            P(("expert", "replica"), None),
            P(("expert", "replica"), None),
            P("expert", None, None),
        ),
        out_specs=(
            P(("expert", "replica"), None),
            P("expert", "replica", None),
            P("expert", "replica", None),
        ),
        check_vma=False,
    )
```

time: 111 us -> 107 us (0.964)
  starting transfers between devices: 25 us -> 32 us
  Pallas kernels: 31.6 us -> 26.3 us
  waiting for transfers between devices: 50.9 us -> 47.5 us
  local copies, waits for them, and re-layouts: 2.82 us -> 0.03 us
    ppermute x9 -> x15, starting transfers between devices: 11.5 us -> 18.1 us  [swap(): return lax.ppermute(array, 'expert', [(e, e ^ k) for e in range(experts)])]
    ppermute x6 -> x9, starting transfers between devices: 8.06 us -> 13.5 us  [ring(): return lax.ppermute(array, 'expert', pairs)]
    all_to_all x1 -> x0, starting transfers between devices: 5.41 us -> none  [exchange(): lax.all_to_all(array, 'expert', split_axis=0, concat_axis=0, tiled=True)]
    pallas_call x13 -> x22, Pallas kernels: 31.6 us -> 26.3 us  [the longest x4 8.29 us: stage(): call(functools.partial(stage_kernel, place, [span for _, span in parts],...]
    ppermute x9 -> x15, waiting for transfers between devices: 9.65 us -> 6.19 us  [swap(): return lax.ppermute(array, 'expert', [(e, e ^ k) for e in range(experts)])]
    ppermute x6 -> x9, waiting for transfers between devices: 38.5 us -> 41.3 us  [ring(): return lax.ppermute(array, 'expert', pairs)]
    unnamed x12 -> x10, local copies, waits for them, and re-layouts: 2.82 us -> 0.03 us
    all_to_all x1 -> x0, waiting for transfers between devices: 2.77 us -> none  [exchange(): lax.all_to_all(array, 'expert', split_axis=0, concat_axis=0, tiled=True)]
  transfers between devices with their start and end apart: 17 -> 26, of which waited for: 6 -> 11; matrix products, arithmetic and copies ran while one was open for 0% -> 0% of each run, Pallas kernels for 21% -> 18%
where the time goes in v5:
time: 107 us
  waiting for transfers between devices  47.5 us (44%)
  starting transfers between devices  32 us (30%)
  Pallas kernels  26.3 us (25%)
    ppermute x9, waiting for transfers between devices, ring(): return lax.ppermute(array, 'expert', pairs)  41.3 us
    ppermute x15, starting transfers between devices, swap(): return lax.ppermute(array, 'expert', [(e, e ^ k) for e in range(experts)])  18.1 us
    ppermute x9, starting transfers between devices, ring(): return lax.ppermute(array, 'expert', pairs)  13.5 us
    pallas_call x4, Pallas kernels, stage(): call(functools.partial(stage_kernel, place, [span for _, span in parts],...  8.29 us
    ppermute x15, waiting for transfers between devices, swap(): return lax.ppermute(array, 'expert', [(e, e ^ k) for e in range(experts)])  6.19 us
    pallas_call x1, Pallas kernels, per_device(): call(functools.partial(open_kernel, slots, flip), [sds((tokens, model + B...  5.6 us
    pallas_call x2, Pallas kernels, partial(): call(partial_kernel, [sds((half, model // 2), BF)] * 2, grid=(middle_step...  3.66 us
    pallas_call x2, Pallas kernels, finish(): call(functools.partial(joined, len(own), len(out)), outs, grid=(middle_st...  3.51 us
  transfers between devices with their start and end apart: 26, of which 11 were waited for; matrix products, arithmetic and copies ran while one was open for 0% of the time, Pallas kernels for 18%

profile of v5, /device:TPU:0, one launch (start us, length us, event | category | flops | bytes accessed | tf_op | source)
XLA Modules:
  0.0 106.7 jit_solution(5008093119357363222)
XLA Ops:
  0.6 5.6 %shard_map.76 = (bf16[128,2176]{1,0:T(8,128)(2,1)}, bf16[72,4096]{1,0:T(8,128)(2,1)}, bf16[72,4096]{1,0:T(8,128)(2,1)}, bf16[72,4096]{1,0:T(8,128)(2,1)}, bf16[72,4096]{1,0:T(8,128)(2,1)}, /*index=5*/f32[16,128]{1,0:T(8,128)}) custom-call(s32[6,128]{1,0:T(8,128)} %bitcast.17, s32[6,128]{1,0:T(8,128)} %bitcast.22, bf16[6,704,128]{2,1,0:T(8,128)(2,1)} %bitcast.20, ...), custom_call_target="tpu_custom_call" | custom-call | flops 1024 | bytes 1024 | tf_op jit(solution)/shard_map/pallas_call | solution.py:315
  6.3 3.1 %collective-permute-start.3 = (bf16[128,2176]{1,0:T(8,128)(2,1)}, bf16[128,2176]{1,0:T(8,128)(2,1)S(1)}, u32[]{:S(2)}, u32[]{:S(2)}) collective-permute-start(bf16[128,2176]{1,0:T(8,128)(2,1)} %get-tuple-element.63.refs_0_), channel_id=1, source_target_pairs={{0,8},{2,10},{4,12},{6,14},{8,16},{10,18},{12,20},{14,22},{16,24},... | collective-permute-start | bytes 1671176 | tf_op jit(solution)/shard_map/ppermute | solution.py:305
  9.3 1.5 %collective-permute-start = (bf16[72,4096]{1,0:T(8,128)(2,1)}, bf16[72,4096]{1,0:T(8,128)(2,1)S(1)}, u32[]{:S(2)}, u32[]{:S(2)}) collective-permute-start(bf16[72,4096]{1,0:T(8,128)(2,1)} %get-tuple-element.60), channel_id=1, source_target_pairs={{0,2},{2,0},{4,6},{6,4},{8,10},{10,8},{12,14},{14,12},{16,18},{18,... | collective-permute-start | bytes 1769480 | tf_op jit(solution)/shard_map/ppermute | solution.py:308
  10.8 1.5 %collective-permute-start.1 = (bf16[72,4096]{1,0:T(8,128)(2,1)}, bf16[72,4096]{1,0:T(8,128)(2,1)S(1)}, u32[]{:S(2)}, u32[]{:S(2)}) collective-permute-start(bf16[72,4096]{1,0:T(8,128)(2,1)} %get-tuple-element.61), channel_id=1, source_target_pairs={{0,4},{2,6},{4,0},{6,2},{8,12},{10,14},{12,8},{14,10},{16,20},{18,... | collective-permute-start | bytes 1769480 | tf_op jit(solution)/shard_map/ppermute | solution.py:308
  12.8 2.1 %collective-permute-start.4 = (bf16[128,2176]{1,0:T(8,128)(2,1)}, bf16[128,2176]{1,0:T(8,128)(2,1)S(1)}, u32[]{:S(2)}, u32[]{:S(2)}) collective-permute-start(bf16[128,2176]{1,0:T(8,128)(2,1)} %get-tuple-element.63.refs_0_), channel_id=1, source_target_pairs={{0,24},{2,26},{4,28},{6,30},{8,0},{10,2},{12,4},{14,6},{16,8},{18,... | collective-permute-start | bytes 1671176 | tf_op jit(solution)/shard_map/ppermute | solution.py:305
  14.9 10.1 %collective-permute-done.3.refs_0_ = bf16[128,2176]{1,0:T(8,128)(2,1)S(1)} collective-permute-done((bf16[128,2176]{1,0:T(8,128)(2,1)}, bf16[128,2176]{1,0:T(8,128)(2,1)S(1)}, u32[]{:S(2)}, u32[]{:S(2)}) %collective-permute-start.3) | collective-permute-done | bytes 557088 | tf_op jit(solution)/shard_map/ppermute | solution.py:305
  25.1 11.8 %collective-permute-done.4.refs_1_ = bf16[128,2176]{1,0:T(8,128)(2,1)S(1)} collective-permute-done((bf16[128,2176]{1,0:T(8,128)(2,1)}, bf16[128,2176]{1,0:T(8,128)(2,1)S(1)}, u32[]{:S(2)}, u32[]{:S(2)}) %collective-permute-start.4) | collective-permute-done | bytes 557088 | tf_op jit(solution)/shard_map/ppermute | solution.py:305
  38.2 1.4 %collective-permute-start.5 = (bf16[72,4096]{1,0:T(8,128)(2,1)S(1)}, bf16[72,4096]{1,0:T(8,128)(2,1)S(1)}, u32[]{:S(2)}, u32[]{:S(2)}) collective-permute-start(bf16[72,4096]{1,0:T(8,128)(2,1)S(1)} %get-tuple-element.71), channel_id=1, source_target_pairs={{0,2},{2,0},{4,6},{6,4},{8,10},{10,8},{12,14},{14,12},{16,18},{18,... | collective-permute-start | bytes 1769480 | tf_op jit(solution)/shard_map/ppermute | solution.py:308
  39.6 1.5 %collective-permute-start.6 = (bf16[72,4096]{1,0:T(8,128)(2,1)S(1)}, bf16[72,4096]{1,0:T(8,128)(2,1)S(1)}, u32[]{:S(2)}, u32[]{:S(2)}) collective-permute-start(bf16[72,4096]{1,0:T(8,128)(2,1)S(1)} %get-tuple-element.72), channel_id=1, source_target_pairs={{0,4},{2,6},{4,0},{6,2},{8,12},{10,14},{12,8},{14,10},{16,20},{18,... | collective-permute-start | bytes 1769480 | tf_op jit(solution)/shard_map/ppermute | solution.py:308
  41.7 1.6 %collective-permute-start.13 = (bf16[4,72,768]{2,1,0:T(8,128)(2,1)S(1)}, bf16[4,72,768]{2,1,0:T(8,128)(2,1)S(1)}, u32[]{:S(2)}, u32[]{:S(2)}) collective-permute-start(bf16[4,72,768]{2,1,0:T(8,128)(2,1)S(1)} %shard_map.84), channel_id=1, source_target_pairs={{0,8},{2,10},{4,12},{6,14},{8,16},{10,18},{12,20},{14,22},{16,24},... | collective-permute-start | bytes 1327112 | tf_op jit(solution)/shard_map/ppermute | solution.py:305
  43.3 7.2 %collective-permute-done.8.refs_4_.refs_0_ = bf16[128,2176]{1,0:T(8,128)(2,1)S(1)} collective-permute-done((bf16[128,2176]{1,0:T(8,128)(2,1)S(1)}, bf16[128,2176]{1,0:T(8,128)(2,1)S(1)}, u32[]{:S(2)}, u32[]{:S(2)}) %collective-permute-start.8) | collective-permute-done | bytes 557088 | tf_op jit(solution)/shard_map/ppermute | solution.py:305
  50.6 1.9 %collective-permute-start.9 = (bf16[4,72,768]{2,1,0:T(8,128)(2,1)S(1)}, bf16[4,72,768]{2,1,0:T(8,128)(2,1)S(1)}, u32[]{:S(2)}, u32[]{:S(2)}) collective-permute-start(bf16[4,72,768]{2,1,0:T(8,128)(2,1)S(1)} %shard_map.80), channel_id=1, source_target_pairs={{0,24},{2,26},{4,28},{6,30},{8,0},{10,2},{12,4},{14,6},{16,8},{18,... | collective-permute-start | bytes 1327112 | tf_op jit(solution)/shard_map/ppermute | solution.py:305
  53.5 6.4 %collective-permute-done.13.refs_3_.refs_5_ = bf16[4,72,768]{2,1,0:T(8,128)(2,1)S(1)} collective-permute-done((bf16[4,72,768]{2,1,0:T(8,128)(2,1)S(1)}, bf16[4,72,768]{2,1,0:T(8,128)(2,1)S(1)}, u32[]{:S(2)}, u32[]{:S(2)}) %collective-permute-start.13) | collective-permute-done | bytes 442400 | tf_op jit(solution)/shard_map/ppermute | solution.py:305
  59.9 1.5 %collective-permute-start.14 = (bf16[72,2048]{1,0:T(8,128)(2,1)S(1)}, bf16[72,2048]{1,0:T(8,128)(2,1)S(1)}, u32[]{:S(2)}, u32[]{:S(2)}) collective-permute-start(bf16[72,2048]{1,0:T(8,128)(2,1)S(1)} %get-tuple-element.81), channel_id=1, source_target_pairs={{0,2},{2,0},{4,6},{6,4},{8,10},{10,8},{12,14},{14,12},{16,18},{18,... | collective-permute-start | bytes 884744 | tf_op jit(solution)/shard_map/ppermute | solution.py:308
  61.5 1.6 %collective-permute-start.15 = (bf16[72,2048]{1,0:T(8,128)(2,1)S(1)}, bf16[72,2048]{1,0:T(8,128)(2,1)S(1)}, u32[]{:S(2)}, u32[]{:S(2)}) collective-permute-start(bf16[72,2048]{1,0:T(8,128)(2,1)S(1)} %get-tuple-element.82), channel_id=1, source_target_pairs={{0,4},{2,6},{4,0},{6,2},{8,12},{10,14},{12,8},{14,10},{16,20},{18,... | collective-permute-start | bytes 884744 | tf_op jit(solution)/shard_map/ppermute | solution.py:308
  63.1 4.3 %collective-permute-done.6.refs_4_.refs_2_ = bf16[72,4096]{1,0:T(8,128)(2,1)S(1)} collective-permute-done((bf16[72,4096]{1,0:T(8,128)(2,1)S(1)}, bf16[72,4096]{1,0:T(8,128)(2,1)S(1)}, u32[]{:S(2)}, u32[]{:S(2)}) %collective-permute-start.6) | collective-permute-done | bytes 589856 | tf_op jit(solution)/shard_map/ppermute | solution.py:308
  68.0 2.7 %collective-permute-start.17 = (bf16[4,72,768]{2,1,0:T(8,128)(2,1)S(1)}, bf16[4,72,768]{2,1,0:T(8,128)(2,1)S(1)}, u32[]{:S(2)}, u32[]{:S(2)}) collective-permute-start(bf16[4,72,768]{2,1,0:T(8,128)(2,1)S(1)} %shard_map.86), channel_id=1, source_target_pairs={{0,16},{2,18},{4,20},{6,22},{8,24},{10,26},{12,28},{14,30},{16,0},... | collective-permute-start | bytes 1327112 | tf_op jit(solution)/shard_map/ppermute | solution.py:305
  70.7 2.1 %shard_map.87 = (bf16[768,2048]{1,0:T(8,128)(2,1)S(1)}, bf16[704,768]{1,0:T(8,128)(2,1)S(1)}, f32[4,128]{1,0:T(4,128)S(1)}) custom-call(bf16[72,4096]{1,0:T(8,128)(2,1)S(1)} %get-tuple-element.84.refs_0_, bf16[72,4096]{1,0:T(8,128)(2,1)S(1)} %collective-permute-done.5.refs_3_.refs_1_, bf16[72,4096]{1,0:T(8,128)(2,1)S(1)} %collective-permute-done.6.refs_4_.refs_2_, ...), custom_call_target="tpu_custom_call" | custom-call | flops 2000000000 | bytes 1024 | tf_op jit(solution)/shard_map/pallas_call | solution.py:379
  73.5 2.1 %shard_map.88 = (bf16[768,2048]{1,0:T(8,128)(2,1)S(1)}, bf16[704,768]{1,0:T(8,128)(2,1)S(1)}, f32[4,128]{1,0:T(4,128)S(1)}) custom-call(bf16[72,4096]{1,0:T(8,128)(2,1)S(1)} %get-tuple-element.84.refs_0_, bf16[72,4096]{1,0:T(8,128)(2,1)S(1)} %collective-permute-done.5.refs_3_.refs_1_, ...), custom_call_target="tpu_custom_call", output_to_operand_aliasing={{0}: (6, {}), {1}: (7, {})} | custom-call | flops 2000000000 | bytes 1024 | tf_op jit(solution)/shard_map/pallas_call | solution.py:379
  75.6 3.4 %shard_map.89 = (bf16[704,2048]{1,0:T(8,128)(2,1)S(1)}, f32[8,128]{1,0:T(8,128)S(1)}) custom-call(bf16[768,2048]{1,0:T(8,128)(2,1)S(1)} %get-tuple-element.87.rows_ref, bf16[704,768]{1,0:T(8,128)(2,1)S(1)} %get-tuple-element.88.hidw_ref), custom_call_target="tpu_custom_call" | custom-call | flops 3500000000 | bytes 1024 | tf_op jit(solution)/shard_map/pallas_call | solution.py:411
  78.9 1.1 %collective-permute-start.11 = (bf16[72,1024]{1,0:T(8,128)(2,1)S(1)}, bf16[72,1024]{1,0:T(8,128)(2,1)S(1)}, u32[]{:S(2)}, u32[]{:S(2)}) collective-permute-start(bf16[72,1024]{1,0:T(8,128)(2,1)S(1)} %get-tuple-element.75), channel_id=1, source_target_pairs={{0,4},{2,6},{4,0},{6,2},{8,12},{10,14},{12,8},{14,10},{16,20},{18,... | collective-permute-start | bytes 442376 | tf_op jit(solution)/shard_map/ppermute | solution.py:308
  80.1 1.8 %collective-permute-start.12 = (bf16[72,1024]{1,0:T(8,128)(2,1)S(1)}, bf16[72,1024]{1,0:T(8,128)(2,1)S(1)}, u32[]{:S(2)}, u32[]{:S(2)}) collective-permute-start(bf16[72,1024]{1,0:T(8,128)(2,1)S(1)} %get-tuple-element.76), channel_id=1, source_target_pairs={{0,6},{2,4},{4,2},{6,0},{8,14},{10,12},{12,10},{14,8},{16,22},{18,... | collective-permute-start | bytes 442376 | tf_op jit(solution)/shard_map/ppermute | solution.py:308
  81.9 5.4 %collective-permute-done.17.refs_5_ = bf16[4,72,768]{2,1,0:T(8,128)(2,1)S(1)} collective-permute-done((bf16[4,72,768]{2,1,0:T(8,128)(2,1)S(1)}, bf16[4,72,768]{2,1,0:T(8,128)(2,1)S(1)}, u32[]{:S(2)}, u32[]{:S(2)}) %collective-permute-start.17) | collective-permute-done | bytes 442400 | tf_op jit(solution)/shard_map/ppermute | solution.py:305
  87.3 2.1 %shard_map.90 = (bf16[768,2048]{1,0:T(8,128)(2,1)S(1)}, bf16[704,768]{1,0:T(8,128)(2,1)S(1)}, f32[4,128]{1,0:T(4,128)S(1)}) custom-call(bf16[72,2048]{1,0:T(8,128)(2,1)S(1)} %get-tuple-element.77.refs_0_, bf16[72,2048]{1,0:T(8,128)(2,1)S(1)} %collective-permute-done.14.refs_1_, bf16[72,2048]{1,0:T(8,128)(2,1)S(1)} %collective-permute-done.15.refs_2_, ...), custom_call_target="tpu_custom_call" | custom-call | flops 2000000000 | bytes 1024 | tf_op jit(solution)/shard_map/pallas_call | solution.py:379
  90.4 1.1 %collective-permute-start.20 = (f32[4,128]{1,0:T(4,128)S(1)}, f32[4,128]{1,0:T(4,128)S(1)}, u32[]{:S(2)}, u32[]{:S(2)}) collective-permute-start(f32[4,128]{1,0:T(4,128)S(1)} %get-tuple-element.99), channel_id=1, source_target_pairs={{0,8},{2,10},{4,12},{6,14},{8,16},{10,18},{12,20},{14,22},{16,24},... | collective-permute-start | bytes 6152 | tf_op jit(solution)/shard_map/ppermute | solution.py:305
  91.5 2.1 %shard_map.91 = (bf16[768,2048]{1,0:T(8,128)(2,1)S(1)}, bf16[704,768]{1,0:T(8,128)(2,1)S(1)}, f32[4,128]{1,0:T(4,128)S(1)}) custom-call(bf16[72,4096]{1,0:T(8,128)(2,1)S(1)} %copy-done, bf16[72,4096]{1,0:T(8,128)(2,1)S(1)} %collective-permute-done.refs_3_.refs_1_, ...), custom_call_target="tpu_custom_call", output_to_operand_aliasing={{0}: (10, {}), {1}: (11, {})} | custom-call | flops 2000000000 | bytes 1024 | tf_op jit(solution)/shard_map/pallas_call | solution.py:379
  93.6 1.8 %shard_map.95 = (bf16[352,1024]{1,0:T(8,128)(2,1)S(1)}, bf16[352,1024]{1,0:T(8,128)(2,1)S(1)}) custom-call(bf16[768,2048]{1,0:T(8,128)(2,1)S(1)} %get-tuple-element.92.rows_ref, bf16[704,768]{1,0:T(8,128)(2,1)S(1)} %get-tuple-element.93.hidw_ref, bf16[704,2048]{1,0:T(8,128)(2,1)S(1)} %get-tuple-element.94.early_ref), custom_call_target="tpu_custom_call" | custom-call | flops 1024 | bytes 1024 | tf_op jit(solution)/shard_map/pallas_call | solution.py:437
  95.8 1.8 %shard_map.93 = (bf16[352,1024]{1,0:T(8,128)(2,1)S(1)}, bf16[352,1024]{1,0:T(8,128)(2,1)S(1)}) custom-call(bf16[768,2048]{1,0:T(8,128)(2,1)S(1)} %get-tuple-element.92.rows_ref, bf16[704,768]{1,0:T(8,128)(2,1)S(1)} %get-tuple-element.93.hidw_ref, bf16[704,2048]{1,0:T(8,128)(2,1)S(1)} %get-tuple-element.94.early_ref, ...), custom_call_target="tpu_custom_call" | custom-call | flops 1024 | bytes 1024 | tf_op jit(solution)/shard_map/pallas_call | solution.py:437
  98.0 2.4 %collective-permute-start.22 = (f32[4,128]{1,0:T(4,128)S(1)}, f32[4,128]{1,0:T(4,128)S(1)}, u32[]{:S(2)}, u32[]{:S(2)}) collective-permute-start(f32[4,128]{1,0:T(4,128)S(1)} %get-tuple-element.105), channel_id=1, source_target_pairs={{0,2},{2,0},{4,6},{6,4},{8,10},{10,8},{12,14},{14,12},{16,18},{18,... | collective-permute-start | bytes 6152 | tf_op jit(solution)/shard_map/ppermute | solution.py:308
  100.3 1.5 %collective-permute-start.24 = (f32[4,128]{1,0:T(4,128)S(1)}, f32[4,128]{1,0:T(4,128)S(1)}, u32[]{:S(2)}, u32[]{:S(2)}) collective-permute-start(f32[4,128]{1,0:T(4,128)S(1)} %get-tuple-element.107), channel_id=1, source_target_pairs={{0,6},{2,4},{4,2},{6,0},{8,14},{10,12},{12,10},{14,8},{16,22},{18,... | collective-permute-start | bytes 6152 | tf_op jit(solution)/shard_map/ppermute | solution.py:308
  101.9 1.7 %shard_map.96 = (f32[352,2048]{1,0:T(8,128)}, f32[16,352]{1,0:T(8,128)}) custom-call(bf16[352,1024]{1,0:T(8,128)(2,1)S(1)} %get-tuple-element.108.refs_0_, bf16[1,352,1024]{2,1,0:T(8,128)(2,1)S(1)} %bitcast.16), custom_call_target="tpu_custom_call" | custom-call | flops 1024 | bytes 1024 | tf_op jit(solution)/shard_map/pallas_call | solution.py:473
  104.8 1.8 %shard_map.97 = (f32[352,2048]{1,0:T(8,128)}, f32[16,352]{1,0:T(8,128)}, f32[6,128]{1,0:T(8,128)}) custom-call(bf16[352,1024]{1,0:T(8,128)(2,1)S(1)} %get-tuple-element.100.refs_0_, bf16[1,352,1024]{2,1,0:T(8,128)(2,1)S(1)} %bitcast.15, f32[16,128]{1,0:T(8,128)S(1)} %copy-done.4, ...), custom_call_target="tpu_custom_call", output_to_operand_aliasing={{0}: (8, {}), {1}: (9, {})} | custom-call | flops 1024 | bytes 1024 | tf_op jit(solution)/shard_map/pallas_call | solution.py:473
  (52 shorter events, 7.7 us)
Async XLA Ops:
  6.2 35.4 %copy-start = (bf16[72,4096]{1,0:T(8,128)(2,1)S(1)}, bf16[72,4096]{1,0:T(8,128)(2,1)}, u32[]{:S(2)}) copy-start(bf16[72,4096]{1,0:T(8,128)(2,1)} %get-tuple-element.59.refs_0_) | copy-start | bytes 1769476
  6.3 18.8 %collective-permute-start.3 = (bf16[128,2176]{1,0:T(8,128)(2,1)}, bf16[128,2176]{1,0:T(8,128)(2,1)S(1)}, u32[]{:S(2)}, u32[]{:S(2)}) collective-permute-start(bf16[128,2176]{1,0:T(8,128)(2,1)} %get-tuple-element.63.refs_0_), channel_id=1, source_target_pairs={{0,8},{2,10},{4,12},{6,14},{8,16},{10,18},{12,20},{14,22},{16,24},... | collective-permute-start | bytes 1671176 | tf_op jit(solution)/shard_map/ppermute | solution.py:305
  9.3 28.4 %collective-permute-start = (bf16[72,4096]{1,0:T(8,128)(2,1)}, bf16[72,4096]{1,0:T(8,128)(2,1)S(1)}, u32[]{:S(2)}, u32[]{:S(2)}) collective-permute-start(bf16[72,4096]{1,0:T(8,128)(2,1)} %get-tuple-element.60), channel_id=1, source_target_pairs={{0,2},{2,0},{4,6},{6,4},{8,10},{10,8},{12,14},{14,12},{16,18},{18,... | collective-permute-start | bytes 1769480 | tf_op jit(solution)/shard_map/ppermute | solution.py:308
  10.8 27.3 %collective-permute-start.1 = (bf16[72,4096]{1,0:T(8,128)(2,1)}, bf16[72,4096]{1,0:T(8,128)(2,1)S(1)}, u32[]{:S(2)}, u32[]{:S(2)}) collective-permute-start(bf16[72,4096]{1,0:T(8,128)(2,1)} %get-tuple-element.61), channel_id=1, source_target_pairs={{0,4},{2,6},{4,0},{6,2},{8,12},{10,14},{12,8},{14,10},{16,20},{18,... | collective-permute-start | bytes 1769480 | tf_op jit(solution)/shard_map/ppermute | solution.py:308
  12.3 25.8 %collective-permute-start.2 = (bf16[72,4096]{1,0:T(8,128)(2,1)}, bf16[72,4096]{1,0:T(8,128)(2,1)S(1)}, u32[]{:S(2)}, u32[]{:S(2)}) collective-permute-start(bf16[72,4096]{1,0:T(8,128)(2,1)} %get-tuple-element.62), channel_id=1, source_target_pairs={{0,6},{2,4},{4,2},{6,0},{8,14},{10,12},{12,10},{14,8},{16,22},{18,... | collective-permute-start | bytes 1769480 | tf_op jit(solution)/shard_map/ppermute | solution.py:308
  12.8 24.1 %collective-permute-start.4 = (bf16[128,2176]{1,0:T(8,128)(2,1)}, bf16[128,2176]{1,0:T(8,128)(2,1)S(1)}, u32[]{:S(2)}, u32[]{:S(2)}) collective-permute-start(bf16[128,2176]{1,0:T(8,128)(2,1)} %get-tuple-element.63.refs_0_), channel_id=1, source_target_pairs={{0,24},{2,26},{4,28},{6,30},{8,0},{10,2},{12,4},{14,6},{16,8},{18,... | collective-permute-start | bytes 1671176 | tf_op jit(solution)/shard_map/ppermute | solution.py:305
  25.1 25.5 %collective-permute-start.8 = (bf16[128,2176]{1,0:T(8,128)(2,1)S(1)}, bf16[128,2176]{1,0:T(8,128)(2,1)S(1)}, u32[]{:S(2)}, u32[]{:S(2)}) collective-permute-start(bf16[128,2176]{1,0:T(8,128)(2,1)S(1)} %collective-permute-done.3.refs_0_), channel_id=1, source_target_pairs={{0,8},{2,10},{4,12},{6,14},{8,16},{10,18},{12,20},{14,22},{16,24},... | collective-permute-start | bytes 1671176 | tf_op jit(solution)/shard_map/ppermute | solution.py:305
  38.2 23.3 %collective-permute-start.5 = (bf16[72,4096]{1,0:T(8,128)(2,1)S(1)}, bf16[72,4096]{1,0:T(8,128)(2,1)S(1)}, u32[]{:S(2)}, u32[]{:S(2)}) collective-permute-start(bf16[72,4096]{1,0:T(8,128)(2,1)S(1)} %get-tuple-element.71), channel_id=1, source_target_pairs={{0,2},{2,0},{4,6},{6,4},{8,10},{10,8},{12,14},{14,12},{16,18},{18,... | collective-permute-start | bytes 1769480 | tf_op jit(solution)/shard_map/ppermute | solution.py:308
  39.6 27.8 %collective-permute-start.6 = (bf16[72,4096]{1,0:T(8,128)(2,1)S(1)}, bf16[72,4096]{1,0:T(8,128)(2,1)S(1)}, u32[]{:S(2)}, u32[]{:S(2)}) collective-permute-start(bf16[72,4096]{1,0:T(8,128)(2,1)S(1)} %get-tuple-element.72), channel_id=1, source_target_pairs={{0,4},{2,6},{4,0},{6,2},{8,12},{10,14},{12,8},{14,10},{16,20},{18,... | collective-permute-start | bytes 1769480 | tf_op jit(solution)/shard_map/ppermute | solution.py:308
  41.1 26.9 %collective-permute-start.7 = (bf16[72,4096]{1,0:T(8,128)(2,1)S(1)}, bf16[72,4096]{1,0:T(8,128)(2,1)S(1)}, u32[]{:S(2)}, u32[]{:S(2)}) collective-permute-start(bf16[72,4096]{1,0:T(8,128)(2,1)S(1)} %get-tuple-element.73), channel_id=1, source_target_pairs={{0,6},{2,4},{4,2},{6,0},{8,14},{10,12},{12,10},{14,8},{16,22},{18,... | collective-permute-start | bytes 1769480 | tf_op jit(solution)/shard_map/ppermute | solution.py:308
  41.7 10.9 %copy-start.2 = (bf16[128,2176]{1,0:T(8,128)(2,1)S(1)}, bf16[128,2176]{1,0:T(8,128)(2,1)}, u32[]{:S(2)}) copy-start(bf16[128,2176]{1,0:T(8,128)(2,1)} %get-tuple-element.63.refs_0_) | copy-start | bytes 1671172
  41.7 18.2 %collective-permute-start.13 = (bf16[4,72,768]{2,1,0:T(8,128)(2,1)S(1)}, bf16[4,72,768]{2,1,0:T(8,128)(2,1)S(1)}, u32[]{:S(2)}, u32[]{:S(2)}) collective-permute-start(bf16[4,72,768]{2,1,0:T(8,128)(2,1)S(1)} %shard_map.84), channel_id=1, source_target_pairs={{0,8},{2,10},{4,12},{6,14},{8,16},{10,18},{12,20},{14,22},{16,24},... | collective-permute-start | bytes 1327112 | tf_op jit(solution)/shard_map/ppermute | solution.py:305
  50.6 22.2 %collective-permute-start.9 = (bf16[4,72,768]{2,1,0:T(8,128)(2,1)S(1)}, bf16[4,72,768]{2,1,0:T(8,128)(2,1)S(1)}, u32[]{:S(2)}, u32[]{:S(2)}) collective-permute-start(bf16[4,72,768]{2,1,0:T(8,128)(2,1)S(1)} %shard_map.80), channel_id=1, source_target_pairs={{0,24},{2,26},{4,28},{6,30},{8,0},{10,2},{12,4},{14,6},{16,8},{18,... | collective-permute-start | bytes 1327112 | tf_op jit(solution)/shard_map/ppermute | solution.py:305
  52.9 17.8 %copy-start.1 = (bf16[1,704,2048]{2,1,0:T(8,128)(2,1)S(1)}, bf16[1,704,2048]{2,1,0:T(8,128)(2,1)}, u32[]{:S(2)}) copy-start(bf16[1,704,2048]{2,1,0:T(8,128)(2,1)} %param.9) | copy-start | bytes 8650756
  59.9 19.0 %collective-permute-start.14 = (bf16[72,2048]{1,0:T(8,128)(2,1)S(1)}, bf16[72,2048]{1,0:T(8,128)(2,1)S(1)}, u32[]{:S(2)}, u32[]{:S(2)}) collective-permute-start(bf16[72,2048]{1,0:T(8,128)(2,1)S(1)} %get-tuple-element.81), channel_id=1, source_target_pairs={{0,2},{2,0},{4,6},{6,4},{8,10},{10,8},{12,14},{14,12},{16,18},{18,... | collective-permute-start | bytes 884744 | tf_op jit(solution)/shard_map/ppermute | solution.py:308
  61.5 18.6 %collective-permute-start.15 = (bf16[72,2048]{1,0:T(8,128)(2,1)S(1)}, bf16[72,2048]{1,0:T(8,128)(2,1)S(1)}, u32[]{:S(2)}, u32[]{:S(2)}) collective-permute-start(bf16[72,2048]{1,0:T(8,128)(2,1)S(1)} %get-tuple-element.82), channel_id=1, source_target_pairs={{0,4},{2,6},{4,0},{6,2},{8,12},{10,14},{12,8},{14,10},{16,20},{18,... | collective-permute-start | bytes 884744 | tf_op jit(solution)/shard_map/ppermute | solution.py:308
  67.4 14.5 %collective-permute-start.16 = (bf16[72,2048]{1,0:T(8,128)(2,1)S(1)}, bf16[72,2048]{1,0:T(8,128)(2,1)S(1)}, u32[]{:S(2)}, u32[]{:S(2)}) collective-permute-start(bf16[72,2048]{1,0:T(8,128)(2,1)S(1)} %get-tuple-element.83), channel_id=1, source_target_pairs={{0,6},{2,4},{4,2},{6,0},{8,14},{10,12},{12,10},{14,8},{16,22},{18,... | collective-permute-start | bytes 884744 | tf_op jit(solution)/shard_map/ppermute | solution.py:308
  68.0 19.2 %collective-permute-start.17 = (bf16[4,72,768]{2,1,0:T(8,128)(2,1)S(1)}, bf16[4,72,768]{2,1,0:T(8,128)(2,1)S(1)}, u32[]{:S(2)}, u32[]{:S(2)}) collective-permute-start(bf16[4,72,768]{2,1,0:T(8,128)(2,1)S(1)} %shard_map.86), channel_id=1, source_target_pairs={{0,16},{2,18},{4,20},{6,22},{8,24},{10,26},{12,28},{14,30},{16,0},... | collective-permute-start | bytes 1327112 | tf_op jit(solution)/shard_map/ppermute | solution.py:305
  72.8 17.6 %collective-permute-start.10 = (bf16[72,1024]{1,0:T(8,128)(2,1)S(1)}, bf16[72,1024]{1,0:T(8,128)(2,1)S(1)}, u32[]{:S(2)}, u32[]{:S(2)}) collective-permute-start(bf16[72,1024]{1,0:T(8,128)(2,1)S(1)} %get-tuple-element.74), channel_id=1, source_target_pairs={{0,2},{2,0},{4,6},{6,4},{8,10},{10,8},{12,14},{14,12},{16,18},{18,... | collective-permute-start | bytes 442376 | tf_op jit(solution)/shard_map/ppermute | solution.py:308
  78.9 12.6 %collective-permute-start.11 = (bf16[72,1024]{1,0:T(8,128)(2,1)S(1)}, bf16[72,1024]{1,0:T(8,128)(2,1)S(1)}, u32[]{:S(2)}, u32[]{:S(2)}) collective-permute-start(bf16[72,1024]{1,0:T(8,128)(2,1)S(1)} %get-tuple-element.75), channel_id=1, source_target_pairs={{0,4},{2,6},{4,0},{6,2},{8,12},{10,14},{12,8},{14,10},{16,20},{18,... | collective-permute-start | bytes 442376 | tf_op jit(solution)/shard_map/ppermute | solution.py:308
  80.1 11.4 %collective-permute-start.12 = (bf16[72,1024]{1,0:T(8,128)(2,1)S(1)}, bf16[72,1024]{1,0:T(8,128)(2,1)S(1)}, u32[]{:S(2)}, u32[]{:S(2)}) collective-permute-start(bf16[72,1024]{1,0:T(8,128)(2,1)S(1)} %get-tuple-element.76), channel_id=1, source_target_pairs={{0,6},{2,4},{4,2},{6,0},{8,14},{10,12},{12,10},{14,8},{16,22},{18,... | collective-permute-start | bytes 442376 | tf_op jit(solution)/shard_map/ppermute | solution.py:308
  89.4 6.4 %collective-permute-start.19 = (f32[4,128]{1,0:T(4,128)S(1)}, f32[4,128]{1,0:T(4,128)S(1)}, u32[]{:S(2)}, u32[]{:S(2)}) collective-permute-start(f32[4,128]{1,0:T(4,128)S(1)} %get-tuple-element.97.refs_2_), channel_id=1, source_target_pairs={{0,16},{2,18},{4,20},{6,22},{8,24},{10,26},{12,28},{14,30},{16,0},... | collective-permute-start | bytes 6152 | tf_op jit(solution)/shard_map/ppermute | solution.py:305
  89.4 6.1 %collective-permute-start.18 = (f32[4,128]{1,0:T(4,128)S(1)}, f32[4,128]{1,0:T(4,128)S(1)}, u32[]{:S(2)}, u32[]{:S(2)}) collective-permute-start(f32[4,128]{1,0:T(4,128)S(1)} %get-tuple-element.98), channel_id=1, source_target_pairs={{0,24},{2,26},{4,28},{6,30},{8,0},{10,2},{12,4},{14,6},{16,8},{18,... | collective-permute-start | bytes 6152 | tf_op jit(solution)/shard_map/ppermute | solution.py:305
  90.4 5.4 %collective-permute-start.20 = (f32[4,128]{1,0:T(4,128)S(1)}, f32[4,128]{1,0:T(4,128)S(1)}, u32[]{:S(2)}, u32[]{:S(2)}) collective-permute-start(f32[4,128]{1,0:T(4,128)S(1)} %get-tuple-element.99), channel_id=1, source_target_pairs={{0,8},{2,10},{4,12},{6,14},{8,16},{10,18},{12,20},{14,22},{16,24},... | collective-permute-start | bytes 6152 | tf_op jit(solution)/shard_map/ppermute | solution.py:305
  95.5 9.4 %copy-start.3 = (s32[128,6]{0,1:T(8,128)S(1)}, s32[128,6]{0,1:T(8,128)}, u32[]{:S(2)}) copy-start(s32[128,6]{0,1:T(8,128)} %param.7) | copy-start | bytes 9220
  95.5 9.4 %copy-start.4 = (f32[16,128]{1,0:T(8,128)S(1)}, f32[16,128]{1,0:T(8,128)}, u32[]{:S(2)}) copy-start(f32[16,128]{1,0:T(8,128)} %get-tuple-element.102.refs_2_) | copy-start | bytes 24580
  95.5 6.4 %collective-permute-start.25 = (bf16[352,1024]{1,0:T(8,128)(2,1)S(1)}, bf16[352,1024]{1,0:T(8,128)(2,1)S(1)}, u32[]{:S(2)}, u32[]{:S(2)}) collective-permute-start(bf16[352,1024]{1,0:T(8,128)(2,1)S(1)} %get-tuple-element.109), channel_id=1, source_target_pairs={{0,1},{1,0},{2,3},{3,2},{4,5},{5,4},{6,7},{7,6},{8,9},{9,8},{10,11... | collective-permute-start | bytes 2162696 | tf_op jit(solution)/shard_map/ppermute | solution.py:452
  97.6 7.2 %collective-permute-start.21 = (bf16[352,1024]{1,0:T(8,128)(2,1)S(1)}, bf16[352,1024]{1,0:T(8,128)(2,1)S(1)}, u32[]{:S(2)}, u32[]{:S(2)}) collective-permute-start(bf16[352,1024]{1,0:T(8,128)(2,1)S(1)} %get-tuple-element.101.refs_4_), channel_id=1, source_target_pairs={{0,1},{1,0},{2,3},{3,2},{4,5},{5,4},{6,7},{7,6},{8,9},{9,8},{10,11... | collective-permute-start | bytes 2162696 | tf_op jit(solution)/shard_map/ppermute | solution.py:452
  98.0 5.6 %collective-permute-start.22 = (f32[4,128]{1,0:T(4,128)S(1)}, f32[4,128]{1,0:T(4,128)S(1)}, u32[]{:S(2)}, u32[]{:S(2)}) collective-permute-start(f32[4,128]{1,0:T(4,128)S(1)} %get-tuple-element.105), channel_id=1, source_target_pairs={{0,2},{2,0},{4,6},{6,4},{8,10},{10,8},{12,14},{14,12},{16,18},{18,... | collective-permute-start | bytes 6152 | tf_op jit(solution)/shard_map/ppermute | solution.py:308
  100.3 3.6 %collective-permute-start.23 = (f32[4,128]{1,0:T(4,128)S(1)}, f32[4,128]{1,0:T(4,128)S(1)}, u32[]{:S(2)}, u32[]{:S(2)}) collective-permute-start(f32[4,128]{1,0:T(4,128)S(1)} %get-tuple-element.106), channel_id=1, source_target_pairs={{0,4},{2,6},{4,0},{6,2},{8,12},{10,14},{12,8},{14,10},{16,20},{18,... | collective-permute-start | bytes 6152 | tf_op jit(solution)/shard_map/ppermute | solution.py:308
  100.3 4.5 %collective-permute-start.24 = (f32[4,128]{1,0:T(4,128)S(1)}, f32[4,128]{1,0:T(4,128)S(1)}, u32[]{:S(2)}, u32[]{:S(2)}) collective-permute-start(f32[4,128]{1,0:T(4,128)S(1)} %get-tuple-element.107), channel_id=1, source_target_pairs={{0,6},{2,4},{4,2},{6,0},{8,14},{10,12},{12,10},{14,8},{16,22},{18,... | collective-permute-start | bytes 6152 | tf_op jit(solution)/shard_map/ppermute | solution.py:308

commit v6 on v5

--- a/solution.py
+++ b/solution.py
@@ -55,7 +55,8 @@
     top_k, width = hid_ref.shape[:2]
     model = cot_hbm.shape[1]
     half = width // 2
-    padded = table.shape[0] // 2
+    spare = up(width, BLOCK) - width
+    pair = 2 * width
     pairs = (
         (routes_hbm, routes_ref),
         (cot_hbm, ext.at[:, pl.ds(0, model)]),
@@ -66,6 +67,16 @@
     copies = [pltpu.make_async_copy(*pair, done.at[n]) for n, pair in enumerate(pairs)]
     for copy in copies[:4]:
         copy.start()
+
+    def leave(first, count, n):
+        for k in range(PLANE):
+            lanes = pl.ds(first, count)
+            copy = pltpu.make_async_copy(
+                sent.at[k, :, lanes], sent_hbm[k].at[:, lanes], done.at[5 + n * PLANE + k]
+            )
+            copy.start()
+            copies.append(copy)
+
     copies[0].wait()
     routes = routes_ref[...]
     ids = lax.broadcasted_iota(jnp.int32, (experts, tokens), 0)
@@ -84,9 +95,10 @@
     ext[:, model : model + BLOCK] = wide.T.astype(BF)
     copies[1].wait()
     copies[4].start()
-    parts = experts // PLANE * 2 * padded
+    parts = experts // PLANE * width
     lead = sent.shape[2] - parts
     select(slots, slot_ref, ext.at[:, pl.ds(0, lead)], [sent.at[k] for k in range(PLANE)], parts)
+    leave(parts, lead, 0)
     me = lax.axis_index("expert")
     steps = (routes >> 2) - (me >> 2)
     steps = jnp.where(steps < 0, steps + experts // PLANE, steps)
@@ -102,27 +114,36 @@
     pick = jnp.where(rows == code, 1.0, 0.0).astype(BF)
     copies[2].wait()
     copies[3].wait()
-    for n, part in enumerate(halves(flip)):
-        at = pl.multiple_of(part * half, 16) if flip else part * half
-        for k in range(top_k):
-            lanes = slice(k * tokens, (k + 1) * tokens)
-            table[n * padded : n * padded + half, lanes] = hid_ref[k, pl.ds(at, half), :]
-            weight = num_ref[k : k + 1, :].astype(F32) * (1.0 / 1024.0)
-            high = weight.astype(BF).astype(F32)
-            rows = lax.broadcasted_iota(jnp.int32, (padded - half, tokens), 0)
-            tail = jnp.where(rows == 0, high, jnp.where(rows == 1, weight - high, 0.0))
-            table[n * padded + half : (n + 1) * padded, lanes] = tail.astype(BF)
-    got = lax.dot_general(pick, table[...], NT, preferred_element_type=F32)
-    for s in range(experts // PLANE):
-        lanes = slice(s * 2 * padded, (s + 1) * 2 * padded)
+    blank = jnp.zeros((spare, top_k * tokens), BF)
+    table[0:spare, :] = blank
+    table[spare + width :, :] = blank
+    for k in range(top_k):
+        weight = num_ref[k : k + 1, :].astype(F32) * (1.0 / 1024.0)
+        for n, part in enumerate(halves(flip)):
+            at = pl.multiple_of(part * half, 16) if flip else part * half
+            rows = (hid_ref[k, pl.ds(at, half), :].astype(F32) * weight).astype(BF)
+            first = spare + n * half
+            table[first : first + half, k * tokens : (k + 1) * tokens] = rows
+    size = PLANE * slots
+    whole = width + spare
+    cut = whole - BLOCK
+    for s in range(0, experts // PLANE, 2):
+        left = lax.dot_general(
+            pick[s * size : (s + 1) * size], table[spare:], NT, preferred_element_type=F32
+        )
+        right = lax.dot_general(
+            pick[(s + 1) * size : (s + 2) * size], table[0:whole], NT, preferred_element_type=F32
+        )
+        at = s * width
         for k in range(PLANE):
-            at = (s * PLANE + k) * slots
-            sent[k, :, lanes] = got[at : at + slots, :].astype(BF)
-    copies = copies[4:]
-    for k in range(PLANE):
-        copies.append(pltpu.make_async_copy(sent.at[k], sent_hbm[k], done.at[5 + k]))
-        copies[-1].start()
-    for copy in copies:
+            these = slice(k * slots, (k + 1) * slots)
+            sent[k, :, at : at + cut] = left[these, 0:cut].astype(BF)
+            sent[k, :, at + cut : at + whole] = (
+                left[these, cut:] + right[these, 0:BLOCK]
+            ).astype(BF)
+            sent[k, :, at + whole : at + pair] = right[these, BLOCK:].astype(BF)
+        leave(at, pair, 1 + s // 2)
+    for copy in copies[4:]:
         copy.wait()
 
 
@@ -139,11 +160,25 @@
     del refs
 
 
-def regroup_kernel(s, *refs):
+def moved(piece, by):
+    return pltpu.roll(piece.astype(F32), by % piece.shape[1], 1) if by else piece.astype(F32)
+
+
+def regroup_kernel(s, width, *refs):
     out_ref = refs[-1]
-    padded = out_ref.shape[2]
-    for k in range(PLANE):
-        out_ref[k] = refs[k][:, s * padded : (s + 1) * padded]
+    whole = up(width, BLOCK)
+    spare = whole - width
+    cut = whole - BLOCK
+    at = s // 2 * 2 * width + s % 2 * (width - spare)
+    lanes = lax.broadcasted_iota(jnp.int32, (out_ref.shape[1], BLOCK), 1)
+    for k in range(0, PLANE, 2):
+        left = moved(refs[k][:, at : at + whole], -(s % 2) * spare)
+        right = moved(refs[k + 1][:, at : at + whole], (1 - s % 2) * spare)
+        out_ref[k // 2, :, 0:cut] = left[:, 0:cut].astype(BF)
+        out_ref[k // 2, :, cut:whole] = jnp.where(
+            lanes < width - cut, left[:, cut:], right[:, 0:BLOCK]
+        ).astype(BF)
+        out_ref[k // 2, :, whole:] = right[:, BLOCK:].astype(BF)
 
 
 def fill(table, at, piece, stride):
@@ -167,7 +202,8 @@
     group = PLANE * stride
     width, model = w_ref.shape
     half = width // 2
-    padded = hids.shape[1] // 2
+    whole = hids.shape[1]
+    spare = whole - width
     to = 0
     for n, (at, count) in enumerate(spans):
         for k in range(PLANE):
@@ -177,18 +213,17 @@
     copy = pltpu.make_async_copy(rows, all_rows.at[pl.ds(place * group, group)], done.at[0])
     copy.start()
     for k in range(PLANE):
-        fill(hids, k * stride, hid_ref[k], stride)
+        at = k % 2 * (width - spare)
+        fill(hids, k * stride, moved(hid_ref[k // 2, :, at : at + whole], -(k % 2) * spare), stride)
+    flipped = hids[...].T
+    hidw[...] = flipped[0:width, :].astype(BF)
     gate = 0.0
     for n, part in enumerate(halves(flip)):
         at = pl.multiple_of(part * half, 16) if flip else part * half
-        flipped = hids[:, n * padded : (n + 1) * padded].T
-        hid = flipped[0:half, :]
-        weight = flipped[half : half + 1, :] + flipped[half + 1 : half + 2, :]
-        hidw[n * half : (n + 1) * half, :] = (hid * weight).astype(BF)
         back = lax.dot_general(
             w_ref[pl.ds(at, half), :], rows[...], NT, preferred_element_type=F32
         )
-        gate += jnp.sum(back * hid, axis=0, keepdims=True)
+        gate += jnp.sum(back * flipped[n * half : (n + 1) * half, :], axis=0, keepdims=True)
     second = pltpu.make_async_copy(
         hidw, all_hidw.at[:, pl.ds(place * group, group)], done.at[1]
     )
@@ -228,7 +263,7 @@
             out_ref[s : s + 1, :] = gate_ref[k : k + 1, :]
 
 
-def pick_gates(slot_ref, routes_ref, homes, gate_ref, rows):
+def pick_gates(slot_ref, routes_ref, num_ref, homes, gate_ref, rows):
     experts, tokens = slot_ref.shape
     for k in range(PLANE):
         for s in range(experts // PLANE):
@@ -237,20 +272,21 @@
     value = jnp.take_along_axis(rows[...], slot, axis=1)
     ids = lax.broadcasted_iota(jnp.int32, (experts, tokens), 0)
     for k in range(gate_ref.shape[0]):
-        gate_ref[k : k + 1, :] = jnp.sum(
+        got = jnp.sum(
             jnp.where(routes_ref[k : k + 1, :] == ids, value, 0.0), axis=0, keepdims=True
         )
+        gate_ref[k : k + 1, :] = got / (num_ref[k : k + 1, :].astype(F32) * (1.0 / 1024.0))
 
 
 def finish_kernel(count, *refs):
     own, others_ref, refs = refs[:count], refs[count], refs[count + 1 :]
     if len(refs) > 3:
-        slot_ref, routes_ref, *homes = refs[: 2 + PLANE]
+        slot_ref, routes_ref, num_ref, *homes = refs[: 3 + PLANE]
         out_ref, scale_ref, gate_ref, table, rows = refs[-5:]
 
         @pl.when(pl.program_id(0) == 0)
         def _():
-            pick_gates(slot_ref, routes_ref, homes, gate_ref, rows)
+            pick_gates(slot_ref, routes_ref, num_ref, homes, gate_ref, rows)
 
     else:
         out_ref, scale_ref, table = refs
@@ -280,7 +316,7 @@
 
 def joined(count, spare, *refs):
     if spare:
-        refs = refs[: count + 3 + PLANE] + refs[count + 3 + PLANE + spare :]
+        refs = refs[: count + 4 + PLANE] + refs[count + 4 + PLANE + spare :]
     finish_kernel(count, *refs)
 
 
@@ -292,7 +328,6 @@
     slots = up(3 * tokens * top_k // (2 * experts), 8)
     stride = up(slots, 32)
     half = width // 2
-    padded = up(half + 2, 128)
     share = width // replicas
     group = PLANE * stride
     flip = replicas == 2
@@ -311,7 +346,7 @@
     inside = pl.BlockSpec(memory_space=pltpu.VMEM)
 
     lead = model // 2
-    wide = outer * 2 * padded + lead
+    wide = outer * width + lead
     ext, *packed, slot = call(
         functools.partial(open_kernel, slots, flip),
         [sds((tokens, model + BLOCK), BF)]
@@ -323,11 +358,11 @@
         scratch_shapes=[
             pltpu.VMEM((tokens, model + BLOCK), BF),
             pltpu.VMEM((PLANE, slots, wide), BF),
-            pltpu.VMEM((2 * padded, top_k * tokens), BF),
+            pltpu.VMEM((2 * up(width, BLOCK) - width, top_k * tokens), BF),
             pltpu.VMEM((top_k, tokens), jnp.int32),
             pltpu.VMEM((top_k, tokens), jnp.int32),
             pltpu.VMEM((top_k, width, tokens), BF),
-            pltpu.SemaphoreType.DMA((5 + PLANE,)),
+            pltpu.SemaphoreType.DMA((5 + PLANE * (1 + outer // 2),)),
         ],
     )(routes.T, numerators.T, jnp.transpose(hidden, (1, 2, 0)), cotangent)
     opening = [packed[0]] + [swap(packed[k], k) for k in range(1, PLANE)]
@@ -342,8 +377,8 @@
             order.append(outer - s)
     def regroup(s, after):
         return call(
-            functools.partial(regroup_kernel, s),
-            sds((PLANE, slots, 2 * padded), BF),
+            functools.partial(regroup_kernel, s, width),
+            sds((PLANE // 2, slots, 2 * width), BF),
             in_specs=[inside] * PLANE + [anywhere] * len(after),
         )(*opening, *after)
 
@@ -389,7 +424,7 @@
             input_output_aliases={fixed + i: i for i in range(len(rows))},
             scratch_shapes=[
                 pltpu.VMEM((group, model), BF),
-                pltpu.VMEM((group, 2 * padded), F32),
+                pltpu.VMEM((group, up(width, BLOCK)), F32),
                 pltpu.VMEM((width, group), BF),
                 pltpu.SemaphoreType.DMA((2,)),
             ],
@@ -464,7 +499,7 @@
         ]
         scratch = [pltpu.VMEM((up(share, 128), BLOCK), F32)]
         if extra:
-            specs += [pl.BlockSpec((experts, tokens), lambda j: (0, 0)), token_spec]
+            specs += [pl.BlockSpec((experts, tokens), lambda j: (0, 0)), token_spec, token_spec]
             specs += [home] * PLANE
             outs.append(sds((top_k, tokens), F32))
             out_specs.append(token_spec)
@@ -489,7 +524,7 @@
     )(*gates, right[0])
     homes = [homes[0]] + [swap(homes[k], k) for k in range(1, PLANE)]
     out = finish(0, *left, [], [])
-    out, scales, gate_grad = finish(middle_step, *right, out, [slot, routes.T, *homes])
+    out, scales, gate_grad = finish(middle_step, *right, out, [slot, routes.T, numerators.T, *homes])
     return gate_grad.T, scales.T[None], out[None]
 
 

time: 107 us -> 104 us (0.972)
  starting transfers between devices: 32 us -> 28.3 us
    ppermute x15, waiting for transfers between devices: 6.19 us -> 9.96 us  [swap(): return lax.ppermute(array, 'expert', [(e, e ^ k) for e in range(experts)])]
    ppermute x9, waiting for transfers between devices: 41.3 us -> 38 us  [ring(): return lax.ppermute(array, 'expert', pairs)]
    ppermute x9, starting transfers between devices: 13.5 us -> 10.3 us  [ring(): return lax.ppermute(array, 'expert', pairs)]
  transfers between devices with their start and end apart: 26 -> 26, of which waited for: 11 -> 11; matrix products, arithmetic and copies ran while one was open for 0% -> 0% of each run, Pallas kernels for 18% -> 19%
where the time goes in v6:
time: 104 us; the launch traced here: 103 us
  waiting for transfers between devices  48 us (46%)
  starting transfers between devices  28.3 us (27%)
  Pallas kernels  26.1 us (25%)
    ppermute x9, waiting for transfers between devices, ring(): return lax.ppermute(array, 'expert', pairs)  38 us
    ppermute x15, starting transfers between devices, swap(): return lax.ppermute(array, 'expert', [(e, e ^ k) for e in range(experts)])  17.9 us
    ppermute x9, starting transfers between devices, ring(): return lax.ppermute(array, 'expert', pairs)  10.3 us
    ppermute x15, waiting for transfers between devices, swap(): return lax.ppermute(array, 'expert', [(e, e ^ k) for e in range(experts)])  9.96 us
    pallas_call x4, Pallas kernels, stage(): call(functools.partial(stage_kernel, place, [span for _, span in parts],...  8.17 us
    pallas_call x1, Pallas kernels, per_device(): call(functools.partial(open_kernel, slots, flip), [sds((tokens, model + B...  5.15 us
    pallas_call x2, Pallas kernels, partial(): call(partial_kernel, [sds((half, model // 2), BF)] * 2, grid=(middle_step...  3.66 us
    pallas_call x2, Pallas kernels, finish(): call(functools.partial(joined, len(own), len(out)), outs, grid=(middle_st...  3.51 us
  transfers between devices with their start and end apart: 26, of which 11 were waited for; matrix products, arithmetic and copies ran while one was open for 0% of the time, Pallas kernels for 19%

profile of v6, /device:TPU:0, one launch (start us, length us, event | category | flops | bytes accessed | tf_op | source)
XLA Modules:
  0.0 103.4 jit_solution(6159875094070456314)
XLA Ops:
  0.6 5.2 %shard_map.76 = (bf16[128,2176]{1,0:T(8,128)(2,1)}, bf16[72,3840]{1,0:T(8,128)(2,1)}, bf16[72,3840]{1,0:T(8,128)(2,1)}, bf16[72,3840]{1,0:T(8,128)(2,1)}, bf16[72,3840]{1,0:T(8,128)(2,1)}, /*index=5*/f32[16,128]{1,0:T(8,128)}) custom-call(s32[6,128]{1,0:T(8,128)} %bitcast.17, s32[6,128]{1,0:T(8,128)} %bitcast.19, bf16[6,704,128]{2,1,0:T(8,128)(2,1)} %bitcast.22, ...), custom_call_target="tpu_custom_call" | custom-call | flops 1024 | bytes 1024 | tf_op jit(solution)/shard_map/pallas_call | solution.py:350
  5.8 3.1 %collective-permute-start.3 = (bf16[128,2176]{1,0:T(8,128)(2,1)}, bf16[128,2176]{1,0:T(8,128)(2,1)S(1)}, u32[]{:S(2)}, u32[]{:S(2)}) collective-permute-start(bf16[128,2176]{1,0:T(8,128)(2,1)} %get-tuple-element.63.refs_0_), channel_id=1, source_target_pairs={{0,8},{2,10},{4,12},{6,14},{8,16},{10,18},{12,20},{14,22},{16,24},... | collective-permute-start | bytes 1671176 | tf_op jit(solution)/shard_map/ppermute | solution.py:340
  8.9 2.1 %collective-permute-start.4 = (bf16[128,2176]{1,0:T(8,128)(2,1)}, bf16[128,2176]{1,0:T(8,128)(2,1)S(1)}, u32[]{:S(2)}, u32[]{:S(2)}) collective-permute-start(bf16[128,2176]{1,0:T(8,128)(2,1)} %get-tuple-element.63.refs_0_), channel_id=1, source_target_pairs={{0,24},{2,26},{4,28},{6,30},{8,0},{10,2},{12,4},{14,6},{16,8},{18,... | collective-permute-start | bytes 1671176 | tf_op jit(solution)/shard_map/ppermute | solution.py:340
  11.0 1.6 %collective-permute-start = (bf16[72,3840]{1,0:T(8,128)(2,1)}, bf16[72,3840]{1,0:T(8,128)(2,1)S(1)}, u32[]{:S(2)}, u32[]{:S(2)}) collective-permute-start(bf16[72,3840]{1,0:T(8,128)(2,1)} %get-tuple-element.60), channel_id=1, source_target_pairs={{0,2},{2,0},{4,6},{6,4},{8,10},{10,8},{12,14},{14,12},{16,18},{18,... | collective-permute-start | bytes 1658888 | tf_op jit(solution)/shard_map/ppermute | solution.py:343
  12.6 1.5 %collective-permute-start.1 = (bf16[72,3840]{1,0:T(8,128)(2,1)}, bf16[72,3840]{1,0:T(8,128)(2,1)S(1)}, u32[]{:S(2)}, u32[]{:S(2)}) collective-permute-start(bf16[72,3840]{1,0:T(8,128)(2,1)} %get-tuple-element.61), channel_id=1, source_target_pairs={{0,4},{2,6},{4,0},{6,2},{8,12},{10,14},{12,8},{14,10},{16,20},{18,... | collective-permute-start | bytes 1658888 | tf_op jit(solution)/shard_map/ppermute | solution.py:343
  14.5 10.2 %collective-permute-done.3.refs_0_ = bf16[128,2176]{1,0:T(8,128)(2,1)S(1)} collective-permute-done((bf16[128,2176]{1,0:T(8,128)(2,1)}, bf16[128,2176]{1,0:T(8,128)(2,1)S(1)}, u32[]{:S(2)}, u32[]{:S(2)}) %collective-permute-start.3) | collective-permute-done | bytes 557088 | tf_op jit(solution)/shard_map/ppermute | solution.py:340
  24.6 10.7 %collective-permute-done.4.refs_1_ = bf16[128,2176]{1,0:T(8,128)(2,1)S(1)} collective-permute-done((bf16[128,2176]{1,0:T(8,128)(2,1)}, bf16[128,2176]{1,0:T(8,128)(2,1)S(1)}, u32[]{:S(2)}, u32[]{:S(2)}) %collective-permute-start.4) | collective-permute-done | bytes 557088 | tf_op jit(solution)/shard_map/ppermute | solution.py:340
  36.2 2.0 %collective-permute-done.1.refs_4_.refs_2_ = bf16[72,3840]{1,0:T(8,128)(2,1)S(1)} collective-permute-done((bf16[72,3840]{1,0:T(8,128)(2,1)}, bf16[72,3840]{1,0:T(8,128)(2,1)S(1)}, u32[]{:S(2)}, u32[]{:S(2)}) %collective-permute-start.1) | collective-permute-done | bytes 552992 | tf_op jit(solution)/shard_map/ppermute | solution.py:343
  38.2 1.2 %collective-permute-start.5 = (bf16[72,4096]{1,0:T(8,128)(2,1)S(1)}, bf16[72,4096]{1,0:T(8,128)(2,1)S(1)}, u32[]{:S(2)}, u32[]{:S(2)}) collective-permute-start(bf16[72,4096]{1,0:T(8,128)(2,1)S(1)} %get-tuple-element.71), channel_id=1, source_target_pairs={{0,2},{2,0},{4,6},{6,4},{8,10},{10,8},{12,14},{14,12},{16,18},{18,... | collective-permute-start | bytes 1769480 | tf_op jit(solution)/shard_map/ppermute | solution.py:343
  40.3 1.4 %collective-permute-start.7 = (bf16[72,4096]{1,0:T(8,128)(2,1)S(1)}, bf16[72,4096]{1,0:T(8,128)(2,1)S(1)}, u32[]{:S(2)}, u32[]{:S(2)}) collective-permute-start(bf16[72,4096]{1,0:T(8,128)(2,1)S(1)} %get-tuple-element.73), channel_id=1, source_target_pairs={{0,6},{2,4},{4,2},{6,0},{8,14},{10,12},{12,10},{14,8},{16,22},{18,... | collective-permute-start | bytes 1769480 | tf_op jit(solution)/shard_map/ppermute | solution.py:343
  41.9 8.2 %collective-permute-done.8.refs_4_.refs_0_ = bf16[128,2176]{1,0:T(8,128)(2,1)S(1)} collective-permute-done((bf16[128,2176]{1,0:T(8,128)(2,1)S(1)}, bf16[128,2176]{1,0:T(8,128)(2,1)S(1)}, u32[]{:S(2)}, u32[]{:S(2)}) %collective-permute-start.8) | collective-permute-done | bytes 557088 | tf_op jit(solution)/shard_map/ppermute | solution.py:340
  50.3 1.9 %collective-permute-start.9 = (bf16[2,72,1408]{2,1,0:T(8,128)(2,1)S(1)}, bf16[2,72,1408]{2,1,0:T(8,128)(2,1)S(1)}, u32[]{:S(2)}, u32[]{:S(2)}) collective-permute-start(bf16[2,72,1408]{2,1,0:T(8,128)(2,1)S(1)} %shard_map.80), channel_id=1, source_target_pairs={{0,24},{2,26},{4,28},{6,30},{8,0},{10,2},{12,4},{14,6},{16,8},{18,... | collective-permute-start | bytes 1216520 | tf_op jit(solution)/shard_map/ppermute | solution.py:340
  53.3 5.4 %collective-permute-done.13.refs_3_.refs_5_ = bf16[2,72,1408]{2,1,0:T(8,128)(2,1)S(1)} collective-permute-done((bf16[2,72,1408]{2,1,0:T(8,128)(2,1)S(1)}, bf16[2,72,1408]{2,1,0:T(8,128)(2,1)S(1)}, u32[]{:S(2)}, u32[]{:S(2)}) %collective-permute-start.13) | collective-permute-done | bytes 405536 | tf_op jit(solution)/shard_map/ppermute | solution.py:340
  58.7 1.5 %collective-permute-start.14 = (bf16[72,2048]{1,0:T(8,128)(2,1)S(1)}, bf16[72,2048]{1,0:T(8,128)(2,1)S(1)}, u32[]{:S(2)}, u32[]{:S(2)}) collective-permute-start(bf16[72,2048]{1,0:T(8,128)(2,1)S(1)} %get-tuple-element.81), channel_id=1, source_target_pairs={{0,2},{2,0},{4,6},{6,4},{8,10},{10,8},{12,14},{14,12},{16,18},{18,... | collective-permute-start | bytes 884744 | tf_op jit(solution)/shard_map/ppermute | solution.py:343
  60.4 1.6 %collective-permute-start.15 = (bf16[72,2048]{1,0:T(8,128)(2,1)S(1)}, bf16[72,2048]{1,0:T(8,128)(2,1)S(1)}, u32[]{:S(2)}, u32[]{:S(2)}) collective-permute-start(bf16[72,2048]{1,0:T(8,128)(2,1)S(1)} %get-tuple-element.82), channel_id=1, source_target_pairs={{0,4},{2,6},{4,0},{6,2},{8,12},{10,14},{12,8},{14,10},{16,20},{18,... | collective-permute-start | bytes 884744 | tf_op jit(solution)/shard_map/ppermute | solution.py:343
  61.9 2.7 %collective-permute-done.6.refs_4_.refs_2_ = bf16[72,4096]{1,0:T(8,128)(2,1)S(1)} collective-permute-done((bf16[72,4096]{1,0:T(8,128)(2,1)S(1)}, bf16[72,4096]{1,0:T(8,128)(2,1)S(1)}, u32[]{:S(2)}, u32[]{:S(2)}) %collective-permute-start.6) | collective-permute-done | bytes 589856 | tf_op jit(solution)/shard_map/ppermute | solution.py:343
  64.6 3.5 %collective-permute-done.7.refs_5_.refs_3_ = bf16[72,4096]{1,0:T(8,128)(2,1)S(1)} collective-permute-done((bf16[72,4096]{1,0:T(8,128)(2,1)S(1)}, bf16[72,4096]{1,0:T(8,128)(2,1)S(1)}, u32[]{:S(2)}, u32[]{:S(2)}) %collective-permute-start.7) | collective-permute-done | bytes 589856 | tf_op jit(solution)/shard_map/ppermute | solution.py:343
  68.8 2.0 %shard_map.87 = (bf16[768,2048]{1,0:T(8,128)(2,1)S(1)}, bf16[704,768]{1,0:T(8,128)(2,1)S(1)}, f32[4,128]{1,0:T(4,128)S(1)}) custom-call(bf16[72,4096]{1,0:T(8,128)(2,1)S(1)} %get-tuple-element.84.refs_0_, bf16[72,4096]{1,0:T(8,128)(2,1)S(1)} %collective-permute-done.5.refs_3_.refs_1_, bf16[72,4096]{1,0:T(8,128)(2,1)S(1)} %collective-permute-done.6.refs_4_.refs_2_, ...), custom_call_target="tpu_custom_call" | custom-call | flops 2000000000 | bytes 1024 | tf_op jit(solution)/shard_map/pallas_call | solution.py:414
  71.8 2.0 %shard_map.88 = (bf16[768,2048]{1,0:T(8,128)(2,1)S(1)}, bf16[704,768]{1,0:T(8,128)(2,1)S(1)}, f32[4,128]{1,0:T(4,128)S(1)}) custom-call(bf16[72,4096]{1,0:T(8,128)(2,1)S(1)} %get-tuple-element.84.refs_0_, bf16[72,4096]{1,0:T(8,128)(2,1)S(1)} %collective-permute-done.5.refs_3_.refs_1_, ...), custom_call_target="tpu_custom_call", output_to_operand_aliasing={{0}: (6, {}), {1}: (7, {})} | custom-call | flops 2000000000 | bytes 1024 | tf_op jit(solution)/shard_map/pallas_call | solution.py:414
  73.9 3.4 %shard_map.89 = (bf16[704,2048]{1,0:T(8,128)(2,1)S(1)}, f32[8,128]{1,0:T(8,128)S(1)}) custom-call(bf16[768,2048]{1,0:T(8,128)(2,1)S(1)} %get-tuple-element.87.rows_ref, bf16[704,768]{1,0:T(8,128)(2,1)S(1)} %get-tuple-element.88.hidw_ref), custom_call_target="tpu_custom_call" | custom-call | flops 3500000000 | bytes 1024 | tf_op jit(solution)/shard_map/pallas_call | solution.py:446
  78.2 1.8 %collective-permute-start.12 = (bf16[72,1024]{1,0:T(8,128)(2,1)S(1)}, bf16[72,1024]{1,0:T(8,128)(2,1)S(1)}, u32[]{:S(2)}, u32[]{:S(2)}) collective-permute-start(bf16[72,1024]{1,0:T(8,128)(2,1)S(1)} %get-tuple-element.76), channel_id=1, source_target_pairs={{0,6},{2,4},{4,2},{6,0},{8,14},{10,12},{12,10},{14,8},{16,22},{18,... | collective-permute-start | bytes 442376 | tf_op jit(solution)/shard_map/ppermute | solution.py:343
  79.9 2.5 %collective-permute-done.17.refs_5_ = bf16[2,72,1408]{2,1,0:T(8,128)(2,1)S(1)} collective-permute-done((bf16[2,72,1408]{2,1,0:T(8,128)(2,1)S(1)}, bf16[2,72,1408]{2,1,0:T(8,128)(2,1)S(1)}, u32[]{:S(2)}, u32[]{:S(2)}) %collective-permute-start.17) | collective-permute-done | bytes 405536 | tf_op jit(solution)/shard_map/ppermute | solution.py:340
  82.4 2.0 %shard_map.90 = (bf16[768,2048]{1,0:T(8,128)(2,1)S(1)}, bf16[704,768]{1,0:T(8,128)(2,1)S(1)}, f32[4,128]{1,0:T(4,128)S(1)}) custom-call(bf16[72,2048]{1,0:T(8,128)(2,1)S(1)} %get-tuple-element.77.refs_0_, bf16[72,2048]{1,0:T(8,128)(2,1)S(1)} %collective-permute-done.14.refs_1_, bf16[72,2048]{1,0:T(8,128)(2,1)S(1)} %collective-permute-done.15.refs_2_, ...), custom_call_target="tpu_custom_call" | custom-call | flops 2000000000 | bytes 1024 | tf_op jit(solution)/shard_map/pallas_call | solution.py:414
  84.6 2.1 %collective-permute-start.18 = (f32[4,128]{1,0:T(4,128)S(1)}, f32[4,128]{1,0:T(4,128)S(1)}, u32[]{:S(2)}, u32[]{:S(2)}) collective-permute-start(f32[4,128]{1,0:T(4,128)S(1)} %get-tuple-element.98), channel_id=1, source_target_pairs={{0,24},{2,26},{4,28},{6,30},{8,0},{10,2},{12,4},{14,6},{16,8},{18,... | collective-permute-start | bytes 6152 | tf_op jit(solution)/shard_map/ppermute | solution.py:340
  87.0 2.0 %shard_map.91 = (bf16[768,2048]{1,0:T(8,128)(2,1)S(1)}, bf16[704,768]{1,0:T(8,128)(2,1)S(1)}, f32[4,128]{1,0:T(4,128)S(1)}) custom-call(bf16[72,3840]{1,0:T(8,128)(2,1)S(1)} %copy-done, bf16[72,3840]{1,0:T(8,128)(2,1)S(1)} %collective-permute-done.refs_3_.refs_1_, ...), custom_call_target="tpu_custom_call", output_to_operand_aliasing={{0}: (10, {}), {1}: (11, {})} | custom-call | flops 2000000000 | bytes 1024 | tf_op jit(solution)/shard_map/pallas_call | solution.py:414
  89.0 1.8 %shard_map.95 = (bf16[352,1024]{1,0:T(8,128)(2,1)S(1)}, bf16[352,1024]{1,0:T(8,128)(2,1)S(1)}) custom-call(bf16[768,2048]{1,0:T(8,128)(2,1)S(1)} %get-tuple-element.92.rows_ref, bf16[704,768]{1,0:T(8,128)(2,1)S(1)} %get-tuple-element.93.hidw_ref, bf16[704,2048]{1,0:T(8,128)(2,1)S(1)} %get-tuple-element.94.early_ref), custom_call_target="tpu_custom_call" | custom-call | flops 1024 | bytes 1024 | tf_op jit(solution)/shard_map/pallas_call | solution.py:472
  92.0 1.8 %shard_map.93 = (bf16[352,1024]{1,0:T(8,128)(2,1)S(1)}, bf16[352,1024]{1,0:T(8,128)(2,1)S(1)}) custom-call(bf16[768,2048]{1,0:T(8,128)(2,1)S(1)} %get-tuple-element.92.rows_ref, bf16[704,768]{1,0:T(8,128)(2,1)S(1)} %get-tuple-element.93.hidw_ref, bf16[704,2048]{1,0:T(8,128)(2,1)S(1)} %get-tuple-element.94.early_ref, ...), custom_call_target="tpu_custom_call" | custom-call | flops 1024 | bytes 1024 | tf_op jit(solution)/shard_map/pallas_call | solution.py:472
  93.9 2.7 %collective-permute-start.22 = (f32[4,128]{1,0:T(4,128)S(1)}, f32[4,128]{1,0:T(4,128)S(1)}, u32[]{:S(2)}, u32[]{:S(2)}) collective-permute-start(f32[4,128]{1,0:T(4,128)S(1)} %get-tuple-element.105), channel_id=1, source_target_pairs={{0,2},{2,0},{4,6},{6,4},{8,10},{10,8},{12,14},{14,12},{16,18},{18,... | collective-permute-start | bytes 6152 | tf_op jit(solution)/shard_map/ppermute | solution.py:343
  97.0 1.2 %collective-permute-start.24 = (f32[4,128]{1,0:T(4,128)S(1)}, f32[4,128]{1,0:T(4,128)S(1)}, u32[]{:S(2)}, u32[]{:S(2)}) collective-permute-start(f32[4,128]{1,0:T(4,128)S(1)} %get-tuple-element.107), channel_id=1, source_target_pairs={{0,6},{2,4},{4,2},{6,0},{8,14},{10,12},{12,10},{14,8},{16,22},{18,... | collective-permute-start | bytes 6152 | tf_op jit(solution)/shard_map/ppermute | solution.py:343
  98.2 1.7 %shard_map.96 = (f32[352,2048]{1,0:T(8,128)}, f32[16,352]{1,0:T(8,128)}) custom-call(bf16[352,1024]{1,0:T(8,128)(2,1)S(1)} %get-tuple-element.108.refs_0_, bf16[1,352,1024]{2,1,0:T(8,128)(2,1)S(1)} %bitcast.15), custom_call_target="tpu_custom_call" | custom-call | flops 1024 | bytes 1024 | tf_op jit(solution)/shard_map/pallas_call | solution.py:508
  100.2 1.3 %collective-permute-done.24.refs_8_ = f32[4,128]{1,0:T(4,128)S(1)} collective-permute-done((f32[4,128]{1,0:T(4,128)S(1)}, f32[4,128]{1,0:T(4,128)S(1)}, u32[]{:S(2)}, u32[]{:S(2)}) %collective-permute-start.24) | collective-permute-done | bytes 2080 | tf_op jit(solution)/shard_map/ppermute | solution.py:343
  101.5 1.8 %shard_map.97 = (f32[352,2048]{1,0:T(8,128)}, f32[16,352]{1,0:T(8,128)}, f32[6,128]{1,0:T(8,128)}) custom-call(bf16[352,1024]{1,0:T(8,128)(2,1)S(1)} %get-tuple-element.100.refs_0_, bf16[1,352,1024]{2,1,0:T(8,128)(2,1)S(1)} %bitcast.16, f32[16,128]{1,0:T(8,128)S(1)} %copy-done.5, ...), custom_call_target="tpu_custom_call", output_to_operand_aliasing={{0}: (9, {}), {1}: (10, {})} | custom-call | flops 1024 | bytes 1024 | tf_op jit(solution)/shard_map/pallas_call | solution.py:508
  (54 shorter events, 8.4 us)
Async XLA Ops:
  5.8 35.9 %copy-start = (bf16[72,3840]{1,0:T(8,128)(2,1)S(1)}, bf16[72,3840]{1,0:T(8,128)(2,1)}, u32[]{:S(2)}) copy-start(bf16[72,3840]{1,0:T(8,128)(2,1)} %get-tuple-element.59.refs_0_) | copy-start | bytes 1658884
  5.8 18.8 %collective-permute-start.3 = (bf16[128,2176]{1,0:T(8,128)(2,1)}, bf16[128,2176]{1,0:T(8,128)(2,1)S(1)}, u32[]{:S(2)}, u32[]{:S(2)}) collective-permute-start(bf16[128,2176]{1,0:T(8,128)(2,1)} %get-tuple-element.63.refs_0_), channel_id=1, source_target_pairs={{0,8},{2,10},{4,12},{6,14},{8,16},{10,18},{12,20},{14,22},{16,24},... | collective-permute-start | bytes 1671176 | tf_op jit(solution)/shard_map/ppermute | solution.py:340
  8.9 26.5 %collective-permute-start.4 = (bf16[128,2176]{1,0:T(8,128)(2,1)}, bf16[128,2176]{1,0:T(8,128)(2,1)S(1)}, u32[]{:S(2)}, u32[]{:S(2)}) collective-permute-start(bf16[128,2176]{1,0:T(8,128)(2,1)} %get-tuple-element.63.refs_0_), channel_id=1, source_target_pairs={{0,24},{2,26},{4,28},{6,30},{8,0},{10,2},{12,4},{14,6},{16,8},{18,... | collective-permute-start | bytes 1671176 | tf_op jit(solution)/shard_map/ppermute | solution.py:340
  11.0 25.2 %collective-permute-start = (bf16[72,3840]{1,0:T(8,128)(2,1)}, bf16[72,3840]{1,0:T(8,128)(2,1)S(1)}, u32[]{:S(2)}, u32[]{:S(2)}) collective-permute-start(bf16[72,3840]{1,0:T(8,128)(2,1)} %get-tuple-element.60), channel_id=1, source_target_pairs={{0,2},{2,0},{4,6},{6,4},{8,10},{10,8},{12,14},{14,12},{16,18},{18,... | collective-permute-start | bytes 1658888 | tf_op jit(solution)/shard_map/ppermute | solution.py:343
  12.6 25.6 %collective-permute-start.1 = (bf16[72,3840]{1,0:T(8,128)(2,1)}, bf16[72,3840]{1,0:T(8,128)(2,1)S(1)}, u32[]{:S(2)}, u32[]{:S(2)}) collective-permute-start(bf16[72,3840]{1,0:T(8,128)(2,1)} %get-tuple-element.61), channel_id=1, source_target_pairs={{0,4},{2,6},{4,0},{6,2},{8,12},{10,14},{12,8},{14,10},{16,20},{18,... | collective-permute-start | bytes 1658888 | tf_op jit(solution)/shard_map/ppermute | solution.py:343
  14.1 24.1 %collective-permute-start.2 = (bf16[72,3840]{1,0:T(8,128)(2,1)}, bf16[72,3840]{1,0:T(8,128)(2,1)S(1)}, u32[]{:S(2)}, u32[]{:S(2)}) collective-permute-start(bf16[72,3840]{1,0:T(8,128)(2,1)} %get-tuple-element.62), channel_id=1, source_target_pairs={{0,6},{2,4},{4,2},{6,0},{8,14},{10,12},{12,10},{14,8},{16,22},{18,... | collective-permute-start | bytes 1658888 | tf_op jit(solution)/shard_map/ppermute | solution.py:343
  24.6 25.5 %collective-permute-start.8 = (bf16[128,2176]{1,0:T(8,128)(2,1)S(1)}, bf16[128,2176]{1,0:T(8,128)(2,1)S(1)}, u32[]{:S(2)}, u32[]{:S(2)}) collective-permute-start(bf16[128,2176]{1,0:T(8,128)(2,1)S(1)} %collective-permute-done.3.refs_0_), channel_id=1, source_target_pairs={{0,8},{2,10},{4,12},{6,14},{8,16},{10,18},{12,20},{14,22},{16,24},... | collective-permute-start | bytes 1671176 | tf_op jit(solution)/shard_map/ppermute | solution.py:340
  38.2 22.1 %collective-permute-start.5 = (bf16[72,4096]{1,0:T(8,128)(2,1)S(1)}, bf16[72,4096]{1,0:T(8,128)(2,1)S(1)}, u32[]{:S(2)}, u32[]{:S(2)}) collective-permute-start(bf16[72,4096]{1,0:T(8,128)(2,1)S(1)} %get-tuple-element.71), channel_id=1, source_target_pairs={{0,2},{2,0},{4,6},{6,4},{8,10},{10,8},{12,14},{14,12},{16,18},{18,... | collective-permute-start | bytes 1769480 | tf_op jit(solution)/shard_map/ppermute | solution.py:343
  39.5 25.2 %collective-permute-start.6 = (bf16[72,4096]{1,0:T(8,128)(2,1)S(1)}, bf16[72,4096]{1,0:T(8,128)(2,1)S(1)}, u32[]{:S(2)}, u32[]{:S(2)}) collective-permute-start(bf16[72,4096]{1,0:T(8,128)(2,1)S(1)} %get-tuple-element.72), channel_id=1, source_target_pairs={{0,4},{2,6},{4,0},{6,2},{8,12},{10,14},{12,8},{14,10},{16,20},{18,... | collective-permute-start | bytes 1769480 | tf_op jit(solution)/shard_map/ppermute | solution.py:343
  40.3 27.9 %collective-permute-start.7 = (bf16[72,4096]{1,0:T(8,128)(2,1)S(1)}, bf16[72,4096]{1,0:T(8,128)(2,1)S(1)}, u32[]{:S(2)}, u32[]{:S(2)}) collective-permute-start(bf16[72,4096]{1,0:T(8,128)(2,1)S(1)} %get-tuple-element.73), channel_id=1, source_target_pairs={{0,6},{2,4},{4,2},{6,0},{8,14},{10,12},{12,10},{14,8},{16,22},{18,... | collective-permute-start | bytes 1769480 | tf_op jit(solution)/shard_map/ppermute | solution.py:343
  41.7 10.5 %copy-start.2 = (bf16[128,2176]{1,0:T(8,128)(2,1)S(1)}, bf16[128,2176]{1,0:T(8,128)(2,1)}, u32[]{:S(2)}) copy-start(bf16[128,2176]{1,0:T(8,128)(2,1)} %get-tuple-element.63.refs_0_) | copy-start | bytes 1671172
  41.9 16.9 %collective-permute-start.13 = (bf16[2,72,1408]{2,1,0:T(8,128)(2,1)S(1)}, bf16[2,72,1408]{2,1,0:T(8,128)(2,1)S(1)}, u32[]{:S(2)}, u32[]{:S(2)}) collective-permute-start(bf16[2,72,1408]{2,1,0:T(8,128)(2,1)S(1)} %shard_map.84), channel_id=1, source_target_pairs={{0,8},{2,10},{4,12},{6,14},{8,16},{10,18},{12,20},{14,22},{16,24},... | collective-permute-start | bytes 1216520 | tf_op jit(solution)/shard_map/ppermute | solution.py:340
  50.3 20.6 %collective-permute-start.9 = (bf16[2,72,1408]{2,1,0:T(8,128)(2,1)S(1)}, bf16[2,72,1408]{2,1,0:T(8,128)(2,1)S(1)}, u32[]{:S(2)}, u32[]{:S(2)}) collective-permute-start(bf16[2,72,1408]{2,1,0:T(8,128)(2,1)S(1)} %shard_map.80), channel_id=1, source_target_pairs={{0,24},{2,26},{4,28},{6,30},{8,0},{10,2},{12,4},{14,6},{16,8},{18,... | collective-permute-start | bytes 1216520 | tf_op jit(solution)/shard_map/ppermute | solution.py:340
  52.7 16.1 %copy-start.1 = (bf16[1,704,2048]{2,1,0:T(8,128)(2,1)S(1)}, bf16[1,704,2048]{2,1,0:T(8,128)(2,1)}, u32[]{:S(2)}) copy-start(bf16[1,704,2048]{2,1,0:T(8,128)(2,1)} %param.9) | copy-start | bytes 8650756
  58.7 18.5 %collective-permute-start.14 = (bf16[72,2048]{1,0:T(8,128)(2,1)S(1)}, bf16[72,2048]{1,0:T(8,128)(2,1)S(1)}, u32[]{:S(2)}, u32[]{:S(2)}) collective-permute-start(bf16[72,2048]{1,0:T(8,128)(2,1)S(1)} %get-tuple-element.81), channel_id=1, source_target_pairs={{0,2},{2,0},{4,6},{6,4},{8,10},{10,8},{12,14},{14,12},{16,18},{18,... | collective-permute-start | bytes 884744 | tf_op jit(solution)/shard_map/ppermute | solution.py:343
  60.4 17.8 %collective-permute-start.15 = (bf16[72,2048]{1,0:T(8,128)(2,1)S(1)}, bf16[72,2048]{1,0:T(8,128)(2,1)S(1)}, u32[]{:S(2)}, u32[]{:S(2)}) collective-permute-start(bf16[72,2048]{1,0:T(8,128)(2,1)S(1)} %get-tuple-element.82), channel_id=1, source_target_pairs={{0,4},{2,6},{4,0},{6,2},{8,12},{10,14},{12,8},{14,10},{16,20},{18,... | collective-permute-start | bytes 884744 | tf_op jit(solution)/shard_map/ppermute | solution.py:343
  64.6 15.3 %collective-permute-start.16 = (bf16[72,2048]{1,0:T(8,128)(2,1)S(1)}, bf16[72,2048]{1,0:T(8,128)(2,1)S(1)}, u32[]{:S(2)}, u32[]{:S(2)}) collective-permute-start(bf16[72,2048]{1,0:T(8,128)(2,1)S(1)} %get-tuple-element.83), channel_id=1, source_target_pairs={{0,6},{2,4},{4,2},{6,0},{8,14},{10,12},{12,10},{14,8},{16,22},{18,... | collective-permute-start | bytes 884744 | tf_op jit(solution)/shard_map/ppermute | solution.py:343
  68.2 14.2 %collective-permute-start.17 = (bf16[2,72,1408]{2,1,0:T(8,128)(2,1)S(1)}, bf16[2,72,1408]{2,1,0:T(8,128)(2,1)S(1)}, u32[]{:S(2)}, u32[]{:S(2)}) collective-permute-start(bf16[2,72,1408]{2,1,0:T(8,128)(2,1)S(1)} %shard_map.86), channel_id=1, source_target_pairs={{0,16},{2,18},{4,20},{6,22},{8,24},{10,26},{12,28},{14,30},{16,0},... | collective-permute-start | bytes 1216520 | tf_op jit(solution)/shard_map/ppermute | solution.py:340
  70.9 15.7 %collective-permute-start.10 = (bf16[72,1024]{1,0:T(8,128)(2,1)S(1)}, bf16[72,1024]{1,0:T(8,128)(2,1)S(1)}, u32[]{:S(2)}, u32[]{:S(2)}) collective-permute-start(bf16[72,1024]{1,0:T(8,128)(2,1)S(1)} %get-tuple-element.74), channel_id=1, source_target_pairs={{0,2},{2,0},{4,6},{6,4},{8,10},{10,8},{12,14},{14,12},{16,18},{18,... | collective-permute-start | bytes 442376 | tf_op jit(solution)/shard_map/ppermute | solution.py:343
  77.3 9.7 %collective-permute-start.11 = (bf16[72,1024]{1,0:T(8,128)(2,1)S(1)}, bf16[72,1024]{1,0:T(8,128)(2,1)S(1)}, u32[]{:S(2)}, u32[]{:S(2)}) collective-permute-start(bf16[72,1024]{1,0:T(8,128)(2,1)S(1)} %get-tuple-element.75), channel_id=1, source_target_pairs={{0,4},{2,6},{4,0},{6,2},{8,12},{10,14},{12,8},{14,10},{16,20},{18,... | collective-permute-start | bytes 442376 | tf_op jit(solution)/shard_map/ppermute | solution.py:343
  78.2 8.8 %collective-permute-start.12 = (bf16[72,1024]{1,0:T(8,128)(2,1)S(1)}, bf16[72,1024]{1,0:T(8,128)(2,1)S(1)}, u32[]{:S(2)}, u32[]{:S(2)}) collective-permute-start(bf16[72,1024]{1,0:T(8,128)(2,1)S(1)} %get-tuple-element.76), channel_id=1, source_target_pairs={{0,6},{2,4},{4,2},{6,0},{8,14},{10,12},{12,10},{14,8},{16,22},{18,... | collective-permute-start | bytes 442376 | tf_op jit(solution)/shard_map/ppermute | solution.py:343
  84.5 7.5 %collective-permute-start.19 = (f32[4,128]{1,0:T(4,128)S(1)}, f32[4,128]{1,0:T(4,128)S(1)}, u32[]{:S(2)}, u32[]{:S(2)}) collective-permute-start(f32[4,128]{1,0:T(4,128)S(1)} %get-tuple-element.97.refs_2_), channel_id=1, source_target_pairs={{0,16},{2,18},{4,20},{6,22},{8,24},{10,26},{12,28},{14,30},{16,0},... | collective-permute-start | bytes 6152 | tf_op jit(solution)/shard_map/ppermute | solution.py:340
  84.6 6.4 %collective-permute-start.18 = (f32[4,128]{1,0:T(4,128)S(1)}, f32[4,128]{1,0:T(4,128)S(1)}, u32[]{:S(2)}, u32[]{:S(2)}) collective-permute-start(f32[4,128]{1,0:T(4,128)S(1)} %get-tuple-element.98), channel_id=1, source_target_pairs={{0,24},{2,26},{4,28},{6,30},{8,0},{10,2},{12,4},{14,6},{16,8},{18,... | collective-permute-start | bytes 6152 | tf_op jit(solution)/shard_map/ppermute | solution.py:340
  86.6 5.4 %collective-permute-start.20 = (f32[4,128]{1,0:T(4,128)S(1)}, f32[4,128]{1,0:T(4,128)S(1)}, u32[]{:S(2)}, u32[]{:S(2)}) collective-permute-start(f32[4,128]{1,0:T(4,128)S(1)} %get-tuple-element.99), channel_id=1, source_target_pairs={{0,8},{2,10},{4,12},{6,14},{8,16},{10,18},{12,20},{14,22},{16,24},... | collective-permute-start | bytes 6152 | tf_op jit(solution)/shard_map/ppermute | solution.py:340
  90.9 10.6 %copy-start.3 = (s32[128,6]{0,1:T(8,128)S(1)}, s32[128,6]{0,1:T(8,128)}, u32[]{:S(2)}) copy-start(s32[128,6]{0,1:T(8,128)} %param.7) | copy-start | bytes 9220
  90.9 10.6 %copy-start.4 = (s32[128,6]{0,1:T(8,128)S(1)}, s32[128,6]{0,1:T(8,128)}, u32[]{:S(2)}) copy-start(s32[128,6]{0,1:T(8,128)} %param.8) | copy-start | bytes 9220
  90.9 10.6 %copy-start.5 = (f32[16,128]{1,0:T(8,128)S(1)}, f32[16,128]{1,0:T(8,128)}, u32[]{:S(2)}) copy-start(f32[16,128]{1,0:T(8,128)} %get-tuple-element.102.refs_2_) | copy-start | bytes 24580
  90.9 7.3 %collective-permute-start.25 = (bf16[352,1024]{1,0:T(8,128)(2,1)S(1)}, bf16[352,1024]{1,0:T(8,128)(2,1)S(1)}, u32[]{:S(2)}, u32[]{:S(2)}) collective-permute-start(bf16[352,1024]{1,0:T(8,128)(2,1)S(1)} %get-tuple-element.109), channel_id=1, source_target_pairs={{0,1},{1,0},{2,3},{3,2},{4,5},{5,4},{6,7},{7,6},{8,9},{9,8},{10,11... | collective-permute-start | bytes 2162696 | tf_op jit(solution)/shard_map/ppermute | solution.py:487
  93.8 7.7 %collective-permute-start.21 = (bf16[352,1024]{1,0:T(8,128)(2,1)S(1)}, bf16[352,1024]{1,0:T(8,128)(2,1)S(1)}, u32[]{:S(2)}, u32[]{:S(2)}) collective-permute-start(bf16[352,1024]{1,0:T(8,128)(2,1)S(1)} %get-tuple-element.101.refs_4_), channel_id=1, source_target_pairs={{0,1},{1,0},{2,3},{3,2},{4,5},{5,4},{6,7},{7,6},{8,9},{9,8},{10,11... | collective-permute-start | bytes 2162696 | tf_op jit(solution)/shard_map/ppermute | solution.py:487
  93.9 5.9 %collective-permute-start.22 = (f32[4,128]{1,0:T(4,128)S(1)}, f32[4,128]{1,0:T(4,128)S(1)}, u32[]{:S(2)}, u32[]{:S(2)}) collective-permute-start(f32[4,128]{1,0:T(4,128)S(1)} %get-tuple-element.105), channel_id=1, source_target_pairs={{0,2},{2,0},{4,6},{6,4},{8,10},{10,8},{12,14},{14,12},{16,18},{18,... | collective-permute-start | bytes 6152 | tf_op jit(solution)/shard_map/ppermute | solution.py:343
  96.6 3.6 %collective-permute-start.23 = (f32[4,128]{1,0:T(4,128)S(1)}, f32[4,128]{1,0:T(4,128)S(1)}, u32[]{:S(2)}, u32[]{:S(2)}) collective-permute-start(f32[4,128]{1,0:T(4,128)S(1)} %get-tuple-element.106), channel_id=1, source_target_pairs={{0,4},{2,6},{4,0},{6,2},{8,12},{10,14},{12,8},{14,10},{16,20},{18,... | collective-permute-start | bytes 6152 | tf_op jit(solution)/shard_map/ppermute | solution.py:343
  97.0 4.5 %collective-permute-start.24 = (f32[4,128]{1,0:T(4,128)S(1)}, f32[4,128]{1,0:T(4,128)S(1)}, u32[]{:S(2)}, u32[]{:S(2)}) collective-permute-start(f32[4,128]{1,0:T(4,128)S(1)} %get-tuple-element.107), channel_id=1, source_target_pairs={{0,6},{2,4},{4,2},{6,0},{8,14},{10,12},{12,10},{14,8},{16,22},{18,... | collective-permute-start | bytes 6152 | tf_op jit(solution)/shard_map/ppermute | solution.py:343

commit v7 on v6

--- a/solution.py
+++ b/solution.py
@@ -200,6 +200,7 @@
     hid_ref = refs[0]
     all_rows, all_hidw, gate_ref, rows, hids, hidw, done = refs[-7:]
     group = PLANE * stride
+    slots = arrays[0].shape[0]
     width, model = w_ref.shape
     half = width // 2
     whole = hids.shape[1]
@@ -208,7 +209,12 @@
     for n, (at, count) in enumerate(spans):
         for k in range(PLANE):
             piece = arrays[n * PLANE + k][:, at : at + count]
-            fill(rows.at[:, pl.ds(to, count)], k * stride, piece, stride)
+            lanes = slice(to, to + count)
+            clear = slots // 16 * 16
+            rows[k * stride + clear : (k + 1) * stride, lanes] = jnp.zeros(
+                (stride - clear, count), BF
+            )
+            rows[k * stride : k * stride + slots, lanes] = piece
         to += count
     copy = pltpu.make_async_copy(rows, all_rows.at[pl.ds(place * group, group)], done.at[0])
     copy.start()
@@ -217,13 +223,12 @@
         fill(hids, k * stride, moved(hid_ref[k // 2, :, at : at + whole], -(k % 2) * spare), stride)
     flipped = hids[...].T
     hidw[...] = flipped[0:width, :].astype(BF)
-    gate = 0.0
-    for n, part in enumerate(halves(flip)):
-        at = pl.multiple_of(part * half, 16) if flip else part * half
-        back = lax.dot_general(
-            w_ref[pl.ds(at, half), :], rows[...], NT, preferred_element_type=F32
-        )
-        gate += jnp.sum(back * flipped[n * half : (n + 1) * half, :], axis=0, keepdims=True)
+    back = lax.dot_general(w_ref[...], rows[...], NT, preferred_element_type=F32)
+    turned = halves(flip)[0] == 1
+    low, high = flipped[0:half, :], flipped[half:width, :]
+    terms = back[0:half, :] * jnp.where(turned, high, low)
+    terms += back[half:width, :] * jnp.where(turned, low, high)
+    gate = jnp.sum(terms, axis=0, keepdims=True)
     second = pltpu.make_async_copy(
         hidw, all_hidw.at[:, pl.ds(place * group, group)], done.at[1]
     )
@@ -240,20 +245,24 @@
     return lax.rem((me >> 2) - s + outer, outer) * PLANE + ((me & 3) ^ k)
 
 
-def early_kernel(rows_ref, hidw_ref, out_ref, mark_ref):
+def early_kernel(step, rows_ref, hidw_ref, out_ref, mark_ref):
     mark_ref[...] = jnp.zeros_like(mark_ref)
-    got = jnp.dot(hidw_ref[...], rows_ref[...], preferred_element_type=F32)
-    out_ref[...] = got.astype(BF)
-
-
-def partial_kernel(rows_ref, hidw_ref, early_ref, *refs):
+    for c in range(0, out_ref.shape[1], step):
+        span = slice(c, c + step)
+        got = jnp.dot(hidw_ref[...], rows_ref[:, span], preferred_element_type=F32)
+        out_ref[:, span] = got.astype(BF)
+
+
+def partial_kernel(first, step, rows_ref, hidw_ref, early_ref, *refs):
     send_ref, mine_ref = refs[-2:]
     half = mine_ref.shape[0]
-    got = early_ref[...].astype(F32) + jnp.dot(
-        hidw_ref[...], rows_ref[...], preferred_element_type=F32
-    )
-    send_ref[...] = got[0:half].astype(BF)
-    mine_ref[...] = got[half:].astype(BF)
+    for c in range(0, mine_ref.shape[1], step):
+        span, here = slice(first + c, first + c + step), slice(c, c + step)
+        got = early_ref[:, span].astype(F32) + jnp.dot(
+            hidw_ref[...], rows_ref[:, span], preferred_element_type=F32
+        )
+        send_ref[:, here] = got[0:half].astype(BF)
+        mine_ref[:, here] = got[half:].astype(BF)
 
 
 def combine_kernel(outer, *refs):
@@ -278,46 +287,43 @@
         gate_ref[k : k + 1, :] = got / (num_ref[k : k + 1, :].astype(F32) * (1.0 / 1024.0))
 
 
-def finish_kernel(count, *refs):
+def finish_kernel(first, step, count, extra, *refs):
     own, others_ref, refs = refs[:count], refs[count], refs[count + 1 :]
-    if len(refs) > 3:
+    if extra:
         slot_ref, routes_ref, num_ref, *homes = refs[: 3 + PLANE]
-        out_ref, scale_ref, gate_ref, table, rows = refs[-5:]
-
-        @pl.when(pl.program_id(0) == 0)
-        def _():
-            pick_gates(slot_ref, routes_ref, num_ref, homes, gate_ref, rows)
-
+        out_hbm, scale_hbm, gate_ref, out, scales, table, done, rows = refs[5 + PLANE :]
     else:
-        out_ref, scale_ref, table = refs
-    step = pl.program_id(0)
-    share, width = out_ref.shape
+        out_hbm, scale_hbm, out, scales, table, done = refs
+    share, width = out.shape
     lanes = lax.broadcasted_iota(jnp.int32, (share, BLOCK), 1)
-
-    @pl.when(step == 0)
-    def _():
-        table[...] = jnp.zeros_like(table)
-
-    kept = table[0:share, :]
-    for b in range(width // BLOCK):
-        span = slice(b * BLOCK, (b + 1) * BLOCK)
-        terms = [others_ref[n, :, span].astype(F32) for n in range(others_ref.shape[0])]
-        terms += [ref[:, span].astype(F32) for ref in own]
-        top = functools.reduce(jnp.maximum, [jnp.abs(term) for term in terms])
-        scale = jnp.max(top, axis=1, keepdims=True) + 1e-6
-        out_ref[:, span] = functools.reduce(jnp.add, terms) * (1.0 / scale)
-        kept = jnp.where(lanes == step * (width // BLOCK) + b, scale, kept)
+    copies = []
+    kept = jnp.zeros((share, BLOCK), F32)
+    for c in range(0, width, step):
+        for at in range(c, c + step, BLOCK):
+            span = slice(at, at + BLOCK)
+            terms = [others_ref[n, :, span].astype(F32) for n in range(others_ref.shape[0])]
+            terms += [ref[:, span].astype(F32) for ref in own]
+            top = functools.reduce(jnp.maximum, [jnp.abs(term) for term in terms])
+            scale = jnp.max(top, axis=1, keepdims=True) + 1e-6
+            out[:, span] = functools.reduce(jnp.add, terms) * (1.0 / scale)
+            kept = jnp.where(lanes == at // BLOCK, scale, kept)
+        copy = pltpu.make_async_copy(
+            out.at[:, pl.ds(c, step)], out_hbm.at[:, pl.ds(first + c, step)], done.at[len(copies)]
+        )
+        copy.start()
+        copies.append(copy)
+    table[...] = jnp.zeros_like(table)
     table[0:share, :] = kept
-
-    @pl.when(step == pl.num_programs(0) - 1)
-    def _():
-        scale_ref[...] = table[...].T[0 : scale_ref.shape[0], 0:share]
-
-
-def joined(count, spare, *refs):
-    if spare:
-        refs = refs[: count + 4 + PLANE] + refs[count + 4 + PLANE + spare :]
-    finish_kernel(count, *refs)
+    scales[...] = table[...].T[0 : scales.shape[0], 0:share]
+    copy = pltpu.make_async_copy(
+        scales, scale_hbm.at[pl.ds(first // BLOCK, scales.shape[0])], done.at[len(copies)]
+    )
+    copy.start()
+    copies.append(copy)
+    if extra:
+        pick_gates(slot_ref, routes_ref, num_ref, homes, gate_ref, rows)
+    for copy in copies:
+        copy.wait()
 
 
 def per_device(cotangent, hidden, routes, numerators, w_down):
@@ -332,8 +338,7 @@
     group = PLANE * stride
     flip = replicas == 2
     sds = jax.ShapeDtypeStruct
-    step = 512
-    steps = model // step
+    step, fine = 512, 256
 
     def ring(array, by):
         pairs = [(e, (e + by * PLANE) % experts) for e in range(experts)]
@@ -430,26 +435,16 @@
             ],
         )(*arrays, w_down[0], hid, *rows, *after)
 
-    def products(count):
-        return [
-            pl.BlockSpec((count * group, step), lambda j: (0, j)),
-            pl.BlockSpec((width, count * group), lambda j: (0, 0)),
-        ]
-
     sources = {s: [(middle, (n * model, model))] for n, s in enumerate(order[1:-1])}
     sources[order[-1]] = [(late, (0, model))]
     sources[0] = [(opening, (wide - lead, lead)), (final, (0, model - lead))]
     rows, gates = [], {}
     for n, s in enumerate(order[1:-1]):
         *rows, gates[s] = stage(sources[s], hids[s], n, outer - 2, [], rows)
-    full = pl.BlockSpec((width, step), lambda j: (0, j))
     early, mark = call(
-        early_kernel,
+        functools.partial(early_kernel, step),
         [sds((width, model), BF), sds((8, BLOCK), F32)],
         flops=3_500_000_000,
-        grid=(steps,),
-        in_specs=products(outer - 2),
-        out_specs=[full, pl.BlockSpec((8, BLOCK), lambda j: (0, 0))],
     )(*rows)
     *rows, gates[order[-1]] = stage(
         sources[order[-1]], hids[order[-1]], 0, 2, [mark], []
@@ -461,25 +456,11 @@
     *rows, gates[0] = stage(sources[0], hids[0], 1, 2, [], rows)
     gates = [ring(gates[s], -s) if s else gates[s] for s in range(outer)]
 
-    token_spec = pl.BlockSpec((top_k, tokens), lambda j: (0, 0))
-    home = pl.BlockSpec((outer, BLOCK), lambda j: (0, 0))
-    middle_step = steps // 2
-
-    def column(first, height):
-        return pl.BlockSpec((height, step), lambda j: (0, j + first))
-
     def partial(first, after):
         return call(
-            partial_kernel,
+            functools.partial(partial_kernel, first, step),
             [sds((half, model // 2), BF)] * 2,
-            grid=(middle_step,),
-            in_specs=[
-                column(first, 2 * group),
-                pl.BlockSpec((width, 2 * group), lambda j: (0, 0)),
-                column(first, width),
-            ]
-            + [anywhere] * len(after),
-            out_specs=[column(0, half)] * 2,
+            in_specs=[inside] * 3 + [anywhere] * len(after),
         )(*rows, early, *after)
 
     def finish(first, send, mine, out, extra):
@@ -490,41 +471,38 @@
             both = jnp.concatenate([send, mine], axis=0).reshape(replicas, share, model // 2)
             others = lax.all_to_all(both, "replica", 0, 0, tiled=True)
             own = []
-        specs = [column(0, half)] * len(own)
-        specs.append(pl.BlockSpec((others.shape[0], share, step), lambda j: (0, 0, j)))
+        fixed = len(own) + 1 + len(extra)
         outs = [sds((share, model), F32), sds((model // BLOCK, share), F32)]
-        out_specs = [
-            column(first, share),
-            pl.BlockSpec((model // 2 // BLOCK, share), lambda j: (first // middle_step, 0)),
+        out_specs = [anywhere] * 2
+        scratch = [
+            pltpu.VMEM((share, model // 2), F32),
+            pltpu.VMEM((model // 2 // BLOCK, share), F32),
+            pltpu.VMEM((up(share, BLOCK), BLOCK), F32),
+            pltpu.SemaphoreType.DMA((model // 2 // fine + 1,)),
         ]
-        scratch = [pltpu.VMEM((up(share, 128), BLOCK), F32)]
         if extra:
-            specs += [pl.BlockSpec((experts, tokens), lambda j: (0, 0)), token_spec, token_spec]
-            specs += [home] * PLANE
             outs.append(sds((top_k, tokens), F32))
-            out_specs.append(token_spec)
+            out_specs.append(inside)
             scratch.append(pltpu.VMEM((experts, BLOCK), F32))
-        fixed = len(own) + 1 + len(extra)
         return call(
-            functools.partial(joined, len(own), len(out)),
+            functools.partial(finish_kernel, first, fine, len(own), bool(extra)),
             outs,
-            grid=(middle_step,),
-            in_specs=specs + [anywhere] * len(out),
+            in_specs=[inside] * fixed + [anywhere] * len(out),
             out_specs=out_specs,
             input_output_aliases={fixed + n: n for n in range(len(out))},
             scratch_shapes=scratch,
         )(*own, others, *extra, *out)
 
     left = partial(0, [])
-    right = partial(middle_step, gates[1:])
+    right = partial(model // 2, gates[1:])
     homes = call(
         functools.partial(combine_kernel, outer),
         [sds((outer, BLOCK), F32)] * PLANE,
         in_specs=[inside] * outer + [anywhere],
-    )(*gates, right[0])
+    )(*gates, left[0])
     homes = [homes[0]] + [swap(homes[k], k) for k in range(1, PLANE)]
     out = finish(0, *left, [], [])
-    out, scales, gate_grad = finish(middle_step, *right, out, [slot, routes.T, numerators.T, *homes])
+    out, scales, gate_grad = finish(model // 2, *right, out, [slot, routes.T, numerators.T, *homes])
     return gate_grad.T, scales.T[None], out[None]
 
 

time: 104 us -> 103 us (level)
  waiting for transfers between devices: 48 us -> 51 us
  Pallas kernels: 26.1 us -> 24 us
  starting transfers between devices: 28.3 us -> 26.7 us
    ppermute x15, waiting for transfers between devices: 9.96 us -> 12.9 us  [swap(): return lax.ppermute(array, 'expert', [(e, e ^ k) for e in range(experts)])]
    pallas_call x5, Pallas kernels: 10.5 us -> 8.29 us  [the longest x2 3.29 us: finish(): call(functools.partial(finish_kernel, first, fine, len(own), bool(extra))...]
    ppermute x15, starting transfers between devices: 17.9 us -> 16.3 us  [swap(): return lax.ppermute(array, 'expert', [(e, e ^ k) for e in range(experts)])]
  transfers between devices with their start and end apart: 26 -> 26, of which waited for: 11 -> 12; matrix products, arithmetic and copies ran while one was open for 0% -> 0% of each run, Pallas kernels for 19% -> 16%
where the time goes in v7:
time: 103 us
  waiting for transfers between devices  51 us (50%)
  starting transfers between devices  26.7 us (26%)
  Pallas kernels  24 us (23%)
  between operations  1.09 us (1%)
    ppermute x9, waiting for transfers between devices, ring(): return lax.ppermute(array, 'expert', pairs)  38.1 us
    ppermute x15, starting transfers between devices, swap(): return lax.ppermute(array, 'expert', [(e, e ^ k) for e in range(experts)])  16.3 us
    ppermute x15, waiting for transfers between devices, swap(): return lax.ppermute(array, 'expert', [(e, e ^ k) for e in range(experts)])  12.9 us
    ppermute x9, starting transfers between devices, ring(): return lax.ppermute(array, 'expert', pairs)  10.3 us
    pallas_call x4, Pallas kernels, stage(): call(functools.partial(stage_kernel, place, [span for _, span in parts],...  8.22 us
    pallas_call x1, Pallas kernels, per_device(): call(functools.partial(open_kernel, slots, flip), [sds((tokens, model + B...  5.15 us
    pallas_call x2, Pallas kernels, finish(): call(functools.partial(finish_kernel, first, fine, len(own), bool(extra))...  3.29 us
    pallas_call x2, Pallas kernels, partial(): call(functools.partial(partial_kernel, first, step), [sds((half, model //...  2.6 us
  transfers between devices with their start and end apart: 26, of which 12 were waited for; matrix products, arithmetic and copies ran while one was open for 0% of the time, Pallas kernels for 16%

profile of v7, /device:TPU:0, one launch (start us, length us, event | category | flops | bytes accessed | tf_op | source)
XLA Modules:
  0.0 102.7 jit_solution(10227171924989844026)
XLA Ops:
  0.6 5.2 %shard_map.76 = (bf16[128,2176]{1,0:T(8,128)(2,1)}, bf16[72,3840]{1,0:T(8,128)(2,1)}, bf16[72,3840]{1,0:T(8,128)(2,1)}, bf16[72,3840]{1,0:T(8,128)(2,1)}, bf16[72,3840]{1,0:T(8,128)(2,1)}, /*index=5*/f32[16,128]{1,0:T(8,128)}) custom-call(s32[6,128]{1,0:T(8,128)} %bitcast.17, s32[6,128]{1,0:T(8,128)} %bitcast.19, bf16[6,704,128]{2,1,0:T(8,128)(2,1)} %bitcast.22, ...), custom_call_target="tpu_custom_call" | custom-call | flops 1024 | bytes 1024 | tf_op jit(solution)/shard_map/pallas_call | solution.py:355
  5.8 3.1 %collective-permute-start.3 = (bf16[128,2176]{1,0:T(8,128)(2,1)}, bf16[128,2176]{1,0:T(8,128)(2,1)S(1)}, u32[]{:S(2)}, u32[]{:S(2)}) collective-permute-start(bf16[128,2176]{1,0:T(8,128)(2,1)} %get-tuple-element.63.refs_0_), channel_id=1, source_target_pairs={{0,8},{2,10},{4,12},{6,14},{8,16},{10,18},{12,20},{14,22},{16,24},... | collective-permute-start | bytes 1671176 | tf_op jit(solution)/shard_map/ppermute | solution.py:345
  8.9 2.1 %collective-permute-start.4 = (bf16[128,2176]{1,0:T(8,128)(2,1)}, bf16[128,2176]{1,0:T(8,128)(2,1)S(1)}, u32[]{:S(2)}, u32[]{:S(2)}) collective-permute-start(bf16[128,2176]{1,0:T(8,128)(2,1)} %get-tuple-element.63.refs_0_), channel_id=1, source_target_pairs={{0,24},{2,26},{4,28},{6,30},{8,0},{10,2},{12,4},{14,6},{16,8},{18,... | collective-permute-start | bytes 1671176 | tf_op jit(solution)/shard_map/ppermute | solution.py:345
  11.0 1.6 %collective-permute-start = (bf16[72,3840]{1,0:T(8,128)(2,1)}, bf16[72,3840]{1,0:T(8,128)(2,1)S(1)}, u32[]{:S(2)}, u32[]{:S(2)}) collective-permute-start(bf16[72,3840]{1,0:T(8,128)(2,1)} %get-tuple-element.60), channel_id=1, source_target_pairs={{0,2},{2,0},{4,6},{6,4},{8,10},{10,8},{12,14},{14,12},{16,18},{18,... | collective-permute-start | bytes 1658888 | tf_op jit(solution)/shard_map/ppermute | solution.py:348
  12.6 1.5 %collective-permute-start.1 = (bf16[72,3840]{1,0:T(8,128)(2,1)}, bf16[72,3840]{1,0:T(8,128)(2,1)S(1)}, u32[]{:S(2)}, u32[]{:S(2)}) collective-permute-start(bf16[72,3840]{1,0:T(8,128)(2,1)} %get-tuple-element.61), channel_id=1, source_target_pairs={{0,4},{2,6},{4,0},{6,2},{8,12},{10,14},{12,8},{14,10},{16,20},{18,... | collective-permute-start | bytes 1658888 | tf_op jit(solution)/shard_map/ppermute | solution.py:348
  14.5 10.2 %collective-permute-done.3.refs_0_ = bf16[128,2176]{1,0:T(8,128)(2,1)S(1)} collective-permute-done((bf16[128,2176]{1,0:T(8,128)(2,1)}, bf16[128,2176]{1,0:T(8,128)(2,1)S(1)}, u32[]{:S(2)}, u32[]{:S(2)}) %collective-permute-start.3) | collective-permute-done | bytes 557088 | tf_op jit(solution)/shard_map/ppermute | solution.py:345
  24.6 10.7 %collective-permute-done.4.refs_1_ = bf16[128,2176]{1,0:T(8,128)(2,1)S(1)} collective-permute-done((bf16[128,2176]{1,0:T(8,128)(2,1)}, bf16[128,2176]{1,0:T(8,128)(2,1)S(1)}, u32[]{:S(2)}, u32[]{:S(2)}) %collective-permute-start.4) | collective-permute-done | bytes 557088 | tf_op jit(solution)/shard_map/ppermute | solution.py:345
  36.2 2.0 %collective-permute-done.1.refs_4_.refs_2_ = bf16[72,3840]{1,0:T(8,128)(2,1)S(1)} collective-permute-done((bf16[72,3840]{1,0:T(8,128)(2,1)}, bf16[72,3840]{1,0:T(8,128)(2,1)S(1)}, u32[]{:S(2)}, u32[]{:S(2)}) %collective-permute-start.1) | collective-permute-done | bytes 552992 | tf_op jit(solution)/shard_map/ppermute | solution.py:348
  38.2 1.2 %collective-permute-start.5 = (bf16[72,4096]{1,0:T(8,128)(2,1)S(1)}, bf16[72,4096]{1,0:T(8,128)(2,1)S(1)}, u32[]{:S(2)}, u32[]{:S(2)}) collective-permute-start(bf16[72,4096]{1,0:T(8,128)(2,1)S(1)} %get-tuple-element.71), channel_id=1, source_target_pairs={{0,2},{2,0},{4,6},{6,4},{8,10},{10,8},{12,14},{14,12},{16,18},{18,... | collective-permute-start | bytes 1769480 | tf_op jit(solution)/shard_map/ppermute | solution.py:348
  40.3 1.4 %collective-permute-start.7 = (bf16[72,4096]{1,0:T(8,128)(2,1)S(1)}, bf16[72,4096]{1,0:T(8,128)(2,1)S(1)}, u32[]{:S(2)}, u32[]{:S(2)}) collective-permute-start(bf16[72,4096]{1,0:T(8,128)(2,1)S(1)} %get-tuple-element.73), channel_id=1, source_target_pairs={{0,6},{2,4},{4,2},{6,0},{8,14},{10,12},{12,10},{14,8},{16,22},{18,... | collective-permute-start | bytes 1769480 | tf_op jit(solution)/shard_map/ppermute | solution.py:348
  41.9 8.2 %collective-permute-done.8.refs_4_.refs_0_ = bf16[128,2176]{1,0:T(8,128)(2,1)S(1)} collective-permute-done((bf16[128,2176]{1,0:T(8,128)(2,1)S(1)}, bf16[128,2176]{1,0:T(8,128)(2,1)S(1)}, u32[]{:S(2)}, u32[]{:S(2)}) %collective-permute-start.8) | collective-permute-done | bytes 557088 | tf_op jit(solution)/shard_map/ppermute | solution.py:345
  50.3 1.9 %collective-permute-start.9 = (bf16[2,72,1408]{2,1,0:T(8,128)(2,1)S(1)}, bf16[2,72,1408]{2,1,0:T(8,128)(2,1)S(1)}, u32[]{:S(2)}, u32[]{:S(2)}) collective-permute-start(bf16[2,72,1408]{2,1,0:T(8,128)(2,1)S(1)} %shard_map.80), channel_id=1, source_target_pairs={{0,24},{2,26},{4,28},{6,30},{8,0},{10,2},{12,4},{14,6},{16,8},{18,... | collective-permute-start | bytes 1216520 | tf_op jit(solution)/shard_map/ppermute | solution.py:345
  53.3 5.4 %collective-permute-done.13.refs_3_.refs_5_ = bf16[2,72,1408]{2,1,0:T(8,128)(2,1)S(1)} collective-permute-done((bf16[2,72,1408]{2,1,0:T(8,128)(2,1)S(1)}, bf16[2,72,1408]{2,1,0:T(8,128)(2,1)S(1)}, u32[]{:S(2)}, u32[]{:S(2)}) %collective-permute-start.13) | collective-permute-done | bytes 405536 | tf_op jit(solution)/shard_map/ppermute | solution.py:345
  58.7 1.5 %collective-permute-start.14 = (bf16[72,2048]{1,0:T(8,128)(2,1)S(1)}, bf16[72,2048]{1,0:T(8,128)(2,1)S(1)}, u32[]{:S(2)}, u32[]{:S(2)}) collective-permute-start(bf16[72,2048]{1,0:T(8,128)(2,1)S(1)} %get-tuple-element.81), channel_id=1, source_target_pairs={{0,2},{2,0},{4,6},{6,4},{8,10},{10,8},{12,14},{14,12},{16,18},{18,... | collective-permute-start | bytes 884744 | tf_op jit(solution)/shard_map/ppermute | solution.py:348
  60.4 1.6 %collective-permute-start.15 = (bf16[72,2048]{1,0:T(8,128)(2,1)S(1)}, bf16[72,2048]{1,0:T(8,128)(2,1)S(1)}, u32[]{:S(2)}, u32[]{:S(2)}) collective-permute-start(bf16[72,2048]{1,0:T(8,128)(2,1)S(1)} %get-tuple-element.82), channel_id=1, source_target_pairs={{0,4},{2,6},{4,0},{6,2},{8,12},{10,14},{12,8},{14,10},{16,20},{18,... | collective-permute-start | bytes 884744 | tf_op jit(solution)/shard_map/ppermute | solution.py:348
  61.9 2.7 %collective-permute-done.6.refs_4_.refs_2_ = bf16[72,4096]{1,0:T(8,128)(2,1)S(1)} collective-permute-done((bf16[72,4096]{1,0:T(8,128)(2,1)S(1)}, bf16[72,4096]{1,0:T(8,128)(2,1)S(1)}, u32[]{:S(2)}, u32[]{:S(2)}) %collective-permute-start.6) | collective-permute-done | bytes 589856 | tf_op jit(solution)/shard_map/ppermute | solution.py:348
  64.6 3.5 %collective-permute-done.7.refs_5_.refs_3_ = bf16[72,4096]{1,0:T(8,128)(2,1)S(1)} collective-permute-done((bf16[72,4096]{1,0:T(8,128)(2,1)S(1)}, bf16[72,4096]{1,0:T(8,128)(2,1)S(1)}, u32[]{:S(2)}, u32[]{:S(2)}) %collective-permute-start.7) | collective-permute-done | bytes 589856 | tf_op jit(solution)/shard_map/ppermute | solution.py:348
  68.8 2.1 %shard_map.87 = (bf16[768,2048]{1,0:T(8,128)(2,1)S(1)}, bf16[704,768]{1,0:T(8,128)(2,1)S(1)}, f32[4,128]{1,0:T(4,128)S(1)}) custom-call(bf16[72,4096]{1,0:T(8,128)(2,1)S(1)} %get-tuple-element.84.refs_0_, bf16[72,4096]{1,0:T(8,128)(2,1)S(1)} %collective-permute-done.5.refs_3_.refs_1_, bf16[72,4096]{1,0:T(8,128)(2,1)S(1)} %collective-permute-done.6.refs_4_.refs_2_, ...), custom_call_target="tpu_custom_call" | custom-call | flops 2000000000 | bytes 1024 | tf_op jit(solution)/shard_map/pallas_call | solution.py:419
  71.9 2.1 %shard_map.88 = (bf16[768,2048]{1,0:T(8,128)(2,1)S(1)}, bf16[704,768]{1,0:T(8,128)(2,1)S(1)}, f32[4,128]{1,0:T(4,128)S(1)}) custom-call(bf16[72,4096]{1,0:T(8,128)(2,1)S(1)} %get-tuple-element.84.refs_0_, bf16[72,4096]{1,0:T(8,128)(2,1)S(1)} %collective-permute-done.5.refs_3_.refs_1_, ...), custom_call_target="tpu_custom_call", output_to_operand_aliasing={{0}: (6, {}), {1}: (7, {})} | custom-call | flops 2000000000 | bytes 1024 | tf_op jit(solution)/shard_map/pallas_call | solution.py:419
  73.9 2.4 %shard_map.89 = (bf16[704,2048]{1,0:T(8,128)(2,1)S(1)}, f32[8,128]{1,0:T(8,128)S(1)}) custom-call(bf16[768,2048]{1,0:T(8,128)(2,1)S(1)} %get-tuple-element.87.rows_ref, bf16[704,768]{1,0:T(8,128)(2,1)S(1)} %get-tuple-element.88.hidw_ref), custom_call_target="tpu_custom_call" | custom-call | flops 3500000000 | bytes 1024 | tf_op jit(solution)/shard_map/pallas_call | solution.py:444
  77.2 3.0 %collective-permute-done.15.refs_2_ = bf16[72,2048]{1,0:T(8,128)(2,1)S(1)} collective-permute-done((bf16[72,2048]{1,0:T(8,128)(2,1)S(1)}, bf16[72,2048]{1,0:T(8,128)(2,1)S(1)}, u32[]{:S(2)}, u32[]{:S(2)}) %collective-permute-start.15) | collective-permute-done | bytes 294944 | tf_op jit(solution)/shard_map/ppermute | solution.py:348
  80.3 2.1 %collective-permute-done.17.refs_5_ = bf16[2,72,1408]{2,1,0:T(8,128)(2,1)S(1)} collective-permute-done((bf16[2,72,1408]{2,1,0:T(8,128)(2,1)S(1)}, bf16[2,72,1408]{2,1,0:T(8,128)(2,1)S(1)}, u32[]{:S(2)}, u32[]{:S(2)}) %collective-permute-start.17) | collective-permute-done | bytes 405536 | tf_op jit(solution)/shard_map/ppermute | solution.py:345
  82.4 2.1 %shard_map.90 = (bf16[768,2048]{1,0:T(8,128)(2,1)S(1)}, bf16[704,768]{1,0:T(8,128)(2,1)S(1)}, f32[4,128]{1,0:T(4,128)S(1)}) custom-call(bf16[72,2048]{1,0:T(8,128)(2,1)S(1)} %get-tuple-element.77.refs_0_, bf16[72,2048]{1,0:T(8,128)(2,1)S(1)} %collective-permute-done.14.refs_1_, bf16[72,2048]{1,0:T(8,128)(2,1)S(1)} %collective-permute-done.15.refs_2_, ...), custom_call_target="tpu_custom_call" | custom-call | flops 2000000000 | bytes 1024 | tf_op jit(solution)/shard_map/pallas_call | solution.py:419
  84.6 1.9 %collective-permute-start.18 = (f32[4,128]{1,0:T(4,128)S(1)}, f32[4,128]{1,0:T(4,128)S(1)}, u32[]{:S(2)}, u32[]{:S(2)}) collective-permute-start(f32[4,128]{1,0:T(4,128)S(1)} %get-tuple-element.98), channel_id=1, source_target_pairs={{0,24},{2,26},{4,28},{6,30},{8,0},{10,2},{12,4},{14,6},{16,8},{18,... | collective-permute-start | bytes 6152 | tf_op jit(solution)/shard_map/ppermute | solution.py:345
  87.0 2.1 %shard_map.91 = (bf16[768,2048]{1,0:T(8,128)(2,1)S(1)}, bf16[704,768]{1,0:T(8,128)(2,1)S(1)}, f32[4,128]{1,0:T(4,128)S(1)}) custom-call(bf16[72,3840]{1,0:T(8,128)(2,1)S(1)} %copy-done, bf16[72,3840]{1,0:T(8,128)(2,1)S(1)} %collective-permute-done.refs_3_.refs_1_, ...), custom_call_target="tpu_custom_call", output_to_operand_aliasing={{0}: (10, {}), {1}: (11, {})} | custom-call | flops 2000000000 | bytes 1024 | tf_op jit(solution)/shard_map/pallas_call | solution.py:419
  89.1 1.3 %shard_map.94 = (bf16[352,1024]{1,0:T(8,128)(2,1)S(1)}, bf16[352,1024]{1,0:T(8,128)(2,1)S(1)}) custom-call(bf16[768,2048]{1,0:T(8,128)(2,1)S(1)} %get-tuple-element.92.rows_ref, bf16[704,768]{1,0:T(8,128)(2,1)S(1)} %get-tuple-element.93.hidw_ref, bf16[704,2048]{1,0:T(8,128)(2,1)S(1)} %get-tuple-element.94.early_ref), custom_call_target="tpu_custom_call" | custom-call | flops 1024 | bytes 1024 | tf_op jit(solution)/shard_map/pallas_call | solution.py:460
  90.5 1.4 %collective-permute-done.20.refs_2_.refs_3_ = f32[4,128]{1,0:T(4,128)S(1)} collective-permute-done((f32[4,128]{1,0:T(4,128)S(1)}, f32[4,128]{1,0:T(4,128)S(1)}, u32[]{:S(2)}, u32[]{:S(2)}) %collective-permute-start.20) | collective-permute-done | bytes 2080 | tf_op jit(solution)/shard_map/ppermute | solution.py:345
  91.9 1.3 %shard_map.93 = (bf16[352,1024]{1,0:T(8,128)(2,1)S(1)}, bf16[352,1024]{1,0:T(8,128)(2,1)S(1)}) custom-call(bf16[768,2048]{1,0:T(8,128)(2,1)S(1)} %get-tuple-element.92.rows_ref, bf16[704,768]{1,0:T(8,128)(2,1)S(1)} %get-tuple-element.93.hidw_ref, bf16[704,2048]{1,0:T(8,128)(2,1)S(1)} %get-tuple-element.94.early_ref, ...), custom_call_target="tpu_custom_call" | custom-call | flops 1024 | bytes 1024 | tf_op jit(solution)/shard_map/pallas_call | solution.py:460
  93.3 2.8 %collective-permute-start.22 = (f32[4,128]{1,0:T(4,128)S(1)}, f32[4,128]{1,0:T(4,128)S(1)}, u32[]{:S(2)}, u32[]{:S(2)}) collective-permute-start(f32[4,128]{1,0:T(4,128)S(1)} %get-tuple-element.106), channel_id=1, source_target_pairs={{0,2},{2,0},{4,6},{6,4},{8,10},{10,8},{12,14},{14,12},{16,18},{18,... | collective-permute-start | bytes 6152 | tf_op jit(solution)/shard_map/ppermute | solution.py:348
  96.1 1.5 %collective-permute-start.24 = (f32[4,128]{1,0:T(4,128)S(1)}, f32[4,128]{1,0:T(4,128)S(1)}, u32[]{:S(2)}, u32[]{:S(2)}) collective-permute-start(f32[4,128]{1,0:T(4,128)S(1)} %get-tuple-element.108), channel_id=1, source_target_pairs={{0,6},{2,4},{4,2},{6,0},{8,14},{10,12},{12,10},{14,8},{16,22},{18,... | collective-permute-start | bytes 6152 | tf_op jit(solution)/shard_map/ppermute | solution.py:348
  97.7 1.3 %shard_map.96 = (f32[352,2048]{1,0:T(8,128)}, f32[16,352]{1,0:T(8,128)}) custom-call(bf16[352,1024]{1,0:T(8,128)(2,1)S(1)} %get-tuple-element.109.refs_0_, bf16[1,352,1024]{2,1,0:T(8,128)(2,1)S(1)} %bitcast.15), custom_call_target="tpu_custom_call" | custom-call | flops 1024 | bytes 1024 | tf_op jit(solution)/shard_map/pallas_call | solution.py:487
  100.6 1.9 %shard_map.97 = (f32[352,2048]{1,0:T(8,128)}, f32[16,352]{1,0:T(8,128)}, f32[6,128]{1,0:T(8,128)}) custom-call(bf16[352,1024]{1,0:T(8,128)(2,1)S(1)} %get-tuple-element.100.refs_0_, bf16[1,352,1024]{2,1,0:T(8,128)(2,1)S(1)} %bitcast.16, f32[16,128]{1,0:T(8,128)S(1)} %copy-done.5, ...), custom_call_target="tpu_custom_call", output_to_operand_aliasing={{0}: (9, {}), {1}: (10, {})} | custom-call | flops 1024 | bytes 1024 | tf_op jit(solution)/shard_map/pallas_call | solution.py:487
  (54 shorter events, 8.4 us)
Async XLA Ops:
  5.8 35.9 %copy-start = (bf16[72,3840]{1,0:T(8,128)(2,1)S(1)}, bf16[72,3840]{1,0:T(8,128)(2,1)}, u32[]{:S(2)}) copy-start(bf16[72,3840]{1,0:T(8,128)(2,1)} %get-tuple-element.59.refs_0_) | copy-start | bytes 1658884
  5.8 18.8 %collective-permute-start.3 = (bf16[128,2176]{1,0:T(8,128)(2,1)}, bf16[128,2176]{1,0:T(8,128)(2,1)S(1)}, u32[]{:S(2)}, u32[]{:S(2)}) collective-permute-start(bf16[128,2176]{1,0:T(8,128)(2,1)} %get-tuple-element.63.refs_0_), channel_id=1, source_target_pairs={{0,8},{2,10},{4,12},{6,14},{8,16},{10,18},{12,20},{14,22},{16,24},... | collective-permute-start | bytes 1671176 | tf_op jit(solution)/shard_map/ppermute | solution.py:345
  8.9 26.5 %collective-permute-start.4 = (bf16[128,2176]{1,0:T(8,128)(2,1)}, bf16[128,2176]{1,0:T(8,128)(2,1)S(1)}, u32[]{:S(2)}, u32[]{:S(2)}) collective-permute-start(bf16[128,2176]{1,0:T(8,128)(2,1)} %get-tuple-element.63.refs_0_), channel_id=1, source_target_pairs={{0,24},{2,26},{4,28},{6,30},{8,0},{10,2},{12,4},{14,6},{16,8},{18,... | collective-permute-start | bytes 1671176 | tf_op jit(solution)/shard_map/ppermute | solution.py:345
  11.0 25.2 %collective-permute-start = (bf16[72,3840]{1,0:T(8,128)(2,1)}, bf16[72,3840]{1,0:T(8,128)(2,1)S(1)}, u32[]{:S(2)}, u32[]{:S(2)}) collective-permute-start(bf16[72,3840]{1,0:T(8,128)(2,1)} %get-tuple-element.60), channel_id=1, source_target_pairs={{0,2},{2,0},{4,6},{6,4},{8,10},{10,8},{12,14},{14,12},{16,18},{18,... | collective-permute-start | bytes 1658888 | tf_op jit(solution)/shard_map/ppermute | solution.py:348
  12.6 25.6 %collective-permute-start.1 = (bf16[72,3840]{1,0:T(8,128)(2,1)}, bf16[72,3840]{1,0:T(8,128)(2,1)S(1)}, u32[]{:S(2)}, u32[]{:S(2)}) collective-permute-start(bf16[72,3840]{1,0:T(8,128)(2,1)} %get-tuple-element.61), channel_id=1, source_target_pairs={{0,4},{2,6},{4,0},{6,2},{8,12},{10,14},{12,8},{14,10},{16,20},{18,... | collective-permute-start | bytes 1658888 | tf_op jit(solution)/shard_map/ppermute | solution.py:348
  14.1 24.1 %collective-permute-start.2 = (bf16[72,3840]{1,0:T(8,128)(2,1)}, bf16[72,3840]{1,0:T(8,128)(2,1)S(1)}, u32[]{:S(2)}, u32[]{:S(2)}) collective-permute-start(bf16[72,3840]{1,0:T(8,128)(2,1)} %get-tuple-element.62), channel_id=1, source_target_pairs={{0,6},{2,4},{4,2},{6,0},{8,14},{10,12},{12,10},{14,8},{16,22},{18,... | collective-permute-start | bytes 1658888 | tf_op jit(solution)/shard_map/ppermute | solution.py:348
  24.6 25.5 %collective-permute-start.8 = (bf16[128,2176]{1,0:T(8,128)(2,1)S(1)}, bf16[128,2176]{1,0:T(8,128)(2,1)S(1)}, u32[]{:S(2)}, u32[]{:S(2)}) collective-permute-start(bf16[128,2176]{1,0:T(8,128)(2,1)S(1)} %collective-permute-done.3.refs_0_), channel_id=1, source_target_pairs={{0,8},{2,10},{4,12},{6,14},{8,16},{10,18},{12,20},{14,22},{16,24},... | collective-permute-start | bytes 1671176 | tf_op jit(solution)/shard_map/ppermute | solution.py:345
  38.2 22.1 %collective-permute-start.5 = (bf16[72,4096]{1,0:T(8,128)(2,1)S(1)}, bf16[72,4096]{1,0:T(8,128)(2,1)S(1)}, u32[]{:S(2)}, u32[]{:S(2)}) collective-permute-start(bf16[72,4096]{1,0:T(8,128)(2,1)S(1)} %get-tuple-element.71), channel_id=1, source_target_pairs={{0,2},{2,0},{4,6},{6,4},{8,10},{10,8},{12,14},{14,12},{16,18},{18,... | collective-permute-start | bytes 1769480 | tf_op jit(solution)/shard_map/ppermute | solution.py:348
  39.5 25.2 %collective-permute-start.6 = (bf16[72,4096]{1,0:T(8,128)(2,1)S(1)}, bf16[72,4096]{1,0:T(8,128)(2,1)S(1)}, u32[]{:S(2)}, u32[]{:S(2)}) collective-permute-start(bf16[72,4096]{1,0:T(8,128)(2,1)S(1)} %get-tuple-element.72), channel_id=1, source_target_pairs={{0,4},{2,6},{4,0},{6,2},{8,12},{10,14},{12,8},{14,10},{16,20},{18,... | collective-permute-start | bytes 1769480 | tf_op jit(solution)/shard_map/ppermute | solution.py:348
  40.3 27.9 %collective-permute-start.7 = (bf16[72,4096]{1,0:T(8,128)(2,1)S(1)}, bf16[72,4096]{1,0:T(8,128)(2,1)S(1)}, u32[]{:S(2)}, u32[]{:S(2)}) collective-permute-start(bf16[72,4096]{1,0:T(8,128)(2,1)S(1)} %get-tuple-element.73), channel_id=1, source_target_pairs={{0,6},{2,4},{4,2},{6,0},{8,14},{10,12},{12,10},{14,8},{16,22},{18,... | collective-permute-start | bytes 1769480 | tf_op jit(solution)/shard_map/ppermute | solution.py:348
  41.7 10.5 %copy-start.2 = (bf16[128,2176]{1,0:T(8,128)(2,1)S(1)}, bf16[128,2176]{1,0:T(8,128)(2,1)}, u32[]{:S(2)}) copy-start(bf16[128,2176]{1,0:T(8,128)(2,1)} %get-tuple-element.63.refs_0_) | copy-start | bytes 1671172
  41.9 16.9 %collective-permute-start.13 = (bf16[2,72,1408]{2,1,0:T(8,128)(2,1)S(1)}, bf16[2,72,1408]{2,1,0:T(8,128)(2,1)S(1)}, u32[]{:S(2)}, u32[]{:S(2)}) collective-permute-start(bf16[2,72,1408]{2,1,0:T(8,128)(2,1)S(1)} %shard_map.84), channel_id=1, source_target_pairs={{0,8},{2,10},{4,12},{6,14},{8,16},{10,18},{12,20},{14,22},{16,24},... | collective-permute-start | bytes 1216520 | tf_op jit(solution)/shard_map/ppermute | solution.py:345
  50.3 20.6 %collective-permute-start.9 = (bf16[2,72,1408]{2,1,0:T(8,128)(2,1)S(1)}, bf16[2,72,1408]{2,1,0:T(8,128)(2,1)S(1)}, u32[]{:S(2)}, u32[]{:S(2)}) collective-permute-start(bf16[2,72,1408]{2,1,0:T(8,128)(2,1)S(1)} %shard_map.80), channel_id=1, source_target_pairs={{0,24},{2,26},{4,28},{6,30},{8,0},{10,2},{12,4},{14,6},{16,8},{18,... | collective-permute-start | bytes 1216520 | tf_op jit(solution)/shard_map/ppermute | solution.py:345
  52.7 16.1 %copy-start.1 = (bf16[1,704,2048]{2,1,0:T(8,128)(2,1)S(1)}, bf16[1,704,2048]{2,1,0:T(8,128)(2,1)}, u32[]{:S(2)}) copy-start(bf16[1,704,2048]{2,1,0:T(8,128)(2,1)} %param.9) | copy-start | bytes 8650756
  58.7 17.6 %collective-permute-start.14 = (bf16[72,2048]{1,0:T(8,128)(2,1)S(1)}, bf16[72,2048]{1,0:T(8,128)(2,1)S(1)}, u32[]{:S(2)}, u32[]{:S(2)}) collective-permute-start(bf16[72,2048]{1,0:T(8,128)(2,1)S(1)} %get-tuple-element.81), channel_id=1, source_target_pairs={{0,2},{2,0},{4,6},{6,4},{8,10},{10,8},{12,14},{14,12},{16,18},{18,... | collective-permute-start | bytes 884744 | tf_op jit(solution)/shard_map/ppermute | solution.py:348
  60.4 19.9 %collective-permute-start.15 = (bf16[72,2048]{1,0:T(8,128)(2,1)S(1)}, bf16[72,2048]{1,0:T(8,128)(2,1)S(1)}, u32[]{:S(2)}, u32[]{:S(2)}) collective-permute-start(bf16[72,2048]{1,0:T(8,128)(2,1)S(1)} %get-tuple-element.82), channel_id=1, source_target_pairs={{0,4},{2,6},{4,0},{6,2},{8,12},{10,14},{12,8},{14,10},{16,20},{18,... | collective-permute-start | bytes 884744 | tf_op jit(solution)/shard_map/ppermute | solution.py:348
  64.6 15.6 %collective-permute-start.16 = (bf16[72,2048]{1,0:T(8,128)(2,1)S(1)}, bf16[72,2048]{1,0:T(8,128)(2,1)S(1)}, u32[]{:S(2)}, u32[]{:S(2)}) collective-permute-start(bf16[72,2048]{1,0:T(8,128)(2,1)S(1)} %get-tuple-element.83), channel_id=1, source_target_pairs={{0,6},{2,4},{4,2},{6,0},{8,14},{10,12},{12,10},{14,8},{16,22},{18,... | collective-permute-start | bytes 884744 | tf_op jit(solution)/shard_map/ppermute | solution.py:348
  68.2 14.2 %collective-permute-start.17 = (bf16[2,72,1408]{2,1,0:T(8,128)(2,1)S(1)}, bf16[2,72,1408]{2,1,0:T(8,128)(2,1)S(1)}, u32[]{:S(2)}, u32[]{:S(2)}) collective-permute-start(bf16[2,72,1408]{2,1,0:T(8,128)(2,1)S(1)} %shard_map.86), channel_id=1, source_target_pairs={{0,16},{2,18},{4,20},{6,22},{8,24},{10,26},{12,28},{14,30},{16,0},... | collective-permute-start | bytes 1216520 | tf_op jit(solution)/shard_map/ppermute | solution.py:345
  70.9 15.6 %collective-permute-start.10 = (bf16[72,1024]{1,0:T(8,128)(2,1)S(1)}, bf16[72,1024]{1,0:T(8,128)(2,1)S(1)}, u32[]{:S(2)}, u32[]{:S(2)}) collective-permute-start(bf16[72,1024]{1,0:T(8,128)(2,1)S(1)} %get-tuple-element.74), channel_id=1, source_target_pairs={{0,2},{2,0},{4,6},{6,4},{8,10},{10,8},{12,14},{14,12},{16,18},{18,... | collective-permute-start | bytes 442376 | tf_op jit(solution)/shard_map/ppermute | solution.py:348
  76.3 10.7 %collective-permute-start.11 = (bf16[72,1024]{1,0:T(8,128)(2,1)S(1)}, bf16[72,1024]{1,0:T(8,128)(2,1)S(1)}, u32[]{:S(2)}, u32[]{:S(2)}) collective-permute-start(bf16[72,1024]{1,0:T(8,128)(2,1)S(1)} %get-tuple-element.75), channel_id=1, source_target_pairs={{0,4},{2,6},{4,0},{6,2},{8,12},{10,14},{12,8},{14,10},{16,20},{18,... | collective-permute-start | bytes 442376 | tf_op jit(solution)/shard_map/ppermute | solution.py:348
  80.3 6.7 %collective-permute-start.12 = (bf16[72,1024]{1,0:T(8,128)(2,1)S(1)}, bf16[72,1024]{1,0:T(8,128)(2,1)S(1)}, u32[]{:S(2)}, u32[]{:S(2)}) collective-permute-start(bf16[72,1024]{1,0:T(8,128)(2,1)S(1)} %get-tuple-element.76), channel_id=1, source_target_pairs={{0,6},{2,4},{4,2},{6,0},{8,14},{10,12},{12,10},{14,8},{16,22},{18,... | collective-permute-start | bytes 442376 | tf_op jit(solution)/shard_map/ppermute | solution.py:348
  84.5 7.4 %collective-permute-start.19 = (f32[4,128]{1,0:T(4,128)S(1)}, f32[4,128]{1,0:T(4,128)S(1)}, u32[]{:S(2)}, u32[]{:S(2)}) collective-permute-start(f32[4,128]{1,0:T(4,128)S(1)} %get-tuple-element.97.refs_2_), channel_id=1, source_target_pairs={{0,16},{2,18},{4,20},{6,22},{8,24},{10,26},{12,28},{14,30},{16,0},... | collective-permute-start | bytes 6152 | tf_op jit(solution)/shard_map/ppermute | solution.py:345
  84.6 5.9 %collective-permute-start.18 = (f32[4,128]{1,0:T(4,128)S(1)}, f32[4,128]{1,0:T(4,128)S(1)}, u32[]{:S(2)}, u32[]{:S(2)}) collective-permute-start(f32[4,128]{1,0:T(4,128)S(1)} %get-tuple-element.98), channel_id=1, source_target_pairs={{0,24},{2,26},{4,28},{6,30},{8,0},{10,2},{12,4},{14,6},{16,8},{18,... | collective-permute-start | bytes 6152 | tf_op jit(solution)/shard_map/ppermute | solution.py:345
  86.5 5.4 %collective-permute-start.20 = (f32[4,128]{1,0:T(4,128)S(1)}, f32[4,128]{1,0:T(4,128)S(1)}, u32[]{:S(2)}, u32[]{:S(2)}) collective-permute-start(f32[4,128]{1,0:T(4,128)S(1)} %get-tuple-element.99), channel_id=1, source_target_pairs={{0,8},{2,10},{4,12},{6,14},{8,16},{10,18},{12,20},{14,22},{16,24},... | collective-permute-start | bytes 6152 | tf_op jit(solution)/shard_map/ppermute | solution.py:345
  90.4 10.3 %copy-start.3 = (s32[128,6]{0,1:T(8,128)S(1)}, s32[128,6]{0,1:T(8,128)}, u32[]{:S(2)}) copy-start(s32[128,6]{0,1:T(8,128)} %param.7) | copy-start | bytes 9220
  90.4 10.2 %copy-start.4 = (s32[128,6]{0,1:T(8,128)S(1)}, s32[128,6]{0,1:T(8,128)}, u32[]{:S(2)}) copy-start(s32[128,6]{0,1:T(8,128)} %param.8) | copy-start | bytes 9220
  90.4 10.2 %copy-start.5 = (f32[16,128]{1,0:T(8,128)S(1)}, f32[16,128]{1,0:T(8,128)}, u32[]{:S(2)}) copy-start(f32[16,128]{1,0:T(8,128)} %get-tuple-element.102.refs_2_) | copy-start | bytes 24580
  90.4 7.3 %collective-permute-start.25 = (bf16[352,1024]{1,0:T(8,128)(2,1)S(1)}, bf16[352,1024]{1,0:T(8,128)(2,1)S(1)}, u32[]{:S(2)}, u32[]{:S(2)}) collective-permute-start(bf16[352,1024]{1,0:T(8,128)(2,1)S(1)} %get-tuple-element.104.refs_4_), channel_id=1, source_target_pairs={{0,1},{1,0},{2,3},{3,2},{4,5},{5,4},{6,7},{7,6},{8,9},{9,8},{10,11... | collective-permute-start | bytes 2162696 | tf_op jit(solution)/shard_map/ppermute | solution.py:468
  93.2 7.4 %collective-permute-start.21 = (bf16[352,1024]{1,0:T(8,128)(2,1)S(1)}, bf16[352,1024]{1,0:T(8,128)(2,1)S(1)}, u32[]{:S(2)}, u32[]{:S(2)}) collective-permute-start(bf16[352,1024]{1,0:T(8,128)(2,1)S(1)} %get-tuple-element.101), channel_id=1, source_target_pairs={{0,1},{1,0},{2,3},{3,2},{4,5},{5,4},{6,7},{7,6},{8,9},{9,8},{10,11... | collective-permute-start | bytes 2162696 | tf_op jit(solution)/shard_map/ppermute | solution.py:468
  93.3 5.7 %collective-permute-start.22 = (f32[4,128]{1,0:T(4,128)S(1)}, f32[4,128]{1,0:T(4,128)S(1)}, u32[]{:S(2)}, u32[]{:S(2)}) collective-permute-start(f32[4,128]{1,0:T(4,128)S(1)} %get-tuple-element.106), channel_id=1, source_target_pairs={{0,2},{2,0},{4,6},{6,4},{8,10},{10,8},{12,14},{14,12},{16,18},{18,... | collective-permute-start | bytes 6152 | tf_op jit(solution)/shard_map/ppermute | solution.py:348
  96.1 3.6 %collective-permute-start.23 = (f32[4,128]{1,0:T(4,128)S(1)}, f32[4,128]{1,0:T(4,128)S(1)}, u32[]{:S(2)}, u32[]{:S(2)}) collective-permute-start(f32[4,128]{1,0:T(4,128)S(1)} %get-tuple-element.107), channel_id=1, source_target_pairs={{0,4},{2,6},{4,0},{6,2},{8,12},{10,14},{12,8},{14,10},{16,20},{18,... | collective-permute-start | bytes 6152 | tf_op jit(solution)/shard_map/ppermute | solution.py:348
  96.1 4.5 %collective-permute-start.24 = (f32[4,128]{1,0:T(4,128)S(1)}, f32[4,128]{1,0:T(4,128)S(1)}, u32[]{:S(2)}, u32[]{:S(2)}) collective-permute-start(f32[4,128]{1,0:T(4,128)S(1)} %get-tuple-element.108), channel_id=1, source_target_pairs={{0,6},{2,4},{4,2},{6,0},{8,14},{10,12},{12,10},{14,8},{16,22},{18,... | collective-permute-start | bytes 6152 | tf_op jit(solution)/shard_map/ppermute | solution.py:348

commit v8 on v7

--- a/solution.py
+++ b/solution.py
@@ -49,8 +49,8 @@
 
 def open_kernel(slots, flip, *refs):
     routes_hbm, num_hbm, hid_hbm, cot_hbm, ext_hbm, *refs = refs
-    sent_hbm, (slot_ref, *refs) = refs[:PLANE], refs[PLANE:]
-    ext, sent, table, routes_ref, num_ref, hid_ref, done = refs
+    sent, (slot_ref, *refs) = refs[:PLANE], refs[PLANE:]
+    ext, table, routes_ref, num_ref, hid_ref, done = refs
     experts, tokens = slot_ref.shape
     top_k, width = hid_ref.shape[:2]
     model = cot_hbm.shape[1]
@@ -68,15 +68,6 @@
     for copy in copies[:4]:
         copy.start()
 
-    def leave(first, count, n):
-        for k in range(PLANE):
-            lanes = pl.ds(first, count)
-            copy = pltpu.make_async_copy(
-                sent.at[k, :, lanes], sent_hbm[k].at[:, lanes], done.at[5 + n * PLANE + k]
-            )
-            copy.start()
-            copies.append(copy)
-
     copies[0].wait()
     routes = routes_ref[...]
     ids = lax.broadcasted_iota(jnp.int32, (experts, tokens), 0)
@@ -96,9 +87,8 @@
     copies[1].wait()
     copies[4].start()
     parts = experts // PLANE * width
-    lead = sent.shape[2] - parts
-    select(slots, slot_ref, ext.at[:, pl.ds(0, lead)], [sent.at[k] for k in range(PLANE)], parts)
-    leave(parts, lead, 0)
+    lead = sent[0].shape[1] - parts
+    select(slots, slot_ref, ext.at[:, pl.ds(0, lead)], sent, parts)
     me = lax.axis_index("expert")
     steps = (routes >> 2) - (me >> 2)
     steps = jnp.where(steps < 0, steps + experts // PLANE, steps)
@@ -137,12 +127,11 @@
         at = s * width
         for k in range(PLANE):
             these = slice(k * slots, (k + 1) * slots)
-            sent[k, :, at : at + cut] = left[these, 0:cut].astype(BF)
-            sent[k, :, at + cut : at + whole] = (
+            sent[k][:, at : at + cut] = left[these, 0:cut].astype(BF)
+            sent[k][:, at + cut : at + whole] = (
                 left[these, cut:] + right[these, 0:BLOCK]
             ).astype(BF)
-            sent[k, :, at + whole : at + pair] = right[these, BLOCK:].astype(BF)
-        leave(at, pair, 1 + s // 2)
+            sent[k][:, at + whole : at + pair] = right[these, BLOCK:].astype(BF)
     for copy in copies[4:]:
         copy.wait()
 
@@ -200,7 +189,6 @@
     hid_ref = refs[0]
     all_rows, all_hidw, gate_ref, rows, hids, hidw, done = refs[-7:]
     group = PLANE * stride
-    slots = arrays[0].shape[0]
     width, model = w_ref.shape
     half = width // 2
     whole = hids.shape[1]
@@ -209,12 +197,7 @@
     for n, (at, count) in enumerate(spans):
         for k in range(PLANE):
             piece = arrays[n * PLANE + k][:, at : at + count]
-            lanes = slice(to, to + count)
-            clear = slots // 16 * 16
-            rows[k * stride + clear : (k + 1) * stride, lanes] = jnp.zeros(
-                (stride - clear, count), BF
-            )
-            rows[k * stride : k * stride + slots, lanes] = piece
+            fill(rows.at[:, pl.ds(to, count)], k * stride, piece, stride)
         to += count
     copy = pltpu.make_async_copy(rows, all_rows.at[pl.ds(place * group, group)], done.at[0])
     copy.start()
@@ -359,15 +342,14 @@
         + [sds((experts, tokens), F32)],
         ALL_VMEM,
         in_specs=[anywhere] * 4,
-        out_specs=[anywhere] * (1 + PLANE) + [inside],
+        out_specs=[anywhere] + [inside] * (1 + PLANE),
         scratch_shapes=[
             pltpu.VMEM((tokens, model + BLOCK), BF),
-            pltpu.VMEM((PLANE, slots, wide), BF),
             pltpu.VMEM((2 * up(width, BLOCK) - width, top_k * tokens), BF),
             pltpu.VMEM((top_k, tokens), jnp.int32),
             pltpu.VMEM((top_k, tokens), jnp.int32),
             pltpu.VMEM((top_k, width, tokens), BF),
-            pltpu.SemaphoreType.DMA((5 + PLANE * (1 + outer // 2),)),
+            pltpu.SemaphoreType.DMA((5,)),
         ],
     )(routes.T, numerators.T, jnp.transpose(hidden, (1, 2, 0)), cotangent)
     opening = [packed[0]] + [swap(packed[k], k) for k in range(1, PLANE)]

time: 103 us -> 103 us (level)
  no operation moved by 1% of the time
where the time goes in v8:
time: 103 us
  waiting for transfers between devices  51 us (50%)
  starting transfers between devices  26.7 us (26%)
  Pallas kernels  23.7 us (23%)
  between operations  1.09 us (1%)
    ppermute x9, waiting for transfers between devices, ring(): return lax.ppermute(array, 'expert', pairs)  38 us
    ppermute x15, starting transfers between devices, swap(): return lax.ppermute(array, 'expert', [(e, e ^ k) for e in range(experts)])  16.3 us
    ppermute x15, waiting for transfers between devices, swap(): return lax.ppermute(array, 'expert', [(e, e ^ k) for e in range(experts)])  13 us
    ppermute x9, starting transfers between devices, ring(): return lax.ppermute(array, 'expert', pairs)  10.3 us
    pallas_call x4, Pallas kernels, stage(): call(functools.partial(stage_kernel, place, [span for _, span in parts],...  8.22 us
    pallas_call x1, Pallas kernels, per_device(): call(functools.partial(open_kernel, slots, flip), [sds((tokens, model + B...  4.9 us
    pallas_call x2, Pallas kernels, finish(): call(functools.partial(finish_kernel, first, fine, len(own), bool(extra))...  3.29 us
    pallas_call x2, Pallas kernels, partial(): call(functools.partial(partial_kernel, first, step), [sds((half, model //...  2.6 us
  transfers between devices with their start and end apart: 26, of which 12 were waited for; matrix products, arithmetic and copies ran while one was open for 0% of the time, Pallas kernels for 16%

profile of v8, /device:TPU:0, one launch (start us, length us, event | category | flops | bytes accessed | tf_op | source)
XLA Modules:
  0.0 102.5 jit_solution(16424821975289092270)
XLA Ops:
  0.6 4.9 %shard_map.76 = (bf16[128,2176]{1,0:T(8,128)(2,1)}, bf16[72,3840]{1,0:T(8,128)(2,1)}, bf16[72,3840]{1,0:T(8,128)(2,1)}, bf16[72,3840]{1,0:T(8,128)(2,1)}, bf16[72,3840]{1,0:T(8,128)(2,1)}, /*index=5*/f32[16,128]{1,0:T(8,128)}) custom-call(s32[6,128]{1,0:T(8,128)} %bitcast.17, s32[6,128]{1,0:T(8,128)} %bitcast.19, bf16[6,704,128]{2,1,0:T(8,128)(2,1)} %bitcast.22, ...), custom_call_target="tpu_custom_call" | custom-call | flops 1024 | bytes 1024 | tf_op jit(solution)/shard_map/pallas_call | solution.py:338
  5.5 3.1 %collective-permute-start.3 = (bf16[128,2176]{1,0:T(8,128)(2,1)}, bf16[128,2176]{1,0:T(8,128)(2,1)S(1)}, u32[]{:S(2)}, u32[]{:S(2)}) collective-permute-start(bf16[128,2176]{1,0:T(8,128)(2,1)} %get-tuple-element.63.refs_0_), channel_id=1, source_target_pairs={{0,8},{2,10},{4,12},{6,14},{8,16},{10,18},{12,20},{14,22},{16,24},... | collective-permute-start | bytes 1671176 | tf_op jit(solution)/shard_map/ppermute | solution.py:328
  8.6 2.1 %collective-permute-start.4 = (bf16[128,2176]{1,0:T(8,128)(2,1)}, bf16[128,2176]{1,0:T(8,128)(2,1)S(1)}, u32[]{:S(2)}, u32[]{:S(2)}) collective-permute-start(bf16[128,2176]{1,0:T(8,128)(2,1)} %get-tuple-element.63.refs_0_), channel_id=1, source_target_pairs={{0,24},{2,26},{4,28},{6,30},{8,0},{10,2},{12,4},{14,6},{16,8},{18,... | collective-permute-start | bytes 1671176 | tf_op jit(solution)/shard_map/ppermute | solution.py:328
  10.7 1.6 %collective-permute-start = (bf16[72,3840]{1,0:T(8,128)(2,1)}, bf16[72,3840]{1,0:T(8,128)(2,1)S(1)}, u32[]{:S(2)}, u32[]{:S(2)}) collective-permute-start(bf16[72,3840]{1,0:T(8,128)(2,1)} %get-tuple-element.60), channel_id=1, source_target_pairs={{0,2},{2,0},{4,6},{6,4},{8,10},{10,8},{12,14},{14,12},{16,18},{18,... | collective-permute-start | bytes 1658888 | tf_op jit(solution)/shard_map/ppermute | solution.py:331
  12.4 1.5 %collective-permute-start.1 = (bf16[72,3840]{1,0:T(8,128)(2,1)}, bf16[72,3840]{1,0:T(8,128)(2,1)S(1)}, u32[]{:S(2)}, u32[]{:S(2)}) collective-permute-start(bf16[72,3840]{1,0:T(8,128)(2,1)} %get-tuple-element.61), channel_id=1, source_target_pairs={{0,4},{2,6},{4,0},{6,2},{8,12},{10,14},{12,8},{14,10},{16,20},{18,... | collective-permute-start | bytes 1658888 | tf_op jit(solution)/shard_map/ppermute | solution.py:331
  14.2 10.2 %collective-permute-done.3.refs_0_ = bf16[128,2176]{1,0:T(8,128)(2,1)S(1)} collective-permute-done((bf16[128,2176]{1,0:T(8,128)(2,1)}, bf16[128,2176]{1,0:T(8,128)(2,1)S(1)}, u32[]{:S(2)}, u32[]{:S(2)}) %collective-permute-start.3) | collective-permute-done | bytes 557088 | tf_op jit(solution)/shard_map/ppermute | solution.py:328
  24.4 10.7 %collective-permute-done.4.refs_1_ = bf16[128,2176]{1,0:T(8,128)(2,1)S(1)} collective-permute-done((bf16[128,2176]{1,0:T(8,128)(2,1)}, bf16[128,2176]{1,0:T(8,128)(2,1)S(1)}, u32[]{:S(2)}, u32[]{:S(2)}) %collective-permute-start.4) | collective-permute-done | bytes 557088 | tf_op jit(solution)/shard_map/ppermute | solution.py:328
  35.9 2.0 %collective-permute-done.1.refs_4_.refs_2_ = bf16[72,3840]{1,0:T(8,128)(2,1)S(1)} collective-permute-done((bf16[72,3840]{1,0:T(8,128)(2,1)}, bf16[72,3840]{1,0:T(8,128)(2,1)S(1)}, u32[]{:S(2)}, u32[]{:S(2)}) %collective-permute-start.1) | collective-permute-done | bytes 552992 | tf_op jit(solution)/shard_map/ppermute | solution.py:331
  38.0 1.2 %collective-permute-start.5 = (bf16[72,4096]{1,0:T(8,128)(2,1)S(1)}, bf16[72,4096]{1,0:T(8,128)(2,1)S(1)}, u32[]{:S(2)}, u32[]{:S(2)}) collective-permute-start(bf16[72,4096]{1,0:T(8,128)(2,1)S(1)} %get-tuple-element.71), channel_id=1, source_target_pairs={{0,2},{2,0},{4,6},{6,4},{8,10},{10,8},{12,14},{14,12},{16,18},{18,... | collective-permute-start | bytes 1769480 | tf_op jit(solution)/shard_map/ppermute | solution.py:331
  40.0 1.4 %collective-permute-start.7 = (bf16[72,4096]{1,0:T(8,128)(2,1)S(1)}, bf16[72,4096]{1,0:T(8,128)(2,1)S(1)}, u32[]{:S(2)}, u32[]{:S(2)}) collective-permute-start(bf16[72,4096]{1,0:T(8,128)(2,1)S(1)} %get-tuple-element.73), channel_id=1, source_target_pairs={{0,6},{2,4},{4,2},{6,0},{8,14},{10,12},{12,10},{14,8},{16,22},{18,... | collective-permute-start | bytes 1769480 | tf_op jit(solution)/shard_map/ppermute | solution.py:331
  41.7 8.2 %collective-permute-done.8.refs_4_.refs_0_ = bf16[128,2176]{1,0:T(8,128)(2,1)S(1)} collective-permute-done((bf16[128,2176]{1,0:T(8,128)(2,1)S(1)}, bf16[128,2176]{1,0:T(8,128)(2,1)S(1)}, u32[]{:S(2)}, u32[]{:S(2)}) %collective-permute-start.8) | collective-permute-done | bytes 557088 | tf_op jit(solution)/shard_map/ppermute | solution.py:328
  50.0 1.9 %collective-permute-start.9 = (bf16[2,72,1408]{2,1,0:T(8,128)(2,1)S(1)}, bf16[2,72,1408]{2,1,0:T(8,128)(2,1)S(1)}, u32[]{:S(2)}, u32[]{:S(2)}) collective-permute-start(bf16[2,72,1408]{2,1,0:T(8,128)(2,1)S(1)} %shard_map.80), channel_id=1, source_target_pairs={{0,24},{2,26},{4,28},{6,30},{8,0},{10,2},{12,4},{14,6},{16,8},{18,... | collective-permute-start | bytes 1216520 | tf_op jit(solution)/shard_map/ppermute | solution.py:328
  53.0 5.4 %collective-permute-done.13.refs_3_.refs_5_ = bf16[2,72,1408]{2,1,0:T(8,128)(2,1)S(1)} collective-permute-done((bf16[2,72,1408]{2,1,0:T(8,128)(2,1)S(1)}, bf16[2,72,1408]{2,1,0:T(8,128)(2,1)S(1)}, u32[]{:S(2)}, u32[]{:S(2)}) %collective-permute-start.13) | collective-permute-done | bytes 405536 | tf_op jit(solution)/shard_map/ppermute | solution.py:328
  58.5 1.5 %collective-permute-start.14 = (bf16[72,2048]{1,0:T(8,128)(2,1)S(1)}, bf16[72,2048]{1,0:T(8,128)(2,1)S(1)}, u32[]{:S(2)}, u32[]{:S(2)}) collective-permute-start(bf16[72,2048]{1,0:T(8,128)(2,1)S(1)} %get-tuple-element.81), channel_id=1, source_target_pairs={{0,2},{2,0},{4,6},{6,4},{8,10},{10,8},{12,14},{14,12},{16,18},{18,... | collective-permute-start | bytes 884744 | tf_op jit(solution)/shard_map/ppermute | solution.py:331
  60.1 1.6 %collective-permute-start.15 = (bf16[72,2048]{1,0:T(8,128)(2,1)S(1)}, bf16[72,2048]{1,0:T(8,128)(2,1)S(1)}, u32[]{:S(2)}, u32[]{:S(2)}) collective-permute-start(bf16[72,2048]{1,0:T(8,128)(2,1)S(1)} %get-tuple-element.82), channel_id=1, source_target_pairs={{0,4},{2,6},{4,0},{6,2},{8,12},{10,14},{12,8},{14,10},{16,20},{18,... | collective-permute-start | bytes 884744 | tf_op jit(solution)/shard_map/ppermute | solution.py:331
  61.7 2.8 %collective-permute-done.6.refs_4_.refs_2_ = bf16[72,4096]{1,0:T(8,128)(2,1)S(1)} collective-permute-done((bf16[72,4096]{1,0:T(8,128)(2,1)S(1)}, bf16[72,4096]{1,0:T(8,128)(2,1)S(1)}, u32[]{:S(2)}, u32[]{:S(2)}) %collective-permute-start.6) | collective-permute-done | bytes 589856 | tf_op jit(solution)/shard_map/ppermute | solution.py:331
  64.4 3.5 %collective-permute-done.7.refs_5_.refs_3_ = bf16[72,4096]{1,0:T(8,128)(2,1)S(1)} collective-permute-done((bf16[72,4096]{1,0:T(8,128)(2,1)S(1)}, bf16[72,4096]{1,0:T(8,128)(2,1)S(1)}, u32[]{:S(2)}, u32[]{:S(2)}) %collective-permute-start.7) | collective-permute-done | bytes 589856 | tf_op jit(solution)/shard_map/ppermute | solution.py:331
  68.6 2.1 %shard_map.87 = (bf16[768,2048]{1,0:T(8,128)(2,1)S(1)}, bf16[704,768]{1,0:T(8,128)(2,1)S(1)}, f32[4,128]{1,0:T(4,128)S(1)}) custom-call(bf16[72,4096]{1,0:T(8,128)(2,1)S(1)} %get-tuple-element.84.refs_0_, bf16[72,4096]{1,0:T(8,128)(2,1)S(1)} %collective-permute-done.5.refs_3_.refs_1_, bf16[72,4096]{1,0:T(8,128)(2,1)S(1)} %collective-permute-done.6.refs_4_.refs_2_, ...), custom_call_target="tpu_custom_call" | custom-call | flops 2000000000 | bytes 1024 | tf_op jit(solution)/shard_map/pallas_call | solution.py:401
  71.6 2.1 %shard_map.88 = (bf16[768,2048]{1,0:T(8,128)(2,1)S(1)}, bf16[704,768]{1,0:T(8,128)(2,1)S(1)}, f32[4,128]{1,0:T(4,128)S(1)}) custom-call(bf16[72,4096]{1,0:T(8,128)(2,1)S(1)} %get-tuple-element.84.refs_0_, bf16[72,4096]{1,0:T(8,128)(2,1)S(1)} %collective-permute-done.5.refs_3_.refs_1_, ...), custom_call_target="tpu_custom_call", output_to_operand_aliasing={{0}: (6, {}), {1}: (7, {})} | custom-call | flops 2000000000 | bytes 1024 | tf_op jit(solution)/shard_map/pallas_call | solution.py:401
  73.7 2.4 %shard_map.89 = (bf16[704,2048]{1,0:T(8,128)(2,1)S(1)}, f32[8,128]{1,0:T(8,128)S(1)}) custom-call(bf16[768,2048]{1,0:T(8,128)(2,1)S(1)} %get-tuple-element.87.rows_ref, bf16[704,768]{1,0:T(8,128)(2,1)S(1)} %get-tuple-element.88.hidw_ref), custom_call_target="tpu_custom_call" | custom-call | flops 3500000000 | bytes 1024 | tf_op jit(solution)/shard_map/pallas_call | solution.py:426
  77.0 3.1 %collective-permute-done.15.refs_2_ = bf16[72,2048]{1,0:T(8,128)(2,1)S(1)} collective-permute-done((bf16[72,2048]{1,0:T(8,128)(2,1)S(1)}, bf16[72,2048]{1,0:T(8,128)(2,1)S(1)}, u32[]{:S(2)}, u32[]{:S(2)}) %collective-permute-start.15) | collective-permute-done | bytes 294944 | tf_op jit(solution)/shard_map/ppermute | solution.py:331
  80.1 2.1 %collective-permute-done.17.refs_5_ = bf16[2,72,1408]{2,1,0:T(8,128)(2,1)S(1)} collective-permute-done((bf16[2,72,1408]{2,1,0:T(8,128)(2,1)S(1)}, bf16[2,72,1408]{2,1,0:T(8,128)(2,1)S(1)}, u32[]{:S(2)}, u32[]{:S(2)}) %collective-permute-start.17) | collective-permute-done | bytes 405536 | tf_op jit(solution)/shard_map/ppermute | solution.py:328
  82.2 2.1 %shard_map.90 = (bf16[768,2048]{1,0:T(8,128)(2,1)S(1)}, bf16[704,768]{1,0:T(8,128)(2,1)S(1)}, f32[4,128]{1,0:T(4,128)S(1)}) custom-call(bf16[72,2048]{1,0:T(8,128)(2,1)S(1)} %get-tuple-element.77.refs_0_, bf16[72,2048]{1,0:T(8,128)(2,1)S(1)} %collective-permute-done.14.refs_1_, bf16[72,2048]{1,0:T(8,128)(2,1)S(1)} %collective-permute-done.15.refs_2_, ...), custom_call_target="tpu_custom_call" | custom-call | flops 2000000000 | bytes 1024 | tf_op jit(solution)/shard_map/pallas_call | solution.py:401
  84.3 1.9 %collective-permute-start.18 = (f32[4,128]{1,0:T(4,128)S(1)}, f32[4,128]{1,0:T(4,128)S(1)}, u32[]{:S(2)}, u32[]{:S(2)}) collective-permute-start(f32[4,128]{1,0:T(4,128)S(1)} %get-tuple-element.98), channel_id=1, source_target_pairs={{0,24},{2,26},{4,28},{6,30},{8,0},{10,2},{12,4},{14,6},{16,8},{18,... | collective-permute-start | bytes 6152 | tf_op jit(solution)/shard_map/ppermute | solution.py:328
  86.7 2.1 %shard_map.91 = (bf16[768,2048]{1,0:T(8,128)(2,1)S(1)}, bf16[704,768]{1,0:T(8,128)(2,1)S(1)}, f32[4,128]{1,0:T(4,128)S(1)}) custom-call(bf16[72,3840]{1,0:T(8,128)(2,1)S(1)} %copy-done, bf16[72,3840]{1,0:T(8,128)(2,1)S(1)} %collective-permute-done.refs_3_.refs_1_, ...), custom_call_target="tpu_custom_call", output_to_operand_aliasing={{0}: (10, {}), {1}: (11, {})} | custom-call | flops 2000000000 | bytes 1024 | tf_op jit(solution)/shard_map/pallas_call | solution.py:401
  88.8 1.3 %shard_map.94 = (bf16[352,1024]{1,0:T(8,128)(2,1)S(1)}, bf16[352,1024]{1,0:T(8,128)(2,1)S(1)}) custom-call(bf16[768,2048]{1,0:T(8,128)(2,1)S(1)} %get-tuple-element.92.rows_ref, bf16[704,768]{1,0:T(8,128)(2,1)S(1)} %get-tuple-element.93.hidw_ref, bf16[704,2048]{1,0:T(8,128)(2,1)S(1)} %get-tuple-element.94.early_ref), custom_call_target="tpu_custom_call" | custom-call | flops 1024 | bytes 1024 | tf_op jit(solution)/shard_map/pallas_call | solution.py:442
  90.2 1.4 %collective-permute-done.20.refs_2_.refs_3_ = f32[4,128]{1,0:T(4,128)S(1)} collective-permute-done((f32[4,128]{1,0:T(4,128)S(1)}, f32[4,128]{1,0:T(4,128)S(1)}, u32[]{:S(2)}, u32[]{:S(2)}) %collective-permute-start.20) | collective-permute-done | bytes 2080 | tf_op jit(solution)/shard_map/ppermute | solution.py:328
  91.6 1.3 %shard_map.93 = (bf16[352,1024]{1,0:T(8,128)(2,1)S(1)}, bf16[352,1024]{1,0:T(8,128)(2,1)S(1)}) custom-call(bf16[768,2048]{1,0:T(8,128)(2,1)S(1)} %get-tuple-element.92.rows_ref, bf16[704,768]{1,0:T(8,128)(2,1)S(1)} %get-tuple-element.93.hidw_ref, bf16[704,2048]{1,0:T(8,128)(2,1)S(1)} %get-tuple-element.94.early_ref, ...), custom_call_target="tpu_custom_call" | custom-call | flops 1024 | bytes 1024 | tf_op jit(solution)/shard_map/pallas_call | solution.py:442
  93.0 2.9 %collective-permute-start.22 = (f32[4,128]{1,0:T(4,128)S(1)}, f32[4,128]{1,0:T(4,128)S(1)}, u32[]{:S(2)}, u32[]{:S(2)}) collective-permute-start(f32[4,128]{1,0:T(4,128)S(1)} %get-tuple-element.106), channel_id=1, source_target_pairs={{0,2},{2,0},{4,6},{6,4},{8,10},{10,8},{12,14},{14,12},{16,18},{18,... | collective-permute-start | bytes 6152 | tf_op jit(solution)/shard_map/ppermute | solution.py:331
  95.9 1.5 %collective-permute-start.24 = (f32[4,128]{1,0:T(4,128)S(1)}, f32[4,128]{1,0:T(4,128)S(1)}, u32[]{:S(2)}, u32[]{:S(2)}) collective-permute-start(f32[4,128]{1,0:T(4,128)S(1)} %get-tuple-element.108), channel_id=1, source_target_pairs={{0,6},{2,4},{4,2},{6,0},{8,14},{10,12},{12,10},{14,8},{16,22},{18,... | collective-permute-start | bytes 6152 | tf_op jit(solution)/shard_map/ppermute | solution.py:331
  97.4 1.3 %shard_map.96 = (f32[352,2048]{1,0:T(8,128)}, f32[16,352]{1,0:T(8,128)}) custom-call(bf16[352,1024]{1,0:T(8,128)(2,1)S(1)} %get-tuple-element.109.refs_0_, bf16[1,352,1024]{2,1,0:T(8,128)(2,1)S(1)} %bitcast.15), custom_call_target="tpu_custom_call" | custom-call | flops 1024 | bytes 1024 | tf_op jit(solution)/shard_map/pallas_call | solution.py:469
  100.4 1.9 %shard_map.97 = (f32[352,2048]{1,0:T(8,128)}, f32[16,352]{1,0:T(8,128)}, f32[6,128]{1,0:T(8,128)}) custom-call(bf16[352,1024]{1,0:T(8,128)(2,1)S(1)} %get-tuple-element.100.refs_0_, bf16[1,352,1024]{2,1,0:T(8,128)(2,1)S(1)} %bitcast.16, f32[16,128]{1,0:T(8,128)S(1)} %copy-done.5, ...), custom_call_target="tpu_custom_call", output_to_operand_aliasing={{0}: (9, {}), {1}: (10, {})} | custom-call | flops 1024 | bytes 1024 | tf_op jit(solution)/shard_map/pallas_call | solution.py:469
  (54 shorter events, 8.4 us)
Async XLA Ops:
  5.5 35.9 %copy-start = (bf16[72,3840]{1,0:T(8,128)(2,1)S(1)}, bf16[72,3840]{1,0:T(8,128)(2,1)}, u32[]{:S(2)}) copy-start(bf16[72,3840]{1,0:T(8,128)(2,1)} %get-tuple-element.59.refs_0_) | copy-start | bytes 1658884
  5.5 18.8 %collective-permute-start.3 = (bf16[128,2176]{1,0:T(8,128)(2,1)}, bf16[128,2176]{1,0:T(8,128)(2,1)S(1)}, u32[]{:S(2)}, u32[]{:S(2)}) collective-permute-start(bf16[128,2176]{1,0:T(8,128)(2,1)} %get-tuple-element.63.refs_0_), channel_id=1, source_target_pairs={{0,8},{2,10},{4,12},{6,14},{8,16},{10,18},{12,20},{14,22},{16,24},... | collective-permute-start | bytes 1671176 | tf_op jit(solution)/shard_map/ppermute | solution.py:328
  8.6 26.5 %collective-permute-start.4 = (bf16[128,2176]{1,0:T(8,128)(2,1)}, bf16[128,2176]{1,0:T(8,128)(2,1)S(1)}, u32[]{:S(2)}, u32[]{:S(2)}) collective-permute-start(bf16[128,2176]{1,0:T(8,128)(2,1)} %get-tuple-element.63.refs_0_), channel_id=1, source_target_pairs={{0,24},{2,26},{4,28},{6,30},{8,0},{10,2},{12,4},{14,6},{16,8},{18,... | collective-permute-start | bytes 1671176 | tf_op jit(solution)/shard_map/ppermute | solution.py:328
  10.7 25.2 %collective-permute-start = (bf16[72,3840]{1,0:T(8,128)(2,1)}, bf16[72,3840]{1,0:T(8,128)(2,1)S(1)}, u32[]{:S(2)}, u32[]{:S(2)}) collective-permute-start(bf16[72,3840]{1,0:T(8,128)(2,1)} %get-tuple-element.60), channel_id=1, source_target_pairs={{0,2},{2,0},{4,6},{6,4},{8,10},{10,8},{12,14},{14,12},{16,18},{18,... | collective-permute-start | bytes 1658888 | tf_op jit(solution)/shard_map/ppermute | solution.py:331
  12.4 25.6 %collective-permute-start.1 = (bf16[72,3840]{1,0:T(8,128)(2,1)}, bf16[72,3840]{1,0:T(8,128)(2,1)S(1)}, u32[]{:S(2)}, u32[]{:S(2)}) collective-permute-start(bf16[72,3840]{1,0:T(8,128)(2,1)} %get-tuple-element.61), channel_id=1, source_target_pairs={{0,4},{2,6},{4,0},{6,2},{8,12},{10,14},{12,8},{14,10},{16,20},{18,... | collective-permute-start | bytes 1658888 | tf_op jit(solution)/shard_map/ppermute | solution.py:331
  13.9 24.1 %collective-permute-start.2 = (bf16[72,3840]{1,0:T(8,128)(2,1)}, bf16[72,3840]{1,0:T(8,128)(2,1)S(1)}, u32[]{:S(2)}, u32[]{:S(2)}) collective-permute-start(bf16[72,3840]{1,0:T(8,128)(2,1)} %get-tuple-element.62), channel_id=1, source_target_pairs={{0,6},{2,4},{4,2},{6,0},{8,14},{10,12},{12,10},{14,8},{16,22},{18,... | collective-permute-start | bytes 1658888 | tf_op jit(solution)/shard_map/ppermute | solution.py:331
  24.4 25.5 %collective-permute-start.8 = (bf16[128,2176]{1,0:T(8,128)(2,1)S(1)}, bf16[128,2176]{1,0:T(8,128)(2,1)S(1)}, u32[]{:S(2)}, u32[]{:S(2)}) collective-permute-start(bf16[128,2176]{1,0:T(8,128)(2,1)S(1)} %collective-permute-done.3.refs_0_), channel_id=1, source_target_pairs={{0,8},{2,10},{4,12},{6,14},{8,16},{10,18},{12,20},{14,22},{16,24},... | collective-permute-start | bytes 1671176 | tf_op jit(solution)/shard_map/ppermute | solution.py:328
  38.0 22.1 %collective-permute-start.5 = (bf16[72,4096]{1,0:T(8,128)(2,1)S(1)}, bf16[72,4096]{1,0:T(8,128)(2,1)S(1)}, u32[]{:S(2)}, u32[]{:S(2)}) collective-permute-start(bf16[72,4096]{1,0:T(8,128)(2,1)S(1)} %get-tuple-element.71), channel_id=1, source_target_pairs={{0,2},{2,0},{4,6},{6,4},{8,10},{10,8},{12,14},{14,12},{16,18},{18,... | collective-permute-start | bytes 1769480 | tf_op jit(solution)/shard_map/ppermute | solution.py:331
  39.2 25.2 %collective-permute-start.6 = (bf16[72,4096]{1,0:T(8,128)(2,1)S(1)}, bf16[72,4096]{1,0:T(8,128)(2,1)S(1)}, u32[]{:S(2)}, u32[]{:S(2)}) collective-permute-start(bf16[72,4096]{1,0:T(8,128)(2,1)S(1)} %get-tuple-element.72), channel_id=1, source_target_pairs={{0,4},{2,6},{4,0},{6,2},{8,12},{10,14},{12,8},{14,10},{16,20},{18,... | collective-permute-start | bytes 1769480 | tf_op jit(solution)/shard_map/ppermute | solution.py:331
  40.0 27.9 %collective-permute-start.7 = (bf16[72,4096]{1,0:T(8,128)(2,1)S(1)}, bf16[72,4096]{1,0:T(8,128)(2,1)S(1)}, u32[]{:S(2)}, u32[]{:S(2)}) collective-permute-start(bf16[72,4096]{1,0:T(8,128)(2,1)S(1)} %get-tuple-element.73), channel_id=1, source_target_pairs={{0,6},{2,4},{4,2},{6,0},{8,14},{10,12},{12,10},{14,8},{16,22},{18,... | collective-permute-start | bytes 1769480 | tf_op jit(solution)/shard_map/ppermute | solution.py:331
  41.5 10.5 %copy-start.2 = (bf16[128,2176]{1,0:T(8,128)(2,1)S(1)}, bf16[128,2176]{1,0:T(8,128)(2,1)}, u32[]{:S(2)}) copy-start(bf16[128,2176]{1,0:T(8,128)(2,1)} %get-tuple-element.63.refs_0_) | copy-start | bytes 1671172
  41.6 16.9 %collective-permute-start.13 = (bf16[2,72,1408]{2,1,0:T(8,128)(2,1)S(1)}, bf16[2,72,1408]{2,1,0:T(8,128)(2,1)S(1)}, u32[]{:S(2)}, u32[]{:S(2)}) collective-permute-start(bf16[2,72,1408]{2,1,0:T(8,128)(2,1)S(1)} %shard_map.84), channel_id=1, source_target_pairs={{0,8},{2,10},{4,12},{6,14},{8,16},{10,18},{12,20},{14,22},{16,24},... | collective-permute-start | bytes 1216520 | tf_op jit(solution)/shard_map/ppermute | solution.py:328
  50.0 20.6 %collective-permute-start.9 = (bf16[2,72,1408]{2,1,0:T(8,128)(2,1)S(1)}, bf16[2,72,1408]{2,1,0:T(8,128)(2,1)S(1)}, u32[]{:S(2)}, u32[]{:S(2)}) collective-permute-start(bf16[2,72,1408]{2,1,0:T(8,128)(2,1)S(1)} %shard_map.80), channel_id=1, source_target_pairs={{0,24},{2,26},{4,28},{6,30},{8,0},{10,2},{12,4},{14,6},{16,8},{18,... | collective-permute-start | bytes 1216520 | tf_op jit(solution)/shard_map/ppermute | solution.py:328
  52.5 16.1 %copy-start.1 = (bf16[1,704,2048]{2,1,0:T(8,128)(2,1)S(1)}, bf16[1,704,2048]{2,1,0:T(8,128)(2,1)}, u32[]{:S(2)}) copy-start(bf16[1,704,2048]{2,1,0:T(8,128)(2,1)} %param.9) | copy-start | bytes 8650756
  58.5 17.6 %collective-permute-start.14 = (bf16[72,2048]{1,0:T(8,128)(2,1)S(1)}, bf16[72,2048]{1,0:T(8,128)(2,1)S(1)}, u32[]{:S(2)}, u32[]{:S(2)}) collective-permute-start(bf16[72,2048]{1,0:T(8,128)(2,1)S(1)} %get-tuple-element.81), channel_id=1, source_target_pairs={{0,2},{2,0},{4,6},{6,4},{8,10},{10,8},{12,14},{14,12},{16,18},{18,... | collective-permute-start | bytes 884744 | tf_op jit(solution)/shard_map/ppermute | solution.py:331
  60.1 20.0 %collective-permute-start.15 = (bf16[72,2048]{1,0:T(8,128)(2,1)S(1)}, bf16[72,2048]{1,0:T(8,128)(2,1)S(1)}, u32[]{:S(2)}, u32[]{:S(2)}) collective-permute-start(bf16[72,2048]{1,0:T(8,128)(2,1)S(1)} %get-tuple-element.82), channel_id=1, source_target_pairs={{0,4},{2,6},{4,0},{6,2},{8,12},{10,14},{12,8},{14,10},{16,20},{18,... | collective-permute-start | bytes 884744 | tf_op jit(solution)/shard_map/ppermute | solution.py:331
  64.4 15.6 %collective-permute-start.16 = (bf16[72,2048]{1,0:T(8,128)(2,1)S(1)}, bf16[72,2048]{1,0:T(8,128)(2,1)S(1)}, u32[]{:S(2)}, u32[]{:S(2)}) collective-permute-start(bf16[72,2048]{1,0:T(8,128)(2,1)S(1)} %get-tuple-element.83), channel_id=1, source_target_pairs={{0,6},{2,4},{4,2},{6,0},{8,14},{10,12},{12,10},{14,8},{16,22},{18,... | collective-permute-start | bytes 884744 | tf_op jit(solution)/shard_map/ppermute | solution.py:331
  67.9 14.2 %collective-permute-start.17 = (bf16[2,72,1408]{2,1,0:T(8,128)(2,1)S(1)}, bf16[2,72,1408]{2,1,0:T(8,128)(2,1)S(1)}, u32[]{:S(2)}, u32[]{:S(2)}) collective-permute-start(bf16[2,72,1408]{2,1,0:T(8,128)(2,1)S(1)} %shard_map.86), channel_id=1, source_target_pairs={{0,16},{2,18},{4,20},{6,22},{8,24},{10,26},{12,28},{14,30},{16,0},... | collective-permute-start | bytes 1216520 | tf_op jit(solution)/shard_map/ppermute | solution.py:328
  70.7 15.6 %collective-permute-start.10 = (bf16[72,1024]{1,0:T(8,128)(2,1)S(1)}, bf16[72,1024]{1,0:T(8,128)(2,1)S(1)}, u32[]{:S(2)}, u32[]{:S(2)}) collective-permute-start(bf16[72,1024]{1,0:T(8,128)(2,1)S(1)} %get-tuple-element.74), channel_id=1, source_target_pairs={{0,2},{2,0},{4,6},{6,4},{8,10},{10,8},{12,14},{14,12},{16,18},{18,... | collective-permute-start | bytes 442376 | tf_op jit(solution)/shard_map/ppermute | solution.py:331
  76.1 10.6 %collective-permute-start.11 = (bf16[72,1024]{1,0:T(8,128)(2,1)S(1)}, bf16[72,1024]{1,0:T(8,128)(2,1)S(1)}, u32[]{:S(2)}, u32[]{:S(2)}) collective-permute-start(bf16[72,1024]{1,0:T(8,128)(2,1)S(1)} %get-tuple-element.75), channel_id=1, source_target_pairs={{0,4},{2,6},{4,0},{6,2},{8,12},{10,14},{12,8},{14,10},{16,20},{18,... | collective-permute-start | bytes 442376 | tf_op jit(solution)/shard_map/ppermute | solution.py:331
  80.1 6.7 %collective-permute-start.12 = (bf16[72,1024]{1,0:T(8,128)(2,1)S(1)}, bf16[72,1024]{1,0:T(8,128)(2,1)S(1)}, u32[]{:S(2)}, u32[]{:S(2)}) collective-permute-start(bf16[72,1024]{1,0:T(8,128)(2,1)S(1)} %get-tuple-element.76), channel_id=1, source_target_pairs={{0,6},{2,4},{4,2},{6,0},{8,14},{10,12},{12,10},{14,8},{16,22},{18,... | collective-permute-start | bytes 442376 | tf_op jit(solution)/shard_map/ppermute | solution.py:331
  84.2 7.4 %collective-permute-start.19 = (f32[4,128]{1,0:T(4,128)S(1)}, f32[4,128]{1,0:T(4,128)S(1)}, u32[]{:S(2)}, u32[]{:S(2)}) collective-permute-start(f32[4,128]{1,0:T(4,128)S(1)} %get-tuple-element.97.refs_2_), channel_id=1, source_target_pairs={{0,16},{2,18},{4,20},{6,22},{8,24},{10,26},{12,28},{14,30},{16,0},... | collective-permute-start | bytes 6152 | tf_op jit(solution)/shard_map/ppermute | solution.py:328
  84.3 5.9 %collective-permute-start.18 = (f32[4,128]{1,0:T(4,128)S(1)}, f32[4,128]{1,0:T(4,128)S(1)}, u32[]{:S(2)}, u32[]{:S(2)}) collective-permute-start(f32[4,128]{1,0:T(4,128)S(1)} %get-tuple-element.98), channel_id=1, source_target_pairs={{0,24},{2,26},{4,28},{6,30},{8,0},{10,2},{12,4},{14,6},{16,8},{18,... | collective-permute-start | bytes 6152 | tf_op jit(solution)/shard_map/ppermute | solution.py:328
  86.2 5.4 %collective-permute-start.20 = (f32[4,128]{1,0:T(4,128)S(1)}, f32[4,128]{1,0:T(4,128)S(1)}, u32[]{:S(2)}, u32[]{:S(2)}) collective-permute-start(f32[4,128]{1,0:T(4,128)S(1)} %get-tuple-element.99), channel_id=1, source_target_pairs={{0,8},{2,10},{4,12},{6,14},{8,16},{10,18},{12,20},{14,22},{16,24},... | collective-permute-start | bytes 6152 | tf_op jit(solution)/shard_map/ppermute | solution.py:328
  90.1 10.3 %copy-start.3 = (s32[128,6]{0,1:T(8,128)S(1)}, s32[128,6]{0,1:T(8,128)}, u32[]{:S(2)}) copy-start(s32[128,6]{0,1:T(8,128)} %param.7) | copy-start | bytes 9220
  90.1 10.3 %copy-start.4 = (s32[128,6]{0,1:T(8,128)S(1)}, s32[128,6]{0,1:T(8,128)}, u32[]{:S(2)}) copy-start(s32[128,6]{0,1:T(8,128)} %param.8) | copy-start | bytes 9220
  90.1 10.3 %copy-start.5 = (f32[16,128]{1,0:T(8,128)S(1)}, f32[16,128]{1,0:T(8,128)}, u32[]{:S(2)}) copy-start(f32[16,128]{1,0:T(8,128)} %get-tuple-element.102.refs_2_) | copy-start | bytes 24580
  90.1 7.3 %collective-permute-start.25 = (bf16[352,1024]{1,0:T(8,128)(2,1)S(1)}, bf16[352,1024]{1,0:T(8,128)(2,1)S(1)}, u32[]{:S(2)}, u32[]{:S(2)}) collective-permute-start(bf16[352,1024]{1,0:T(8,128)(2,1)S(1)} %get-tuple-element.104.refs_4_), channel_id=1, source_target_pairs={{0,1},{1,0},{2,3},{3,2},{4,5},{5,4},{6,7},{7,6},{8,9},{9,8},{10,11... | collective-permute-start | bytes 2162696 | tf_op jit(solution)/shard_map/ppermute | solution.py:450
  92.9 7.5 %collective-permute-start.21 = (bf16[352,1024]{1,0:T(8,128)(2,1)S(1)}, bf16[352,1024]{1,0:T(8,128)(2,1)S(1)}, u32[]{:S(2)}, u32[]{:S(2)}) collective-permute-start(bf16[352,1024]{1,0:T(8,128)(2,1)S(1)} %get-tuple-element.101), channel_id=1, source_target_pairs={{0,1},{1,0},{2,3},{3,2},{4,5},{5,4},{6,7},{7,6},{8,9},{9,8},{10,11... | collective-permute-start | bytes 2162696 | tf_op jit(solution)/shard_map/ppermute | solution.py:450
  93.0 5.8 %collective-permute-start.22 = (f32[4,128]{1,0:T(4,128)S(1)}, f32[4,128]{1,0:T(4,128)S(1)}, u32[]{:S(2)}, u32[]{:S(2)}) collective-permute-start(f32[4,128]{1,0:T(4,128)S(1)} %get-tuple-element.106), channel_id=1, source_target_pairs={{0,2},{2,0},{4,6},{6,4},{8,10},{10,8},{12,14},{14,12},{16,18},{18,... | collective-permute-start | bytes 6152 | tf_op jit(solution)/shard_map/ppermute | solution.py:331
  95.9 3.6 %collective-permute-start.23 = (f32[4,128]{1,0:T(4,128)S(1)}, f32[4,128]{1,0:T(4,128)S(1)}, u32[]{:S(2)}, u32[]{:S(2)}) collective-permute-start(f32[4,128]{1,0:T(4,128)S(1)} %get-tuple-element.107), channel_id=1, source_target_pairs={{0,4},{2,6},{4,0},{6,2},{8,12},{10,14},{12,8},{14,10},{16,20},{18,... | collective-permute-start | bytes 6152 | tf_op jit(solution)/shard_map/ppermute | solution.py:331
  95.9 4.5 %collective-permute-start.24 = (f32[4,128]{1,0:T(4,128)S(1)}, f32[4,128]{1,0:T(4,128)S(1)}, u32[]{:S(2)}, u32[]{:S(2)}) collective-permute-start(f32[4,128]{1,0:T(4,128)S(1)} %get-tuple-element.108), channel_id=1, source_target_pairs={{0,6},{2,4},{4,2},{6,0},{8,14},{10,12},{12,10},{14,8},{16,22},{18,... | collective-permute-start | bytes 6152 | tf_op jit(solution)/shard_map/ppermute | solution.py:331

commit v9 on v8

--- a/solution.py
+++ b/solution.py
@@ -223,6 +223,54 @@
     second.wait()
 
 
+def own_left_kernel(stride, at, *refs):
+    pieces, (w_ref, hid_ref) = refs[:PLANE], refs[PLANE : PLANE + 2]
+    all_rows, all_hidw, back_ref, hidw_ref, rows, hids, done = refs[PLANE + 2 :]
+    group, lead = rows.shape
+    width, whole = hidw_ref.shape[0], hids.shape[1]
+    spare = whole - width
+    for k in range(PLANE):
+        fill(rows, k * stride, pieces[k][:, at : at + lead], stride)
+        first = k % 2 * (width - spare)
+        piece = hid_ref[k // 2, :, first : first + whole]
+        fill(hids, k * stride, moved(piece, -(k % 2) * spare), stride)
+    hidw_ref[...] = hids[...].T[0:width, :].astype(BF)
+    copies = [
+        pltpu.make_async_copy(
+            rows, all_rows.at[pl.ds(group, group), pl.ds(0, lead)], done.at[0]
+        ),
+        pltpu.make_async_copy(hidw_ref, all_hidw.at[:, pl.ds(group, group)], done.at[1]),
+    ]
+    for copy in copies:
+        copy.start()
+    back_ref[...] = lax.dot_general(
+        w_ref[:, 0:lead], rows[...], NT, preferred_element_type=F32
+    )
+    for copy in copies:
+        copy.wait()
+
+
+def own_right_kernel(stride, flip, *refs):
+    pieces, (w_ref, back_ref, hidw_ref) = refs[:PLANE], refs[PLANE : PLANE + 3]
+    rows_ref, gate_ref = refs[-2:]
+    lead = w_ref.shape[1] - rows_ref.shape[1]
+    for k in range(PLANE):
+        fill(rows_ref, k * stride, pieces[k][...], stride)
+    back = back_ref[...] + lax.dot_general(
+        w_ref[:, lead:], rows_ref[...], NT, preferred_element_type=F32
+    )
+    half = back.shape[0] // 2
+    turned = halves(flip)[0] == 1
+    low = hidw_ref[0:half, :].astype(F32)
+    high = hidw_ref[half:, :].astype(F32)
+    terms = back[0:half, :] * jnp.where(turned, high, low)
+    terms += back[half:, :] * jnp.where(turned, low, high)
+    gate = jnp.sum(terms, axis=0, keepdims=True)
+    gate_ref[...] = jnp.zeros_like(gate_ref)
+    for k in range(PLANE):
+        gate_ref[k : k + 1, 0:stride] = gate[:, k * stride : (k + 1) * stride]
+
+
 def source(outer, s, k):
     me = lax.axis_index("expert")
     return lax.rem((me >> 2) - s + outer, outer) * PLANE + ((me & 3) ^ k)
@@ -236,14 +284,19 @@
         out_ref[:, span] = got.astype(BF)
 
 
-def partial_kernel(first, step, rows_ref, hidw_ref, early_ref, *refs):
+def partial_kernel(first, step, late, rows_ref, hidw_ref, early_ref, *refs):
     send_ref, mine_ref = refs[-2:]
     half = mine_ref.shape[0]
     for c in range(0, mine_ref.shape[1], step):
         span, here = slice(first + c, first + c + step), slice(c, c + step)
-        got = early_ref[:, span].astype(F32) + jnp.dot(
-            hidw_ref[...], rows_ref[:, span], preferred_element_type=F32
-        )
+        got = early_ref[:, span].astype(F32)
+        if late:
+            group = refs[0].shape[0]
+            got += jnp.dot(
+                hidw_ref[:, 0:group], rows_ref[0:group, span], preferred_element_type=F32
+            ) + jnp.dot(hidw_ref[:, group:], refs[0][:, here], preferred_element_type=F32)
+        else:
+            got += jnp.dot(hidw_ref[...], rows_ref[:, span], preferred_element_type=F32)
         send_ref[:, here] = got[0:half].astype(BF)
         mine_ref[:, here] = got[half:].astype(BF)
 
@@ -428,22 +481,40 @@
         [sds((width, model), BF), sds((8, BLOCK), F32)],
         flops=3_500_000_000,
     )(*rows)
+    *rows, back, own_hidw = call(
+        functools.partial(own_left_kernel, stride, wide - lead),
+        [
+            sds((2 * group, model), BF),
+            sds((width, 2 * group), BF),
+            sds((width, group), F32),
+            sds((width, group), BF),
+        ],
+        flops=2_000_000_000,
+        in_specs=[inside] * (PLANE + 2),
+        out_specs=[anywhere] * 2 + [inside] * 2,
+        scratch_shapes=[
+            pltpu.VMEM((group, lead), BF),
+            pltpu.VMEM((group, up(width, BLOCK)), F32),
+            pltpu.SemaphoreType.DMA((2,)),
+        ],
+    )(*opening, w_down[0], hids[0])
     *rows, gates[order[-1]] = stage(
-        sources[order[-1]], hids[order[-1]], 0, 2, [mark], []
+        sources[order[-1]], hids[order[-1]], 0, 2, [mark], rows
     )
     for s, gate in zip(
         order[1:-1], gated([gates[s] for s in order[1:-1]], [gates[order[-1]]])
     ):
         gates[s] = gate
-    *rows, gates[0] = stage(sources[0], hids[0], 1, 2, [], rows)
+    gates[0] = None
     gates = [ring(gates[s], -s) if s else gates[s] for s in range(outer)]
 
-    def partial(first, after):
+    def partial(first, more, after):
         return call(
-            functools.partial(partial_kernel, first, step),
+            functools.partial(partial_kernel, first, step, bool(more)),
             [sds((half, model // 2), BF)] * 2,
-            in_specs=[inside] * 3 + [anywhere] * len(after),
-        )(*rows, early, *after)
+            flops=4_000_000_000,
+            in_specs=[inside] * (3 + len(more)) + [anywhere] * len(after),
+        )(*rows, early, *more, *after)
 
     def finish(first, send, mine, out, extra):
         if flip:
@@ -475,8 +546,15 @@
             scratch_shapes=scratch,
         )(*own, others, *extra, *out)
 
-    left = partial(0, [])
-    right = partial(model // 2, gates[1:])
+    left = partial(0, [], [])
+    own_rows, gates[0] = call(
+        functools.partial(own_right_kernel, stride, flip),
+        [sds((group, model - lead), BF), sds((PLANE, BLOCK), F32)],
+        flops=4_000_000_000,
+        in_specs=[inside] * (PLANE + 3) + [anywhere],
+    )(*final, w_down[0], back, own_hidw, left[0])
+    right = partial(model // 2, [own_rows], [])
+    right = [*gated(right[:1], gates[1:]), right[1]]
     homes = call(
         functools.partial(combine_kernel, outer),
         [sds((outer, BLOCK), F32)] * PLANE,

time: 103 us -> 103 us (level)
  waiting for transfers between devices: 51 us -> 49.7 us
    pallas_call x2 -> x4, Pallas kernels: 2.6 us -> 5.51 us  [the longest x2 2.95 us: partial(): call(functools.partial(partial_kernel, first, step, bool(more)), [sds((ha...]
    pallas_call x4 -> x3, Pallas kernels: 8.22 us -> 6.17 us  [stage(): call(functools.partial(stage_kernel, place, [span for _, span in parts],...]
    ppermute x9, waiting for transfers between devices: 38 us -> 36.8 us  [ring(): return lax.ppermute(array, 'expert', pairs)]
  transfers between devices with their start and end apart: 26 -> 26, of which waited for: 12 -> 12; matrix products, arithmetic and copies ran while one was open for 0% -> 0% of each run, Pallas kernels for 16% -> 17%
where the time goes in v9:
time: 103 us
  waiting for transfers between devices  49.7 us (48%)
  starting transfers between devices  27.1 us (26%)
  Pallas kernels  24.6 us (24%)
  between operations  1.11 us (1%)
    ppermute x9, waiting for transfers between devices, ring(): return lax.ppermute(array, 'expert', pairs)  36.8 us
    ppermute x15, starting transfers between devices, swap(): return lax.ppermute(array, 'expert', [(e, e ^ k) for e in range(experts)])  16.3 us
    ppermute x15, waiting for transfers between devices, swap(): return lax.ppermute(array, 'expert', [(e, e ^ k) for e in range(experts)])  13 us
    ppermute x9, starting transfers between devices, ring(): return lax.ppermute(array, 'expert', pairs)  10.7 us
    pallas_call x3, Pallas kernels, stage(): call(functools.partial(stage_kernel, place, [span for _, span in parts],...  6.17 us
    pallas_call x1, Pallas kernels, per_device(): call(functools.partial(open_kernel, slots, flip), [sds((tokens, model + B...  4.89 us
    pallas_call x2, Pallas kernels, finish(): call(functools.partial(finish_kernel, first, fine, len(own), bool(extra))...  3.29 us
    pallas_call x2, Pallas kernels, partial(): call(functools.partial(partial_kernel, first, step, bool(more)), [sds((ha...  2.95 us
  transfers between devices with their start and end apart: 26, of which 12 were waited for; matrix products, arithmetic and copies ran while one was open for 0% of the time, Pallas kernels for 17%

profile of v9, /device:TPU:0, one launch (start us, length us, event | category | flops | bytes accessed | tf_op | source)
XLA Modules:
  0.0 102.5 jit_solution(4032588638950664396)
XLA Ops:
  0.6 4.9 %shard_map.76 = (bf16[128,2176]{1,0:T(8,128)(2,1)}, bf16[72,3840]{1,0:T(8,128)(2,1)}, bf16[72,3840]{1,0:T(8,128)(2,1)}, bf16[72,3840]{1,0:T(8,128)(2,1)}, bf16[72,3840]{1,0:T(8,128)(2,1)}, /*index=5*/f32[16,128]{1,0:T(8,128)}) custom-call(s32[6,128]{1,0:T(8,128)} %bitcast.18, s32[6,128]{1,0:T(8,128)} %bitcast.20, bf16[6,704,128]{2,1,0:T(8,128)(2,1)} %bitcast.23, ...), custom_call_target="tpu_custom_call" | custom-call | flops 1024 | bytes 1024 | tf_op jit(solution)/shard_map/pallas_call | solution.py:391
  5.5 3.1 %collective-permute-start = (bf16[128,2176]{1,0:T(8,128)(2,1)}, bf16[128,2176]{1,0:T(8,128)(2,1)S(1)}, u32[]{:S(2)}, u32[]{:S(2)}) collective-permute-start(bf16[128,2176]{1,0:T(8,128)(2,1)} %get-tuple-element.62.refs_0_), channel_id=1, source_target_pairs={{0,8},{2,10},{4,12},{6,14},{8,16},{10,18},{12,20},{14,22},{16,24},... | collective-permute-start | bytes 1671176 | tf_op jit(solution)/shard_map/ppermute | solution.py:381
  8.6 2.1 %collective-permute-start.10 = (bf16[128,2176]{1,0:T(8,128)(2,1)}, bf16[128,2176]{1,0:T(8,128)(2,1)S(1)}, u32[]{:S(2)}, u32[]{:S(2)}) collective-permute-start(bf16[128,2176]{1,0:T(8,128)(2,1)} %get-tuple-element.62.refs_0_), channel_id=1, source_target_pairs={{0,24},{2,26},{4,28},{6,30},{8,0},{10,2},{12,4},{14,6},{16,8},{18,... | collective-permute-start | bytes 1671176 | tf_op jit(solution)/shard_map/ppermute | solution.py:381
  10.7 1.6 %collective-permute-start.2 = (bf16[72,3840]{1,0:T(8,128)(2,1)}, bf16[72,3840]{1,0:T(8,128)(2,1)S(1)}, u32[]{:S(2)}, u32[]{:S(2)}) collective-permute-start(bf16[72,3840]{1,0:T(8,128)(2,1)} %get-tuple-element.68), channel_id=1, source_target_pairs={{0,2},{2,0},{4,6},{6,4},{8,10},{10,8},{12,14},{14,12},{16,18},{18,... | collective-permute-start | bytes 1658888 | tf_op jit(solution)/shard_map/ppermute | solution.py:384
  12.4 1.5 %collective-permute-start.3 = (bf16[72,3840]{1,0:T(8,128)(2,1)}, bf16[72,3840]{1,0:T(8,128)(2,1)S(1)}, u32[]{:S(2)}, u32[]{:S(2)}) collective-permute-start(bf16[72,3840]{1,0:T(8,128)(2,1)} %get-tuple-element.69), channel_id=1, source_target_pairs={{0,4},{2,6},{4,0},{6,2},{8,12},{10,14},{12,8},{14,10},{16,20},{18,... | collective-permute-start | bytes 1658888 | tf_op jit(solution)/shard_map/ppermute | solution.py:384
  14.2 10.2 %collective-permute-done.refs_0_ = bf16[128,2176]{1,0:T(8,128)(2,1)S(1)} collective-permute-done((bf16[128,2176]{1,0:T(8,128)(2,1)}, bf16[128,2176]{1,0:T(8,128)(2,1)S(1)}, u32[]{:S(2)}, u32[]{:S(2)}) %collective-permute-start) | collective-permute-done | bytes 557088 | tf_op jit(solution)/shard_map/ppermute | solution.py:381
  24.4 10.7 %collective-permute-done.10.refs_1_ = bf16[128,2176]{1,0:T(8,128)(2,1)S(1)} collective-permute-done((bf16[128,2176]{1,0:T(8,128)(2,1)}, bf16[128,2176]{1,0:T(8,128)(2,1)S(1)}, u32[]{:S(2)}, u32[]{:S(2)}) %collective-permute-start.10) | collective-permute-done | bytes 557088 | tf_op jit(solution)/shard_map/ppermute | solution.py:381
  35.9 2.0 %collective-permute-done.3.refs_2_.refs_4_ = bf16[72,3840]{1,0:T(8,128)(2,1)S(1)} collective-permute-done((bf16[72,3840]{1,0:T(8,128)(2,1)}, bf16[72,3840]{1,0:T(8,128)(2,1)S(1)}, u32[]{:S(2)}, u32[]{:S(2)}) %collective-permute-start.3) | collective-permute-done | bytes 552992 | tf_op jit(solution)/shard_map/ppermute | solution.py:384
  38.0 1.2 %collective-permute-start.11 = (bf16[72,4096]{1,0:T(8,128)(2,1)S(1)}, bf16[72,4096]{1,0:T(8,128)(2,1)S(1)}, u32[]{:S(2)}, u32[]{:S(2)}) collective-permute-start(bf16[72,4096]{1,0:T(8,128)(2,1)S(1)} %get-tuple-element.80), channel_id=1, source_target_pairs={{0,2},{2,0},{4,6},{6,4},{8,10},{10,8},{12,14},{14,12},{16,18},{18,... | collective-permute-start | bytes 1769480 | tf_op jit(solution)/shard_map/ppermute | solution.py:384
  40.0 1.4 %collective-permute-start.13 = (bf16[72,4096]{1,0:T(8,128)(2,1)S(1)}, bf16[72,4096]{1,0:T(8,128)(2,1)S(1)}, u32[]{:S(2)}, u32[]{:S(2)}) collective-permute-start(bf16[72,4096]{1,0:T(8,128)(2,1)S(1)} %get-tuple-element.82), channel_id=1, source_target_pairs={{0,6},{2,4},{4,2},{6,0},{8,14},{10,12},{12,10},{14,8},{16,22},{18,... | collective-permute-start | bytes 1769480 | tf_op jit(solution)/shard_map/ppermute | solution.py:384
  41.7 8.2 %collective-permute-done.1.refs_0_.refs_4_ = bf16[128,2176]{1,0:T(8,128)(2,1)S(1)} collective-permute-done((bf16[128,2176]{1,0:T(8,128)(2,1)S(1)}, bf16[128,2176]{1,0:T(8,128)(2,1)S(1)}, u32[]{:S(2)}, u32[]{:S(2)}) %collective-permute-start.1) | collective-permute-done | bytes 557088 | tf_op jit(solution)/shard_map/ppermute | solution.py:381
  50.0 2.1 %collective-permute-start.14 = (bf16[2,72,1408]{2,1,0:T(8,128)(2,1)S(1)}, bf16[2,72,1408]{2,1,0:T(8,128)(2,1)S(1)}, u32[]{:S(2)}, u32[]{:S(2)}) collective-permute-start(bf16[2,72,1408]{2,1,0:T(8,128)(2,1)S(1)} %shard_map.85), channel_id=1, source_target_pairs={{0,24},{2,26},{4,28},{6,30},{8,0},{10,2},{12,4},{14,6},{16,8},{18,... | collective-permute-start | bytes 1216520 | tf_op jit(solution)/shard_map/ppermute | solution.py:381
  52.7 1.4 %shard_map.82 = (bf16[768,2048]{1,0:T(8,128)(2,1)S(1)}, bf16[704,768]{1,0:T(8,128)(2,1)S(1)}, f32[704,384]{1,0:T(8,128)S(1)}, bf16[704,384]{1,0:T(8,128)(2,1)S(1)}) custom-call(bf16[72,3840]{1,0:T(8,128)(2,1)S(1)} %copy-done.1, bf16[72,3840]{1,0:T(8,128)(2,1)S(1)} %collective-permute-done.2.refs_1_.refs_3_, ...), custom_call_target="tpu_custom_call" | custom-call | flops 2000000000 | bytes 1024 | tf_op jit(solution)/shard_map/pallas_call | solution.py:484
  54.6 3.8 %collective-permute-done.5.refs_3_.refs_5_ = bf16[2,72,1408]{2,1,0:T(8,128)(2,1)S(1)} collective-permute-done((bf16[2,72,1408]{2,1,0:T(8,128)(2,1)S(1)}, bf16[2,72,1408]{2,1,0:T(8,128)(2,1)S(1)}, u32[]{:S(2)}, u32[]{:S(2)}) %collective-permute-start.5) | collective-permute-done | bytes 405536 | tf_op jit(solution)/shard_map/ppermute | solution.py:381
  58.5 1.5 %collective-permute-start.6 = (bf16[72,2048]{1,0:T(8,128)(2,1)S(1)}, bf16[72,2048]{1,0:T(8,128)(2,1)S(1)}, u32[]{:S(2)}, u32[]{:S(2)}) collective-permute-start(bf16[72,2048]{1,0:T(8,128)(2,1)S(1)} %get-tuple-element.71), channel_id=1, source_target_pairs={{0,2},{2,0},{4,6},{6,4},{8,10},{10,8},{12,14},{14,12},{16,18},{18,... | collective-permute-start | bytes 884744 | tf_op jit(solution)/shard_map/ppermute | solution.py:384
  60.1 1.6 %collective-permute-start.7 = (bf16[72,2048]{1,0:T(8,128)(2,1)S(1)}, bf16[72,2048]{1,0:T(8,128)(2,1)S(1)}, u32[]{:S(2)}, u32[]{:S(2)}) collective-permute-start(bf16[72,2048]{1,0:T(8,128)(2,1)S(1)} %get-tuple-element.72), channel_id=1, source_target_pairs={{0,4},{2,6},{4,0},{6,2},{8,12},{10,14},{12,8},{14,10},{16,20},{18,... | collective-permute-start | bytes 884744 | tf_op jit(solution)/shard_map/ppermute | solution.py:384
  61.7 2.8 %collective-permute-done.12.refs_2_.refs_4_ = bf16[72,4096]{1,0:T(8,128)(2,1)S(1)} collective-permute-done((bf16[72,4096]{1,0:T(8,128)(2,1)S(1)}, bf16[72,4096]{1,0:T(8,128)(2,1)S(1)}, u32[]{:S(2)}, u32[]{:S(2)}) %collective-permute-start.12) | collective-permute-done | bytes 589856 | tf_op jit(solution)/shard_map/ppermute | solution.py:384
  64.4 3.5 %collective-permute-done.13.refs_3_.refs_5_ = bf16[72,4096]{1,0:T(8,128)(2,1)S(1)} collective-permute-done((bf16[72,4096]{1,0:T(8,128)(2,1)S(1)}, bf16[72,4096]{1,0:T(8,128)(2,1)S(1)}, u32[]{:S(2)}, u32[]{:S(2)}) %collective-permute-start.13) | collective-permute-done | bytes 589856 | tf_op jit(solution)/shard_map/ppermute | solution.py:384
  68.6 2.0 %shard_map.86 = (bf16[768,2048]{1,0:T(8,128)(2,1)S(1)}, bf16[704,768]{1,0:T(8,128)(2,1)S(1)}, f32[4,128]{1,0:T(4,128)S(1)}) custom-call(bf16[72,4096]{1,0:T(8,128)(2,1)S(1)} %get-tuple-element.76.refs_0_, bf16[72,4096]{1,0:T(8,128)(2,1)S(1)} %collective-permute-done.11.refs_1_.refs_3_, bf16[72,4096]{1,0:T(8,128)(2,1)S(1)} %collective-permute-done.12.refs_2_.refs_4_, ...), custom_call_target="tpu_custom_call" | custom-call | flops 2000000000 | bytes 1024 | tf_op jit(solution)/shard_map/pallas_call | solution.py:454
  71.6 2.1 %shard_map.87 = (bf16[768,2048]{1,0:T(8,128)(2,1)S(1)}, bf16[704,768]{1,0:T(8,128)(2,1)S(1)}, f32[4,128]{1,0:T(4,128)S(1)}) custom-call(bf16[72,4096]{1,0:T(8,128)(2,1)S(1)} %get-tuple-element.76.refs_0_, bf16[72,4096]{1,0:T(8,128)(2,1)S(1)} %collective-permute-done.11.refs_1_.refs_3_, ...), custom_call_target="tpu_custom_call", output_to_operand_aliasing={{0}: (6, {}), {1}: (7, {})} | custom-call | flops 2000000000 | bytes 1024 | tf_op jit(solution)/shard_map/pallas_call | solution.py:454
  73.7 2.4 %shard_map.88 = (bf16[704,2048]{1,0:T(8,128)(2,1)S(1)}, f32[8,128]{1,0:T(8,128)S(1)}) custom-call(bf16[768,2048]{1,0:T(8,128)(2,1)S(1)} %get-tuple-element.85.rows_ref, bf16[704,768]{1,0:T(8,128)(2,1)S(1)} %get-tuple-element.86.hidw_ref), custom_call_target="tpu_custom_call" | custom-call | flops 3500000000 | bytes 1024 | tf_op jit(solution)/shard_map/pallas_call | solution.py:479
  77.0 3.1 %collective-permute-done.7.refs_2_ = bf16[72,2048]{1,0:T(8,128)(2,1)S(1)} collective-permute-done((bf16[72,2048]{1,0:T(8,128)(2,1)S(1)}, bf16[72,2048]{1,0:T(8,128)(2,1)S(1)}, u32[]{:S(2)}, u32[]{:S(2)}) %collective-permute-start.7) | collective-permute-done | bytes 294944 | tf_op jit(solution)/shard_map/ppermute | solution.py:384
  80.1 2.1 %collective-permute-done.9.refs_5_ = bf16[2,72,1408]{2,1,0:T(8,128)(2,1)S(1)} collective-permute-done((bf16[2,72,1408]{2,1,0:T(8,128)(2,1)S(1)}, bf16[2,72,1408]{2,1,0:T(8,128)(2,1)S(1)}, u32[]{:S(2)}, u32[]{:S(2)}) %collective-permute-start.9) | collective-permute-done | bytes 405536 | tf_op jit(solution)/shard_map/ppermute | solution.py:381
  82.2 2.1 %shard_map.89 = (bf16[768,2048]{1,0:T(8,128)(2,1)S(1)}, bf16[704,768]{1,0:T(8,128)(2,1)S(1)}, f32[4,128]{1,0:T(4,128)S(1)}) custom-call(bf16[72,2048]{1,0:T(8,128)(2,1)S(1)} %get-tuple-element.63.refs_0_, bf16[72,2048]{1,0:T(8,128)(2,1)S(1)} %collective-permute-done.6.refs_1_, ...), custom_call_target="tpu_custom_call", output_to_operand_aliasing={{0}: (6, {}), {1}: (7, {})} | custom-call | flops 2000000000 | bytes 1024 | tf_op jit(solution)/shard_map/pallas_call | solution.py:454
  84.2 1.3 %shard_map.92 = (bf16[352,1024]{1,0:T(8,128)(2,1)S(1)}, bf16[352,1024]{1,0:T(8,128)(2,1)S(1)}) custom-call(bf16[768,2048]{1,0:T(8,128)(2,1)S(1)} %get-tuple-element.88.rows_ref, bf16[704,768]{1,0:T(8,128)(2,1)S(1)} %get-tuple-element.89.hidw_ref, bf16[704,2048]{1,0:T(8,128)(2,1)S(1)} %get-tuple-element.90.early_ref), custom_call_target="tpu_custom_call" | custom-call | flops 4000000000 | bytes 1024 | tf_op jit(solution)/shard_map/pallas_call | solution.py:512
  85.7 1.9 %collective-permute-start.18 = (f32[4,128]{1,0:T(4,128)S(1)}, f32[4,128]{1,0:T(4,128)S(1)}, u32[]{:S(2)}, u32[]{:S(2)}) collective-permute-start(f32[4,128]{1,0:T(4,128)S(1)} %get-tuple-element.107), channel_id=1, source_target_pairs={{0,24},{2,26},{4,28},{6,30},{8,0},{10,2},{12,4},{14,6},{16,8},{18,... | collective-permute-start | bytes 6152 | tf_op jit(solution)/shard_map/ppermute | solution.py:381
  89.5 1.7 %shard_map.94 = (bf16[352,1024]{1,0:T(8,128)(2,1)S(1)}, bf16[352,1024]{1,0:T(8,128)(2,1)S(1)}) custom-call(bf16[768,2048]{1,0:T(8,128)(2,1)S(1)} %get-tuple-element.88.rows_ref, bf16[704,768]{1,0:T(8,128)(2,1)S(1)} %get-tuple-element.89.hidw_ref, bf16[704,2048]{1,0:T(8,128)(2,1)S(1)} %get-tuple-element.90.early_ref, ...), custom_call_target="tpu_custom_call" | custom-call | flops 4000000000 | bytes 1024 | tf_op jit(solution)/shard_map/pallas_call | solution.py:512
  91.2 1.8 %collective-permute-done.20.refs_3_ = f32[4,128]{1,0:T(4,128)S(1)} collective-permute-done((f32[4,128]{1,0:T(4,128)S(1)}, f32[4,128]{1,0:T(4,128)S(1)}, u32[]{:S(2)}, u32[]{:S(2)}) %collective-permute-start.20) | collective-permute-done | bytes 2080 | tf_op jit(solution)/shard_map/ppermute | solution.py:381
  93.0 2.9 %collective-permute-start.22 = (f32[4,128]{1,0:T(4,128)S(1)}, f32[4,128]{1,0:T(4,128)S(1)}, u32[]{:S(2)}, u32[]{:S(2)}) collective-permute-start(f32[4,128]{1,0:T(4,128)S(1)} %get-tuple-element.112), channel_id=1, source_target_pairs={{0,2},{2,0},{4,6},{6,4},{8,10},{10,8},{12,14},{14,12},{16,18},{18,... | collective-permute-start | bytes 6152 | tf_op jit(solution)/shard_map/ppermute | solution.py:384
  95.9 1.5 %collective-permute-start.24 = (f32[4,128]{1,0:T(4,128)S(1)}, f32[4,128]{1,0:T(4,128)S(1)}, u32[]{:S(2)}, u32[]{:S(2)}) collective-permute-start(f32[4,128]{1,0:T(4,128)S(1)} %get-tuple-element.114), channel_id=1, source_target_pairs={{0,6},{2,4},{4,2},{6,0},{8,14},{10,12},{12,10},{14,8},{16,22},{18,... | collective-permute-start | bytes 6152 | tf_op jit(solution)/shard_map/ppermute | solution.py:384
  97.4 1.3 %shard_map.98 = (f32[352,2048]{1,0:T(8,128)}, f32[16,352]{1,0:T(8,128)}) custom-call(bf16[352,1024]{1,0:T(8,128)(2,1)S(1)} %get-tuple-element.115.refs_0_, bf16[1,352,1024]{2,1,0:T(8,128)(2,1)S(1)} %bitcast.16), custom_call_target="tpu_custom_call" | custom-call | flops 1024 | bytes 1024 | tf_op jit(solution)/shard_map/pallas_call | solution.py:540
  100.4 1.9 %shard_map.99 = (f32[352,2048]{1,0:T(8,128)}, f32[16,352]{1,0:T(8,128)}, f32[6,128]{1,0:T(8,128)}) custom-call(bf16[352,1024]{1,0:T(8,128)(2,1)S(1)} %get-tuple-element.102.refs_0_, bf16[1,352,1024]{2,1,0:T(8,128)(2,1)S(1)} %bitcast.17, f32[16,128]{1,0:T(8,128)S(1)} %copy-done.5, ...), custom_call_target="tpu_custom_call", output_to_operand_aliasing={{0}: (9, {}), {1}: (10, {})} | custom-call | flops 1024 | bytes 1024 | tf_op jit(solution)/shard_map/pallas_call | solution.py:540
  (56 shorter events, 9.7 us)
Async XLA Ops:
  5.5 35.9 %copy-start.1 = (bf16[72,3840]{1,0:T(8,128)(2,1)S(1)}, bf16[72,3840]{1,0:T(8,128)(2,1)}, u32[]{:S(2)}) copy-start(bf16[72,3840]{1,0:T(8,128)(2,1)} %get-tuple-element.67.refs_0_) | copy-start | bytes 1658884
  5.5 18.8 %collective-permute-start = (bf16[128,2176]{1,0:T(8,128)(2,1)}, bf16[128,2176]{1,0:T(8,128)(2,1)S(1)}, u32[]{:S(2)}, u32[]{:S(2)}) collective-permute-start(bf16[128,2176]{1,0:T(8,128)(2,1)} %get-tuple-element.62.refs_0_), channel_id=1, source_target_pairs={{0,8},{2,10},{4,12},{6,14},{8,16},{10,18},{12,20},{14,22},{16,24},... | collective-permute-start | bytes 1671176 | tf_op jit(solution)/shard_map/ppermute | solution.py:381
  8.6 26.5 %collective-permute-start.10 = (bf16[128,2176]{1,0:T(8,128)(2,1)}, bf16[128,2176]{1,0:T(8,128)(2,1)S(1)}, u32[]{:S(2)}, u32[]{:S(2)}) collective-permute-start(bf16[128,2176]{1,0:T(8,128)(2,1)} %get-tuple-element.62.refs_0_), channel_id=1, source_target_pairs={{0,24},{2,26},{4,28},{6,30},{8,0},{10,2},{12,4},{14,6},{16,8},{18,... | collective-permute-start | bytes 1671176 | tf_op jit(solution)/shard_map/ppermute | solution.py:381
  10.7 25.2 %collective-permute-start.2 = (bf16[72,3840]{1,0:T(8,128)(2,1)}, bf16[72,3840]{1,0:T(8,128)(2,1)S(1)}, u32[]{:S(2)}, u32[]{:S(2)}) collective-permute-start(bf16[72,3840]{1,0:T(8,128)(2,1)} %get-tuple-element.68), channel_id=1, source_target_pairs={{0,2},{2,0},{4,6},{6,4},{8,10},{10,8},{12,14},{14,12},{16,18},{18,... | collective-permute-start | bytes 1658888 | tf_op jit(solution)/shard_map/ppermute | solution.py:384
  12.4 25.6 %collective-permute-start.3 = (bf16[72,3840]{1,0:T(8,128)(2,1)}, bf16[72,3840]{1,0:T(8,128)(2,1)S(1)}, u32[]{:S(2)}, u32[]{:S(2)}) collective-permute-start(bf16[72,3840]{1,0:T(8,128)(2,1)} %get-tuple-element.69), channel_id=1, source_target_pairs={{0,4},{2,6},{4,0},{6,2},{8,12},{10,14},{12,8},{14,10},{16,20},{18,... | collective-permute-start | bytes 1658888 | tf_op jit(solution)/shard_map/ppermute | solution.py:384
  13.9 24.1 %collective-permute-start.4 = (bf16[72,3840]{1,0:T(8,128)(2,1)}, bf16[72,3840]{1,0:T(8,128)(2,1)S(1)}, u32[]{:S(2)}, u32[]{:S(2)}) collective-permute-start(bf16[72,3840]{1,0:T(8,128)(2,1)} %get-tuple-element.70), channel_id=1, source_target_pairs={{0,6},{2,4},{4,2},{6,0},{8,14},{10,12},{12,10},{14,8},{16,22},{18,... | collective-permute-start | bytes 1658888 | tf_op jit(solution)/shard_map/ppermute | solution.py:384
  24.4 25.5 %collective-permute-start.1 = (bf16[128,2176]{1,0:T(8,128)(2,1)S(1)}, bf16[128,2176]{1,0:T(8,128)(2,1)S(1)}, u32[]{:S(2)}, u32[]{:S(2)}) collective-permute-start(bf16[128,2176]{1,0:T(8,128)(2,1)S(1)} %collective-permute-done.refs_0_), channel_id=1, source_target_pairs={{0,8},{2,10},{4,12},{6,14},{8,16},{10,18},{12,20},{14,22},{16,24},... | collective-permute-start | bytes 1671176 | tf_op jit(solution)/shard_map/ppermute | solution.py:381
  38.0 22.1 %collective-permute-start.11 = (bf16[72,4096]{1,0:T(8,128)(2,1)S(1)}, bf16[72,4096]{1,0:T(8,128)(2,1)S(1)}, u32[]{:S(2)}, u32[]{:S(2)}) collective-permute-start(bf16[72,4096]{1,0:T(8,128)(2,1)S(1)} %get-tuple-element.80), channel_id=1, source_target_pairs={{0,2},{2,0},{4,6},{6,4},{8,10},{10,8},{12,14},{14,12},{16,18},{18,... | collective-permute-start | bytes 1769480 | tf_op jit(solution)/shard_map/ppermute | solution.py:384
  39.2 25.2 %collective-permute-start.12 = (bf16[72,4096]{1,0:T(8,128)(2,1)S(1)}, bf16[72,4096]{1,0:T(8,128)(2,1)S(1)}, u32[]{:S(2)}, u32[]{:S(2)}) collective-permute-start(bf16[72,4096]{1,0:T(8,128)(2,1)S(1)} %get-tuple-element.81), channel_id=1, source_target_pairs={{0,4},{2,6},{4,0},{6,2},{8,12},{10,14},{12,8},{14,10},{16,20},{18,... | collective-permute-start | bytes 1769480 | tf_op jit(solution)/shard_map/ppermute | solution.py:384
  40.0 27.9 %collective-permute-start.13 = (bf16[72,4096]{1,0:T(8,128)(2,1)S(1)}, bf16[72,4096]{1,0:T(8,128)(2,1)S(1)}, u32[]{:S(2)}, u32[]{:S(2)}) collective-permute-start(bf16[72,4096]{1,0:T(8,128)(2,1)S(1)} %get-tuple-element.82), channel_id=1, source_target_pairs={{0,6},{2,4},{4,2},{6,0},{8,14},{10,12},{12,10},{14,8},{16,22},{18,... | collective-permute-start | bytes 1769480 | tf_op jit(solution)/shard_map/ppermute | solution.py:384
  41.5 10.7 %copy-start.2 = (bf16[128,2176]{1,0:T(8,128)(2,1)S(1)}, bf16[128,2176]{1,0:T(8,128)(2,1)}, u32[]{:S(2)}) copy-start(bf16[128,2176]{1,0:T(8,128)(2,1)} %get-tuple-element.62.refs_0_) | copy-start | bytes 1671172
  41.6 11.1 %copy-start = (bf16[1,704,2048]{2,1,0:T(8,128)(2,1)S(1)}, bf16[1,704,2048]{2,1,0:T(8,128)(2,1)}, u32[]{:S(2)}) copy-start(bf16[1,704,2048]{2,1,0:T(8,128)(2,1)} %param.9) | copy-start | bytes 8650756
  41.6 16.8 %collective-permute-start.5 = (bf16[2,72,1408]{2,1,0:T(8,128)(2,1)S(1)}, bf16[2,72,1408]{2,1,0:T(8,128)(2,1)S(1)}, u32[]{:S(2)}, u32[]{:S(2)}) collective-permute-start(bf16[2,72,1408]{2,1,0:T(8,128)(2,1)S(1)} %shard_map.78), channel_id=1, source_target_pairs={{0,8},{2,10},{4,12},{6,14},{8,16},{10,18},{12,20},{14,22},{16,24},... | collective-permute-start | bytes 1216520 | tf_op jit(solution)/shard_map/ppermute | solution.py:381
  50.0 20.6 %collective-permute-start.14 = (bf16[2,72,1408]{2,1,0:T(8,128)(2,1)S(1)}, bf16[2,72,1408]{2,1,0:T(8,128)(2,1)S(1)}, u32[]{:S(2)}, u32[]{:S(2)}) collective-permute-start(bf16[2,72,1408]{2,1,0:T(8,128)(2,1)S(1)} %shard_map.85), channel_id=1, source_target_pairs={{0,24},{2,26},{4,28},{6,30},{8,0},{10,2},{12,4},{14,6},{16,8},{18,... | collective-permute-start | bytes 1216520 | tf_op jit(solution)/shard_map/ppermute | solution.py:381
  58.5 17.6 %collective-permute-start.6 = (bf16[72,2048]{1,0:T(8,128)(2,1)S(1)}, bf16[72,2048]{1,0:T(8,128)(2,1)S(1)}, u32[]{:S(2)}, u32[]{:S(2)}) collective-permute-start(bf16[72,2048]{1,0:T(8,128)(2,1)S(1)} %get-tuple-element.71), channel_id=1, source_target_pairs={{0,2},{2,0},{4,6},{6,4},{8,10},{10,8},{12,14},{14,12},{16,18},{18,... | collective-permute-start | bytes 884744 | tf_op jit(solution)/shard_map/ppermute | solution.py:384
  60.1 20.0 %collective-permute-start.7 = (bf16[72,2048]{1,0:T(8,128)(2,1)S(1)}, bf16[72,2048]{1,0:T(8,128)(2,1)S(1)}, u32[]{:S(2)}, u32[]{:S(2)}) collective-permute-start(bf16[72,2048]{1,0:T(8,128)(2,1)S(1)} %get-tuple-element.72), channel_id=1, source_target_pairs={{0,4},{2,6},{4,0},{6,2},{8,12},{10,14},{12,8},{14,10},{16,20},{18,... | collective-permute-start | bytes 884744 | tf_op jit(solution)/shard_map/ppermute | solution.py:384
  64.4 15.6 %collective-permute-start.8 = (bf16[72,2048]{1,0:T(8,128)(2,1)S(1)}, bf16[72,2048]{1,0:T(8,128)(2,1)S(1)}, u32[]{:S(2)}, u32[]{:S(2)}) collective-permute-start(bf16[72,2048]{1,0:T(8,128)(2,1)S(1)} %get-tuple-element.73), channel_id=1, source_target_pairs={{0,6},{2,4},{4,2},{6,0},{8,14},{10,12},{12,10},{14,8},{16,22},{18,... | collective-permute-start | bytes 884744 | tf_op jit(solution)/shard_map/ppermute | solution.py:384
  67.9 14.2 %collective-permute-start.9 = (bf16[2,72,1408]{2,1,0:T(8,128)(2,1)S(1)}, bf16[2,72,1408]{2,1,0:T(8,128)(2,1)S(1)}, u32[]{:S(2)}, u32[]{:S(2)}) collective-permute-start(bf16[2,72,1408]{2,1,0:T(8,128)(2,1)S(1)} %shard_map.80), channel_id=1, source_target_pairs={{0,16},{2,18},{4,20},{6,22},{8,24},{10,26},{12,28},{14,30},{16,0},... | collective-permute-start | bytes 1216520 | tf_op jit(solution)/shard_map/ppermute | solution.py:381
  70.7 15.0 %collective-permute-start.15 = (bf16[72,1024]{1,0:T(8,128)(2,1)S(1)}, bf16[72,1024]{1,0:T(8,128)(2,1)S(1)}, u32[]{:S(2)}, u32[]{:S(2)}) collective-permute-start(bf16[72,1024]{1,0:T(8,128)(2,1)S(1)} %get-tuple-element.95), channel_id=1, source_target_pairs={{0,2},{2,0},{4,6},{6,4},{8,10},{10,8},{12,14},{14,12},{16,18},{18,... | collective-permute-start | bytes 442376 | tf_op jit(solution)/shard_map/ppermute | solution.py:384
  76.1 11.5 %collective-permute-start.16 = (bf16[72,1024]{1,0:T(8,128)(2,1)S(1)}, bf16[72,1024]{1,0:T(8,128)(2,1)S(1)}, u32[]{:S(2)}, u32[]{:S(2)}) collective-permute-start(bf16[72,1024]{1,0:T(8,128)(2,1)S(1)} %get-tuple-element.96), channel_id=1, source_target_pairs={{0,4},{2,6},{4,0},{6,2},{8,12},{10,14},{12,8},{14,10},{16,20},{18,... | collective-permute-start | bytes 442376 | tf_op jit(solution)/shard_map/ppermute | solution.py:384
  80.1 8.3 %collective-permute-start.17 = (bf16[72,1024]{1,0:T(8,128)(2,1)S(1)}, bf16[72,1024]{1,0:T(8,128)(2,1)S(1)}, u32[]{:S(2)}, u32[]{:S(2)}) collective-permute-start(bf16[72,1024]{1,0:T(8,128)(2,1)S(1)} %get-tuple-element.97), channel_id=1, source_target_pairs={{0,6},{2,4},{4,2},{6,0},{8,14},{10,12},{12,10},{14,8},{16,22},{18,... | collective-permute-start | bytes 442376 | tf_op jit(solution)/shard_map/ppermute | solution.py:384
  85.5 11.9 %collective-permute-start.25 = (bf16[352,1024]{1,0:T(8,128)(2,1)S(1)}, bf16[352,1024]{1,0:T(8,128)(2,1)S(1)}, u32[]{:S(2)}, u32[]{:S(2)}) collective-permute-start(bf16[352,1024]{1,0:T(8,128)(2,1)S(1)} %get-tuple-element.100.refs_7_.refs_4_), channel_id=1, source_target_pairs={{0,1},{1,0},{2,3},{3,2},{4,5},{5,4},{6,7},{7,6},{8,9},{9,8},{10,11... | collective-permute-start | bytes 2162696 | tf_op jit(solution)/shard_map/ppermute | solution.py:521
  85.6 7.4 %collective-permute-start.19 = (f32[4,128]{1,0:T(4,128)S(1)}, f32[4,128]{1,0:T(4,128)S(1)}, u32[]{:S(2)}, u32[]{:S(2)}) collective-permute-start(f32[4,128]{1,0:T(4,128)S(1)} %get-tuple-element.106.refs_2_), channel_id=1, source_target_pairs={{0,16},{2,18},{4,20},{6,22},{8,24},{10,26},{12,28},{14,30},{16,0},... | collective-permute-start | bytes 6152 | tf_op jit(solution)/shard_map/ppermute | solution.py:381
  85.7 5.5 %collective-permute-start.18 = (f32[4,128]{1,0:T(4,128)S(1)}, f32[4,128]{1,0:T(4,128)S(1)}, u32[]{:S(2)}, u32[]{:S(2)}) collective-permute-start(f32[4,128]{1,0:T(4,128)S(1)} %get-tuple-element.107), channel_id=1, source_target_pairs={{0,24},{2,26},{4,28},{6,30},{8,0},{10,2},{12,4},{14,6},{16,8},{18,... | collective-permute-start | bytes 6152 | tf_op jit(solution)/shard_map/ppermute | solution.py:381
  87.6 5.4 %collective-permute-start.20 = (f32[4,128]{1,0:T(4,128)S(1)}, f32[4,128]{1,0:T(4,128)S(1)}, u32[]{:S(2)}, u32[]{:S(2)}) collective-permute-start(f32[4,128]{1,0:T(4,128)S(1)} %get-tuple-element.108), channel_id=1, source_target_pairs={{0,8},{2,10},{4,12},{6,14},{8,16},{10,18},{12,20},{14,22},{16,24},... | collective-permute-start | bytes 6152 | tf_op jit(solution)/shard_map/ppermute | solution.py:381
  91.2 9.2 %copy-start.3 = (s32[128,6]{0,1:T(8,128)S(1)}, s32[128,6]{0,1:T(8,128)}, u32[]{:S(2)}) copy-start(s32[128,6]{0,1:T(8,128)} %param.7) | copy-start | bytes 9220
  91.2 9.2 %copy-start.4 = (s32[128,6]{0,1:T(8,128)S(1)}, s32[128,6]{0,1:T(8,128)}, u32[]{:S(2)}) copy-start(s32[128,6]{0,1:T(8,128)} %param.8) | copy-start | bytes 9220
  91.2 9.2 %copy-start.5 = (f32[16,128]{1,0:T(8,128)S(1)}, f32[16,128]{1,0:T(8,128)}, u32[]{:S(2)}) copy-start(f32[16,128]{1,0:T(8,128)} %get-tuple-element.109.refs_2_) | copy-start | bytes 24580
  93.0 7.4 %collective-permute-start.21 = (bf16[352,1024]{1,0:T(8,128)(2,1)S(1)}, bf16[352,1024]{1,0:T(8,128)(2,1)S(1)}, u32[]{:S(2)}, u32[]{:S(2)}) collective-permute-start(bf16[352,1024]{1,0:T(8,128)(2,1)S(1)} %shard_map.96), channel_id=1, source_target_pairs={{0,1},{1,0},{2,3},{3,2},{4,5},{5,4},{6,7},{7,6},{8,9},{9,8},{10,11... | collective-permute-start | bytes 2162696 | tf_op jit(solution)/shard_map/ppermute | solution.py:521
  93.0 5.8 %collective-permute-start.22 = (f32[4,128]{1,0:T(4,128)S(1)}, f32[4,128]{1,0:T(4,128)S(1)}, u32[]{:S(2)}, u32[]{:S(2)}) collective-permute-start(f32[4,128]{1,0:T(4,128)S(1)} %get-tuple-element.112), channel_id=1, source_target_pairs={{0,2},{2,0},{4,6},{6,4},{8,10},{10,8},{12,14},{14,12},{16,18},{18,... | collective-permute-start | bytes 6152 | tf_op jit(solution)/shard_map/ppermute | solution.py:384
  95.9 3.6 %collective-permute-start.23 = (f32[4,128]{1,0:T(4,128)S(1)}, f32[4,128]{1,0:T(4,128)S(1)}, u32[]{:S(2)}, u32[]{:S(2)}) collective-permute-start(f32[4,128]{1,0:T(4,128)S(1)} %get-tuple-element.113), channel_id=1, source_target_pairs={{0,4},{2,6},{4,0},{6,2},{8,12},{10,14},{12,8},{14,10},{16,20},{18,... | collective-permute-start | bytes 6152 | tf_op jit(solution)/shard_map/ppermute | solution.py:384
  95.9 4.5 %collective-permute-start.24 = (f32[4,128]{1,0:T(4,128)S(1)}, f32[4,128]{1,0:T(4,128)S(1)}, u32[]{:S(2)}, u32[]{:S(2)}) collective-permute-start(f32[4,128]{1,0:T(4,128)S(1)} %get-tuple-element.114), channel_id=1, source_target_pairs={{0,6},{2,4},{4,2},{6,0},{8,14},{10,12},{12,10},{14,8},{16,22},{18,... | collective-permute-start | bytes 6152 | tf_op jit(solution)/shard_map/ppermute | solution.py:384

commit v10 on v9

--- a/solution.py
+++ b/solution.py
@@ -308,7 +308,8 @@
             out_ref[s : s + 1, :] = gate_ref[k : k + 1, :]
 
 
-def pick_gates(slot_ref, routes_ref, num_ref, homes, gate_ref, rows):
+def pick_kernel(slot_ref, routes_ref, num_ref, *refs):
+    homes, gate_ref, rows = refs[:PLANE], refs[-2], refs[-1]
     experts, tokens = slot_ref.shape
     for k in range(PLANE):
         for s in range(experts // PLANE):
@@ -325,11 +326,8 @@
 
 def finish_kernel(first, step, count, extra, *refs):
     own, others_ref, refs = refs[:count], refs[count], refs[count + 1 :]
-    if extra:
-        slot_ref, routes_ref, num_ref, *homes = refs[: 3 + PLANE]
-        out_hbm, scale_hbm, gate_ref, out, scales, table, done, rows = refs[5 + PLANE :]
-    else:
-        out_hbm, scale_hbm, out, scales, table, done = refs
+    out_hbm, scale_hbm, mark_ref, out, scales, table, done = refs[2 if extra else 0 :]
+    mark_ref[...] = jnp.zeros_like(mark_ref)
     share, width = out.shape
     lanes = lax.broadcasted_iota(jnp.int32, (share, BLOCK), 1)
     copies = []
@@ -356,8 +354,6 @@
     )
     copy.start()
     copies.append(copy)
-    if extra:
-        pick_gates(slot_ref, routes_ref, num_ref, homes, gate_ref, rows)
     for copy in copies:
         copy.wait()
 
@@ -516,7 +512,7 @@
             in_specs=[inside] * (3 + len(more)) + [anywhere] * len(after),
         )(*rows, early, *more, *after)
 
-    def finish(first, send, mine, out, extra):
+    def finish(first, send, mine, out):
         if flip:
             others = lax.ppermute(send, "replica", [(0, 1), (1, 0)])[None]
             own = [mine]
@@ -524,27 +520,23 @@
             both = jnp.concatenate([send, mine], axis=0).reshape(replicas, share, model // 2)
             others = lax.all_to_all(both, "replica", 0, 0, tiled=True)
             own = []
-        fixed = len(own) + 1 + len(extra)
-        outs = [sds((share, model), F32), sds((model // BLOCK, share), F32)]
-        out_specs = [anywhere] * 2
+        fixed = len(own) + 1
+        outs = [sds((share, model), F32), sds((model // BLOCK, share), F32), sds((8, BLOCK), F32)]
+        out_specs = [anywhere] * 2 + [inside]
         scratch = [
             pltpu.VMEM((share, model // 2), F32),
             pltpu.VMEM((model // 2 // BLOCK, share), F32),
             pltpu.VMEM((up(share, BLOCK), BLOCK), F32),
             pltpu.SemaphoreType.DMA((model // 2 // fine + 1,)),
         ]
-        if extra:
-            outs.append(sds((top_k, tokens), F32))
-            out_specs.append(inside)
-            scratch.append(pltpu.VMEM((experts, BLOCK), F32))
         return call(
-            functools.partial(finish_kernel, first, fine, len(own), bool(extra)),
+            functools.partial(finish_kernel, first, fine, len(own), bool(out)),
             outs,
             in_specs=[inside] * fixed + [anywhere] * len(out),
             out_specs=out_specs,
             input_output_aliases={fixed + n: n for n in range(len(out))},
             scratch_shapes=scratch,
-        )(*own, others, *extra, *out)
+        )(*own, others, *out)
 
     left = partial(0, [], [])
     own_rows, gates[0] = call(
@@ -561,8 +553,13 @@
         in_specs=[inside] * outer + [anywhere],
     )(*gates, left[0])
     homes = [homes[0]] + [swap(homes[k], k) for k in range(1, PLANE)]
-    out = finish(0, *left, [], [])
-    out, scales, gate_grad = finish(model // 2, *right, out, [slot, routes.T, numerators.T, *homes])
+    *out, _ = finish(0, *left, [])
+    out, scales, mark = finish(model // 2, *right, out)
+    gate_grad = call(
+        pick_kernel,
+        sds((top_k, tokens), F32),
+        scratch_shapes=[pltpu.VMEM((experts, BLOCK), F32)],
+    )(slot, routes.T, numerators.T, *homes, mark)
     return gate_grad.T, scales.T[None], out[None]
 
 

time: 103 us -> 101 us (0.981)
  waiting for transfers between devices: 49.7 us -> 48.3 us
    ppermute x15, waiting for transfers between devices: 13 us -> 11.4 us  [swap(): return lax.ppermute(array, 'expert', [(e, e ^ k) for e in range(experts)])]
    pallas_call x2 -> x3, Pallas kernels: 3.29 us -> 4.02 us  [the longest x2 3.31 us: finish(): call(functools.partial(finish_kernel, first, fine, len(own), bool(out)),...]
  transfers between devices with their start and end apart: 26 -> 26, of which waited for: 12 -> 10; matrix products, arithmetic and copies ran while one was open for 0% -> 0% of each run, Pallas kernels for 17% -> 19%
where the time goes in v10:
time: 101 us
  waiting for transfers between devices  48.3 us (48%)
  starting transfers between devices  26.7 us (26%)
  Pallas kernels  25.2 us (25%)
    ppermute x9, waiting for transfers between devices, ring(): return lax.ppermute(array, 'expert', pairs)  36.9 us
    ppermute x15, starting transfers between devices, swap(): return lax.ppermute(array, 'expert', [(e, e ^ k) for e in range(experts)])  15.9 us
    ppermute x15, waiting for transfers between devices, swap(): return lax.ppermute(array, 'expert', [(e, e ^ k) for e in range(experts)])  11.4 us
    ppermute x9, starting transfers between devices, ring(): return lax.ppermute(array, 'expert', pairs)  10.7 us
    pallas_call x3, Pallas kernels, stage(): call(functools.partial(stage_kernel, place, [span for _, span in parts],...  6.16 us
    pallas_call x1, Pallas kernels, per_device(): call(functools.partial(open_kernel, slots, flip), [sds((tokens, model + B...  4.9 us
    pallas_call x2, Pallas kernels, finish(): call(functools.partial(finish_kernel, first, fine, len(own), bool(out)),...  3.31 us
    pallas_call x2, Pallas kernels, partial(): call(functools.partial(partial_kernel, first, step, bool(more)), [sds((ha...  2.94 us
  transfers between devices with their start and end apart: 26, of which 10 were waited for; matrix products, arithmetic and copies ran while one was open for 0% of the time, Pallas kernels for 19%

profile of v10, /device:TPU:0, one launch (start us, length us, event | category | flops | bytes accessed | tf_op | source)
XLA Modules:
  0.0 101.1 jit_solution(18361281181840511170)
XLA Ops:
  0.6 4.9 %shard_map.76 = (bf16[128,2176]{1,0:T(8,128)(2,1)}, bf16[72,3840]{1,0:T(8,128)(2,1)}, bf16[72,3840]{1,0:T(8,128)(2,1)}, bf16[72,3840]{1,0:T(8,128)(2,1)}, bf16[72,3840]{1,0:T(8,128)(2,1)}, /*index=5*/f32[16,128]{1,0:T(8,128)}) custom-call(s32[6,128]{1,0:T(8,128)} %bitcast.18, s32[6,128]{1,0:T(8,128)} %bitcast.20, bf16[6,704,128]{2,1,0:T(8,128)(2,1)} %bitcast.23, ...), custom_call_target="tpu_custom_call" | custom-call | flops 1024 | bytes 1024 | tf_op jit(solution)/shard_map/pallas_call | solution.py:387
  5.5 3.1 %collective-permute-start = (bf16[128,2176]{1,0:T(8,128)(2,1)}, bf16[128,2176]{1,0:T(8,128)(2,1)S(1)}, u32[]{:S(2)}, u32[]{:S(2)}) collective-permute-start(bf16[128,2176]{1,0:T(8,128)(2,1)} %get-tuple-element.63.refs_0_), channel_id=1, source_target_pairs={{0,8},{2,10},{4,12},{6,14},{8,16},{10,18},{12,20},{14,22},{16,24},... | collective-permute-start | bytes 1671176 | tf_op jit(solution)/shard_map/ppermute | solution.py:377
  8.6 2.1 %collective-permute-start.1 = (bf16[128,2176]{1,0:T(8,128)(2,1)}, bf16[128,2176]{1,0:T(8,128)(2,1)S(1)}, u32[]{:S(2)}, u32[]{:S(2)}) collective-permute-start(bf16[128,2176]{1,0:T(8,128)(2,1)} %get-tuple-element.63.refs_0_), channel_id=1, source_target_pairs={{0,24},{2,26},{4,28},{6,30},{8,0},{10,2},{12,4},{14,6},{16,8},{18,... | collective-permute-start | bytes 1671176 | tf_op jit(solution)/shard_map/ppermute | solution.py:377
  10.7 1.6 %collective-permute-start.2 = (bf16[72,3840]{1,0:T(8,128)(2,1)}, bf16[72,3840]{1,0:T(8,128)(2,1)S(1)}, u32[]{:S(2)}, u32[]{:S(2)}) collective-permute-start(bf16[72,3840]{1,0:T(8,128)(2,1)} %get-tuple-element.71), channel_id=1, source_target_pairs={{0,2},{2,0},{4,6},{6,4},{8,10},{10,8},{12,14},{14,12},{16,18},{18,... | collective-permute-start | bytes 1658888 | tf_op jit(solution)/shard_map/ppermute | solution.py:380
  12.4 1.5 %collective-permute-start.3 = (bf16[72,3840]{1,0:T(8,128)(2,1)}, bf16[72,3840]{1,0:T(8,128)(2,1)S(1)}, u32[]{:S(2)}, u32[]{:S(2)}) collective-permute-start(bf16[72,3840]{1,0:T(8,128)(2,1)} %get-tuple-element.72), channel_id=1, source_target_pairs={{0,4},{2,6},{4,0},{6,2},{8,12},{10,14},{12,8},{14,10},{16,20},{18,... | collective-permute-start | bytes 1658888 | tf_op jit(solution)/shard_map/ppermute | solution.py:380
  14.2 10.2 %collective-permute-done.refs_0_ = bf16[128,2176]{1,0:T(8,128)(2,1)S(1)} collective-permute-done((bf16[128,2176]{1,0:T(8,128)(2,1)}, bf16[128,2176]{1,0:T(8,128)(2,1)S(1)}, u32[]{:S(2)}, u32[]{:S(2)}) %collective-permute-start) | collective-permute-done | bytes 557088 | tf_op jit(solution)/shard_map/ppermute | solution.py:377
  24.4 10.7 %collective-permute-done.1.refs_1_ = bf16[128,2176]{1,0:T(8,128)(2,1)S(1)} collective-permute-done((bf16[128,2176]{1,0:T(8,128)(2,1)}, bf16[128,2176]{1,0:T(8,128)(2,1)S(1)}, u32[]{:S(2)}, u32[]{:S(2)}) %collective-permute-start.1) | collective-permute-done | bytes 557088 | tf_op jit(solution)/shard_map/ppermute | solution.py:377
  35.9 2.1 %collective-permute-done.3.refs_4_.refs_2_ = bf16[72,3840]{1,0:T(8,128)(2,1)S(1)} collective-permute-done((bf16[72,3840]{1,0:T(8,128)(2,1)}, bf16[72,3840]{1,0:T(8,128)(2,1)S(1)}, u32[]{:S(2)}, u32[]{:S(2)}) %collective-permute-start.3) | collective-permute-done | bytes 552992 | tf_op jit(solution)/shard_map/ppermute | solution.py:380
  38.0 1.2 %collective-permute-start.5 = (bf16[72,4096]{1,0:T(8,128)(2,1)S(1)}, bf16[72,4096]{1,0:T(8,128)(2,1)S(1)}, u32[]{:S(2)}, u32[]{:S(2)}) collective-permute-start(bf16[72,4096]{1,0:T(8,128)(2,1)S(1)} %get-tuple-element.74), channel_id=1, source_target_pairs={{0,2},{2,0},{4,6},{6,4},{8,10},{10,8},{12,14},{14,12},{16,18},{18,... | collective-permute-start | bytes 1769480 | tf_op jit(solution)/shard_map/ppermute | solution.py:380
  40.0 1.4 %collective-permute-start.7 = (bf16[72,4096]{1,0:T(8,128)(2,1)S(1)}, bf16[72,4096]{1,0:T(8,128)(2,1)S(1)}, u32[]{:S(2)}, u32[]{:S(2)}) collective-permute-start(bf16[72,4096]{1,0:T(8,128)(2,1)S(1)} %get-tuple-element.76), channel_id=1, source_target_pairs={{0,6},{2,4},{4,2},{6,0},{8,14},{10,12},{12,10},{14,8},{16,22},{18,... | collective-permute-start | bytes 1769480 | tf_op jit(solution)/shard_map/ppermute | solution.py:380
  41.7 8.2 %collective-permute-done.8.refs_4_.refs_0_ = bf16[128,2176]{1,0:T(8,128)(2,1)S(1)} collective-permute-done((bf16[128,2176]{1,0:T(8,128)(2,1)S(1)}, bf16[128,2176]{1,0:T(8,128)(2,1)S(1)}, u32[]{:S(2)}, u32[]{:S(2)}) %collective-permute-start.8) | collective-permute-done | bytes 557088 | tf_op jit(solution)/shard_map/ppermute | solution.py:377
  50.0 2.1 %collective-permute-start.9 = (bf16[2,72,1408]{2,1,0:T(8,128)(2,1)S(1)}, bf16[2,72,1408]{2,1,0:T(8,128)(2,1)S(1)}, u32[]{:S(2)}, u32[]{:S(2)}) collective-permute-start(bf16[2,72,1408]{2,1,0:T(8,128)(2,1)S(1)} %shard_map.80), channel_id=1, source_target_pairs={{0,24},{2,26},{4,28},{6,30},{8,0},{10,2},{12,4},{14,6},{16,8},{18,... | collective-permute-start | bytes 1216520 | tf_op jit(solution)/shard_map/ppermute | solution.py:377
  52.7 1.4 %shard_map.83 = (bf16[768,2048]{1,0:T(8,128)(2,1)S(1)}, bf16[704,768]{1,0:T(8,128)(2,1)S(1)}, f32[704,384]{1,0:T(8,128)S(1)}, bf16[704,384]{1,0:T(8,128)(2,1)S(1)}) custom-call(bf16[72,3840]{1,0:T(8,128)(2,1)S(1)} %copy-done.1, bf16[72,3840]{1,0:T(8,128)(2,1)S(1)} %collective-permute-done.2.refs_3_.refs_1_, ...), custom_call_target="tpu_custom_call" | custom-call | flops 2000000000 | bytes 1024 | tf_op jit(solution)/shard_map/pallas_call | solution.py:480
  54.6 3.8 %collective-permute-done.13.refs_3_.refs_5_ = bf16[2,72,1408]{2,1,0:T(8,128)(2,1)S(1)} collective-permute-done((bf16[2,72,1408]{2,1,0:T(8,128)(2,1)S(1)}, bf16[2,72,1408]{2,1,0:T(8,128)(2,1)S(1)}, u32[]{:S(2)}, u32[]{:S(2)}) %collective-permute-start.13) | collective-permute-done | bytes 405536 | tf_op jit(solution)/shard_map/ppermute | solution.py:377
  58.5 1.5 %collective-permute-start.14 = (bf16[72,2048]{1,0:T(8,128)(2,1)S(1)}, bf16[72,2048]{1,0:T(8,128)(2,1)S(1)}, u32[]{:S(2)}, u32[]{:S(2)}) collective-permute-start(bf16[72,2048]{1,0:T(8,128)(2,1)S(1)} %get-tuple-element.87), channel_id=1, source_target_pairs={{0,2},{2,0},{4,6},{6,4},{8,10},{10,8},{12,14},{14,12},{16,18},{18,... | collective-permute-start | bytes 884744 | tf_op jit(solution)/shard_map/ppermute | solution.py:380
  60.1 1.6 %collective-permute-start.15 = (bf16[72,2048]{1,0:T(8,128)(2,1)S(1)}, bf16[72,2048]{1,0:T(8,128)(2,1)S(1)}, u32[]{:S(2)}, u32[]{:S(2)}) collective-permute-start(bf16[72,2048]{1,0:T(8,128)(2,1)S(1)} %get-tuple-element.88), channel_id=1, source_target_pairs={{0,4},{2,6},{4,0},{6,2},{8,12},{10,14},{12,8},{14,10},{16,20},{18,... | collective-permute-start | bytes 884744 | tf_op jit(solution)/shard_map/ppermute | solution.py:380
  61.7 2.7 %collective-permute-done.6.refs_4_.refs_2_ = bf16[72,4096]{1,0:T(8,128)(2,1)S(1)} collective-permute-done((bf16[72,4096]{1,0:T(8,128)(2,1)S(1)}, bf16[72,4096]{1,0:T(8,128)(2,1)S(1)}, u32[]{:S(2)}, u32[]{:S(2)}) %collective-permute-start.6) | collective-permute-done | bytes 589856 | tf_op jit(solution)/shard_map/ppermute | solution.py:380
  64.4 3.5 %collective-permute-done.7.refs_5_.refs_3_ = bf16[72,4096]{1,0:T(8,128)(2,1)S(1)} collective-permute-done((bf16[72,4096]{1,0:T(8,128)(2,1)S(1)}, bf16[72,4096]{1,0:T(8,128)(2,1)S(1)}, u32[]{:S(2)}, u32[]{:S(2)}) %collective-permute-start.7) | collective-permute-done | bytes 589856 | tf_op jit(solution)/shard_map/ppermute | solution.py:380
  68.6 2.1 %shard_map.88 = (bf16[768,2048]{1,0:T(8,128)(2,1)S(1)}, bf16[704,768]{1,0:T(8,128)(2,1)S(1)}, f32[4,128]{1,0:T(4,128)S(1)}) custom-call(bf16[72,4096]{1,0:T(8,128)(2,1)S(1)} %get-tuple-element.92.refs_0_, bf16[72,4096]{1,0:T(8,128)(2,1)S(1)} %collective-permute-done.5.refs_3_.refs_1_, bf16[72,4096]{1,0:T(8,128)(2,1)S(1)} %collective-permute-done.6.refs_4_.refs_2_, ...), custom_call_target="tpu_custom_call" | custom-call | flops 2000000000 | bytes 1024 | tf_op jit(solution)/shard_map/pallas_call | solution.py:450
  71.6 2.0 %shard_map.89 = (bf16[768,2048]{1,0:T(8,128)(2,1)S(1)}, bf16[704,768]{1,0:T(8,128)(2,1)S(1)}, f32[4,128]{1,0:T(4,128)S(1)}) custom-call(bf16[72,4096]{1,0:T(8,128)(2,1)S(1)} %get-tuple-element.92.refs_0_, bf16[72,4096]{1,0:T(8,128)(2,1)S(1)} %collective-permute-done.5.refs_3_.refs_1_, ...), custom_call_target="tpu_custom_call", output_to_operand_aliasing={{0}: (6, {}), {1}: (7, {})} | custom-call | flops 2000000000 | bytes 1024 | tf_op jit(solution)/shard_map/pallas_call | solution.py:450
  73.7 2.4 %shard_map.90 = (bf16[704,2048]{1,0:T(8,128)(2,1)S(1)}, f32[8,128]{1,0:T(8,128)S(1)}) custom-call(bf16[768,2048]{1,0:T(8,128)(2,1)S(1)} %get-tuple-element.95.rows_ref, bf16[704,768]{1,0:T(8,128)(2,1)S(1)} %get-tuple-element.96.hidw_ref), custom_call_target="tpu_custom_call" | custom-call | flops 3500000000 | bytes 1024 | tf_op jit(solution)/shard_map/pallas_call | solution.py:475
  77.0 3.0 %collective-permute-done.15.refs_2_ = bf16[72,2048]{1,0:T(8,128)(2,1)S(1)} collective-permute-done((bf16[72,2048]{1,0:T(8,128)(2,1)S(1)}, bf16[72,2048]{1,0:T(8,128)(2,1)S(1)}, u32[]{:S(2)}, u32[]{:S(2)}) %collective-permute-start.15) | collective-permute-done | bytes 294944 | tf_op jit(solution)/shard_map/ppermute | solution.py:380
  80.0 2.1 %collective-permute-done.17.refs_5_ = bf16[2,72,1408]{2,1,0:T(8,128)(2,1)S(1)} collective-permute-done((bf16[2,72,1408]{2,1,0:T(8,128)(2,1)S(1)}, bf16[2,72,1408]{2,1,0:T(8,128)(2,1)S(1)}, u32[]{:S(2)}, u32[]{:S(2)}) %collective-permute-start.17) | collective-permute-done | bytes 405536 | tf_op jit(solution)/shard_map/ppermute | solution.py:377
  82.2 2.1 %shard_map.91 = (bf16[768,2048]{1,0:T(8,128)(2,1)S(1)}, bf16[704,768]{1,0:T(8,128)(2,1)S(1)}, f32[4,128]{1,0:T(4,128)S(1)}) custom-call(bf16[72,2048]{1,0:T(8,128)(2,1)S(1)} %get-tuple-element.83.refs_0_, bf16[72,2048]{1,0:T(8,128)(2,1)S(1)} %collective-permute-done.14.refs_1_, ...), custom_call_target="tpu_custom_call", output_to_operand_aliasing={{0}: (6, {}), {1}: (7, {})} | custom-call | flops 2000000000 | bytes 1024 | tf_op jit(solution)/shard_map/pallas_call | solution.py:450
  84.2 1.3 %shard_map.92 = (bf16[352,1024]{1,0:T(8,128)(2,1)S(1)}, bf16[352,1024]{1,0:T(8,128)(2,1)S(1)}) custom-call(bf16[768,2048]{1,0:T(8,128)(2,1)S(1)} %get-tuple-element.98.rows_ref, bf16[704,768]{1,0:T(8,128)(2,1)S(1)} %get-tuple-element.99.hidw_ref, bf16[704,2048]{1,0:T(8,128)(2,1)S(1)} %get-tuple-element.100.early_ref), custom_call_target="tpu_custom_call" | custom-call | flops 4000000000 | bytes 1024 | tf_op jit(solution)/shard_map/pallas_call | solution.py:508
  85.7 1.9 %collective-permute-start.18 = (f32[4,128]{1,0:T(4,128)S(1)}, f32[4,128]{1,0:T(4,128)S(1)}, u32[]{:S(2)}, u32[]{:S(2)}) collective-permute-start(f32[4,128]{1,0:T(4,128)S(1)} %get-tuple-element.106), channel_id=1, source_target_pairs={{0,24},{2,26},{4,28},{6,30},{8,0},{10,2},{12,4},{14,6},{16,8},{18,... | collective-permute-start | bytes 6152 | tf_op jit(solution)/shard_map/ppermute | solution.py:377
  89.5 1.7 %shard_map.96 = (bf16[352,1024]{1,0:T(8,128)(2,1)S(1)}, bf16[352,1024]{1,0:T(8,128)(2,1)S(1)}) custom-call(bf16[768,2048]{1,0:T(8,128)(2,1)S(1)} %get-tuple-element.98.rows_ref, bf16[704,768]{1,0:T(8,128)(2,1)S(1)} %get-tuple-element.99.hidw_ref, bf16[704,2048]{1,0:T(8,128)(2,1)S(1)} %get-tuple-element.100.early_ref, ...), custom_call_target="tpu_custom_call" | custom-call | flops 4000000000 | bytes 1024 | tf_op jit(solution)/shard_map/pallas_call | solution.py:508
  91.2 1.9 %collective-permute-done.20.refs_3_ = f32[4,128]{1,0:T(4,128)S(1)} collective-permute-done((f32[4,128]{1,0:T(4,128)S(1)}, f32[4,128]{1,0:T(4,128)S(1)}, u32[]{:S(2)}, u32[]{:S(2)}) %collective-permute-start.20) | collective-permute-done | bytes 2080 | tf_op jit(solution)/shard_map/ppermute | solution.py:377
  93.0 2.4 %collective-permute-start.21 = (f32[4,128]{1,0:T(4,128)S(1)}, f32[4,128]{1,0:T(4,128)S(1)}, u32[]{:S(2)}, u32[]{:S(2)}) collective-permute-start(f32[4,128]{1,0:T(4,128)S(1)} %get-tuple-element.109), channel_id=1, source_target_pairs={{0,2},{2,0},{4,6},{6,4},{8,10},{10,8},{12,14},{14,12},{16,18},{18,... | collective-permute-start | bytes 6152 | tf_op jit(solution)/shard_map/ppermute | solution.py:380
  95.9 1.1 %collective-permute-start.23 = (f32[4,128]{1,0:T(4,128)S(1)}, f32[4,128]{1,0:T(4,128)S(1)}, u32[]{:S(2)}, u32[]{:S(2)}) collective-permute-start(f32[4,128]{1,0:T(4,128)S(1)} %get-tuple-element.111), channel_id=1, source_target_pairs={{0,6},{2,4},{4,2},{6,0},{8,14},{10,12},{12,10},{14,8},{16,22},{18,... | collective-permute-start | bytes 6152 | tf_op jit(solution)/shard_map/ppermute | solution.py:380
  97.0 2.0 %shard_map.98 = (f32[352,2048]{1,0:T(8,128)}, f32[16,352]{1,0:T(8,128)}, f32[8,128]{1,0:T(8,128)}) custom-call(bf16[352,1024]{1,0:T(8,128)(2,1)S(1)} %get-tuple-element.115.refs_0_, bf16[1,352,1024]{2,1,0:T(8,128)(2,1)S(1)} %bitcast.16), custom_call_target="tpu_custom_call" | custom-call | flops 1024 | bytes 1024 | tf_op jit(solution)/shard_map/pallas_call | solution.py:532
  99.0 1.4 %shard_map.99 = (f32[352,2048]{1,0:T(8,128)}, f32[16,352]{1,0:T(8,128)}, f32[8,128]{1,0:T(8,128)S(1)}) custom-call(bf16[352,1024]{1,0:T(8,128)(2,1)S(1)} %get-tuple-element.113.refs_0_, bf16[1,352,1024]{2,1,0:T(8,128)(2,1)S(1)} %bitcast.17, f32[352,2048]{1,0:T(8,128)} %get-tuple-element.116.refs_2_, ...), custom_call_target="tpu_custom_call", output_to_operand_aliasing={{0}: (2, {}), {1}: (3, {})} | custom-call | flops 1024 | bytes 1024 | tf_op jit(solution)/shard_map/pallas_call | solution.py:532
  (57 shorter events, 9.2 us)
Async XLA Ops:
  5.5 35.9 %copy-start.1 = (bf16[72,3840]{1,0:T(8,128)(2,1)S(1)}, bf16[72,3840]{1,0:T(8,128)(2,1)}, u32[]{:S(2)}) copy-start(bf16[72,3840]{1,0:T(8,128)(2,1)} %get-tuple-element.77.refs_0_) | copy-start | bytes 1658884
  5.5 18.8 %collective-permute-start = (bf16[128,2176]{1,0:T(8,128)(2,1)}, bf16[128,2176]{1,0:T(8,128)(2,1)S(1)}, u32[]{:S(2)}, u32[]{:S(2)}) collective-permute-start(bf16[128,2176]{1,0:T(8,128)(2,1)} %get-tuple-element.63.refs_0_), channel_id=1, source_target_pairs={{0,8},{2,10},{4,12},{6,14},{8,16},{10,18},{12,20},{14,22},{16,24},... | collective-permute-start | bytes 1671176 | tf_op jit(solution)/shard_map/ppermute | solution.py:377
  8.6 26.5 %collective-permute-start.1 = (bf16[128,2176]{1,0:T(8,128)(2,1)}, bf16[128,2176]{1,0:T(8,128)(2,1)S(1)}, u32[]{:S(2)}, u32[]{:S(2)}) collective-permute-start(bf16[128,2176]{1,0:T(8,128)(2,1)} %get-tuple-element.63.refs_0_), channel_id=1, source_target_pairs={{0,24},{2,26},{4,28},{6,30},{8,0},{10,2},{12,4},{14,6},{16,8},{18,... | collective-permute-start | bytes 1671176 | tf_op jit(solution)/shard_map/ppermute | solution.py:377
  10.7 25.2 %collective-permute-start.2 = (bf16[72,3840]{1,0:T(8,128)(2,1)}, bf16[72,3840]{1,0:T(8,128)(2,1)S(1)}, u32[]{:S(2)}, u32[]{:S(2)}) collective-permute-start(bf16[72,3840]{1,0:T(8,128)(2,1)} %get-tuple-element.71), channel_id=1, source_target_pairs={{0,2},{2,0},{4,6},{6,4},{8,10},{10,8},{12,14},{14,12},{16,18},{18,... | collective-permute-start | bytes 1658888 | tf_op jit(solution)/shard_map/ppermute | solution.py:380
  12.4 25.6 %collective-permute-start.3 = (bf16[72,3840]{1,0:T(8,128)(2,1)}, bf16[72,3840]{1,0:T(8,128)(2,1)S(1)}, u32[]{:S(2)}, u32[]{:S(2)}) collective-permute-start(bf16[72,3840]{1,0:T(8,128)(2,1)} %get-tuple-element.72), channel_id=1, source_target_pairs={{0,4},{2,6},{4,0},{6,2},{8,12},{10,14},{12,8},{14,10},{16,20},{18,... | collective-permute-start | bytes 1658888 | tf_op jit(solution)/shard_map/ppermute | solution.py:380
  13.9 24.1 %collective-permute-start.4 = (bf16[72,3840]{1,0:T(8,128)(2,1)}, bf16[72,3840]{1,0:T(8,128)(2,1)S(1)}, u32[]{:S(2)}, u32[]{:S(2)}) collective-permute-start(bf16[72,3840]{1,0:T(8,128)(2,1)} %get-tuple-element.73), channel_id=1, source_target_pairs={{0,6},{2,4},{4,2},{6,0},{8,14},{10,12},{12,10},{14,8},{16,22},{18,... | collective-permute-start | bytes 1658888 | tf_op jit(solution)/shard_map/ppermute | solution.py:380
  24.4 25.5 %collective-permute-start.8 = (bf16[128,2176]{1,0:T(8,128)(2,1)S(1)}, bf16[128,2176]{1,0:T(8,128)(2,1)S(1)}, u32[]{:S(2)}, u32[]{:S(2)}) collective-permute-start(bf16[128,2176]{1,0:T(8,128)(2,1)S(1)} %collective-permute-done.refs_0_), channel_id=1, source_target_pairs={{0,8},{2,10},{4,12},{6,14},{8,16},{10,18},{12,20},{14,22},{16,24},... | collective-permute-start | bytes 1671176 | tf_op jit(solution)/shard_map/ppermute | solution.py:377
  38.0 22.1 %collective-permute-start.5 = (bf16[72,4096]{1,0:T(8,128)(2,1)S(1)}, bf16[72,4096]{1,0:T(8,128)(2,1)S(1)}, u32[]{:S(2)}, u32[]{:S(2)}) collective-permute-start(bf16[72,4096]{1,0:T(8,128)(2,1)S(1)} %get-tuple-element.74), channel_id=1, source_target_pairs={{0,2},{2,0},{4,6},{6,4},{8,10},{10,8},{12,14},{14,12},{16,18},{18,... | collective-permute-start | bytes 1769480 | tf_op jit(solution)/shard_map/ppermute | solution.py:380
  39.2 25.2 %collective-permute-start.6 = (bf16[72,4096]{1,0:T(8,128)(2,1)S(1)}, bf16[72,4096]{1,0:T(8,128)(2,1)S(1)}, u32[]{:S(2)}, u32[]{:S(2)}) collective-permute-start(bf16[72,4096]{1,0:T(8,128)(2,1)S(1)} %get-tuple-element.75), channel_id=1, source_target_pairs={{0,4},{2,6},{4,0},{6,2},{8,12},{10,14},{12,8},{14,10},{16,20},{18,... | collective-permute-start | bytes 1769480 | tf_op jit(solution)/shard_map/ppermute | solution.py:380
  40.0 27.9 %collective-permute-start.7 = (bf16[72,4096]{1,0:T(8,128)(2,1)S(1)}, bf16[72,4096]{1,0:T(8,128)(2,1)S(1)}, u32[]{:S(2)}, u32[]{:S(2)}) collective-permute-start(bf16[72,4096]{1,0:T(8,128)(2,1)S(1)} %get-tuple-element.76), channel_id=1, source_target_pairs={{0,6},{2,4},{4,2},{6,0},{8,14},{10,12},{12,10},{14,8},{16,22},{18,... | collective-permute-start | bytes 1769480 | tf_op jit(solution)/shard_map/ppermute | solution.py:380
  41.5 10.7 %copy-start.2 = (bf16[128,2176]{1,0:T(8,128)(2,1)S(1)}, bf16[128,2176]{1,0:T(8,128)(2,1)}, u32[]{:S(2)}) copy-start(bf16[128,2176]{1,0:T(8,128)(2,1)} %get-tuple-element.63.refs_0_) | copy-start | bytes 1671172
  41.6 11.1 %copy-start = (bf16[1,704,2048]{2,1,0:T(8,128)(2,1)S(1)}, bf16[1,704,2048]{2,1,0:T(8,128)(2,1)}, u32[]{:S(2)}) copy-start(bf16[1,704,2048]{2,1,0:T(8,128)(2,1)} %param.9) | copy-start | bytes 8650756
  41.6 16.9 %collective-permute-start.13 = (bf16[2,72,1408]{2,1,0:T(8,128)(2,1)S(1)}, bf16[2,72,1408]{2,1,0:T(8,128)(2,1)S(1)}, u32[]{:S(2)}, u32[]{:S(2)}) collective-permute-start(bf16[2,72,1408]{2,1,0:T(8,128)(2,1)S(1)} %shard_map.85), channel_id=1, source_target_pairs={{0,8},{2,10},{4,12},{6,14},{8,16},{10,18},{12,20},{14,22},{16,24},... | collective-permute-start | bytes 1216520 | tf_op jit(solution)/shard_map/ppermute | solution.py:377
  50.0 20.6 %collective-permute-start.9 = (bf16[2,72,1408]{2,1,0:T(8,128)(2,1)S(1)}, bf16[2,72,1408]{2,1,0:T(8,128)(2,1)S(1)}, u32[]{:S(2)}, u32[]{:S(2)}) collective-permute-start(bf16[2,72,1408]{2,1,0:T(8,128)(2,1)S(1)} %shard_map.80), channel_id=1, source_target_pairs={{0,24},{2,26},{4,28},{6,30},{8,0},{10,2},{12,4},{14,6},{16,8},{18,... | collective-permute-start | bytes 1216520 | tf_op jit(solution)/shard_map/ppermute | solution.py:377
  58.5 17.6 %collective-permute-start.14 = (bf16[72,2048]{1,0:T(8,128)(2,1)S(1)}, bf16[72,2048]{1,0:T(8,128)(2,1)S(1)}, u32[]{:S(2)}, u32[]{:S(2)}) collective-permute-start(bf16[72,2048]{1,0:T(8,128)(2,1)S(1)} %get-tuple-element.87), channel_id=1, source_target_pairs={{0,2},{2,0},{4,6},{6,4},{8,10},{10,8},{12,14},{14,12},{16,18},{18,... | collective-permute-start | bytes 884744 | tf_op jit(solution)/shard_map/ppermute | solution.py:380
  60.1 19.9 %collective-permute-start.15 = (bf16[72,2048]{1,0:T(8,128)(2,1)S(1)}, bf16[72,2048]{1,0:T(8,128)(2,1)S(1)}, u32[]{:S(2)}, u32[]{:S(2)}) collective-permute-start(bf16[72,2048]{1,0:T(8,128)(2,1)S(1)} %get-tuple-element.88), channel_id=1, source_target_pairs={{0,4},{2,6},{4,0},{6,2},{8,12},{10,14},{12,8},{14,10},{16,20},{18,... | collective-permute-start | bytes 884744 | tf_op jit(solution)/shard_map/ppermute | solution.py:380
  64.4 15.6 %collective-permute-start.16 = (bf16[72,2048]{1,0:T(8,128)(2,1)S(1)}, bf16[72,2048]{1,0:T(8,128)(2,1)S(1)}, u32[]{:S(2)}, u32[]{:S(2)}) collective-permute-start(bf16[72,2048]{1,0:T(8,128)(2,1)S(1)} %get-tuple-element.89), channel_id=1, source_target_pairs={{0,6},{2,4},{4,2},{6,0},{8,14},{10,12},{12,10},{14,8},{16,22},{18,... | collective-permute-start | bytes 884744 | tf_op jit(solution)/shard_map/ppermute | solution.py:380
  67.9 14.2 %collective-permute-start.17 = (bf16[2,72,1408]{2,1,0:T(8,128)(2,1)S(1)}, bf16[2,72,1408]{2,1,0:T(8,128)(2,1)S(1)}, u32[]{:S(2)}, u32[]{:S(2)}) collective-permute-start(bf16[2,72,1408]{2,1,0:T(8,128)(2,1)S(1)} %shard_map.87), channel_id=1, source_target_pairs={{0,16},{2,18},{4,20},{6,22},{8,24},{10,26},{12,28},{14,30},{16,0},... | collective-permute-start | bytes 1216520 | tf_op jit(solution)/shard_map/ppermute | solution.py:377
  70.6 15.0 %collective-permute-start.10 = (bf16[72,1024]{1,0:T(8,128)(2,1)S(1)}, bf16[72,1024]{1,0:T(8,128)(2,1)S(1)}, u32[]{:S(2)}, u32[]{:S(2)}) collective-permute-start(bf16[72,1024]{1,0:T(8,128)(2,1)S(1)} %get-tuple-element.78), channel_id=1, source_target_pairs={{0,2},{2,0},{4,6},{6,4},{8,10},{10,8},{12,14},{14,12},{16,18},{18,... | collective-permute-start | bytes 442376 | tf_op jit(solution)/shard_map/ppermute | solution.py:380
  76.1 11.5 %collective-permute-start.11 = (bf16[72,1024]{1,0:T(8,128)(2,1)S(1)}, bf16[72,1024]{1,0:T(8,128)(2,1)S(1)}, u32[]{:S(2)}, u32[]{:S(2)}) collective-permute-start(bf16[72,1024]{1,0:T(8,128)(2,1)S(1)} %get-tuple-element.79), channel_id=1, source_target_pairs={{0,4},{2,6},{4,0},{6,2},{8,12},{10,14},{12,8},{14,10},{16,20},{18,... | collective-permute-start | bytes 442376 | tf_op jit(solution)/shard_map/ppermute | solution.py:380
  80.0 8.4 %collective-permute-start.12 = (bf16[72,1024]{1,0:T(8,128)(2,1)S(1)}, bf16[72,1024]{1,0:T(8,128)(2,1)S(1)}, u32[]{:S(2)}, u32[]{:S(2)}) collective-permute-start(bf16[72,1024]{1,0:T(8,128)(2,1)S(1)} %get-tuple-element.80), channel_id=1, source_target_pairs={{0,6},{2,4},{4,2},{6,0},{8,14},{10,12},{12,10},{14,8},{16,22},{18,... | collective-permute-start | bytes 442376 | tf_op jit(solution)/shard_map/ppermute | solution.py:380
  85.5 11.5 %collective-permute-start.25 = (bf16[352,1024]{1,0:T(8,128)(2,1)S(1)}, bf16[352,1024]{1,0:T(8,128)(2,1)S(1)}, u32[]{:S(2)}, u32[]{:S(2)}) collective-permute-start(bf16[352,1024]{1,0:T(8,128)(2,1)S(1)} %get-tuple-element.101.refs_7_.refs_4_), channel_id=1, source_target_pairs={{0,1},{1,0},{2,3},{3,2},{4,5},{5,4},{6,7},{7,6},{8,9},{9,8},{10,11... | collective-permute-start | bytes 2162696 | tf_op jit(solution)/shard_map/ppermute | solution.py:517
  85.6 7.4 %collective-permute-start.19 = (f32[4,128]{1,0:T(4,128)S(1)}, f32[4,128]{1,0:T(4,128)S(1)}, u32[]{:S(2)}, u32[]{:S(2)}) collective-permute-start(f32[4,128]{1,0:T(4,128)S(1)} %get-tuple-element.105.refs_2_), channel_id=1, source_target_pairs={{0,16},{2,18},{4,20},{6,22},{8,24},{10,26},{12,28},{14,30},{16,0},... | collective-permute-start | bytes 6152 | tf_op jit(solution)/shard_map/ppermute | solution.py:377
  85.7 5.5 %collective-permute-start.18 = (f32[4,128]{1,0:T(4,128)S(1)}, f32[4,128]{1,0:T(4,128)S(1)}, u32[]{:S(2)}, u32[]{:S(2)}) collective-permute-start(f32[4,128]{1,0:T(4,128)S(1)} %get-tuple-element.106), channel_id=1, source_target_pairs={{0,24},{2,26},{4,28},{6,30},{8,0},{10,2},{12,4},{14,6},{16,8},{18,... | collective-permute-start | bytes 6152 | tf_op jit(solution)/shard_map/ppermute | solution.py:377
  87.6 5.4 %collective-permute-start.20 = (f32[4,128]{1,0:T(4,128)S(1)}, f32[4,128]{1,0:T(4,128)S(1)}, u32[]{:S(2)}, u32[]{:S(2)}) collective-permute-start(f32[4,128]{1,0:T(4,128)S(1)} %get-tuple-element.107), channel_id=1, source_target_pairs={{0,8},{2,10},{4,12},{6,14},{8,16},{10,18},{12,20},{14,22},{16,24},... | collective-permute-start | bytes 6152 | tf_op jit(solution)/shard_map/ppermute | solution.py:377
  93.0 6.0 %collective-permute-start.24 = (bf16[352,1024]{1,0:T(8,128)(2,1)S(1)}, bf16[352,1024]{1,0:T(8,128)(2,1)S(1)}, u32[]{:S(2)}, u32[]{:S(2)}) collective-permute-start(bf16[352,1024]{1,0:T(8,128)(2,1)S(1)} %shard_map.97), channel_id=1, source_target_pairs={{0,1},{1,0},{2,3},{3,2},{4,5},{5,4},{6,7},{7,6},{8,9},{9,8},{10,11... | collective-permute-start | bytes 2162696 | tf_op jit(solution)/shard_map/ppermute | solution.py:517
  93.0 7.3 %collective-permute-start.21 = (f32[4,128]{1,0:T(4,128)S(1)}, f32[4,128]{1,0:T(4,128)S(1)}, u32[]{:S(2)}, u32[]{:S(2)}) collective-permute-start(f32[4,128]{1,0:T(4,128)S(1)} %get-tuple-element.109), channel_id=1, source_target_pairs={{0,2},{2,0},{4,6},{6,4},{8,10},{10,8},{12,14},{14,12},{16,18},{18,... | collective-permute-start | bytes 6152 | tf_op jit(solution)/shard_map/ppermute | solution.py:380
  95.5 4.9 %collective-permute-start.22 = (f32[4,128]{1,0:T(4,128)S(1)}, f32[4,128]{1,0:T(4,128)S(1)}, u32[]{:S(2)}, u32[]{:S(2)}) collective-permute-start(f32[4,128]{1,0:T(4,128)S(1)} %get-tuple-element.110), channel_id=1, source_target_pairs={{0,4},{2,6},{4,0},{6,2},{8,12},{10,14},{12,8},{14,10},{16,20},{18,... | collective-permute-start | bytes 6152 | tf_op jit(solution)/shard_map/ppermute | solution.py:380
  95.9 4.5 %collective-permute-start.23 = (f32[4,128]{1,0:T(4,128)S(1)}, f32[4,128]{1,0:T(4,128)S(1)}, u32[]{:S(2)}, u32[]{:S(2)}) collective-permute-start(f32[4,128]{1,0:T(4,128)S(1)} %get-tuple-element.111), channel_id=1, source_target_pairs={{0,6},{2,4},{4,2},{6,0},{8,14},{10,12},{12,10},{14,8},{16,22},{18,... | collective-permute-start | bytes 6152 | tf_op jit(solution)/shard_map/ppermute | solution.py:380
  97.0 3.4 %copy-start.3 = (s32[128,6]{0,1:T(8,128)S(1)}, s32[128,6]{0,1:T(8,128)}, u32[]{:S(2)}) copy-start(s32[128,6]{0,1:T(8,128)} %param.7) | copy-start | bytes 9220
  97.0 3.4 %copy-start.4 = (s32[128,6]{0,1:T(8,128)S(1)}, s32[128,6]{0,1:T(8,128)}, u32[]{:S(2)}) copy-start(s32[128,6]{0,1:T(8,128)} %param.8) | copy-start | bytes 9220
  97.0 3.4 %copy-start.5 = (f32[16,128]{1,0:T(8,128)S(1)}, f32[16,128]{1,0:T(8,128)}, u32[]{:S(2)}) copy-start(f32[16,128]{1,0:T(8,128)} %get-tuple-element.62.slot_ref) | copy-start | bytes 24580

commit v11 on v10

--- a/solution.py
+++ b/solution.py
@@ -546,7 +546,7 @@
         in_specs=[inside] * (PLANE + 3) + [anywhere],
     )(*final, w_down[0], back, own_hidw, left[0])
     right = partial(model // 2, [own_rows], [])
-    right = [*gated(right[:1], gates[1:]), right[1]]
+    right = [right[0], *gated(right[1:], gates[1:])]
     homes = call(
         functools.partial(combine_kernel, outer),
         [sds((outer, BLOCK), F32)] * PLANE,

time: 101 us -> 104 us (1.030)
  waiting for transfers between devices: 48.3 us -> 51.8 us
    ppermute x9, waiting for transfers between devices: 36.9 us -> 39.8 us  [ring(): return lax.ppermute(array, 'expert', pairs)]
  transfers between devices with their start and end apart: 26 -> 26, of which waited for: 10 -> 13; matrix products, arithmetic and copies ran while one was open for 0% -> 0% of each run, Pallas kernels for 19% -> 19%
where the time goes in v11:
time: 104 us
  waiting for transfers between devices  51.8 us (50%)
  starting transfers between devices  26.2 us (25%)
  Pallas kernels  25.2 us (24%)
    ppermute x9, waiting for transfers between devices, ring(): return lax.ppermute(array, 'expert', pairs)  39.8 us
    ppermute x15, starting transfers between devices, swap(): return lax.ppermute(array, 'expert', [(e, e ^ k) for e in range(experts)])  15.6 us
    ppermute x15, waiting for transfers between devices, swap(): return lax.ppermute(array, 'expert', [(e, e ^ k) for e in range(experts)])  12.1 us
    ppermute x9, starting transfers between devices, ring(): return lax.ppermute(array, 'expert', pairs)  10.5 us
    pallas_call x3, Pallas kernels, stage(): call(functools.partial(stage_kernel, place, [span for _, span in parts],...  6.16 us
    pallas_call x1, Pallas kernels, per_device(): call(functools.partial(open_kernel, slots, flip), [sds((tokens, model + B...  4.9 us
    pallas_call x2, Pallas kernels, finish(): call(functools.partial(finish_kernel, first, fine, len(own), bool(out)),...  3.31 us
    pallas_call x2, Pallas kernels, partial(): call(functools.partial(partial_kernel, first, step, bool(more)), [sds((ha...  2.95 us
  transfers between devices with their start and end apart: 26, of which 13 were waited for; matrix products, arithmetic and copies ran while one was open for 0% of the time, Pallas kernels for 19%

profile of v11, /device:TPU:0, one launch (start us, length us, event | category | flops | bytes accessed | tf_op | source)
XLA Modules:
  0.0 104.2 jit_solution(4365217526889442308)
XLA Ops:
  0.6 4.9 %shard_map.76 = (bf16[128,2176]{1,0:T(8,128)(2,1)}, bf16[72,3840]{1,0:T(8,128)(2,1)}, bf16[72,3840]{1,0:T(8,128)(2,1)}, bf16[72,3840]{1,0:T(8,128)(2,1)}, bf16[72,3840]{1,0:T(8,128)(2,1)}, /*index=5*/f32[16,128]{1,0:T(8,128)}) custom-call(s32[6,128]{1,0:T(8,128)} %bitcast.18, s32[6,128]{1,0:T(8,128)} %bitcast.20, bf16[6,704,128]{2,1,0:T(8,128)(2,1)} %bitcast.23, ...), custom_call_target="tpu_custom_call" | custom-call | flops 1024 | bytes 1024 | tf_op jit(solution)/shard_map/pallas_call | solution.py:387
  5.5 3.1 %collective-permute-start = (bf16[128,2176]{1,0:T(8,128)(2,1)}, bf16[128,2176]{1,0:T(8,128)(2,1)S(1)}, u32[]{:S(2)}, u32[]{:S(2)}) collective-permute-start(bf16[128,2176]{1,0:T(8,128)(2,1)} %get-tuple-element.63.refs_0_), channel_id=1, source_target_pairs={{0,8},{2,10},{4,12},{6,14},{8,16},{10,18},{12,20},{14,22},{16,24},... | collective-permute-start | bytes 1671176 | tf_op jit(solution)/shard_map/ppermute | solution.py:377
  8.6 2.1 %collective-permute-start.1 = (bf16[128,2176]{1,0:T(8,128)(2,1)}, bf16[128,2176]{1,0:T(8,128)(2,1)S(1)}, u32[]{:S(2)}, u32[]{:S(2)}) collective-permute-start(bf16[128,2176]{1,0:T(8,128)(2,1)} %get-tuple-element.63.refs_0_), channel_id=1, source_target_pairs={{0,24},{2,26},{4,28},{6,30},{8,0},{10,2},{12,4},{14,6},{16,8},{18,... | collective-permute-start | bytes 1671176 | tf_op jit(solution)/shard_map/ppermute | solution.py:377
  10.7 1.6 %collective-permute-start.2 = (bf16[72,3840]{1,0:T(8,128)(2,1)}, bf16[72,3840]{1,0:T(8,128)(2,1)S(1)}, u32[]{:S(2)}, u32[]{:S(2)}) collective-permute-start(bf16[72,3840]{1,0:T(8,128)(2,1)} %get-tuple-element.71), channel_id=1, source_target_pairs={{0,2},{2,0},{4,6},{6,4},{8,10},{10,8},{12,14},{14,12},{16,18},{18,... | collective-permute-start | bytes 1658888 | tf_op jit(solution)/shard_map/ppermute | solution.py:380
  12.4 1.5 %collective-permute-start.3 = (bf16[72,3840]{1,0:T(8,128)(2,1)}, bf16[72,3840]{1,0:T(8,128)(2,1)S(1)}, u32[]{:S(2)}, u32[]{:S(2)}) collective-permute-start(bf16[72,3840]{1,0:T(8,128)(2,1)} %get-tuple-element.72), channel_id=1, source_target_pairs={{0,4},{2,6},{4,0},{6,2},{8,12},{10,14},{12,8},{14,10},{16,20},{18,... | collective-permute-start | bytes 1658888 | tf_op jit(solution)/shard_map/ppermute | solution.py:380
  14.2 10.2 %collective-permute-done.refs_0_ = bf16[128,2176]{1,0:T(8,128)(2,1)S(1)} collective-permute-done((bf16[128,2176]{1,0:T(8,128)(2,1)}, bf16[128,2176]{1,0:T(8,128)(2,1)S(1)}, u32[]{:S(2)}, u32[]{:S(2)}) %collective-permute-start) | collective-permute-done | bytes 557088 | tf_op jit(solution)/shard_map/ppermute | solution.py:377
  24.4 10.7 %collective-permute-done.1.refs_1_ = bf16[128,2176]{1,0:T(8,128)(2,1)S(1)} collective-permute-done((bf16[128,2176]{1,0:T(8,128)(2,1)}, bf16[128,2176]{1,0:T(8,128)(2,1)S(1)}, u32[]{:S(2)}, u32[]{:S(2)}) %collective-permute-start.1) | collective-permute-done | bytes 557088 | tf_op jit(solution)/shard_map/ppermute | solution.py:377
  35.9 2.1 %collective-permute-done.3.refs_4_.refs_2_ = bf16[72,3840]{1,0:T(8,128)(2,1)S(1)} collective-permute-done((bf16[72,3840]{1,0:T(8,128)(2,1)}, bf16[72,3840]{1,0:T(8,128)(2,1)S(1)}, u32[]{:S(2)}, u32[]{:S(2)}) %collective-permute-start.3) | collective-permute-done | bytes 552992 | tf_op jit(solution)/shard_map/ppermute | solution.py:380
  38.0 1.2 %collective-permute-start.5 = (bf16[72,4096]{1,0:T(8,128)(2,1)S(1)}, bf16[72,4096]{1,0:T(8,128)(2,1)S(1)}, u32[]{:S(2)}, u32[]{:S(2)}) collective-permute-start(bf16[72,4096]{1,0:T(8,128)(2,1)S(1)} %get-tuple-element.74), channel_id=1, source_target_pairs={{0,2},{2,0},{4,6},{6,4},{8,10},{10,8},{12,14},{14,12},{16,18},{18,... | collective-permute-start | bytes 1769480 | tf_op jit(solution)/shard_map/ppermute | solution.py:380
  40.0 1.4 %collective-permute-start.7 = (bf16[72,4096]{1,0:T(8,128)(2,1)S(1)}, bf16[72,4096]{1,0:T(8,128)(2,1)S(1)}, u32[]{:S(2)}, u32[]{:S(2)}) collective-permute-start(bf16[72,4096]{1,0:T(8,128)(2,1)S(1)} %get-tuple-element.76), channel_id=1, source_target_pairs={{0,6},{2,4},{4,2},{6,0},{8,14},{10,12},{12,10},{14,8},{16,22},{18,... | collective-permute-start | bytes 1769480 | tf_op jit(solution)/shard_map/ppermute | solution.py:380
  41.7 8.2 %collective-permute-done.8.refs_4_.refs_0_ = bf16[128,2176]{1,0:T(8,128)(2,1)S(1)} collective-permute-done((bf16[128,2176]{1,0:T(8,128)(2,1)S(1)}, bf16[128,2176]{1,0:T(8,128)(2,1)S(1)}, u32[]{:S(2)}, u32[]{:S(2)}) %collective-permute-start.8) | collective-permute-done | bytes 557088 | tf_op jit(solution)/shard_map/ppermute | solution.py:377
  50.0 2.1 %collective-permute-start.9 = (bf16[2,72,1408]{2,1,0:T(8,128)(2,1)S(1)}, bf16[2,72,1408]{2,1,0:T(8,128)(2,1)S(1)}, u32[]{:S(2)}, u32[]{:S(2)}) collective-permute-start(bf16[2,72,1408]{2,1,0:T(8,128)(2,1)S(1)} %shard_map.80), channel_id=1, source_target_pairs={{0,24},{2,26},{4,28},{6,30},{8,0},{10,2},{12,4},{14,6},{16,8},{18,... | collective-permute-start | bytes 1216520 | tf_op jit(solution)/shard_map/ppermute | solution.py:377
  52.7 1.4 %shard_map.83 = (bf16[768,2048]{1,0:T(8,128)(2,1)S(1)}, bf16[704,768]{1,0:T(8,128)(2,1)S(1)}, f32[704,384]{1,0:T(8,128)S(1)}, bf16[704,384]{1,0:T(8,128)(2,1)S(1)}) custom-call(bf16[72,3840]{1,0:T(8,128)(2,1)S(1)} %copy-done.1, bf16[72,3840]{1,0:T(8,128)(2,1)S(1)} %collective-permute-done.2.refs_3_.refs_1_, ...), custom_call_target="tpu_custom_call" | custom-call | flops 2000000000 | bytes 1024 | tf_op jit(solution)/shard_map/pallas_call | solution.py:480
  54.6 3.8 %collective-permute-done.13.refs_3_.refs_5_ = bf16[2,72,1408]{2,1,0:T(8,128)(2,1)S(1)} collective-permute-done((bf16[2,72,1408]{2,1,0:T(8,128)(2,1)S(1)}, bf16[2,72,1408]{2,1,0:T(8,128)(2,1)S(1)}, u32[]{:S(2)}, u32[]{:S(2)}) %collective-permute-start.13) | collective-permute-done | bytes 405536 | tf_op jit(solution)/shard_map/ppermute | solution.py:377
  58.5 1.5 %collective-permute-start.14 = (bf16[72,2048]{1,0:T(8,128)(2,1)S(1)}, bf16[72,2048]{1,0:T(8,128)(2,1)S(1)}, u32[]{:S(2)}, u32[]{:S(2)}) collective-permute-start(bf16[72,2048]{1,0:T(8,128)(2,1)S(1)} %get-tuple-element.87), channel_id=1, source_target_pairs={{0,2},{2,0},{4,6},{6,4},{8,10},{10,8},{12,14},{14,12},{16,18},{18,... | collective-permute-start | bytes 884744 | tf_op jit(solution)/shard_map/ppermute | solution.py:380
  60.1 1.6 %collective-permute-start.15 = (bf16[72,2048]{1,0:T(8,128)(2,1)S(1)}, bf16[72,2048]{1,0:T(8,128)(2,1)S(1)}, u32[]{:S(2)}, u32[]{:S(2)}) collective-permute-start(bf16[72,2048]{1,0:T(8,128)(2,1)S(1)} %get-tuple-element.88), channel_id=1, source_target_pairs={{0,4},{2,6},{4,0},{6,2},{8,12},{10,14},{12,8},{14,10},{16,20},{18,... | collective-permute-start | bytes 884744 | tf_op jit(solution)/shard_map/ppermute | solution.py:380
  61.7 2.7 %collective-permute-done.6.refs_4_.refs_2_ = bf16[72,4096]{1,0:T(8,128)(2,1)S(1)} collective-permute-done((bf16[72,4096]{1,0:T(8,128)(2,1)S(1)}, bf16[72,4096]{1,0:T(8,128)(2,1)S(1)}, u32[]{:S(2)}, u32[]{:S(2)}) %collective-permute-start.6) | collective-permute-done | bytes 589856 | tf_op jit(solution)/shard_map/ppermute | solution.py:380
  64.4 3.5 %collective-permute-done.7.refs_5_.refs_3_ = bf16[72,4096]{1,0:T(8,128)(2,1)S(1)} collective-permute-done((bf16[72,4096]{1,0:T(8,128)(2,1)S(1)}, bf16[72,4096]{1,0:T(8,128)(2,1)S(1)}, u32[]{:S(2)}, u32[]{:S(2)}) %collective-permute-start.7) | collective-permute-done | bytes 589856 | tf_op jit(solution)/shard_map/ppermute | solution.py:380
  68.6 2.1 %shard_map.88 = (bf16[768,2048]{1,0:T(8,128)(2,1)S(1)}, bf16[704,768]{1,0:T(8,128)(2,1)S(1)}, f32[4,128]{1,0:T(4,128)S(1)}) custom-call(bf16[72,4096]{1,0:T(8,128)(2,1)S(1)} %get-tuple-element.92.refs_0_, bf16[72,4096]{1,0:T(8,128)(2,1)S(1)} %collective-permute-done.5.refs_3_.refs_1_, bf16[72,4096]{1,0:T(8,128)(2,1)S(1)} %collective-permute-done.6.refs_4_.refs_2_, ...), custom_call_target="tpu_custom_call" | custom-call | flops 2000000000 | bytes 1024 | tf_op jit(solution)/shard_map/pallas_call | solution.py:450
  71.6 2.0 %shard_map.89 = (bf16[768,2048]{1,0:T(8,128)(2,1)S(1)}, bf16[704,768]{1,0:T(8,128)(2,1)S(1)}, f32[4,128]{1,0:T(4,128)S(1)}) custom-call(bf16[72,4096]{1,0:T(8,128)(2,1)S(1)} %get-tuple-element.92.refs_0_, bf16[72,4096]{1,0:T(8,128)(2,1)S(1)} %collective-permute-done.5.refs_3_.refs_1_, ...), custom_call_target="tpu_custom_call", output_to_operand_aliasing={{0}: (6, {}), {1}: (7, {})} | custom-call | flops 2000000000 | bytes 1024 | tf_op jit(solution)/shard_map/pallas_call | solution.py:450
  73.7 2.4 %shard_map.90 = (bf16[704,2048]{1,0:T(8,128)(2,1)S(1)}, f32[8,128]{1,0:T(8,128)S(1)}) custom-call(bf16[768,2048]{1,0:T(8,128)(2,1)S(1)} %get-tuple-element.95.rows_ref, bf16[704,768]{1,0:T(8,128)(2,1)S(1)} %get-tuple-element.96.hidw_ref), custom_call_target="tpu_custom_call" | custom-call | flops 3500000000 | bytes 1024 | tf_op jit(solution)/shard_map/pallas_call | solution.py:475
  77.0 3.0 %collective-permute-done.15.refs_2_ = bf16[72,2048]{1,0:T(8,128)(2,1)S(1)} collective-permute-done((bf16[72,2048]{1,0:T(8,128)(2,1)S(1)}, bf16[72,2048]{1,0:T(8,128)(2,1)S(1)}, u32[]{:S(2)}, u32[]{:S(2)}) %collective-permute-start.15) | collective-permute-done | bytes 294944 | tf_op jit(solution)/shard_map/ppermute | solution.py:380
  80.0 2.1 %collective-permute-done.17.refs_5_ = bf16[2,72,1408]{2,1,0:T(8,128)(2,1)S(1)} collective-permute-done((bf16[2,72,1408]{2,1,0:T(8,128)(2,1)S(1)}, bf16[2,72,1408]{2,1,0:T(8,128)(2,1)S(1)}, u32[]{:S(2)}, u32[]{:S(2)}) %collective-permute-start.17) | collective-permute-done | bytes 405536 | tf_op jit(solution)/shard_map/ppermute | solution.py:377
  82.2 2.1 %shard_map.91 = (bf16[768,2048]{1,0:T(8,128)(2,1)S(1)}, bf16[704,768]{1,0:T(8,128)(2,1)S(1)}, f32[4,128]{1,0:T(4,128)S(1)}) custom-call(bf16[72,2048]{1,0:T(8,128)(2,1)S(1)} %get-tuple-element.83.refs_0_, bf16[72,2048]{1,0:T(8,128)(2,1)S(1)} %collective-permute-done.14.refs_1_, ...), custom_call_target="tpu_custom_call", output_to_operand_aliasing={{0}: (6, {}), {1}: (7, {})} | custom-call | flops 2000000000 | bytes 1024 | tf_op jit(solution)/shard_map/pallas_call | solution.py:450
  84.2 1.3 %shard_map.92 = (bf16[352,1024]{1,0:T(8,128)(2,1)S(1)}, bf16[352,1024]{1,0:T(8,128)(2,1)S(1)}) custom-call(bf16[768,2048]{1,0:T(8,128)(2,1)S(1)} %get-tuple-element.98.rows_ref, bf16[704,768]{1,0:T(8,128)(2,1)S(1)} %get-tuple-element.99.hidw_ref, bf16[704,2048]{1,0:T(8,128)(2,1)S(1)} %get-tuple-element.100.early_ref), custom_call_target="tpu_custom_call" | custom-call | flops 4000000000 | bytes 1024 | tf_op jit(solution)/shard_map/pallas_call | solution.py:508
  87.2 1.7 %shard_map.96 = (bf16[352,1024]{1,0:T(8,128)(2,1)S(1)}, bf16[352,1024]{1,0:T(8,128)(2,1)S(1)}) custom-call(bf16[768,2048]{1,0:T(8,128)(2,1)S(1)} %get-tuple-element.98.rows_ref, bf16[704,768]{1,0:T(8,128)(2,1)S(1)} %get-tuple-element.99.hidw_ref, bf16[704,2048]{1,0:T(8,128)(2,1)S(1)} %get-tuple-element.100.early_ref, ...), custom_call_target="tpu_custom_call" | custom-call | flops 4000000000 | bytes 1024 | tf_op jit(solution)/shard_map/pallas_call | solution.py:508
  88.9 1.9 %collective-permute-start.18 = (f32[4,128]{1,0:T(4,128)S(1)}, f32[4,128]{1,0:T(4,128)S(1)}, u32[]{:S(2)}, u32[]{:S(2)}) collective-permute-start(f32[4,128]{1,0:T(4,128)S(1)} %get-tuple-element.106), channel_id=1, source_target_pairs={{0,24},{2,26},{4,28},{6,30},{8,0},{10,2},{12,4},{14,6},{16,8},{18,... | collective-permute-start | bytes 6152 | tf_op jit(solution)/shard_map/ppermute | solution.py:377
  91.5 1.1 %collective-permute-done.18.refs_1_ = f32[4,128]{1,0:T(4,128)S(1)} collective-permute-done((f32[4,128]{1,0:T(4,128)S(1)}, f32[4,128]{1,0:T(4,128)S(1)}, u32[]{:S(2)}, u32[]{:S(2)}) %collective-permute-start.18) | collective-permute-done | bytes 2080 | tf_op jit(solution)/shard_map/ppermute | solution.py:377
  92.6 3.6 %collective-permute-done.20.refs_3_ = f32[4,128]{1,0:T(4,128)S(1)} collective-permute-done((f32[4,128]{1,0:T(4,128)S(1)}, f32[4,128]{1,0:T(4,128)S(1)}, u32[]{:S(2)}, u32[]{:S(2)}) %collective-permute-start.20) | collective-permute-done | bytes 2080 | tf_op jit(solution)/shard_map/ppermute | solution.py:377
  96.2 2.2 %collective-permute-start.21 = (f32[4,128]{1,0:T(4,128)S(1)}, f32[4,128]{1,0:T(4,128)S(1)}, u32[]{:S(2)}, u32[]{:S(2)}) collective-permute-start(f32[4,128]{1,0:T(4,128)S(1)} %get-tuple-element.109), channel_id=1, source_target_pairs={{0,2},{2,0},{4,6},{6,4},{8,10},{10,8},{12,14},{14,12},{16,18},{18,... | collective-permute-start | bytes 6152 | tf_op jit(solution)/shard_map/ppermute | solution.py:380
  99.9 1.9 %shard_map.98 = (f32[352,2048]{1,0:T(8,128)}, f32[16,352]{1,0:T(8,128)}, f32[8,128]{1,0:T(8,128)}) custom-call(bf16[352,1024]{1,0:T(8,128)(2,1)S(1)} %get-tuple-element.115.refs_0_, bf16[1,352,1024]{2,1,0:T(8,128)(2,1)S(1)} %bitcast.16), custom_call_target="tpu_custom_call" | custom-call | flops 1024 | bytes 1024 | tf_op jit(solution)/shard_map/pallas_call | solution.py:532
  101.9 1.4 %shard_map.99 = (f32[352,2048]{1,0:T(8,128)}, f32[16,352]{1,0:T(8,128)}, f32[8,128]{1,0:T(8,128)S(1)}) custom-call(bf16[352,1024]{1,0:T(8,128)(2,1)S(1)} %shard_map.97.refs_0_, bf16[1,352,1024]{2,1,0:T(8,128)(2,1)S(1)} %bitcast.17, f32[352,2048]{1,0:T(8,128)} %get-tuple-element.116.refs_2_, ...), custom_call_target="tpu_custom_call", output_to_operand_aliasing={{0}: (2, {}), {1}: (3, {})} | custom-call | flops 1024 | bytes 1024 | tf_op jit(solution)/shard_map/pallas_call | solution.py:532
  (57 shorter events, 10.9 us)
Async XLA Ops:
  5.5 35.9 %copy-start.1 = (bf16[72,3840]{1,0:T(8,128)(2,1)S(1)}, bf16[72,3840]{1,0:T(8,128)(2,1)}, u32[]{:S(2)}) copy-start(bf16[72,3840]{1,0:T(8,128)(2,1)} %get-tuple-element.77.refs_0_) | copy-start | bytes 1658884
  5.5 18.8 %collective-permute-start = (bf16[128,2176]{1,0:T(8,128)(2,1)}, bf16[128,2176]{1,0:T(8,128)(2,1)S(1)}, u32[]{:S(2)}, u32[]{:S(2)}) collective-permute-start(bf16[128,2176]{1,0:T(8,128)(2,1)} %get-tuple-element.63.refs_0_), channel_id=1, source_target_pairs={{0,8},{2,10},{4,12},{6,14},{8,16},{10,18},{12,20},{14,22},{16,24},... | collective-permute-start | bytes 1671176 | tf_op jit(solution)/shard_map/ppermute | solution.py:377
  8.6 26.5 %collective-permute-start.1 = (bf16[128,2176]{1,0:T(8,128)(2,1)}, bf16[128,2176]{1,0:T(8,128)(2,1)S(1)}, u32[]{:S(2)}, u32[]{:S(2)}) collective-permute-start(bf16[128,2176]{1,0:T(8,128)(2,1)} %get-tuple-element.63.refs_0_), channel_id=1, source_target_pairs={{0,24},{2,26},{4,28},{6,30},{8,0},{10,2},{12,4},{14,6},{16,8},{18,... | collective-permute-start | bytes 1671176 | tf_op jit(solution)/shard_map/ppermute | solution.py:377
  10.7 25.2 %collective-permute-start.2 = (bf16[72,3840]{1,0:T(8,128)(2,1)}, bf16[72,3840]{1,0:T(8,128)(2,1)S(1)}, u32[]{:S(2)}, u32[]{:S(2)}) collective-permute-start(bf16[72,3840]{1,0:T(8,128)(2,1)} %get-tuple-element.71), channel_id=1, source_target_pairs={{0,2},{2,0},{4,6},{6,4},{8,10},{10,8},{12,14},{14,12},{16,18},{18,... | collective-permute-start | bytes 1658888 | tf_op jit(solution)/shard_map/ppermute | solution.py:380
  12.4 25.6 %collective-permute-start.3 = (bf16[72,3840]{1,0:T(8,128)(2,1)}, bf16[72,3840]{1,0:T(8,128)(2,1)S(1)}, u32[]{:S(2)}, u32[]{:S(2)}) collective-permute-start(bf16[72,3840]{1,0:T(8,128)(2,1)} %get-tuple-element.72), channel_id=1, source_target_pairs={{0,4},{2,6},{4,0},{6,2},{8,12},{10,14},{12,8},{14,10},{16,20},{18,... | collective-permute-start | bytes 1658888 | tf_op jit(solution)/shard_map/ppermute | solution.py:380
  13.9 24.1 %collective-permute-start.4 = (bf16[72,3840]{1,0:T(8,128)(2,1)}, bf16[72,3840]{1,0:T(8,128)(2,1)S(1)}, u32[]{:S(2)}, u32[]{:S(2)}) collective-permute-start(bf16[72,3840]{1,0:T(8,128)(2,1)} %get-tuple-element.73), channel_id=1, source_target_pairs={{0,6},{2,4},{4,2},{6,0},{8,14},{10,12},{12,10},{14,8},{16,22},{18,... | collective-permute-start | bytes 1658888 | tf_op jit(solution)/shard_map/ppermute | solution.py:380
  24.4 25.5 %collective-permute-start.8 = (bf16[128,2176]{1,0:T(8,128)(2,1)S(1)}, bf16[128,2176]{1,0:T(8,128)(2,1)S(1)}, u32[]{:S(2)}, u32[]{:S(2)}) collective-permute-start(bf16[128,2176]{1,0:T(8,128)(2,1)S(1)} %collective-permute-done.refs_0_), channel_id=1, source_target_pairs={{0,8},{2,10},{4,12},{6,14},{8,16},{10,18},{12,20},{14,22},{16,24},... | collective-permute-start | bytes 1671176 | tf_op jit(solution)/shard_map/ppermute | solution.py:377
  38.0 22.1 %collective-permute-start.5 = (bf16[72,4096]{1,0:T(8,128)(2,1)S(1)}, bf16[72,4096]{1,0:T(8,128)(2,1)S(1)}, u32[]{:S(2)}, u32[]{:S(2)}) collective-permute-start(bf16[72,4096]{1,0:T(8,128)(2,1)S(1)} %get-tuple-element.74), channel_id=1, source_target_pairs={{0,2},{2,0},{4,6},{6,4},{8,10},{10,8},{12,14},{14,12},{16,18},{18,... | collective-permute-start | bytes 1769480 | tf_op jit(solution)/shard_map/ppermute | solution.py:380
  39.2 25.2 %collective-permute-start.6 = (bf16[72,4096]{1,0:T(8,128)(2,1)S(1)}, bf16[72,4096]{1,0:T(8,128)(2,1)S(1)}, u32[]{:S(2)}, u32[]{:S(2)}) collective-permute-start(bf16[72,4096]{1,0:T(8,128)(2,1)S(1)} %get-tuple-element.75), channel_id=1, source_target_pairs={{0,4},{2,6},{4,0},{6,2},{8,12},{10,14},{12,8},{14,10},{16,20},{18,... | collective-permute-start | bytes 1769480 | tf_op jit(solution)/shard_map/ppermute | solution.py:380
  40.0 27.9 %collective-permute-start.7 = (bf16[72,4096]{1,0:T(8,128)(2,1)S(1)}, bf16[72,4096]{1,0:T(8,128)(2,1)S(1)}, u32[]{:S(2)}, u32[]{:S(2)}) collective-permute-start(bf16[72,4096]{1,0:T(8,128)(2,1)S(1)} %get-tuple-element.76), channel_id=1, source_target_pairs={{0,6},{2,4},{4,2},{6,0},{8,14},{10,12},{12,10},{14,8},{16,22},{18,... | collective-permute-start | bytes 1769480 | tf_op jit(solution)/shard_map/ppermute | solution.py:380
  41.5 10.7 %copy-start.2 = (bf16[128,2176]{1,0:T(8,128)(2,1)S(1)}, bf16[128,2176]{1,0:T(8,128)(2,1)}, u32[]{:S(2)}) copy-start(bf16[128,2176]{1,0:T(8,128)(2,1)} %get-tuple-element.63.refs_0_) | copy-start | bytes 1671172
  41.6 11.1 %copy-start = (bf16[1,704,2048]{2,1,0:T(8,128)(2,1)S(1)}, bf16[1,704,2048]{2,1,0:T(8,128)(2,1)}, u32[]{:S(2)}) copy-start(bf16[1,704,2048]{2,1,0:T(8,128)(2,1)} %param.9) | copy-start | bytes 8650756
  41.6 16.9 %collective-permute-start.13 = (bf16[2,72,1408]{2,1,0:T(8,128)(2,1)S(1)}, bf16[2,72,1408]{2,1,0:T(8,128)(2,1)S(1)}, u32[]{:S(2)}, u32[]{:S(2)}) collective-permute-start(bf16[2,72,1408]{2,1,0:T(8,128)(2,1)S(1)} %shard_map.85), channel_id=1, source_target_pairs={{0,8},{2,10},{4,12},{6,14},{8,16},{10,18},{12,20},{14,22},{16,24},... | collective-permute-start | bytes 1216520 | tf_op jit(solution)/shard_map/ppermute | solution.py:377
  50.0 20.6 %collective-permute-start.9 = (bf16[2,72,1408]{2,1,0:T(8,128)(2,1)S(1)}, bf16[2,72,1408]{2,1,0:T(8,128)(2,1)S(1)}, u32[]{:S(2)}, u32[]{:S(2)}) collective-permute-start(bf16[2,72,1408]{2,1,0:T(8,128)(2,1)S(1)} %shard_map.80), channel_id=1, source_target_pairs={{0,24},{2,26},{4,28},{6,30},{8,0},{10,2},{12,4},{14,6},{16,8},{18,... | collective-permute-start | bytes 1216520 | tf_op jit(solution)/shard_map/ppermute | solution.py:377
  58.5 17.6 %collective-permute-start.14 = (bf16[72,2048]{1,0:T(8,128)(2,1)S(1)}, bf16[72,2048]{1,0:T(8,128)(2,1)S(1)}, u32[]{:S(2)}, u32[]{:S(2)}) collective-permute-start(bf16[72,2048]{1,0:T(8,128)(2,1)S(1)} %get-tuple-element.87), channel_id=1, source_target_pairs={{0,2},{2,0},{4,6},{6,4},{8,10},{10,8},{12,14},{14,12},{16,18},{18,... | collective-permute-start | bytes 884744 | tf_op jit(solution)/shard_map/ppermute | solution.py:380
  60.1 19.9 %collective-permute-start.15 = (bf16[72,2048]{1,0:T(8,128)(2,1)S(1)}, bf16[72,2048]{1,0:T(8,128)(2,1)S(1)}, u32[]{:S(2)}, u32[]{:S(2)}) collective-permute-start(bf16[72,2048]{1,0:T(8,128)(2,1)S(1)} %get-tuple-element.88), channel_id=1, source_target_pairs={{0,4},{2,6},{4,0},{6,2},{8,12},{10,14},{12,8},{14,10},{16,20},{18,... | collective-permute-start | bytes 884744 | tf_op jit(solution)/shard_map/ppermute | solution.py:380
  64.4 15.6 %collective-permute-start.16 = (bf16[72,2048]{1,0:T(8,128)(2,1)S(1)}, bf16[72,2048]{1,0:T(8,128)(2,1)S(1)}, u32[]{:S(2)}, u32[]{:S(2)}) collective-permute-start(bf16[72,2048]{1,0:T(8,128)(2,1)S(1)} %get-tuple-element.89), channel_id=1, source_target_pairs={{0,6},{2,4},{4,2},{6,0},{8,14},{10,12},{12,10},{14,8},{16,22},{18,... | collective-permute-start | bytes 884744 | tf_op jit(solution)/shard_map/ppermute | solution.py:380
  67.9 14.2 %collective-permute-start.17 = (bf16[2,72,1408]{2,1,0:T(8,128)(2,1)S(1)}, bf16[2,72,1408]{2,1,0:T(8,128)(2,1)S(1)}, u32[]{:S(2)}, u32[]{:S(2)}) collective-permute-start(bf16[2,72,1408]{2,1,0:T(8,128)(2,1)S(1)} %shard_map.87), channel_id=1, source_target_pairs={{0,16},{2,18},{4,20},{6,22},{8,24},{10,26},{12,28},{14,30},{16,0},... | collective-permute-start | bytes 1216520 | tf_op jit(solution)/shard_map/ppermute | solution.py:377
  70.6 15.0 %collective-permute-start.10 = (bf16[72,1024]{1,0:T(8,128)(2,1)S(1)}, bf16[72,1024]{1,0:T(8,128)(2,1)S(1)}, u32[]{:S(2)}, u32[]{:S(2)}) collective-permute-start(bf16[72,1024]{1,0:T(8,128)(2,1)S(1)} %get-tuple-element.78), channel_id=1, source_target_pairs={{0,2},{2,0},{4,6},{6,4},{8,10},{10,8},{12,14},{14,12},{16,18},{18,... | collective-permute-start | bytes 442376 | tf_op jit(solution)/shard_map/ppermute | solution.py:380
  76.1 9.5 %collective-permute-start.11 = (bf16[72,1024]{1,0:T(8,128)(2,1)S(1)}, bf16[72,1024]{1,0:T(8,128)(2,1)S(1)}, u32[]{:S(2)}, u32[]{:S(2)}) collective-permute-start(bf16[72,1024]{1,0:T(8,128)(2,1)S(1)} %get-tuple-element.79), channel_id=1, source_target_pairs={{0,4},{2,6},{4,0},{6,2},{8,12},{10,14},{12,8},{14,10},{16,20},{18,... | collective-permute-start | bytes 442376 | tf_op jit(solution)/shard_map/ppermute | solution.py:380
  80.0 6.0 %collective-permute-start.12 = (bf16[72,1024]{1,0:T(8,128)(2,1)S(1)}, bf16[72,1024]{1,0:T(8,128)(2,1)S(1)}, u32[]{:S(2)}, u32[]{:S(2)}) collective-permute-start(bf16[72,1024]{1,0:T(8,128)(2,1)S(1)} %get-tuple-element.80), channel_id=1, source_target_pairs={{0,6},{2,4},{4,2},{6,0},{8,14},{10,12},{12,10},{14,8},{16,22},{18,... | collective-permute-start | bytes 442376 | tf_op jit(solution)/shard_map/ppermute | solution.py:380
  85.5 14.4 %collective-permute-start.25 = (bf16[352,1024]{1,0:T(8,128)(2,1)S(1)}, bf16[352,1024]{1,0:T(8,128)(2,1)S(1)}, u32[]{:S(2)}, u32[]{:S(2)}) collective-permute-start(bf16[352,1024]{1,0:T(8,128)(2,1)S(1)} %get-tuple-element.101.refs_7_.refs_4_), channel_id=1, source_target_pairs={{0,1},{1,0},{2,3},{3,2},{4,5},{5,4},{6,7},{7,6},{8,9},{9,8},{10,11... | collective-permute-start | bytes 2162696 | tf_op jit(solution)/shard_map/ppermute | solution.py:517
  88.8 13.1 %collective-permute-start.24 = (bf16[352,1024]{1,0:T(8,128)(2,1)S(1)}, bf16[352,1024]{1,0:T(8,128)(2,1)S(1)}, u32[]{:S(2)}, u32[]{:S(2)}) collective-permute-start(bf16[352,1024]{1,0:T(8,128)(2,1)S(1)} %get-tuple-element.114), channel_id=1, source_target_pairs={{0,1},{1,0},{2,3},{3,2},{4,5},{5,4},{6,7},{7,6},{8,9},{9,8},{10,11... | collective-permute-start | bytes 2162696 | tf_op jit(solution)/shard_map/ppermute | solution.py:517
  88.9 3.6 %collective-permute-start.18 = (f32[4,128]{1,0:T(4,128)S(1)}, f32[4,128]{1,0:T(4,128)S(1)}, u32[]{:S(2)}, u32[]{:S(2)}) collective-permute-start(f32[4,128]{1,0:T(4,128)S(1)} %get-tuple-element.106), channel_id=1, source_target_pairs={{0,24},{2,26},{4,28},{6,30},{8,0},{10,2},{12,4},{14,6},{16,8},{18,... | collective-permute-start | bytes 6152 | tf_op jit(solution)/shard_map/ppermute | solution.py:377
  90.8 5.4 %collective-permute-start.20 = (f32[4,128]{1,0:T(4,128)S(1)}, f32[4,128]{1,0:T(4,128)S(1)}, u32[]{:S(2)}, u32[]{:S(2)}) collective-permute-start(f32[4,128]{1,0:T(4,128)S(1)} %get-tuple-element.107), channel_id=1, source_target_pairs={{0,8},{2,10},{4,12},{6,14},{8,16},{10,18},{12,20},{14,22},{16,24},... | collective-permute-start | bytes 6152 | tf_op jit(solution)/shard_map/ppermute | solution.py:377
  91.0 5.2 %collective-permute-start.19 = (f32[4,128]{1,0:T(4,128)S(1)}, f32[4,128]{1,0:T(4,128)S(1)}, u32[]{:S(2)}, u32[]{:S(2)}) collective-permute-start(f32[4,128]{1,0:T(4,128)S(1)} %get-tuple-element.105.refs_2_), channel_id=1, source_target_pairs={{0,16},{2,18},{4,20},{6,22},{8,24},{10,26},{12,28},{14,30},{16,0},... | collective-permute-start | bytes 6152 | tf_op jit(solution)/shard_map/ppermute | solution.py:377
  96.2 7.1 %collective-permute-start.21 = (f32[4,128]{1,0:T(4,128)S(1)}, f32[4,128]{1,0:T(4,128)S(1)}, u32[]{:S(2)}, u32[]{:S(2)}) collective-permute-start(f32[4,128]{1,0:T(4,128)S(1)} %get-tuple-element.109), channel_id=1, source_target_pairs={{0,2},{2,0},{4,6},{6,4},{8,10},{10,8},{12,14},{14,12},{16,18},{18,... | collective-permute-start | bytes 6152 | tf_op jit(solution)/shard_map/ppermute | solution.py:380
  98.4 4.9 %collective-permute-start.22 = (f32[4,128]{1,0:T(4,128)S(1)}, f32[4,128]{1,0:T(4,128)S(1)}, u32[]{:S(2)}, u32[]{:S(2)}) collective-permute-start(f32[4,128]{1,0:T(4,128)S(1)} %get-tuple-element.110), channel_id=1, source_target_pairs={{0,4},{2,6},{4,0},{6,2},{8,12},{10,14},{12,8},{14,10},{16,20},{18,... | collective-permute-start | bytes 6152 | tf_op jit(solution)/shard_map/ppermute | solution.py:380
  99.0 4.5 %collective-permute-start.23 = (f32[4,128]{1,0:T(4,128)S(1)}, f32[4,128]{1,0:T(4,128)S(1)}, u32[]{:S(2)}, u32[]{:S(2)}) collective-permute-start(f32[4,128]{1,0:T(4,128)S(1)} %get-tuple-element.111), channel_id=1, source_target_pairs={{0,6},{2,4},{4,2},{6,0},{8,14},{10,12},{12,10},{14,8},{16,22},{18,... | collective-permute-start | bytes 6152 | tf_op jit(solution)/shard_map/ppermute | solution.py:380
  99.9 3.6 %copy-start.3 = (s32[128,6]{0,1:T(8,128)S(1)}, s32[128,6]{0,1:T(8,128)}, u32[]{:S(2)}) copy-start(s32[128,6]{0,1:T(8,128)} %param.7) | copy-start | bytes 9220
  99.9 3.6 %copy-start.4 = (s32[128,6]{0,1:T(8,128)S(1)}, s32[128,6]{0,1:T(8,128)}, u32[]{:S(2)}) copy-start(s32[128,6]{0,1:T(8,128)} %param.8) | copy-start | bytes 9220
  99.9 3.6 %copy-start.5 = (f32[16,128]{1,0:T(8,128)S(1)}, f32[16,128]{1,0:T(8,128)}, u32[]{:S(2)}) copy-start(f32[16,128]{1,0:T(8,128)} %get-tuple-element.62.slot_ref) | copy-start | bytes 24580
